TPU v7x, 512 devices: a whole 4x8x8 slice. The times are simulated.
512 devices in a mesh: row: 8 (over y), col: 2 (over z_hi), ctx: 32 (over x, z_lo, core).
Axes of the slice: x: 4, y: 8, z: 8 (z_hi: 2, z_lo: 4; z = z_hi * 4 + z_lo), core: 2. Of those that a mesh axis runs over, the one named last changes fastest.
Arguments:
- featured: bfloat16 [16384, 3, 4096], P('ctx', None, ('row', 'col')), may hold values from -6 to 6
- feat_taps: float32 [3, 7, 4096], P(None, None, ('row', 'col')), may hold values from -2.5 to 2.5
- inner_taps: float32 [7, 4096], P(None, ('row', 'col')), may hold values from -2.5 to 2.5
- out_weight: bfloat16 [4096, 4096], P('row', 'col'), may hold values from -0.09375 to 0.09375
- out_grad: bfloat16 [16384, 4096], P('ctx', ('col', 'row')), may hold values from -6 to 6
Outputs:
- grad_features: bfloat16 [16384, 3, 4096], P('ctx', None, ('row', 'col'))
- grad_weight: bfloat16 [4096, 4096], P(('row', 'ctx'), 'col')
- grad_feat_taps: float32 [3, 7, 4096], P(None, None, ('row', 'col'))
- grad_inner_taps: float32 [7, 4096], P(None, ('row', 'col'))
All inputs are finite; a program needn't handle non-finite values.
Results may differ from a plain program's by a relative error of at most 0.0049.
Values may be sent and summed in bfloat16 or wider, within the bound.
No kernel may reach another device: no remote copies, remote signals or barrier semaphores. Data moves between devices by JAX's collectives and lax.ppermute only.
A program may use at most 64 MiB of HBM per device.

v0:
```python
import math

import jax
import jax.numpy as jnp
from jax import lax
from jax.sharding import PartitionSpec as P

TAPS = 7


def shifted(value, axis, steps):
    count = lax.axis_size(axis)
    first, last = (max(0, -steps), min(count, count - steps))
    return lax.ppermute(value, axis, [(source, source + steps) for source in range(first, last)])


def causal_from(source, taps, out_len, lead):
    result = taps[0] * source[lead : lead + out_len]
    for tap_index in range(1, taps.shape[0]):
        result = result + taps[tap_index] * source[lead - tap_index : lead - tap_index + out_len]
    return result


def body(featured, feat_taps, inner_taps, out_weight, out_grad):
    tok_rows = featured.shape[0]
    reach = TAPS - 1
    inv_root = 1.0 / math.sqrt(tok_rows * lax.axis_size("ctx"))
    before = shifted(featured[tok_rows - 2 * reach :], "ctx", 1)
    extended = jnp.concatenate([before, featured], axis=0).astype(jnp.float32)
    mixed = [
        causal_from(extended[:, j, :], feat_taps[j], tok_rows + reach, reach) for j in range(3)
    ]
    product_ext = mixed[1] * mixed[2]
    window = causal_from(product_ext, inner_taps, tok_rows, reach)
    query = mixed[0][reach:]
    key_part = mixed[1][reach:]
    value = mixed[2][reach:]
    gated = (query * window).astype(jnp.bfloat16)
    gathered_grad = lax.all_gather(out_grad, "row", axis=1, tiled=True)
    full_grad = lax.all_gather(gathered_grad, "col", axis=1, tiled=True)
    own_weight = lax.all_to_all(out_weight, "col", split_axis=0, concat_axis=1, tiled=True)
    grad_gated = lax.dot_general(
        full_grad, own_weight, (((1,), (1,)), ((), ())), preferred_element_type=jnp.float32
    )
    gathered_gated = lax.all_gather(gated, "col", axis=1, tiled=True)
    weight_term = (
        lax.dot_general(
            gathered_gated,
            gathered_grad,
            (((0,), (0,)), ((), ())),
            preferred_element_type=jnp.float32,
        )
        * inv_root
    )
    grad_weight = lax.psum_scatter(weight_term, "ctx", scatter_dimension=0, tiled=True).astype(
        jnp.bfloat16
    )
    grad_query = grad_gated * window
    grad_window = grad_gated * query
    after_window = shifted(grad_window[:reach], "ctx", -1)
    ext_window = jnp.concatenate([grad_window, after_window], axis=0)
    grad_product = inner_taps[0] * ext_window[:tok_rows]
    for tap_index in range(1, TAPS):
        grad_product = (
            grad_product + inner_taps[tap_index] * ext_window[tap_index : tap_index + tok_rows]
        )
    grad_key = grad_product * value
    grad_value = grad_product * key_part
    grad_mixed = jnp.stack([grad_query, grad_key, grad_value], axis=1)
    after_mixed = shifted(grad_mixed[:reach], "ctx", -1)
    ext_mixed = jnp.concatenate([grad_mixed, after_mixed], axis=0)
    grad_local = feat_taps[:, 0, :][None] * ext_mixed[:tok_rows]
    for tap_index in range(1, TAPS):
        grad_local = (
            grad_local
            + feat_taps[:, tap_index, :][None] * ext_mixed[tap_index : tap_index + tok_rows]
        )
    grad_features = grad_local.astype(jnp.bfloat16)
    inner_pieces = []
    feat_pieces = []
    for tap_index in range(TAPS):
        inner_pieces.append(
            jnp.sum(
                grad_window * product_ext[reach - tap_index : reach - tap_index + tok_rows], axis=0
            )
        )
        feat_pieces.append(
            jnp.sum(
                grad_mixed * extended[2 * reach - tap_index : 2 * reach - tap_index + tok_rows],
                axis=0,
            )
        )
    inner_local = jnp.stack(inner_pieces, axis=0)
    feat_local = jnp.stack(feat_pieces, axis=1)
    inner_total, feat_total = lax.psum((inner_local, feat_local), "ctx")
    return (grad_features, grad_weight, feat_total * inv_root, inner_total * inv_root)


def solution(mesh):
    return jax.shard_map(
        body,
        mesh=mesh,
        in_specs=(
            P("ctx", None, ("row", "col")),
            P(None, None, ("row", "col")),
            P(None, ("row", "col")),
            P("row", "col"),
            P("ctx", ("col", "row")),
        ),
        out_specs=(
            P("ctx", None, ("row", "col")),
            P(("row", "ctx"), "col"),
            P(None, None, ("row", "col")),
            P(None, ("row", "col")),
        ),
        check_vma=False,
    )
```

profile of v0, /device:TPU:1, one launch (start us, length us, event | category | flops | bytes accessed | tf_op | source)
XLA Modules:
  0.0 395.6 jit_solution(11997921373618022134)
XLA Ops:
  7.2 0.0 all-gather.3.cloned.1.call-start
  7.2 0.7 all-gather.3.cloned.1.call-update
  7.9 0.0 all-gather.5.cloned.1.call-start
  7.9 53.5 %all-gather.3.cloned.1.call-done = bf16[512,2048]{1,0:T(8,128)(2,1)} async-done(((bf16[512,256]{1,0:T(8,128)(2,1)}), bf16[512,2048]{1,0:T(8,128)(2,1)}) %all-gather.3.cloned.1.call-update) | async-done | bytes 2097168 | tf_op jit(solution)/shard_map/all_gather | solution.py:39
  61.5 7.2 %all-to-all-start = ((bf16[2,256,2048]{2,1,0:T(8,128)(2,1)}), bf16[2,256,2048]{2,1,0:T(8,128)(2,1)}, u32[]{:S(2)}, u32[]{:S(2)}) async-start(bf16[2,256,2048]{2,1,0:T(8,128)(2,1)} %bitcast), calls=%async_computation | async-start | bytes 4194304 | tf_op jit(solution)/shard_map/all_to_all | solution.py:41
  68.7 7.0 %collective-permute-start = (bf16[12,3,256]{2,0,1:T(8,128)(2,1)S(1)}, bf16[12,3,256]{2,0,1:T(8,128)(2,1)S(1)}, u32[]{:S(2)}, u32[]{:S(2)}) collective-permute-start(bf16[12,3,256]{2,0,1:T(8,128)(2,1)S(1)} %slice.413), channel_id=1, source_target_pairs={{0,1},{1,2},{2,3},{3,4},{4,5},{5,6},{6,7},{7,8},{8,9},{9,10},{10,1... | collective-permute-start | bytes 55304 | tf_op jit(solution)/shard_map/ppermute | solution.py:14
  75.8 34.8 %collective-permute-done = bf16[12,3,256]{2,0,1:T(8,128)(2,1)S(1)} collective-permute-done((bf16[12,3,256]{2,0,1:T(8,128)(2,1)S(1)}, bf16[12,3,256]{2,0,1:T(8,128)(2,1)S(1)}, u32[]{:S(2)}, u32[]{:S(2)}) %collective-permute-start) | collective-permute-done | bytes 18464 | tf_op jit(solution)/shard_map/ppermute | solution.py:14
  110.6 0.2 maximum_convert_fusion
  110.8 0.9 fusion.15
  111.7 1.6 slice_bitcast_fusion.4
  113.4 1.7 fusion.67
  115.0 2.1 all-to-all-done
  117.2 3.9 copy.10
  121.1 88.4 %all-gather.5.cloned.1.call-done = bf16[512,4096]{1,0:T(8,128)(2,1)} async-done(((bf16[512,2048]{1,0:T(8,128)(2,1)}), bf16[512,4096]{1,0:T(8,128)(2,1)}) %all-gather.5.cloned.1.call-update) | async-done | bytes 4194320 | tf_op jit(solution)/shard_map/all_gather | solution.py:40
  209.5 6.8 %multiply_reduce_fusion = (f32[256]{0:T(256)S(1)}, f32[256]{0:T(256)S(1)}, f32[256]{0:T(256)S(1)}, f32[256]{0:T(256)S(1)}, f32[256]{0:T(256)S(1)}, /*index=5*/f3...) fusion(f32[518,256]{1,0:T(8,128)S(1)} %get-tuple-element.32, ...), kind=kOutput, calls=%fused_computation.121 | convolution fusion | flops 1077147904 | bytes 15216640 | tf_op jit(solution)/shard_map/dot_general | solution.py:42
  216.3 1.3 multiply_convert_fusion
  217.6 12.6 %all_gather.11 = bf16[512,512]{1,0:T(8,128)(2,1)S(1)} all-gather(bf16[512,256]{1,0:T(8,128)(2,1)S(1)} %get-tuple-element.30), channel_id=1, replica_groups=mesh['row'=8,'col'=2,'ctx'=32] {'col'}, dimensions={1}, use_global_device_ids=true | all-gather | bytes 786432 | tf_op jit(solution)/shard_map/all_gather | solution.py:45
  230.1 3.2 convolution_multiply_fusion
  233.5 0.8 slice.554
  234.2 8.1 %collective-permute-start.1 = (f32[6,256]{1,0:T(8,128)S(1)}, f32[6,256]{1,0:T(8,128)S(1)}, u32[]{:S(2)}, u32[]{:S(2)}) collective-permute-start(f32[6,256]{1,0:T(8,128)S(1)} %slice.554), channel_id=1, source_target_pairs={{1,0},{2,1},{3,2},{4,3},{5,4},{6,5},{7,6},{8,7},{9,8},{10,9},{11,1... | collective-permute-start | bytes 18440 | tf_op jit(solution)/shard_map/ppermute | solution.py:14
  242.3 1.1 multiply_bitcast_fusion
  243.4 1.1 collective-permute-done.1
  244.6 3.2 fusion.59
  247.7 1.2 fusion.58
  248.9 1.4 fusion
  250.3 1.9 collective-permute-start.2
  252.3 131.6 %all-reduce = (f32[3,7,256]{2,0,1:T(4,128)S(1)}, f32[7,256]{1,0:T(8,128)S(1)}) all-reduce(f32[3,7,256]{2,0,1:T(4,128)S(1)} %constant_dynamic-update-slice_fusion, f32[7,256]{1,0:T(8,128)S(1)} %stack.79), channel_id=1, replica_groups=mesh['row'=8,'col'=2,'ctx'=32] {'ctx'}, use_global_device_ids=true, to_apply=%region_8.0 | all-reduce | flops 7168 | bytes 57344 | tf_op jit(solution)/shard_map/psum | solution.py:95
  383.9 0.6 broadcast_multiply_fusion.1
  384.6 0.6 copy.11
  385.2 0.1 pad_maximum_fusion
  385.3 2.2 fusion.8
  387.5 1.5 convert_element_type.15
  (34 shorter events, 0.2 us)
Async XLA Ops:
  7.2 54.3 %all-gather.3.cloned.1.call-start = ((), (), s32[]{:S(2)}) async-start(), calls=%async_computation.2 | async-start | bytes 2359296 | tf_op jit(solution)/shard_map/all_gather | solution.py:39
  7.9 201.6 %all-gather.5.cloned.1.call-start = ((), (), s32[]{:S(2)}) async-start(), calls=%async_computation.3 | async-start | bytes 6291456 | tf_op jit(solution)/shard_map/all_gather | solution.py:40
  61.5 7.3 %copy-start.2 = (bf16[512,3,256]{2,0,1:T(8,128)(2,1)S(1)}, bf16[512,3,256]{2,0,1:T(8,128)(2,1)}, u32[]{:S(2)}) copy-start(bf16[512,3,256]{2,0,1:T(8,128)(2,1)} %param.5) | copy-start | bytes 2359300
  61.5 14.3 %copy-start.4 = (f32[7,256]{1,0:T(8,128)S(1)}, f32[7,256]{1,0:T(8,128)}, u32[]{:S(2)}) copy-start(f32[7,256]{1,0:T(8,128)} %param.7) | copy-start | bytes 21508
  61.5 14.3 %copy-start.3 = (f32[3,7,256]{2,1,0:T(8,128)S(1)}, f32[3,7,256]{2,1,0:T(8,128)}, u32[]{:S(2)}) copy-start(f32[3,7,256]{2,1,0:T(8,128)} %param.6) | copy-start | bytes 64516
  61.5 55.7 %all-to-all-start = ((bf16[2,256,2048]{2,1,0:T(8,128)(2,1)}), bf16[2,256,2048]{2,1,0:T(8,128)(2,1)}, u32[]{:S(2)}, u32[]{:S(2)}) async-start(bf16[2,256,2048]{2,1,0:T(8,128)(2,1)} %bitcast), calls=%async_computation | async-start | bytes 4194304 | tf_op jit(solution)/shard_map/all_to_all | solution.py:41
  68.7 318.8 %reduce-scatter.2.cloned.1.call-start = ((), (), s32[]{:S(2)}) async-start(), calls=%async_computation.4 | async-start | bytes 4325376 | tf_op jit(solution)/shard_map/reduce_scatter | solution.py:55
  68.7 41.9 %collective-permute-start = (bf16[12,3,256]{2,0,1:T(8,128)(2,1)S(1)}, bf16[12,3,256]{2,0,1:T(8,128)(2,1)S(1)}, u32[]{:S(2)}, u32[]{:S(2)}) collective-permute-start(bf16[12,3,256]{2,0,1:T(8,128)(2,1)S(1)} %slice.413), channel_id=1, source_target_pairs={{0,1},{1,2},{2,3},{3,4},{4,5},{5,6},{6,7},{7,8},{8,9},{9,10},{10,1... | collective-permute-start | bytes 55304 | tf_op jit(solution)/shard_map/ppermute | solution.py:14
  216.3 13.8 %copy-start = (bf16[512,2048]{1,0:T(8,128)(2,1)S(1)}, bf16[512,2048]{1,0:T(8,128)(2,1)}, u32[]{:S(2)}) copy-start(bf16[512,2048]{1,0:T(8,128)(2,1)} %all-gather.3.cloned.1.call-done) | copy-start | bytes 6291460
  233.4 8.9 %copy-start.1 = (f32[512,256]{1,0:T(8,128)S(1)}, f32[512,256]{1,0:T(8,128)}, u32[]{:S(2)}) copy-start(f32[512,256]{1,0:T(8,128)} %get-tuple-element.31) | copy-start | bytes 1572868
  234.2 10.4 %collective-permute-start.1 = (f32[6,256]{1,0:T(8,128)S(1)}, f32[6,256]{1,0:T(8,128)S(1)}, u32[]{:S(2)}, u32[]{:S(2)}) collective-permute-start(f32[6,256]{1,0:T(8,128)S(1)} %slice.554), channel_id=1, source_target_pairs={{1,0},{2,1},{3,2},{4,3},{5,4},{6,5},{7,6},{8,7},{9,8},{10,9},{11,1... | collective-permute-start | bytes 18440 | tf_op jit(solution)/shard_map/ppermute | solution.py:14
  250.3 134.8 %collective-permute-start.2 = (f32[6,3,256]{2,0,1:T(8,128)S(1)}, f32[6,3,256]{2,0,1:T(8,128)S(1)}, u32[]{:S(2)}, u32[]{:S(2)}) collective-permute-start(f32[6,3,256]{2,0,1:T(8,128)S(1)} %slice.567), channel_id=1, source_target_pairs={{1,0},{2,1},{3,2},{4,3},{5,4},{6,5},{7,6},{8,7},{9,8},{10,9},{11,1... | collective-permute-start | bytes 55304 | tf_op jit(solution)/shard_map/ppermute | solution.py:14
Sparse Core Ops, SparseCore 0:
  10.0 51.3 all-gather.2
  63.5 145.9 all-gather.4
  233.5 151.7 reduce-scatter.1
where the time goes:
time: 400 us; the launch traced here: 396 us
  waiting for transfers between devices  181 us (45%)
  blocking collectives  144 us (36%)
  starting transfers between devices  24.3 us (6%)
  other arithmetic  15.4 us (4%)
  between operations  13.9 us (3%)
  matrix products  10 us (2%)
  local copies, waits for them, and re-layouts  7.13 us (2%)
    psum x1, blocking collectives, body(): inner_total, feat_total = lax.psum((inner_local, feat_local), 'ctx')  132 us
    all_gather x1, waiting for transfers between devices, body(): full_grad = lax.all_gather(gathered_grad, 'col', axis=1, tiled=True)  88.4 us
    all_gather x1, waiting for transfers between devices, body(): gathered_grad = lax.all_gather(out_grad, 'row', axis=1, tiled=True)  53.5 us
    ppermute x3, waiting for transfers between devices, shifted(): lax.ppermute(value, axis, [(source, source + steps) for source in range(f...  35.9 us
    ppermute x3, starting transfers between devices, shifted(): lax.ppermute(value, axis, [(source, source + steps) for source in range(f...  17 us
    all_gather x1, blocking collectives, body(): gathered_gated = lax.all_gather(gated, 'col', axis=1, tiled=True)  12.6 us
  transfers between devices with their start and end apart: 7, of which 5 were waited for; matrix products, arithmetic and copies ran while one was open for 5% of the time, Pallas kernels for 0%

commit v1 on v0

v1 whole, which is shorter than its diff:
```python
import math

import jax
import jax.numpy as jnp
from jax import lax
from jax.experimental import pallas as pl
from jax.experimental.pallas import tpu as pltpu
from jax.sharding import Mesh
from jax.sharding import PartitionSpec as P

TAPS = 7
REACH = TAPS - 1
HALO = 16
LEAD = 8
CHUNK = 64
LANES = 128
CTX = ("x", "zl", "core")
F32 = jnp.float32
BF16 = jnp.bfloat16


def chunks(total):
    return [(start, min(CHUNK, total - start)) for start in range(0, total, CHUNK)]


def load_features(before, own, scratch, after=None):
    rows = own.shape[1]
    for j in range(3):
        scratch[j, 0:HALO, :] = before[j].astype(F32)
        for start, count in chunks(rows):
            scratch[j, HALO + start : HALO + start + count, :] = own[
                j, start : start + count, :
            ].astype(F32)
        if after is not None:
            scratch[j, HALO + rows : 2 * HALO + rows, :] = after[j].astype(F32)


def forward_kernel(
    before, own, after, feat_taps, inner_taps, gated, query, window, key, value, product, feats
):
    rows = own.shape[1]
    load_features(before, own, feats, after)
    for start, count in chunks(rows + HALO + LEAD):
        parts = []
        for j in range(3):
            base = HALO - LEAD + start
            total = feat_taps[j, 0:1, :] * feats[j, base : base + count, :]
            for s in range(1, TAPS):
                total = total + feat_taps[j, s : s + 1, :] * feats[j, base - s : base - s + count, :]
            parts.append(total)
        query[start : start + count, :] = parts[0]
        key[start : start + count, :] = parts[1]
        value[start : start + count, :] = parts[2]
        product[start : start + count, :] = parts[1] * parts[2]
    for start, count in chunks(rows + HALO):
        base = LEAD + start
        total = inner_taps[0:1, :] * product[base : base + count, :]
        for s in range(1, TAPS):
            total = total + inner_taps[s : s + 1, :] * product[base - s : base - s + count, :]
        window[start : start + count, :] = total
        if start < rows:
            kept = min(count, rows - start)
            gated[start : start + kept, :] = (
                query[base : base + kept, :] * total[:kept]
            ).astype(BF16)


def backward_kernel(
    near, far, query, window, key, value, product, before, own, feat_taps, inner_taps,
    grads, tap_sums, feats, grad_window, grad_mixed,
):
    rows = own.shape[1]
    load_features(before, own, feats)
    for start, count in chunks(rows + HALO):
        total = near[start : start + count, :] + far[start : start + count, :].astype(F32)
        grad_window[start : start + count, :] = (
            total * query[LEAD + start : LEAD + start + count, :]
        )
        grad_mixed[0, start : start + count, :] = total * window[start : start + count, :]
    for start, count in chunks(rows + LEAD):
        total = inner_taps[0:1, :] * grad_window[start : start + count, :]
        for s in range(1, TAPS):
            total = total + inner_taps[s : s + 1, :] * grad_window[start + s : start + s + count, :]
        grad_mixed[1, start : start + count, :] = (
            total * value[LEAD + start : LEAD + start + count, :]
        )
        grad_mixed[2, start : start + count, :] = total * key[LEAD + start : LEAD + start + count, :]

    def folded(value):
        return jnp.sum(value.reshape(value.shape[0] // 8, 8, value.shape[1]), axis=0)

    def put(at, sums):
        for s in range(TAPS):
            tap_sums[at, s : s + 1, :] = jnp.sum(sums[s], axis=0, keepdims=True)
        tap_sums[at, TAPS : TAPS + 1, :] = jnp.zeros((1, LANES), F32)

    for j in range(3):
        sums = [jnp.zeros((8, LANES), F32) for _ in range(TAPS)]
        for start, count in chunks(rows):
            here = grad_mixed[j, start : start + count, :]
            total = feat_taps[j, 0:1, :] * here
            for s in range(1, TAPS):
                total = (
                    total
                    + feat_taps[j, s : s + 1, :] * grad_mixed[j, start + s : start + s + count, :]
                )
            grads[j, start : start + count, :] = total.astype(BF16)
            for s in range(TAPS):
                base = HALO + start - s
                sums[s] = sums[s] + folded(here * feats[j, base : base + count, :])
        put(j, sums)
    sums = [jnp.zeros((8, LANES), F32) for _ in range(TAPS)]
    for start, count in chunks(rows):
        here = grad_window[start : start + count, :]
        for s in range(TAPS):
            base = LEAD + start - s
            sums[s] = sums[s] + folded(here * product[base : base + count, :])
    put(3, sums)


def lane_spec(*lead):
    return pl.BlockSpec((*lead, LANES), lambda i: (0,) * len(lead) + (i,))


def forward(before, own, after, feat_taps, inner_taps):
    _, rows, channels = own.shape
    saved = jax.ShapeDtypeStruct((rows + HALO + LEAD, channels), F32)
    saved_spec = lane_spec(rows + HALO + LEAD)
    return pl.pallas_call(
        forward_kernel,
        grid=(channels // LANES,),
        in_specs=[
            lane_spec(3, HALO), lane_spec(3, rows), lane_spec(3, HALO),
            lane_spec(3, TAPS), lane_spec(TAPS),
        ],
        out_specs=[
            lane_spec(rows), saved_spec, lane_spec(rows + HALO),
            saved_spec, saved_spec, saved_spec,
        ],
        out_shape=[
            jax.ShapeDtypeStruct((rows, channels), BF16),
            saved,
            jax.ShapeDtypeStruct((rows + HALO, channels), F32),
            saved, saved, saved,
        ],
        scratch_shapes=[pltpu.VMEM((3, rows + 2 * HALO, LANES), F32)],
        compiler_params=pltpu.CompilerParams(vmem_limit_bytes=32 << 20),
        cost_estimate=pl.CostEstimate(
            flops=60 * rows * channels, bytes_accessed=30 * rows * channels, transcendentals=0
        ),
        name="forward",
    )(before, own, after, feat_taps, inner_taps)


def backward(near, far, saved, before, own, feat_taps, inner_taps):
    _, rows, channels = own.shape
    saved_spec = lane_spec(rows + HALO + LEAD)
    long_spec = lane_spec(rows + HALO)
    return pl.pallas_call(
        backward_kernel,
        grid=(channels // LANES,),
        in_specs=[
            long_spec, long_spec, saved_spec, long_spec, saved_spec, saved_spec, saved_spec,
            lane_spec(3, HALO), lane_spec(3, rows), lane_spec(3, TAPS), lane_spec(TAPS),
        ],
        out_specs=[lane_spec(3, rows), lane_spec(4, 8)],
        out_shape=[
            jax.ShapeDtypeStruct((3, rows, channels), BF16),
            jax.ShapeDtypeStruct((4, 8, channels), F32),
        ],
        scratch_shapes=[
            pltpu.VMEM((3, rows + HALO, LANES), F32),
            pltpu.VMEM((rows + HALO, LANES), F32),
            pltpu.VMEM((3, rows + HALO, LANES), F32),
        ],
        compiler_params=pltpu.CompilerParams(vmem_limit_bytes=32 << 20),
        cost_estimate=pl.CostEstimate(
            flops=120 * rows * channels, bytes_accessed=40 * rows * channels, transcendentals=0
        ),
        name="backward",
    )(near, far, *saved, before, own, feat_taps, inner_taps)


def gated_grad_kernel(grad, weight, far, near, total):
    at = pl.program_id(0)
    term = lax.dot_general(
        grad[0], weight[...], (((1,), (1,)), ((), ())), preferred_element_type=F32
    )

    @pl.when(at == 0)
    def _():
        total[...] = term

    @pl.when(at > 0)
    def _():
        total[...] += term

    @pl.when(at == pl.num_programs(0) - 1)
    def _():
        half = far.shape[1]
        far[...] = total[:, :half].astype(BF16)
        near[...] = total[:, half:]


def gated_grad(grads, weight):
    blocks, rows, width = grads.shape
    channels = weight.shape[0]
    half = channels // 2
    return pl.pallas_call(
        gated_grad_kernel,
        grid=(blocks,),
        in_specs=[
            pl.BlockSpec((1, rows, width), lambda i: (i, 0, 0)),
            pl.BlockSpec((channels, width), lambda i: (0, i)),
        ],
        out_specs=[
            pl.BlockSpec((rows, half), lambda i: (0, 0)),
            pl.BlockSpec((rows, half), lambda i: (0, 0)),
        ],
        out_shape=[
            jax.ShapeDtypeStruct((rows, half), BF16),
            jax.ShapeDtypeStruct((rows, half), F32),
        ],
        scratch_shapes=[pltpu.VMEM((rows, channels), F32)],
        compiler_params=pltpu.CompilerParams(vmem_limit_bytes=32 << 20),
        cost_estimate=pl.CostEstimate(
            flops=2 * rows * channels * blocks * width,
            bytes_accessed=2 * blocks * width * (rows + channels) + 6 * rows * half,
            transcendentals=0,
        ),
        name="gated_grad",
    )(grads, weight)


def weight_grad_kernel(gated, grad, out):
    rows = gated.shape[1]
    out[0] = jnp.dot(gated[...], grad[0, :rows, :], preferred_element_type=F32).astype(out.dtype)


def weight_grad(gated, grads, dtype):
    channels, rows = gated.shape
    blocks, _, width = grads.shape
    return pl.pallas_call(
        weight_grad_kernel,
        grid=(blocks,),
        in_specs=[
            pl.BlockSpec((channels, rows), lambda i: (0, 0)),
            pl.BlockSpec((1, grads.shape[1], width), lambda i: (i, 0, 0)),
        ],
        out_specs=pl.BlockSpec((1, channels, width), lambda i: (i, 0, 0)),
        out_shape=jax.ShapeDtypeStruct((blocks, channels, width), dtype),
        compiler_params=pltpu.CompilerParams(vmem_limit_bytes=32 << 20),
        cost_estimate=pl.CostEstimate(
            flops=2 * rows * channels * blocks * width,
            bytes_accessed=2 * blocks * width * (rows + 2 * channels) + 2 * rows * channels,
            transcendentals=0,
        ),
        name="weight_grad",
    )(gated, grads)


def ctx_permute(value, target):
    nx, nz, nc = (lax.axis_size(a) for a in CTX)
    pairs = []
    for x in range(nx):
        for z in range(nz):
            for c in range(nc):
                to = target(x, z, c)
                if to is not None:
                    pairs.append(((x * nz + z) * nc + c, (to[0] * nz + to[1]) * nc + to[2]))
    return lax.ppermute(value, CTX, pairs)


def ctx_shift(value, steps):
    nx, nz, nc = (lax.axis_size(a) for a in CTX)
    count = nx * nz * nc
    return lax.ppermute(
        value, CTX, [(i, i + steps) for i in range(count) if 0 <= i + steps < count]
    )


def scatter_sum(kept, axis, dim, wire):
    count = lax.axis_size(axis)
    me = lax.axis_index(axis)
    size = kept.shape[dim] // count
    total = None
    arrived = []
    for step in range(1, count):
        to = lax.rem(me + step, count)
        piece = lax.dynamic_slice_in_dim(wire, to * size, size, dim)
        arrived.append(
            lax.ppermute(piece, axis, [(i, (i + step) % count) for i in range(count)])
        )
    total = lax.dynamic_slice_in_dim(kept, me * size, size, dim)
    for piece in arrived:
        total = total + piece.astype(F32)
    return total


def body(featured, feat_taps, inner_taps, out_weight, out_grad):
    rows = featured.shape[0]
    nx, nz, nc = (lax.axis_size(a) for a in CTX)
    inv_root = 1.0 / math.sqrt(rows * nx * nz * nc)
    col = lax.axis_index("col")
    core = lax.axis_index("core")

    grad_after = ctx_shift(out_grad[:HALO], -1)
    own = jnp.transpose(featured, (1, 0, 2))
    before = ctx_shift(own[:, rows - HALO :], 1)
    after = ctx_shift(own[:, :HALO], -1)
    grads = lax.all_gather(jnp.concatenate([out_grad, grad_after], axis=0), "row", axis=0)

    gated, *saved = forward(before, own, after, feat_taps, inner_taps)
    both = lax.all_gather(gated, "col", axis=1, tiled=True)
    channels = both.shape[1]
    slots = channels // (nx * nz * nc)
    split = both.T.reshape(nx * nz, nc, slots, rows)
    keep_gated = lax.dynamic_index_in_dim(split, core, 1, keepdims=False)
    send_gated = lax.dynamic_index_in_dim(split, 1 - core, 1, keepdims=False)
    keep_gated = keep_gated.reshape(channels // nc, rows)
    send_gated = send_gated.reshape(channels // nc, rows)
    half = channels // 2
    weight = jnp.concatenate(
        [
            lax.dynamic_slice_in_dim(out_weight, (1 - col) * half, half, 0),
            lax.dynamic_slice_in_dim(out_weight, col * half, half, 0),
        ],
        axis=0,
    )

    far, near = gated_grad(grads, weight)
    far = lax.ppermute(far, "col", [(0, 1), (1, 0)])

    sent = ctx_permute(
        weight_grad(send_gated, grads, BF16), lambda x, z, c: (x, z, 1 - c)
    )
    pair = weight_grad(keep_gated, grads, F32) + sent.astype(F32)
    along_x = scatter_sum(pair, "x", 1, pair.astype(BF16))
    along_z = scatter_sum(along_x, "zl", 1, along_x.astype(BF16))
    grad_weight = (along_z * inv_root).astype(BF16)
    grad_weight = jnp.transpose(grad_weight, (1, 0, 2)).reshape(slots, -1)

    grad_own, taps = backward(near, far, saved, before, own, feat_taps, inner_taps)
    for target in (
        lambda x, z, c: (x, z, c ^ 1),
        lambda x, z, c: (x ^ 1, z, c),
        lambda x, z, c: (nx - 1 - x, z, c),
        lambda x, z, c: (x, z ^ 1, c),
        lambda x, z, c: (x, z ^ 2, c),
    ):
        taps = taps + ctx_permute(taps, target)
    taps = taps * inv_root
    return (
        jnp.transpose(grad_own, (1, 0, 2)),
        grad_weight,
        taps[:3, :TAPS],
        taps[3, :TAPS],
    )


def fine_mesh(mesh):
    row, col, ctx = mesh.devices.shape
    depth = ctx // 8
    return Mesh(
        mesh.devices.reshape(row, col, ctx // (2 * depth), depth, 2), ("row", "col", *CTX)
    )


def solution(mesh):
    return jax.shard_map(
        body,
        mesh=fine_mesh(mesh),
        in_specs=(
            P(CTX, None, ("row", "col")),
            P(None, None, ("row", "col")),
            P(None, ("row", "col")),
            P("row", "col"),
            P(CTX, ("col", "row")),
        ),
        out_specs=(
            P(CTX, None, ("row", "col")),
            P(("row", *CTX), "col"),
            P(None, None, ("row", "col")),
            P(None, ("row", "col")),
        ),
        check_vma=False,
    )
```

time: 400 us -> 164 us (0.41)
  the two profiles are of different devices: /device:TPU:1 before, /device:TPU:8 now
where the time goes in v1:
time: 164 us; the launch traced here: 163 us
  starting transfers between devices  58.5 us (36%)
  waiting for transfers between devices  43.3 us (26%)
  local copies, waits for them, and re-layouts  15.1 us (9%)
  blocking collectives  14.6 us (9%)
  between operations  14.5 us (9%)
  Pallas kernels  12.5 us (8%)
  other arithmetic  4.5 us (3%)
    ppermute x6, starting transfers between devices, ctx_permute(): return lax.ppermute(value, CTX, pairs)  23 us
    all_gather x1, waiting for transfers between devices, body(): lax.all_gather(jnp.concatenate([out_grad, grad_after], axis=0), 'row', ax...  20.9 us
    ppermute x6, starting transfers between devices, scatter_sum(): lax.ppermute(piece, axis, [(i, (i + step) % count) for i in range(count)])  20.3 us
    all_gather x1, blocking collectives, body(): both = lax.all_gather(gated, 'col', axis=1, tiled=True)  14.6 us
    unnamed x36, local copies, waits for them, and re-layouts  9.71 us
    ppermute x1, waiting for transfers between devices, body(): far = lax.ppermute(far, 'col', [(0, 1), (1, 0)])  8.78 us
    ppermute x1, starting transfers between devices, body(): far = lax.ppermute(far, 'col', [(0, 1), (1, 0)])  8.02 us
    ppermute x3, starting transfers between devices, ctx_shift(): lax.ppermute(value, CTX, [(i, i + steps) for i in range(count) if 0 <= i...  7.12 us
  transfers between devices with their start and end apart: 17, of which 11 were waited for; matrix products, arithmetic and copies ran while one was open for 4% of the time, Pallas kernels for 7%

profile of v1, /device:TPU:8, one launch (start us, length us, event | category | flops | bytes accessed | tf_op | source)
XLA Modules:
  0.0 163.0 jit_solution(6566865421454935900)
XLA Ops:
  9.2 1.8 %collective-permute-done = bf16[16,256]{1,0:T(8,128)(2,1)S(1)} collective-permute-done((bf16[16,256]{1,0:T(8,128)(2,1)S(1)}, bf16[16,256]{1,0:T(8,128)(2,1)S(1)}, u32[]{:S(2)}, u32[]{:S(2)}) %collective-permute-start) | collective-permute-done | bytes 8224 | tf_op jit(solution)/shard_map/ppermute | solution.py:277
  11.0 1.7 %pad_maximum_fusion.1 = bf16[528,256]{1,0:T(8,128)(2,1)} fusion(bf16[16,256]{1,0:T(8,128)(2,1)S(1)} %collective-permute-done, bf16[512,256]{1,0:T(8,128)(2,1)} %param.9), kind=kLoop, calls=%fused_computation.3 | loop fusion | flops 540672 | bytes 540672 | tf_op jit(solution)/shard_map/concatenate | solution.py:311
  13.4 4.6 %collective-permute-start.2 = (bf16[3,16,256]{2,1,0:T(8,128)(2,1)S(1)}, bf16[3,16,256]{2,1,0:T(8,128)(2,1)S(1)}, u32[]{:S(2)}, u32[]{:S(2)}) collective-permute-start(bf16[3,16,256]{2,1,0:T(8,128)(2,1)S(1)} %get-tuple-element.34), channel_id=1, source_target_pairs={{0,1},{1,2},{2,3},{3,4},{4,5},{5,6},{6,7},{7,8},{8,9},{9,10},{10,1... | collective-permute-start | bytes 73736 | tf_op jit(solution)/shard_map/ppermute | solution.py:277
  19.3 1.8 %collective-permute-done.3.after = bf16[3,16,256]{2,1,0:T(8,128)(2,1)S(1)} collective-permute-done((bf16[3,16,256]{2,1,0:T(8,128)(2,1)S(1)}, bf16[3,16,256]{2,1,0:T(8,128)(2,1)S(1)}, u32[]{:S(2)}, u32[]{:S(2)}) %collective-permute-start.3) | collective-permute-done | bytes 24608 | tf_op jit(solution)/shard_map/ppermute | solution.py:277
  23.7 1.6 forward.1
  29.3 14.6 %all_gather.11 = bf16[512,512]{1,0:T(8,128)(2,1)S(1)} all-gather(bf16[512,256]{1,0:T(8,128)(2,1)S(1)} %get-tuple-element.22), channel_id=1, replica_groups=mesh['row'=8,'col'=2,'x'=4,'zl'=4,'core'=2] {'col'}, dimensions={1}, use_global_device_ids=true | all-gather | bytes 786432 | tf_op jit(solution)/shard_map/all_gather | solution.py:314
  44.1 20.9 %all-gather.3.cloned.1.call-done = bf16[4224,256]{1,0:T(8,128)(2,1)} async-done(((bf16[528,256]{1,0:T(8,128)(2,1)}), bf16[4224,256]{1,0:T(8,128)(2,1)}) %all-gather.3.cloned.1.call-update) | async-done | bytes 2162704 | tf_op jit(solution)/shard_map/all_gather | solution.py:311
  65.0 1.6 copy-done
  66.6 1.9 %weight_grad.3 = bf16[8,256,256]{2,1,0:T(8,128)(2,1)S(1)} custom-call(bf16[256,512]{1,0:T(8,128)(2,1)S(1)} %bitcast.20, bf16[8,528,256]{2,1,0:T(8,128)(2,1)S(1)} %bitcast.13), custom_call_target="tpu_custom_call" | custom-call | flops 536870912 | bytes 4456448 | tf_op jit(solution)/shard_map/weight_grad/pallas_call | solution.py:243
  68.5 1.9 %collective-permute-start.4 = (bf16[8,256,256]{2,1,0:T(8,128)(2,1)S(1)}, bf16[8,256,256]{2,1,0:T(8,128)(2,1)}, u32[]{:S(2)}, u32[]{:S(2)}) collective-permute-start(bf16[8,256,256]{2,1,0:T(8,128)(2,1)S(1)} %weight_grad.3), channel_id=1, source_target_pairs={{0,1},{1,0},{2,3},{3,2},{4,5},{5,4},{6,7},{7,6},{8,9},{9,8},{10,11... | collective-permute-start | bytes 3145736 | tf_op jit(solution)/shard_map/ppermute | solution.py:271
  70.5 1.8 %constant_dynamic-slice_fusion.9 = (bf16[256,2048]{1,0:T(8,128)(2,1)S(1)}, bf16[256,2048]{1,0:T(8,128)(2,1)S(1)}) fusion(bf16[512,2048]{1,0:T(8,128)(2,1)} %param.8, s32[]{:T(128)S(6)} %select_n.37, s32[]{:T(128)S(6)} %select_n.38), kind=kLoop, calls=%fused_computation.17 | loop fusion | bytes 4194312 | tf_op jit(solution)/shard_map/dynamic_slice | solution.py:325
  72.4 1.5 copy-done.1
  73.9 3.9 %gated_grad.1 = (bf16[528,256]{1,0:T(8,128)(2,1)S(1)}, f32[528,256]{1,0:T(8,128)S(1)}) custom-call(bf16[8,528,256]{2,1,0:T(8,128)(2,1)S(1)} %bitcast.14, bf16[512,2048]{1,0:T(8,128)(2,1)S(1)} %pad_maximum_fusion.weight), custom_call_target="tpu_custom_call" | custom-call | flops 1107296256 | bytes 5070848 | tf_op jit(solution)/shard_map/gated_grad/pallas_call | solution.py:209
  77.8 8.0 %collective-permute-start.1 = (bf16[528,256]{1,0:T(8,128)(2,1)S(1)}, bf16[528,256]{1,0:T(8,128)(2,1)S(1)}, u32[]{:S(2)}, u32[]{:S(2)}) collective-permute-start(bf16[528,256]{1,0:T(8,128)(2,1)S(1)} %get-tuple-element.15), channel_id=1, source_target_pairs={{0,32},{32,0},{1,33},{33,1},{2,34},{34,2},{3,35},{35,3},{4,36},{36... | collective-permute-start | bytes 811016 | tf_op jit(solution)/shard_map/ppermute | solution.py:332
  85.9 8.8 %collective-permute-done.1.far = bf16[528,256]{1,0:T(8,128)(2,1)S(1)} collective-permute-done((bf16[528,256]{1,0:T(8,128)(2,1)S(1)}, bf16[528,256]{1,0:T(8,128)(2,1)S(1)}, u32[]{:S(2)}, u32[]{:S(2)}) %collective-permute-start.1) | collective-permute-done | bytes 270368 | tf_op jit(solution)/shard_map/ppermute | solution.py:332
  94.7 3.3 %backward.1 = (bf16[3,512,256]{2,1,0:T(8,128)(2,1)}, f32[4,8,256]{2,1,0:T(8,128)S(1)}) custom-call(f32[528,256]{1,0:T(8,128)S(1)} %get-tuple-element.14.near, bf16[528,256]{1,0:T(8,128)(2,1)S(1)} %collective-permute-done.1.far, f32[536,256]{1,0:T(8,128)S(1)} %copy-done.5, f32[528,256]{1,0:T(8,128)S(1)} %copy-done.13, f32[536,256]{1,0:T(8,128)S(1)} %copy-done.7, ...), custom_call_target="tpu_custom_call" | custom-call | flops 15728640 | bytes 5242880 | tf_op jit(solution)/shard_map/backward/pallas_call | solution.py:159
  98.0 1.9 %collective-permute-start.11 = (f32[4,8,256]{2,1,0:T(8,128)S(1)}, f32[4,8,256]{2,1,0:T(8,128)S(1)}, u32[]{:S(2)}, u32[]{:S(2)}) collective-permute-start(f32[4,8,256]{2,1,0:T(8,128)S(1)} %get-tuple-element.23), channel_id=1, source_target_pairs={{0,1},{1,0},{2,3},{3,2},{4,5},{5,4},{6,7},{7,6},{8,9},{9,8},{10,11... | collective-permute-start | bytes 98312 | tf_op jit(solution)/shard_map/ppermute | solution.py:271
  101.1 3.4 %collective-permute-start.12 = (f32[4,8,256]{2,1,0:T(8,128)S(1)}, f32[4,8,256]{2,1,0:T(8,128)S(1)}, u32[]{:S(2)}, u32[]{:S(2)}) collective-permute-start(f32[4,8,256]{2,1,0:T(8,128)S(1)} %add.117), channel_id=1, source_target_pairs={{0,8},{1,9},{2,10},{3,11},{4,12},{5,13},{6,14},{7,15},{8,0},{9,1},... | collective-permute-start | bytes 98312 | tf_op jit(solution)/shard_map/ppermute | solution.py:271
  104.5 2.4 %collective-permute-done.12 = f32[4,8,256]{2,1,0:T(8,128)S(1)} collective-permute-done((f32[4,8,256]{2,1,0:T(8,128)S(1)}, f32[4,8,256]{2,1,0:T(8,128)S(1)}, u32[]{:S(2)}, u32[]{:S(2)}) %collective-permute-start.12) | collective-permute-done | bytes 32800 | tf_op jit(solution)/shard_map/ppermute | solution.py:271
  106.9 4.6 %collective-permute-start.13 = (f32[4,8,256]{2,1,0:T(8,128)S(1)}, f32[4,8,256]{2,1,0:T(8,128)S(1)}, u32[]{:S(2)}, u32[]{:S(2)}) collective-permute-start(f32[4,8,256]{2,1,0:T(8,128)S(1)} %add.118), channel_id=1, source_target_pairs={{0,24},{1,25},{2,26},{3,27},{4,28},{5,29},{6,30},{7,31},{8,16},{9,... | collective-permute-start | bytes 98312 | tf_op jit(solution)/shard_map/ppermute | solution.py:271
  111.5 1.9 %weight_grad.2 = f32[8,256,256]{2,1,0:T(8,128)S(1)} custom-call(bf16[256,512]{1,0:T(8,128)(2,1)S(1)} %bitcast.19, bf16[8,528,256]{2,1,0:T(8,128)(2,1)S(1)} %bitcast.15), custom_call_target="tpu_custom_call" | custom-call | flops 536870912 | bytes 4456448 | tf_op jit(solution)/shard_map/weight_grad/pallas_call | solution.py:243
  113.9 6.9 %collective-permute-start.14 = (f32[4,8,256]{2,1,0:T(8,128)S(1)}, f32[4,8,256]{2,1,0:T(8,128)S(1)}, u32[]{:S(2)}, u32[]{:S(2)}) collective-permute-start(f32[4,8,256]{2,1,0:T(8,128)S(1)} %add.119), channel_id=1, source_target_pairs={{0,2},{1,3},{2,0},{3,1},{4,6},{5,7},{6,4},{7,5},{8,10},{9,11},{10,... | collective-permute-start | bytes 98312 | tf_op jit(solution)/shard_map/ppermute | solution.py:271
  120.8 1.5 fusion.2
  122.4 2.2 %collective-permute-start.5 = (bf16[8,64,256]{2,1,0:T(8,128)(2,1)S(1)}, bf16[8,64,256]{2,1,0:T(8,128)(2,1)S(1)}, u32[]{:S(2)}, u32[]{:S(2)}) collective-permute-start(bf16[8,64,256]{2,1,0:T(8,128)(2,1)S(1)} %get-tuple-element.30), channel_id=1, source_target_pairs={{0,8},{8,16},{16,24},{24,0},{1,9},{9,17},{17,25},{25,1},{2,10},{10... | collective-permute-start | bytes 786440 | tf_op jit(solution)/shard_map/ppermute | solution.py:292
  124.6 5.8 %collective-permute-start.6 = (bf16[8,64,256]{2,1,0:T(8,128)(2,1)S(1)}, bf16[8,64,256]{2,1,0:T(8,128)(2,1)S(1)}, u32[]{:S(2)}, u32[]{:S(2)}) collective-permute-start(bf16[8,64,256]{2,1,0:T(8,128)(2,1)S(1)} %get-tuple-element.32), channel_id=1, source_target_pairs={{0,16},{8,24},{16,0},{24,8},{1,17},{9,25},{17,1},{25,9},{2,18},{10... | collective-permute-start | bytes 786440 | tf_op jit(solution)/shard_map/ppermute | solution.py:292
  130.4 2.1 %collective-permute-start.7 = (bf16[8,64,256]{2,1,0:T(8,128)(2,1)S(1)}, bf16[8,64,256]{2,1,0:T(8,128)(2,1)}, u32[]{:S(2)}, u32[]{:S(2)}) collective-permute-start(bf16[8,64,256]{2,1,0:T(8,128)(2,1)S(1)} %get-tuple-element.31), channel_id=1, source_target_pairs={{0,24},{8,0},{16,8},{24,16},{1,25},{9,1},{17,9},{25,17},{2,26},{10... | collective-permute-start | bytes 786440 | tf_op jit(solution)/shard_map/ppermute | solution.py:292
  132.6 4.3 %collective-permute-start.15 = (f32[4,8,256]{2,1,0:T(8,128)S(1)}, f32[4,8,256]{2,1,0:T(8,128)S(1)}, u32[]{:S(2)}, u32[]{:S(2)}) collective-permute-start(f32[4,8,256]{2,1,0:T(8,128)S(1)} %add.120), channel_id=1, source_target_pairs={{0,4},{1,5},{2,6},{3,7},{4,0},{5,1},{6,2},{7,3},{8,12},{9,13},{10,... | collective-permute-start | bytes 98312 | tf_op jit(solution)/shard_map/ppermute | solution.py:271
  136.9 2.7 %collective-permute-done.15 = f32[4,8,256]{2,1,0:T(8,128)S(1)} collective-permute-done((f32[4,8,256]{2,1,0:T(8,128)S(1)}, f32[4,8,256]{2,1,0:T(8,128)S(1)}, u32[]{:S(2)}, u32[]{:S(2)}) %collective-permute-start.15) | collective-permute-done | bytes 32800 | tf_op jit(solution)/shard_map/ppermute | solution.py:271
  141.5 5.0 %collective-permute-start.10 = (bf16[8,16,256]{2,1,0:T(8,128)(2,1)S(1)}, bf16[8,16,256]{2,1,0:T(8,128)(2,1)S(1)}, u32[]{:S(2)}, u32[]{:S(2)}) collective-permute-start(bf16[8,16,256]{2,1,0:T(8,128)(2,1)S(1)} %get-tuple-element.38), channel_id=1, source_target_pairs={{0,6},{2,0},{4,2},{6,4},{1,7},{3,1},{5,3},{7,5},{8,14},{10,8},{12,... | collective-permute-start | bytes 196616 | tf_op jit(solution)/shard_map/ppermute | solution.py:292
  146.5 1.9 %collective-permute-start.8 = (bf16[8,16,256]{2,1,0:T(8,128)(2,1)S(1)}, bf16[8,16,256]{2,1,0:T(8,128)(2,1)S(1)}, u32[]{:S(2)}, u32[]{:S(2)}) collective-permute-start(bf16[8,16,256]{2,1,0:T(8,128)(2,1)S(1)} %get-tuple-element.37), channel_id=1, source_target_pairs={{0,2},{2,4},{4,6},{6,0},{1,3},{3,5},{5,7},{7,1},{8,10},{10,12},{12... | collective-permute-start | bytes 196616 | tf_op jit(solution)/shard_map/ppermute | solution.py:292
  148.4 3.2 %collective-permute-start.9 = (bf16[8,16,256]{2,1,0:T(8,128)(2,1)S(1)}, bf16[8,16,256]{2,1,0:T(8,128)(2,1)S(1)}, u32[]{:S(2)}, u32[]{:S(2)}) collective-permute-start(bf16[8,16,256]{2,1,0:T(8,128)(2,1)S(1)} %get-tuple-element.39), channel_id=1, source_target_pairs={{0,4},{2,6},{4,0},{6,2},{1,5},{3,7},{5,1},{7,3},{8,12},{10,14},{12... | collective-permute-start | bytes 196616 | tf_op jit(solution)/shard_map/ppermute | solution.py:292
  152.9 1.6 collective-permute-done.8
  (65 shorter events, 17.6 us)
Async XLA Ops:
  7.2 57.9 %all-gather.3.cloned.1.call-start = ((), (), s32[]{:S(2)}) async-start(), calls=%async_computation | async-start | bytes 2433024 | tf_op jit(solution)/shard_map/all_gather | solution.py:311
  7.9 3.1 %collective-permute-start = (bf16[16,256]{1,0:T(8,128)(2,1)S(1)}, bf16[16,256]{1,0:T(8,128)(2,1)S(1)}, u32[]{:S(2)}, u32[]{:S(2)}) collective-permute-start(bf16[16,256]{1,0:T(8,128)(2,1)S(1)} %slice.15), channel_id=1, source_target_pairs={{1,0},{2,1},{3,2},{4,3},{5,4},{6,5},{7,6},{8,7},{9,8},{10,9},{11,1... | collective-permute-start | bytes 24584 | tf_op jit(solution)/shard_map/ppermute | solution.py:277
  13.4 5.9 %collective-permute-start.2 = (bf16[3,16,256]{2,1,0:T(8,128)(2,1)S(1)}, bf16[3,16,256]{2,1,0:T(8,128)(2,1)S(1)}, u32[]{:S(2)}, u32[]{:S(2)}) collective-permute-start(bf16[3,16,256]{2,1,0:T(8,128)(2,1)S(1)} %get-tuple-element.34), channel_id=1, source_target_pairs={{0,1},{1,2},{2,3},{3,4},{4,5},{5,6},{6,7},{7,8},{8,9},{9,10},{10,1... | collective-permute-start | bytes 73736 | tf_op jit(solution)/shard_map/ppermute | solution.py:277
  18.0 3.1 %collective-permute-start.3 = (bf16[3,16,256]{2,1,0:T(8,128)(2,1)S(1)}, bf16[3,16,256]{2,1,0:T(8,128)(2,1)S(1)}, u32[]{:S(2)}, u32[]{:S(2)}) collective-permute-start(bf16[3,16,256]{2,1,0:T(8,128)(2,1)S(1)} %get-tuple-element.33), channel_id=1, source_target_pairs={{1,0},{2,1},{3,2},{4,3},{5,4},{6,5},{7,6},{8,7},{9,8},{10,9},{11,1... | collective-permute-start | bytes 73736 | tf_op jit(solution)/shard_map/ppermute | solution.py:277
  21.1 1.1 copy-start.2
  25.2 0.8 copy-start.4
  26.9 0.8 copy-start.8
  27.7 0.8 copy-start.10
  28.5 0.8 copy-start.12
  65.0 1.6 copy-start
  68.5 52.2 %collective-permute-start.4 = (bf16[8,256,256]{2,1,0:T(8,128)(2,1)S(1)}, bf16[8,256,256]{2,1,0:T(8,128)(2,1)}, u32[]{:S(2)}, u32[]{:S(2)}) collective-permute-start(bf16[8,256,256]{2,1,0:T(8,128)(2,1)S(1)} %weight_grad.3), channel_id=1, source_target_pairs={{0,1},{1,0},{2,3},{3,2},{4,5},{5,4},{6,7},{7,6},{8,9},{9,8},{10,11... | collective-permute-start | bytes 3145736 | tf_op jit(solution)/shard_map/ppermute | solution.py:271
  72.3 1.6 copy-start.1
  73.9 20.8 %copy-start.3 = (bf16[512,3,256]{2,0,1:T(8,128)(2,1)S(1)}, bf16[512,3,256]{2,0,1:T(8,128)(2,1)}, u32[]{:S(2)}) copy-start(bf16[512,3,256]{2,0,1:T(8,128)(2,1)} %param.5) | copy-start | bytes 2359300
  73.9 20.8 %copy-start.5 = (f32[536,256]{1,0:T(8,128)S(1)}, f32[536,256]{1,0:T(8,128)}, u32[]{:S(2)}) copy-start(f32[536,256]{1,0:T(8,128)} %copy-done.4) | copy-start | bytes 1646596
  73.9 20.8 %copy-start.7 = (f32[536,256]{1,0:T(8,128)S(1)}, f32[536,256]{1,0:T(8,128)}, u32[]{:S(2)}) copy-start(f32[536,256]{1,0:T(8,128)} %copy-done.6) | copy-start | bytes 1646596
  73.9 20.8 %copy-start.9 = (f32[536,256]{1,0:T(8,128)S(1)}, f32[536,256]{1,0:T(8,128)}, u32[]{:S(2)}) copy-start(f32[536,256]{1,0:T(8,128)} %copy-done.8) | copy-start | bytes 1646596
  73.9 20.8 %copy-start.11 = (f32[536,256]{1,0:T(8,128)S(1)}, f32[536,256]{1,0:T(8,128)}, u32[]{:S(2)}) copy-start(f32[536,256]{1,0:T(8,128)} %copy-done.10) | copy-start | bytes 1646596
  73.9 20.8 %copy-start.13 = (f32[528,256]{1,0:T(8,128)S(1)}, f32[528,256]{1,0:T(8,128)}, u32[]{:S(2)}) copy-start(f32[528,256]{1,0:T(8,128)} %copy-done.12) | copy-start | bytes 1622020
  73.9 20.8 %copy-start.15 = (f32[3,7,256]{2,1,0:T(8,128)S(1)}, f32[3,7,256]{2,1,0:T(8,128)}, u32[]{:S(2)}) copy-start(f32[3,7,256]{2,1,0:T(8,128)} %feat_taps.3) | copy-start | bytes 64516
  73.9 20.8 %copy-start.17 = (f32[7,256]{1,0:T(8,128)S(1)}, f32[7,256]{1,0:T(8,128)}, u32[]{:S(2)}) copy-start(f32[7,256]{1,0:T(8,128)} %inner_taps.3) | copy-start | bytes 21508
  77.8 16.8 %collective-permute-start.1 = (bf16[528,256]{1,0:T(8,128)(2,1)S(1)}, bf16[528,256]{1,0:T(8,128)(2,1)S(1)}, u32[]{:S(2)}, u32[]{:S(2)}) collective-permute-start(bf16[528,256]{1,0:T(8,128)(2,1)S(1)} %get-tuple-element.15), channel_id=1, source_target_pairs={{0,32},{32,0},{1,33},{33,1},{2,34},{34,2},{3,35},{35,3},{4,36},{36... | collective-permute-start | bytes 811016 | tf_op jit(solution)/shard_map/ppermute | solution.py:332
  98.0 3.1 %collective-permute-start.11 = (f32[4,8,256]{2,1,0:T(8,128)S(1)}, f32[4,8,256]{2,1,0:T(8,128)S(1)}, u32[]{:S(2)}, u32[]{:S(2)}) collective-permute-start(f32[4,8,256]{2,1,0:T(8,128)S(1)} %get-tuple-element.23), channel_id=1, source_target_pairs={{0,1},{1,0},{2,3},{3,2},{4,5},{5,4},{6,7},{7,6},{8,9},{9,8},{10,11... | collective-permute-start | bytes 98312 | tf_op jit(solution)/shard_map/ppermute | solution.py:271
  101.1 5.8 %collective-permute-start.12 = (f32[4,8,256]{2,1,0:T(8,128)S(1)}, f32[4,8,256]{2,1,0:T(8,128)S(1)}, u32[]{:S(2)}, u32[]{:S(2)}) collective-permute-start(f32[4,8,256]{2,1,0:T(8,128)S(1)} %add.117), channel_id=1, source_target_pairs={{0,8},{1,9},{2,10},{3,11},{4,12},{5,13},{6,14},{7,15},{8,0},{9,1},... | collective-permute-start | bytes 98312 | tf_op jit(solution)/shard_map/ppermute | solution.py:271
  106.9 7.0 %collective-permute-start.13 = (f32[4,8,256]{2,1,0:T(8,128)S(1)}, f32[4,8,256]{2,1,0:T(8,128)S(1)}, u32[]{:S(2)}, u32[]{:S(2)}) collective-permute-start(f32[4,8,256]{2,1,0:T(8,128)S(1)} %add.118), channel_id=1, source_target_pairs={{0,24},{1,25},{2,26},{3,27},{4,28},{5,29},{6,30},{7,31},{8,16},{9,... | collective-permute-start | bytes 98312 | tf_op jit(solution)/shard_map/ppermute | solution.py:271
  113.9 18.7 %collective-permute-start.14 = (f32[4,8,256]{2,1,0:T(8,128)S(1)}, f32[4,8,256]{2,1,0:T(8,128)S(1)}, u32[]{:S(2)}, u32[]{:S(2)}) collective-permute-start(f32[4,8,256]{2,1,0:T(8,128)S(1)} %add.119), channel_id=1, source_target_pairs={{0,2},{1,3},{2,0},{3,1},{4,6},{5,7},{6,4},{7,5},{8,10},{9,11},{10,... | collective-permute-start | bytes 98312 | tf_op jit(solution)/shard_map/ppermute | solution.py:271
  122.4 17.2 %collective-permute-start.5 = (bf16[8,64,256]{2,1,0:T(8,128)(2,1)S(1)}, bf16[8,64,256]{2,1,0:T(8,128)(2,1)S(1)}, u32[]{:S(2)}, u32[]{:S(2)}) collective-permute-start(bf16[8,64,256]{2,1,0:T(8,128)(2,1)S(1)} %get-tuple-element.30), channel_id=1, source_target_pairs={{0,8},{8,16},{16,24},{24,0},{1,9},{9,17},{17,25},{25,1},{2,10},{10... | collective-permute-start | bytes 786440 | tf_op jit(solution)/shard_map/ppermute | solution.py:292
  124.6 15.1 %collective-permute-start.6 = (bf16[8,64,256]{2,1,0:T(8,128)(2,1)S(1)}, bf16[8,64,256]{2,1,0:T(8,128)(2,1)S(1)}, u32[]{:S(2)}, u32[]{:S(2)}) collective-permute-start(bf16[8,64,256]{2,1,0:T(8,128)(2,1)S(1)} %get-tuple-element.32), channel_id=1, source_target_pairs={{0,16},{8,24},{16,0},{24,8},{1,17},{9,25},{17,1},{25,9},{2,18},{10... | collective-permute-start | bytes 786440 | tf_op jit(solution)/shard_map/ppermute | solution.py:292
  130.4 10.0 %collective-permute-start.7 = (bf16[8,64,256]{2,1,0:T(8,128)(2,1)S(1)}, bf16[8,64,256]{2,1,0:T(8,128)(2,1)}, u32[]{:S(2)}, u32[]{:S(2)}) collective-permute-start(bf16[8,64,256]{2,1,0:T(8,128)(2,1)S(1)} %get-tuple-element.31), channel_id=1, source_target_pairs={{0,24},{8,0},{16,8},{24,16},{1,25},{9,1},{17,9},{25,17},{2,26},{10... | collective-permute-start | bytes 786440 | tf_op jit(solution)/shard_map/ppermute | solution.py:292
  132.6 7.1 %collective-permute-start.15 = (f32[4,8,256]{2,1,0:T(8,128)S(1)}, f32[4,8,256]{2,1,0:T(8,128)S(1)}, u32[]{:S(2)}, u32[]{:S(2)}) collective-permute-start(f32[4,8,256]{2,1,0:T(8,128)S(1)} %add.120), channel_id=1, source_target_pairs={{0,4},{1,5},{2,6},{3,7},{4,0},{5,1},{6,2},{7,3},{8,12},{9,13},{10,... | collective-permute-start | bytes 98312 | tf_op jit(solution)/shard_map/ppermute | solution.py:271
  141.5 11.4 %collective-permute-start.10 = (bf16[8,16,256]{2,1,0:T(8,128)(2,1)S(1)}, bf16[8,16,256]{2,1,0:T(8,128)(2,1)S(1)}, u32[]{:S(2)}, u32[]{:S(2)}) collective-permute-start(bf16[8,16,256]{2,1,0:T(8,128)(2,1)S(1)} %get-tuple-element.38), channel_id=1, source_target_pairs={{0,6},{2,0},{4,2},{6,4},{1,7},{3,1},{5,3},{7,5},{8,14},{10,8},{12,... | collective-permute-start | bytes 196616 | tf_op jit(solution)/shard_map/ppermute | solution.py:292
  146.5 8.0 %collective-permute-start.8 = (bf16[8,16,256]{2,1,0:T(8,128)(2,1)S(1)}, bf16[8,16,256]{2,1,0:T(8,128)(2,1)S(1)}, u32[]{:S(2)}, u32[]{:S(2)}) collective-permute-start(bf16[8,16,256]{2,1,0:T(8,128)(2,1)S(1)} %get-tuple-element.37), channel_id=1, source_target_pairs={{0,2},{2,4},{4,6},{6,0},{1,3},{3,5},{5,7},{7,1},{8,10},{10,12},{12... | collective-permute-start | bytes 196616 | tf_op jit(solution)/shard_map/ppermute | solution.py:292
  148.4 7.1 %collective-permute-start.9 = (bf16[8,16,256]{2,1,0:T(8,128)(2,1)S(1)}, bf16[8,16,256]{2,1,0:T(8,128)(2,1)S(1)}, u32[]{:S(2)}, u32[]{:S(2)}) collective-permute-start(bf16[8,16,256]{2,1,0:T(8,128)(2,1)S(1)} %get-tuple-element.39), channel_id=1, source_target_pairs={{0,4},{2,6},{4,0},{6,2},{1,5},{3,7},{5,1},{7,3},{8,12},{10,14},{12... | collective-permute-start | bytes 196616 | tf_op jit(solution)/shard_map/ppermute | solution.py:292
  (3 other events, 2.2 us)
Sparse Core Ops, SparseCore 0:
  12.8 52.1 all-gather.2

commit v2 on v0

v2 whole, which is shorter than its diff:
```python
import math

import jax
import jax.numpy as jnp
from jax import lax
from jax.experimental import pallas as pl
from jax.experimental.pallas import tpu as pltpu
from jax.sharding import Mesh
from jax.sharding import PartitionSpec as P

TAPS = 7
HALO = 16
LEAD = 8
CHUNK = 64
LANES = 128
CTX = ("x", "zl", "core")
F32 = jnp.float32
BF16 = jnp.bfloat16
VMEM_BYTES = 56 << 20


def spread(total):
    return [(start, min(CHUNK, total - start)) for start in range(0, total, CHUNK)]


def lane_spec(*lead):
    return pl.BlockSpec((*lead, LANES), lambda i: (0,) * len(lead) + (i,))


def whole(shape):
    return pl.BlockSpec(shape, lambda *_: (0,) * len(shape))


SCALAR = pl.BlockSpec(memory_space=pltpu.SMEM)
UNREAD = pl.BlockSpec(memory_space=pl.ANY)


def call(kernel, name, flops, moved, **kwargs):
    return pl.pallas_call(
        kernel,
        name=name,
        compiler_params=pltpu.CompilerParams(vmem_limit_bytes=VMEM_BYTES),
        cost_estimate=pl.CostEstimate(flops=flops, bytes_accessed=moved, transcendentals=0),
        **kwargs,
    )


def load_features(before, own, feats):
    rows = own.shape[1]
    for j in range(3):
        feats[j, 0:HALO, :] = before[j].astype(F32)
        for start, count in spread(rows):
            feats[j, HALO + start : HALO + start + count, :] = own[
                j, start : start + count, :
            ].astype(F32)


def forward_kernel(
    before, own, feat_taps, inner_taps, gated, query, window, key, value, product, feats
):
    rows = own.shape[1]
    load_features(before, own, feats)
    for start, count in spread(rows + LEAD):
        base = HALO - LEAD + start
        parts = []
        for j in range(3):
            total = feat_taps[j, 0:1, :] * feats[j, base : base + count, :]
            for s in range(1, TAPS):
                total = total + feat_taps[j, s : s + 1, :] * feats[j, base - s : base - s + count, :]
            parts.append(total)
        query[start : start + count, :] = parts[0]
        key[start : start + count, :] = parts[1]
        value[start : start + count, :] = parts[2]
        product[start : start + count, :] = parts[1] * parts[2]
    for start, count in spread(rows):
        base = LEAD + start
        total = inner_taps[0:1, :] * product[base : base + count, :]
        for s in range(1, TAPS):
            total = total + inner_taps[s : s + 1, :] * product[base - s : base - s + count, :]
        window[start : start + count, :] = total
        gated[start : start + count, :] = (query[base : base + count, :] * total).astype(BF16)


def forward(before, own, feat_taps, inner_taps):
    _, rows, channels = own.shape
    saved = jax.ShapeDtypeStruct((rows + LEAD, channels), F32)
    saved_spec = lane_spec(rows + LEAD)
    return call(
        forward_kernel,
        "forward",
        60 * rows * channels,
        30 * rows * channels,
        grid=(channels // LANES,),
        in_specs=[lane_spec(3, HALO), lane_spec(3, rows), lane_spec(3, TAPS), lane_spec(TAPS)],
        out_specs=[lane_spec(rows), saved_spec, lane_spec(rows), saved_spec, saved_spec, saved_spec],
        out_shape=[
            jax.ShapeDtypeStruct((rows, channels), BF16),
            saved,
            jax.ShapeDtypeStruct((rows, channels), F32),
            saved,
            saved,
            saved,
        ],
        scratch_shapes=[pltpu.VMEM((3, rows + HALO, LANES), F32)],
    )(before, own, feat_taps, inner_taps)


def backward_kernel(
    near, far, query, window, key, value, product, before, own, feat_taps, inner_taps, _,
    grads, head, tail, tap_sums, feats, grad_window, grad_mixed,
):
    rows = own.shape[1]
    load_features(before, own, feats)
    zeros = jnp.zeros((HALO, LANES), F32)
    grad_window[0:HALO, :] = zeros
    grad_window[HALO + rows :, :] = zeros[:LEAD]
    for j in range(3):
        grad_mixed[j, 0:HALO, :] = zeros
        grad_mixed[j, HALO + rows :, :] = zeros[:LEAD]
    for start, count in spread(rows):
        at = HALO + start
        total = near[start : start + count, :] + far[start : start + count, :].astype(F32)
        grad_window[at : at + count, :] = total * query[LEAD + start : LEAD + start + count, :]
        grad_mixed[0, at : at + count, :] = total * window[start : start + count, :]
    for start, count in spread(rows + LEAD):
        at = HALO - LEAD + start
        total = inner_taps[0:1, :] * grad_window[at : at + count, :]
        for s in range(1, TAPS):
            total = total + inner_taps[s : s + 1, :] * grad_window[at + s : at + s + count, :]
        grad_mixed[1, at : at + count, :] = total * value[start : start + count, :]
        grad_mixed[2, at : at + count, :] = total * key[start : start + count, :]

    def folded(terms):
        return jnp.sum(terms.reshape(terms.shape[0] // 8, 8, LANES), axis=0)

    def put(place, sums):
        for s in range(TAPS):
            tap_sums[place, s : s + 1, :] = jnp.sum(sums[s], axis=0, keepdims=True)
        tap_sums[place, TAPS : TAPS + 1, :] = jnp.zeros((1, LANES), F32)

    def transposed(j, at, count):
        total = feat_taps[j, 0:1, :] * grad_mixed[j, at : at + count, :]
        for s in range(1, TAPS):
            total = total + feat_taps[j, s : s + 1, :] * grad_mixed[j, at + s : at + s + count, :]
        return total

    for j in range(3):
        head[j] = transposed(j, 0, HALO)
        sums = [jnp.zeros((8, LANES), F32) for _ in range(TAPS)]
        spans = [(HALO + start, count) for start, count in spread(rows)]
        for at, count in ([(HALO - LEAD, LEAD)] if j > 0 else []) + spans:
            here = grad_mixed[j, at : at + count, :]
            for s in range(TAPS):
                sums[s] = sums[s] + folded(here * feats[j, at - s : at - s + count, :])
            if at >= HALO:
                total = transposed(j, at, count)
                grads[j, at - HALO : at - HALO + count, :] = total.astype(BF16)
                if at + count == HALO + rows:
                    tail[j] = total[count - HALO :]
        put(j, sums)
    sums = [jnp.zeros((8, LANES), F32) for _ in range(TAPS)]
    for start, count in spread(rows):
        here = grad_window[HALO + start : HALO + start + count, :]
        for s in range(TAPS):
            base = LEAD + start - s
            sums[s] = sums[s] + folded(here * product[base : base + count, :])
    put(3, sums)


def backward(near, far, saved, before, own, feat_taps, inner_taps, after):
    _, rows, channels = own.shape
    saved_spec = lane_spec(rows + LEAD)
    edge = jax.ShapeDtypeStruct((3, HALO, channels), F32)
    return call(
        backward_kernel,
        "backward",
        120 * rows * channels,
        40 * rows * channels,
        grid=(channels // LANES,),
        in_specs=[
            lane_spec(rows), lane_spec(rows), saved_spec, lane_spec(rows), saved_spec, saved_spec,
            saved_spec, lane_spec(3, HALO), lane_spec(3, rows), lane_spec(3, TAPS),
            lane_spec(TAPS), UNREAD,
        ],
        out_specs=[lane_spec(3, rows), lane_spec(3, HALO), lane_spec(3, HALO), lane_spec(4, 8)],
        out_shape=[
            jax.ShapeDtypeStruct((3, rows, channels), BF16),
            edge,
            edge,
            jax.ShapeDtypeStruct((4, 8, channels), F32),
        ],
        scratch_shapes=[
            pltpu.VMEM((3, rows + HALO, LANES), F32),
            pltpu.VMEM((rows + HALO + LEAD, LANES), F32),
            pltpu.VMEM((3, rows + HALO + LEAD, LANES), F32),
        ],
    )(near, far, *saved, before, own, feat_taps, inner_taps, after)


def gated_grad_kernel(col, grads, weight, far, near):
    wide = jnp.concatenate([grads[b] for b in range(grads.shape[0])], axis=1)
    total = lax.dot_general(
        wide, weight[...], (((1,), (1,)), ((), ())), preferred_element_type=F32
    )
    half = near.shape[1]

    @pl.when(col[0] == 0)
    def _():
        near[...] = total[:, :half]
        far[...] = total[:, half:].astype(BF16)

    @pl.when(col[0] != 0)
    def _():
        near[...] = total[:, half:]
        far[...] = total[:, :half].astype(BF16)


def gated_grad(col, grads, weight):
    blocks, rows, width = grads.shape
    channels = weight.shape[0]
    half = channels // 2
    step = min(rows, 128)
    return call(
        gated_grad_kernel,
        "gated_grad",
        2 * rows * channels * blocks * width,
        2 * blocks * width * (rows + channels) + 6 * rows * half,
        grid=(rows // step,),
        in_specs=[
            SCALAR,
            pl.BlockSpec((blocks, step, width), lambda i: (0, i, 0)),
            whole(weight.shape),
        ],
        out_specs=[pl.BlockSpec((step, half), lambda i: (i, 0))] * 2,
        out_shape=[
            jax.ShapeDtypeStruct((rows, half), BF16),
            jax.ShapeDtypeStruct((rows, half), F32),
        ],
    )(col, grads, weight)


def sent_weight_kernel(gated, grad, _, out):
    out[0] = jnp.dot(gated[...], grad[0], preferred_element_type=F32).astype(BF16)


def sent_weight(gated, grads, after):
    channels, rows = gated.shape
    blocks, _, width = grads.shape
    return call(
        sent_weight_kernel,
        "sent_weight",
        2 * rows * channels * blocks * width,
        2 * blocks * width * (rows + channels) + 2 * rows * channels,
        grid=(blocks,),
        in_specs=[
            whole(gated.shape),
            pl.BlockSpec((1, rows, width), lambda i: (i, 0, 0)),
            UNREAD,
        ],
        out_specs=pl.BlockSpec((1, channels, width), lambda i: (i, 0, 0)),
        out_shape=jax.ShapeDtypeStruct((blocks, channels, width), BF16),
    )(gated, grads, after)


def slices(place, held, parts, out_own, out_far):
    size = held.shape[-2] // parts
    out_own[...] = held[..., pl.ds(pl.multiple_of(place * size, size), size), :]
    for step, out in enumerate(out_far, 1):
        to = lax.rem(place + step, parts)
        out[...] = held[..., pl.ds(pl.multiple_of(to * size, size), size), :].astype(BF16)


def kept_weight_kernel(x, gated, grad, arrived, own, *rest):
    *far, held = rest
    held[0] = jnp.dot(gated[...], grad[0], preferred_element_type=F32) + arrived[0].astype(F32)
    slices(x[0], held, len(far) + 1, own, far)


def kept_weight(x, parts, gated, grads, arrived):
    channels, rows = gated.shape
    blocks, _, width = grads.shape
    shape = (blocks, channels // parts, width)
    spec = pl.BlockSpec((1, *shape[1:]), lambda i: (i, 0, 0))
    return call(
        kept_weight_kernel,
        "kept_weight",
        2 * rows * channels * blocks * width,
        2 * blocks * width * (rows + 3 * channels) + 2 * rows * channels,
        grid=(blocks,),
        in_specs=[
            SCALAR,
            whole(gated.shape),
            pl.BlockSpec((1, rows, width), lambda i: (i, 0, 0)),
            pl.BlockSpec((1, channels, width), lambda i: (i, 0, 0)),
        ],
        out_specs=[spec] * parts,
        out_shape=[jax.ShapeDtypeStruct(shape, F32)]
        + [jax.ShapeDtypeStruct(shape, BF16)] * (parts - 1),
        scratch_shapes=[pltpu.VMEM((1, channels, width), F32)],
    )(x, gated, grads, arrived)


def middle_kernel(parts, z, own, *rest):
    arrived, rest = rest[: parts - 1], rest[parts - 1 :]
    taps, taps_arrived, tail, head, _, out_own, out_taps, *far, out_grads, held = rest
    total = own[...]
    for piece in arrived:
        total = total + piece[...].astype(F32)
    held[...] = total
    blocks = held.shape[0]
    slices(z[0], held, len(far) + 1, out_own, [out.at[0:blocks] for out in far])
    sums = taps[...] + taps_arrived[...]
    out_taps[...] = sums
    high = sums.astype(BF16).astype(F32)
    both = jnp.concatenate([high, sums - high], axis=1).astype(BF16)
    for out in far:
        out[blocks:, :, :] = both
    out_grads[...] = (tail[...] + head[...]).astype(BF16)


def middle(z, parts, own, arrived, taps, taps_arrived, tail, head, grads):
    blocks, channels, width = own.shape
    shape = (blocks, channels // parts, width)
    wire = (blocks + taps.shape[0], *shape[1:])
    last = grads.shape[1] // HALO - 1
    return call(
        lambda *refs: middle_kernel(len(arrived) + 1, *refs),
        "middle",
        4 * own.size,
        10 * own.size,
        grid=(1,),
        in_specs=[SCALAR]
        + [whole(v.shape) for v in (own, *arrived, taps, taps_arrived, tail, head)]
        + [UNREAD],
        out_specs=[whole(shape), whole(taps.shape)]
        + [whole(wire)] * (parts - 1)
        + [pl.BlockSpec(tail.shape, lambda i: (0, last, 0))],
        out_shape=[jax.ShapeDtypeStruct(shape, F32), jax.ShapeDtypeStruct(taps.shape, F32)]
        + [jax.ShapeDtypeStruct(wire, BF16)] * (parts - 1)
        + [jax.ShapeDtypeStruct(grads.shape, grads.dtype)],
        scratch_shapes=[pltpu.VMEM(own.shape, F32)],
        input_output_aliases={len(arrived) + 6: parts + 1},
    )(z, own, *arrived, taps, taps_arrived, tail, head, grads)


def last_kernel(scale, own, taps, *rest):
    *arrived, out, out_feat, out_inner = rest
    blocks, _, width = own.shape
    for b in range(blocks):
        total = own[b]
        for piece in arrived:
            total = total + piece[b].astype(F32)
        out[:, b * width : (b + 1) * width] = (total * scale).astype(BF16)
    for j in range(4):
        total = taps[j]
        for piece in arrived:
            both = piece[blocks + j].astype(F32)
            total = total + (both[:8] + both[8:])
        total = (total * scale)[:TAPS]
        if j < 3:
            out_feat[j] = total
        else:
            out_inner[...] = total


def last(scale, own, taps, arrived):
    blocks, channels, width = own.shape
    shapes = [
        jax.ShapeDtypeStruct((channels, blocks * width), BF16),
        jax.ShapeDtypeStruct((3, TAPS, width), F32),
        jax.ShapeDtypeStruct((TAPS, width), F32),
    ]
    return call(
        lambda *refs: last_kernel(scale, *refs),
        "last",
        4 * own.size,
        12 * own.size,
        grid=(1,),
        in_specs=[whole(v.shape) for v in (own, taps, *arrived)],
        out_specs=[whole(s.shape) for s in shapes],
        out_shape=shapes,
    )(own, taps, *arrived)


def ctx_permute(value, target):
    nx, nz, nc = (lax.axis_size(a) for a in CTX)
    pairs = []
    for x in range(nx):
        for z in range(nz):
            for c in range(nc):
                to = target(x, z, c)
                pairs.append(((x * nz + z) * nc + c, (to[0] * nz + to[1]) * nc + to[2]))
    return lax.ppermute(value, CTX, pairs)


def ctx_shift(value, steps):
    count = math.prod(lax.axis_size(a) for a in CTX)
    return lax.ppermute(
        value, CTX, [(i, i + steps) for i in range(count) if 0 <= i + steps < count]
    )


def rotated(pieces, axis):
    count = lax.axis_size(axis)
    return [
        lax.ppermute(piece, axis, [(i, (i + step) % count) for i in range(count)])
        for step, piece in enumerate(pieces, 1)
    ]


def body(featured, feat_taps, inner_taps, out_weight, out_grad):
    rows = featured.shape[0]
    nx, nz, nc = (lax.axis_size(a) for a in CTX)
    inv_root = 1.0 / math.sqrt(rows * nx * nz * nc)
    col, x, z, core = (lax.axis_index(a) for a in ("col", "x", "zl", "core"))

    grads = lax.all_gather(out_grad, "row", axis=0)

    own = jnp.transpose(featured, (1, 0, 2))
    before = ctx_shift(own[:, rows - HALO :], 1)
    gated, *saved = forward(before, own, feat_taps, inner_taps)
    other = lax.ppermute(gated, "col", [(0, 1), (1, 0)])
    both = jnp.concatenate(
        [jnp.where(col == 0, gated, other), jnp.where(col == 0, other, gated)], axis=1
    )
    channels = both.shape[1]
    split = both.T.reshape(nx * nz, nc, channels // (nx * nz * nc), rows)
    kept, sent = (
        lax.dynamic_index_in_dim(split, c, 1, keepdims=False).reshape(channels // nc, rows)
        for c in (core, 1 - core)
    )

    far, near = gated_grad(jnp.full((1,), col, jnp.int32), grads, out_weight)
    arrived_far = lax.ppermute(far, "col", [(0, 1), (1, 0)])

    arrived = ctx_permute(sent_weight(sent, grads, far), lambda x, z, c: (x, z, 1 - c))
    own_x, *pieces = kept_weight(jnp.full((1,), x, jnp.int32), nx, kept, grads, arrived)
    arrived = rotated(pieces, "x")

    grad_own, head, tail, taps = backward(
        near, arrived_far, saved, before, own, feat_taps, inner_taps, own_x
    )
    head = ctx_shift(head, -1)
    taps = taps + ctx_permute(taps, lambda x, z, c: (x, z, c ^ 1))
    taps = taps + ctx_permute(taps, lambda x, z, c: (x ^ 1, z, c))
    taps_arrived = ctx_permute(taps, lambda x, z, c: (nx - 1 - x, z, c))
    own_z, taps, *rest = middle(
        jnp.full((1,), z, jnp.int32), nz, own_x, arrived, taps, taps_arrived, tail, head, grad_own
    )
    *pieces, grad_own = rest
    grad_weight, grad_feat_taps, grad_inner_taps = last(
        inv_root, own_z, taps, rotated(pieces, "zl")
    )
    return jnp.transpose(grad_own, (1, 0, 2)), grad_weight, grad_feat_taps, grad_inner_taps


def fine_mesh(mesh):
    row, col, ctx = mesh.devices.shape
    return Mesh(mesh.devices.reshape(row, col, ctx // 8, 4, 2), ("row", "col", *CTX))


def solution(mesh):
    return jax.shard_map(
        body,
        mesh=fine_mesh(mesh),
        in_specs=(
            P(CTX, None, ("row", "col")),
            P(None, None, ("row", "col")),
            P(None, ("row", "col")),
            P("row", "col"),
            P(CTX, ("col", "row")),
        ),
        out_specs=(
            P(CTX, None, ("row", "col")),
            P(("row", *CTX), "col"),
            P(None, None, ("row", "col")),
            P(None, ("row", "col")),
        ),
        check_vma=False,
    )
```

time: 400 us -> 148 us (0.37)
  blocking collectives: 144 us -> 0 us
  waiting for transfers between devices: 181 us -> 38.1 us
  starting transfers between devices: 24.3 us -> 56 us
  Pallas kernels: 0 us -> 30.6 us
  other arithmetic: 15.4 us -> 1.8 us
  matrix products: 10 us -> 0 us
    psum x1 -> x0, blocking collectives: 132 us -> none  [body(): inner_total, feat_total = lax.psum((inner_local, feat_local), 'ctx')]
    all_gather x2 -> x1, waiting for transfers between devices: 142 us -> 18.5 us  [body(): grads = lax.all_gather(out_grad, 'row', axis=0)]
    ppermute x3 -> x14, starting transfers between devices: 17 us -> 56 us  [the longest x6 19.7 us: rotated(): lax.ppermute(piece, axis, [(i, (i + step) % count) for i in range(count)])]
    pallas_call x0 -> x7, Pallas kernels: none -> 30.6 us  [the longest x1 6.68 us: kept_weight(): call(kept_weight_kernel, 'kept_weight', 2 * rows * channels * blocks * wi...]
    ppermute x3 -> x14, waiting for transfers between devices: 35.9 us -> 18.9 us  [the longest x1 6.53 us: body(): other = lax.ppermute(gated, 'col', [(0, 1), (1, 0)])]
    all_gather x1 -> x0, blocking collectives: 12.6 us -> none  [body(): gathered_gated = lax.all_gather(gated, 'col', axis=1, tiled=True)]
    dot_general x2 -> x0, matrix products: 10 us -> none  [the longest x1 6.8 us: body(): lax.dot_general(full_grad, own_weight, (((1,), (1,)), ((), ())), preferre...]
    all_to_all x1 -> x0, starting transfers between devices: 7.23 us -> none  [body(): lax.all_to_all(out_weight, 'col', split_axis=0, concat_axis=1, tiled=True)]
  transfers between devices with their start and end apart: 7 -> 15, of which waited for: 5 -> 8; matrix products, arithmetic and copies ran while one was open for 5% -> 2% of each run, Pallas kernels for 0% -> 10%
where the time goes in v2:
time: 148 us; the launch traced here: 146 us
  starting transfers between devices  56 us (38%)
  waiting for transfers between devices  38.1 us (26%)
  Pallas kernels  30.6 us (21%)
  between operations  14.3 us (10%)
  local copies, waits for them, and re-layouts  5.61 us (4%)
  other arithmetic  1.8 us (1%)
    ppermute x6, starting transfers between devices, rotated(): lax.ppermute(piece, axis, [(i, (i + step) % count) for i in range(count)])  19.7 us
    all_gather x1, waiting for transfers between devices, body(): grads = lax.all_gather(out_grad, 'row', axis=0)  18.5 us
    ppermute x4, starting transfers between devices, ctx_permute(): return lax.ppermute(value, CTX, pairs)  13.3 us
    ppermute x2, starting transfers between devices, ctx_shift(): lax.ppermute(value, CTX, [(i, i + steps) for i in range(count) if 0 <= i...  7.91 us
    ppermute x1, starting transfers between devices, body(): arrived_far = lax.ppermute(far, 'col', [(0, 1), (1, 0)])  7.76 us
    ppermute x1, starting transfers between devices, body(): other = lax.ppermute(gated, 'col', [(0, 1), (1, 0)])  7.22 us
    pallas_call x1, Pallas kernels, kept_weight(): call(kept_weight_kernel, 'kept_weight', 2 * rows * channels * blocks * wi...  6.68 us
    ppermute x1, waiting for transfers between devices, body(): other = lax.ppermute(gated, 'col', [(0, 1), (1, 0)])  6.53 us
  transfers between devices with their start and end apart: 15, of which 8 were waited for; matrix products, arithmetic and copies ran while one was open for 2% of the time, Pallas kernels for 10%

profile of v2, /device:TPU:1, one launch (start us, length us, event | category | flops | bytes accessed | tf_op | source)
XLA Modules:
  0.0 146.4 jit_solution(7167541874759754224)
XLA Ops:
  8.6 5.4 %collective-permute-start = (bf16[3,16,256]{2,1,0:T(8,128)(2,1)S(1)}, bf16[3,16,256]{2,1,0:T(8,128)(2,1)S(1)}, u32[]{:S(2)}, u32[]{:S(2)}) collective-permute-start(bf16[3,16,256]{2,1,0:T(8,128)(2,1)S(1)} %slice.4), channel_id=1, source_target_pairs={{0,1},{1,2},{2,3},{3,4},{4,5},{5,6},{6,7},{7,8},{8,9},{9,10},{10,1... | collective-permute-start | bytes 73736 | tf_op jit(solution)/shard_map/ppermute | solution.py:398
  14.0 3.4 %collective-permute-done.before = bf16[3,16,256]{2,1,0:T(8,128)(2,1)S(1)} collective-permute-done((bf16[3,16,256]{2,1,0:T(8,128)(2,1)S(1)}, bf16[3,16,256]{2,1,0:T(8,128)(2,1)S(1)}, u32[]{:S(2)}, u32[]{:S(2)}) %collective-permute-start) | collective-permute-done | bytes 24608 | tf_op jit(solution)/shard_map/ppermute | solution.py:398
  18.1 3.0 %forward.1 = (bf16[512,256]{1,0:T(8,128)(2,1)}, f32[520,256]{1,0:T(8,128)}, f32[512,256]{1,0:T(8,128)}, f32[520,256]{1,0:T(8,128)}, f32[520,256]{1,0:T(8,128)}, /*index=5*/f32[520,256]{1,0:T(8,128)}) custom-call(bf16[3,16,256]{2,1,0:T(8,128)(2,1)} %copy-done.7, bf16[3,512,256]{2,1,0:T(8,128)(2,1)} %bitcast.15, f32[3,7,256]{2,1,0:T(8,128)} %feat_taps.3, ...), custom_call_target="tpu_custom_call" | custom-call | flops 7864320 | bytes 3932160 | tf_op jit(solution)/shard_map/forward/pallas_call | solution.py:88
  21.1 7.2 %collective-permute-start.1 = (bf16[512,256]{1,0:T(8,128)(2,1)}, bf16[512,256]{1,0:T(8,128)(2,1)S(1)}, u32[]{:S(2)}, u32[]{:S(2)}) collective-permute-start(bf16[512,256]{1,0:T(8,128)(2,1)} %get-tuple-element.29), channel_id=1, source_target_pairs={{0,32},{32,0},{1,33},{33,1},{2,34},{34,2},{3,35},{35,3},{4,36},{36... | collective-permute-start | bytes 786440 | tf_op jit(solution)/shard_map/ppermute | solution.py:422
  28.3 6.5 %collective-permute-done.1 = bf16[512,256]{1,0:T(8,128)(2,1)S(1)} collective-permute-done((bf16[512,256]{1,0:T(8,128)(2,1)}, bf16[512,256]{1,0:T(8,128)(2,1)S(1)}, u32[]{:S(2)}, u32[]{:S(2)}) %collective-permute-start.1) | collective-permute-done | bytes 262176 | tf_op jit(solution)/shard_map/ppermute | solution.py:422
  34.8 1.0 broadcast_select_fusion.1
  36.1 0.9 constant_dynamic-slice_fusion
  37.0 18.5 %all-gather.3.cloned.1.call-done = bf16[4096,256]{1,0:T(8,128)(2,1)} async-done(((bf16[512,256]{1,0:T(8,128)(2,1)}), bf16[4096,256]{1,0:T(8,128)(2,1)}) %all-gather.3.cloned.1.call-update) | async-done | bytes 2097168 | tf_op jit(solution)/shard_map/all_gather | solution.py:417
  55.5 6.1 %gated_grad.1 = (bf16[512,256]{1,0:T(8,128)(2,1)}, f32[512,256]{1,0:T(8,128)}) custom-call(s32[1]{0:T(128)} %bitcast.8.col, bf16[8,512,256]{2,1,0:T(8,128)(2,1)} %bitcast.11, bf16[512,2048]{1,0:T(8,128)(2,1)} %weight.1), custom_call_target="tpu_custom_call" | custom-call | flops 1073741824 | bytes 4980736 | tf_op jit(solution)/shard_map/gated_grad/pallas_call | solution.py:223
  61.6 6.3 %sent_weight.1 = bf16[8,256,256]{2,1,0:T(8,128)(2,1)} custom-call(bf16[256,512]{1,0:T(8,128)(2,1)} %bitcast.18, bf16[8,512,256]{2,1,0:T(8,128)(2,1)} %bitcast.12, bf16[512,256]{1,0:T(8,128)(2,1)} %get-tuple-element.30._), custom_call_target="tpu_custom_call" | custom-call | flops 536870912 | bytes 3407872 | tf_op jit(solution)/shard_map/sent_weight/pallas_call | solution.py:249
  67.9 6.2 %collective-permute-start.2 = (bf16[8,256,256]{2,1,0:T(8,128)(2,1)}, bf16[8,256,256]{2,1,0:T(8,128)(2,1)S(1)}, u32[]{:S(2)}, u32[]{:S(2)}) collective-permute-start(bf16[8,256,256]{2,1,0:T(8,128)(2,1)} %sent_weight.1), channel_id=1, source_target_pairs={{0,1},{1,0},{2,3},{3,2},{4,5},{5,4},{6,7},{7,6},{8,9},{9,8},{10,11... | collective-permute-start | bytes 3145736 | tf_op jit(solution)/shard_map/ppermute | solution.py:393
  74.2 7.8 %collective-permute-start.6 = (bf16[512,256]{1,0:T(8,128)(2,1)S(1)}, bf16[512,256]{1,0:T(8,128)(2,1)S(1)}, u32[]{:S(2)}, u32[]{:S(2)}) collective-permute-start(bf16[512,256]{1,0:T(8,128)(2,1)S(1)} %copy-done.1), channel_id=1, source_target_pairs={{0,32},{32,0},{1,33},{33,1},{2,34},{34,2},{3,35},{35,3},{4,36},{36... | collective-permute-start | bytes 786440 | tf_op jit(solution)/shard_map/ppermute | solution.py:434
  82.0 1.0 copy-done
  82.9 6.7 %kept_weight.1 = (f32[8,64,256]{2,1,0:T(8,128)}, bf16[8,64,256]{2,1,0:T(8,128)(2,1)}, bf16[8,64,256]{2,1,0:T(8,128)(2,1)}, bf16[8,64,256]{2,1,0:T(8,128)(2,1)}) custom-call(s32[1]{0:T(128)} %bitcast.1.x, bf16[256,512]{1,0:T(8,128)(2,1)} %bitcast.19, bf16[8,512,256]{2,1,0:T(8,128)(2,1)} %bitcast.13, bf16[8,256,256]{2,1,0:T(8,128)(2,1)} %copy-done), custom_call_target="tpu_custom_call" | custom-call | flops 536870912 | bytes 5505024 | tf_op jit(solution)/shard_map/kept_weight/pallas_call | solution.py:284
  89.6 3.4 %collective-permute-start.3 = (bf16[8,64,256]{2,1,0:T(8,128)(2,1)}, bf16[8,64,256]{2,1,0:T(8,128)(2,1)S(1)}, u32[]{:S(2)}, u32[]{:S(2)}) collective-permute-start(bf16[8,64,256]{2,1,0:T(8,128)(2,1)} %get-tuple-element.32), channel_id=1, source_target_pairs={{0,8},{8,16},{16,24},{24,0},{1,9},{9,17},{17,25},{25,1},{2,10},{10... | collective-permute-start | bytes 786440 | tf_op jit(solution)/shard_map/ppermute | solution.py:406
  93.0 4.3 %collective-permute-start.4 = (bf16[8,64,256]{2,1,0:T(8,128)(2,1)}, bf16[8,64,256]{2,1,0:T(8,128)(2,1)S(1)}, u32[]{:S(2)}, u32[]{:S(2)}) collective-permute-start(bf16[8,64,256]{2,1,0:T(8,128)(2,1)} %get-tuple-element.33), channel_id=1, source_target_pairs={{0,16},{8,24},{16,0},{24,8},{1,17},{9,25},{17,1},{25,9},{2,18},{10... | collective-permute-start | bytes 786440 | tf_op jit(solution)/shard_map/ppermute | solution.py:406
  97.3 3.1 %collective-permute-start.5 = (bf16[8,64,256]{2,1,0:T(8,128)(2,1)}, bf16[8,64,256]{2,1,0:T(8,128)(2,1)S(1)}, u32[]{:S(2)}, u32[]{:S(2)}) collective-permute-start(bf16[8,64,256]{2,1,0:T(8,128)(2,1)} %get-tuple-element.34), channel_id=1, source_target_pairs={{0,24},{8,0},{16,8},{24,16},{1,25},{9,1},{17,9},{25,17},{2,26},{10... | collective-permute-start | bytes 786440 | tf_op jit(solution)/shard_map/ppermute | solution.py:406
  101.1 4.5 %backward.1 = (bf16[3,512,256]{2,1,0:T(8,128)(2,1)}, f32[3,16,256]{2,1,0:T(8,128)}, f32[3,16,256]{2,1,0:T(8,128)}, f32[4,8,256]{2,1,0:T(8,128)}) custom-call(f32[512,256]{1,0:T(8,128)} %get-tuple-element.35.near, bf16[512,256]{1,0:T(8,128)(2,1)} %copy-done.5, f32[520,256]{1,0:T(8,128)} %get-tuple-element.36.query, f32[512,256]{1,0:T(8,128)} %get-tuple-element.37.window, ...), custom_call_target="tpu_custom_call" | custom-call | flops 15728640 | bytes 5242880 | tf_op jit(solution)/shard_map/backward/pallas_call | solution.py:174
  105.6 3.0 %collective-permute-start.7 = (f32[4,8,256]{2,1,0:T(8,128)}, f32[4,8,256]{2,1,0:T(8,128)S(1)}, u32[]{:S(2)}, u32[]{:S(2)}) collective-permute-start(f32[4,8,256]{2,1,0:T(8,128)} %get-tuple-element.41), channel_id=1, source_target_pairs={{0,1},{1,0},{2,3},{3,2},{4,5},{5,4},{6,7},{7,6},{8,9},{9,8},{10,11... | collective-permute-start | bytes 98312 | tf_op jit(solution)/shard_map/ppermute | solution.py:393
  108.6 1.0 collective-permute-done.7
  110.4 2.2 %collective-permute-start.8 = (f32[4,8,256]{2,1,0:T(8,128)S(1)}, f32[4,8,256]{2,1,0:T(8,128)S(1)}, u32[]{:S(2)}, u32[]{:S(2)}) collective-permute-start(f32[4,8,256]{2,1,0:T(8,128)S(1)} %add.16), channel_id=1, source_target_pairs={{0,8},{1,9},{2,10},{3,11},{4,12},{5,13},{6,14},{7,15},{8,0},{9,1},... | collective-permute-start | bytes 98312 | tf_op jit(solution)/shard_map/ppermute | solution.py:393
  112.6 2.5 %collective-permute-start.10 = (f32[3,16,256]{2,1,0:T(8,128)}, f32[3,16,256]{2,1,0:T(8,128)S(1)}, u32[]{:S(2)}, u32[]{:S(2)}) collective-permute-start(f32[3,16,256]{2,1,0:T(8,128)} %get-tuple-element.43), channel_id=1, source_target_pairs={{1,0},{2,1},{3,2},{4,3},{5,4},{6,5},{7,6},{8,7},{9,8},{10,9},{11,1... | collective-permute-start | bytes 147464 | tf_op jit(solution)/shard_map/ppermute | solution.py:398
  115.2 1.9 %collective-permute-start.9 = (f32[4,8,256]{2,1,0:T(8,128)S(1)}, f32[4,8,256]{2,1,0:T(8,128)S(1)}, u32[]{:S(2)}, u32[]{:S(2)}) collective-permute-start(f32[4,8,256]{2,1,0:T(8,128)S(1)} %add.17.refs_5_), channel_id=1, source_target_pairs={{0,24},{1,25},{2,26},{3,27},{4,28},{5,29},{6,30},{7,31},{8,16},{9,... | collective-permute-start | bytes 98312 | tf_op jit(solution)/shard_map/ppermute | solution.py:393
  117.1 1.1 collective-permute-done.10.refs_8_
  118.2 2.8 %collective-permute-done.9.refs_6_ = f32[4,8,256]{2,1,0:T(8,128)S(1)} collective-permute-done((f32[4,8,256]{2,1,0:T(8,128)S(1)}, f32[4,8,256]{2,1,0:T(8,128)S(1)}, u32[]{:S(2)}, u32[]{:S(2)}) %collective-permute-start.9) | collective-permute-done | bytes 32800 | tf_op jit(solution)/shard_map/ppermute | solution.py:393
  122.0 2.3 %middle.1 = (f32[8,16,256]{2,1,0:T(8,128)}, f32[4,8,256]{2,1,0:T(8,128)}, bf16[12,16,256]{2,1,0:T(8,128)(2,1)}, bf16[12,16,256]{2,1,0:T(8,128)(2,1)}, bf16[12,16...) custom-call(s32[1]{0:T(128)} %bitcast.refs_0_, ...), custom_call_target="tpu_custom_call", output_to_operand_aliasing={{5}: (9, {})} | custom-call | flops 524288 | bytes 1310720 | tf_op jit(solution)/shard_map/middle/pallas_call | solution.py:326
  124.2 2.3 %collective-permute-start.11 = (bf16[12,16,256]{2,1,0:T(8,128)(2,1)}, bf16[12,16,256]{2,1,0:T(8,128)(2,1)S(1)}, u32[]{:S(2)}, u32[]{:S(2)}) collective-permute-start(bf16[12,16,256]{2,1,0:T(8,128)(2,1)} %get-tuple-element.48), channel_id=1, source_target_pairs={{0,2},{2,4},{4,6},{6,0},{1,3},{3,5},{5,7},{7,1},{8,10},{10,12},{12... | collective-permute-start | bytes 294920 | tf_op jit(solution)/shard_map/ppermute | solution.py:406
  126.5 2.5 %collective-permute-start.12 = (bf16[12,16,256]{2,1,0:T(8,128)(2,1)}, bf16[12,16,256]{2,1,0:T(8,128)(2,1)S(1)}, u32[]{:S(2)}, u32[]{:S(2)}) collective-permute-start(bf16[12,16,256]{2,1,0:T(8,128)(2,1)} %get-tuple-element.49), channel_id=1, source_target_pairs={{0,4},{2,6},{4,0},{6,2},{1,5},{3,7},{5,1},{7,3},{8,12},{10,14},{12... | collective-permute-start | bytes 294920 | tf_op jit(solution)/shard_map/ppermute | solution.py:406
  129.1 4.2 %collective-permute-start.13 = (bf16[12,16,256]{2,1,0:T(8,128)(2,1)}, bf16[12,16,256]{2,1,0:T(8,128)(2,1)S(1)}, u32[]{:S(2)}, u32[]{:S(2)}) collective-permute-start(bf16[12,16,256]{2,1,0:T(8,128)(2,1)} %get-tuple-element.50), channel_id=1, source_target_pairs={{0,6},{2,0},{4,2},{6,4},{1,7},{3,1},{5,3},{7,5},{8,14},{10,8},{12,... | collective-permute-start | bytes 294920 | tf_op jit(solution)/shard_map/ppermute | solution.py:406
  133.3 2.1 %collective-permute-done.12.refs_3_ = bf16[12,16,256]{2,1,0:T(8,128)(2,1)S(1)} collective-permute-done((bf16[12,16,256]{2,1,0:T(8,128)(2,1)}, bf16[12,16,256]{2,1,0:T(8,128)(2,1)S(1)}, u32[]{:S(2)}, u32[]{:S(2)}) %collective-permute-start.12) | collective-permute-done | bytes 98336 | tf_op jit(solution)/shard_map/ppermute | solution.py:406
  135.4 1.8 %collective-permute-done.13.refs_4_ = bf16[12,16,256]{2,1,0:T(8,128)(2,1)S(1)} collective-permute-done((bf16[12,16,256]{2,1,0:T(8,128)(2,1)}, bf16[12,16,256]{2,1,0:T(8,128)(2,1)S(1)}, u32[]{:S(2)}, u32[]{:S(2)}) %collective-permute-start.13) | collective-permute-done | bytes 98336 | tf_op jit(solution)/shard_map/ppermute | solution.py:406
  137.8 1.7 %last.1 = (bf16[16,2048]{1,0:T(8,128)(2,1)}, f32[3,7,256]{2,1,0:T(8,128)}, f32[7,256]{1,0:T(8,128)}) custom-call(f32[8,16,256]{2,1,0:T(8,128)} %get-tuple-element.46.refs_0_, f32[4,8,256]{2,1,0:T(8,128)} %get-tuple-element.47.refs_1_, bf16[12,16,256]{2,1,0:T(8,128)(2,1)} %copy-done.8, bf16[12,16,256]{2,1,0:T(8,128)(2,1)} %copy-done.9, ...), custom_call_target="tpu_custom_call" | custom-call | flops 131072 | bytes 393216 | tf_op jit(solution)/shard_map/last/pallas_call | solution.py:373
  (39 shorter events, 5.3 us)
Async XLA Ops:
  7.2 48.3 %all-gather.3.cloned.1.call-start = ((), (), s32[]{:S(2)}) async-start(), calls=%async_computation | async-start | bytes 2359296 | tf_op jit(solution)/shard_map/all_gather | solution.py:417
  8.6 8.8 %collective-permute-start = (bf16[3,16,256]{2,1,0:T(8,128)(2,1)S(1)}, bf16[3,16,256]{2,1,0:T(8,128)(2,1)S(1)}, u32[]{:S(2)}, u32[]{:S(2)}) collective-permute-start(bf16[3,16,256]{2,1,0:T(8,128)(2,1)S(1)} %slice.4), channel_id=1, source_target_pairs={{0,1},{1,2},{2,3},{3,4},{4,5},{5,6},{6,7},{7,8},{8,9},{9,10},{10,1... | collective-permute-start | bytes 73736 | tf_op jit(solution)/shard_map/ppermute | solution.py:398
  17.5 0.6 copy-start.7
  21.1 13.8 %collective-permute-start.1 = (bf16[512,256]{1,0:T(8,128)(2,1)}, bf16[512,256]{1,0:T(8,128)(2,1)S(1)}, u32[]{:S(2)}, u32[]{:S(2)}) collective-permute-start(bf16[512,256]{1,0:T(8,128)(2,1)} %get-tuple-element.29), channel_id=1, source_target_pairs={{0,32},{32,0},{1,33},{33,1},{2,34},{34,2},{3,35},{35,3},{4,36},{36... | collective-permute-start | bytes 786440 | tf_op jit(solution)/shard_map/ppermute | solution.py:422
  61.6 12.5 %copy-start.1 = (bf16[512,256]{1,0:T(8,128)(2,1)S(1)}, bf16[512,256]{1,0:T(8,128)(2,1)}, u32[]{:S(2)}) copy-start(bf16[512,256]{1,0:T(8,128)(2,1)} %get-tuple-element.30._) | copy-start | bytes 786436
  67.9 14.0 %collective-permute-start.2 = (bf16[8,256,256]{2,1,0:T(8,128)(2,1)}, bf16[8,256,256]{2,1,0:T(8,128)(2,1)S(1)}, u32[]{:S(2)}, u32[]{:S(2)}) collective-permute-start(bf16[8,256,256]{2,1,0:T(8,128)(2,1)} %sent_weight.1), channel_id=1, source_target_pairs={{0,1},{1,0},{2,3},{3,2},{4,5},{5,4},{6,7},{7,6},{8,9},{9,8},{10,11... | collective-permute-start | bytes 3145736 | tf_op jit(solution)/shard_map/ppermute | solution.py:393
  74.2 26.2 %collective-permute-start.6 = (bf16[512,256]{1,0:T(8,128)(2,1)S(1)}, bf16[512,256]{1,0:T(8,128)(2,1)S(1)}, u32[]{:S(2)}, u32[]{:S(2)}) collective-permute-start(bf16[512,256]{1,0:T(8,128)(2,1)S(1)} %copy-done.1), channel_id=1, source_target_pairs={{0,32},{32,0},{1,33},{33,1},{2,34},{34,2},{3,35},{35,3},{4,36},{36... | collective-permute-start | bytes 786440 | tf_op jit(solution)/shard_map/ppermute | solution.py:434
  81.9 1.0 copy-start
  89.6 31.5 %collective-permute-start.3 = (bf16[8,64,256]{2,1,0:T(8,128)(2,1)}, bf16[8,64,256]{2,1,0:T(8,128)(2,1)S(1)}, u32[]{:S(2)}, u32[]{:S(2)}) collective-permute-start(bf16[8,64,256]{2,1,0:T(8,128)(2,1)} %get-tuple-element.32), channel_id=1, source_target_pairs={{0,8},{8,16},{16,24},{24,0},{1,9},{9,17},{17,25},{25,1},{2,10},{10... | collective-permute-start | bytes 786440 | tf_op jit(solution)/shard_map/ppermute | solution.py:406
  93.0 28.1 %collective-permute-start.4 = (bf16[8,64,256]{2,1,0:T(8,128)(2,1)}, bf16[8,64,256]{2,1,0:T(8,128)(2,1)S(1)}, u32[]{:S(2)}, u32[]{:S(2)}) collective-permute-start(bf16[8,64,256]{2,1,0:T(8,128)(2,1)} %get-tuple-element.33), channel_id=1, source_target_pairs={{0,16},{8,24},{16,0},{24,8},{1,17},{9,25},{17,1},{25,9},{2,18},{10... | collective-permute-start | bytes 786440 | tf_op jit(solution)/shard_map/ppermute | solution.py:406
  97.3 23.8 %collective-permute-start.5 = (bf16[8,64,256]{2,1,0:T(8,128)(2,1)}, bf16[8,64,256]{2,1,0:T(8,128)(2,1)S(1)}, u32[]{:S(2)}, u32[]{:S(2)}) collective-permute-start(bf16[8,64,256]{2,1,0:T(8,128)(2,1)} %get-tuple-element.34), channel_id=1, source_target_pairs={{0,24},{8,0},{16,8},{24,16},{1,25},{9,1},{17,9},{25,17},{2,26},{10... | collective-permute-start | bytes 786440 | tf_op jit(solution)/shard_map/ppermute | solution.py:406
  100.4 0.7 copy-start.5
  105.6 4.1 %collective-permute-start.7 = (f32[4,8,256]{2,1,0:T(8,128)}, f32[4,8,256]{2,1,0:T(8,128)S(1)}, u32[]{:S(2)}, u32[]{:S(2)}) collective-permute-start(f32[4,8,256]{2,1,0:T(8,128)} %get-tuple-element.41), channel_id=1, source_target_pairs={{0,1},{1,0},{2,3},{3,2},{4,5},{5,4},{6,7},{7,6},{8,9},{9,8},{10,11... | collective-permute-start | bytes 98312 | tf_op jit(solution)/shard_map/ppermute | solution.py:393
  110.4 4.7 %collective-permute-start.8 = (f32[4,8,256]{2,1,0:T(8,128)S(1)}, f32[4,8,256]{2,1,0:T(8,128)S(1)}, u32[]{:S(2)}, u32[]{:S(2)}) collective-permute-start(f32[4,8,256]{2,1,0:T(8,128)S(1)} %add.16), channel_id=1, source_target_pairs={{0,8},{1,9},{2,10},{3,11},{4,12},{5,13},{6,14},{7,15},{8,0},{9,1},... | collective-permute-start | bytes 98312 | tf_op jit(solution)/shard_map/ppermute | solution.py:393
  112.6 5.6 %collective-permute-start.10 = (f32[3,16,256]{2,1,0:T(8,128)}, f32[3,16,256]{2,1,0:T(8,128)S(1)}, u32[]{:S(2)}, u32[]{:S(2)}) collective-permute-start(f32[3,16,256]{2,1,0:T(8,128)} %get-tuple-element.43), channel_id=1, source_target_pairs={{1,0},{2,1},{3,2},{4,3},{5,4},{6,5},{7,6},{8,7},{9,8},{10,9},{11,1... | collective-permute-start | bytes 147464 | tf_op jit(solution)/shard_map/ppermute | solution.py:398
  115.2 5.9 %copy-start.6 = (f32[4,8,256]{2,1,0:T(8,128)}, f32[4,8,256]{2,1,0:T(8,128)S(1)}, u32[]{:S(2)}) copy-start(f32[4,8,256]{2,1,0:T(8,128)S(1)} %add.17.refs_5_) | copy-start | bytes 98308
  115.2 5.9 %collective-permute-start.9 = (f32[4,8,256]{2,1,0:T(8,128)S(1)}, f32[4,8,256]{2,1,0:T(8,128)S(1)}, u32[]{:S(2)}, u32[]{:S(2)}) collective-permute-start(f32[4,8,256]{2,1,0:T(8,128)S(1)} %add.17.refs_5_), channel_id=1, source_target_pairs={{0,24},{1,25},{2,26},{3,27},{4,28},{5,29},{6,30},{7,31},{8,16},{9,... | collective-permute-start | bytes 98312 | tf_op jit(solution)/shard_map/ppermute | solution.py:393
  118.2 2.9 %copy-start.11 = (f32[3,16,256]{2,1,0:T(8,128)}, f32[3,16,256]{2,1,0:T(8,128)S(1)}, u32[]{:S(2)}) copy-start(f32[3,16,256]{2,1,0:T(8,128)S(1)} %collective-permute-done.10.refs_8_) | copy-start | bytes 147460
  121.1 0.6 copy-start.12
  121.1 0.7 copy-start.2
  121.1 0.8 copy-start.3
  121.1 0.9 copy-start.4
  124.2 9.0 %collective-permute-start.11 = (bf16[12,16,256]{2,1,0:T(8,128)(2,1)}, bf16[12,16,256]{2,1,0:T(8,128)(2,1)S(1)}, u32[]{:S(2)}, u32[]{:S(2)}) collective-permute-start(bf16[12,16,256]{2,1,0:T(8,128)(2,1)} %get-tuple-element.48), channel_id=1, source_target_pairs={{0,2},{2,4},{4,6},{6,0},{1,3},{3,5},{5,7},{7,1},{8,10},{10,12},{12... | collective-permute-start | bytes 294920 | tf_op jit(solution)/shard_map/ppermute | solution.py:406
  126.5 8.9 %collective-permute-start.12 = (bf16[12,16,256]{2,1,0:T(8,128)(2,1)}, bf16[12,16,256]{2,1,0:T(8,128)(2,1)S(1)}, u32[]{:S(2)}, u32[]{:S(2)}) collective-permute-start(bf16[12,16,256]{2,1,0:T(8,128)(2,1)} %get-tuple-element.49), channel_id=1, source_target_pairs={{0,4},{2,6},{4,0},{6,2},{1,5},{3,7},{5,1},{7,3},{8,12},{10,14},{12... | collective-permute-start | bytes 294920 | tf_op jit(solution)/shard_map/ppermute | solution.py:406
  129.1 8.1 %collective-permute-start.13 = (bf16[12,16,256]{2,1,0:T(8,128)(2,1)}, bf16[12,16,256]{2,1,0:T(8,128)(2,1)S(1)}, u32[]{:S(2)}, u32[]{:S(2)}) collective-permute-start(bf16[12,16,256]{2,1,0:T(8,128)(2,1)} %get-tuple-element.50), channel_id=1, source_target_pairs={{0,6},{2,0},{4,2},{6,4},{1,7},{3,1},{5,3},{7,5},{8,14},{10,8},{12,... | collective-permute-start | bytes 294920 | tf_op jit(solution)/shard_map/ppermute | solution.py:406
  133.3 3.9 %copy-start.8 = (bf16[12,16,256]{2,1,0:T(8,128)(2,1)}, bf16[12,16,256]{2,1,0:T(8,128)(2,1)S(1)}, u32[]{:S(2)}) copy-start(bf16[12,16,256]{2,1,0:T(8,128)(2,1)S(1)} %collective-permute-done.11.refs_2_) | copy-start | bytes 294916
  135.4 1.8 %copy-start.9 = (bf16[12,16,256]{2,1,0:T(8,128)(2,1)}, bf16[12,16,256]{2,1,0:T(8,128)(2,1)S(1)}, u32[]{:S(2)}) copy-start(bf16[12,16,256]{2,1,0:T(8,128)(2,1)S(1)} %collective-permute-done.12.refs_3_) | copy-start | bytes 294916
  137.2 0.6 copy-start.10
Sparse Core Ops, SparseCore 0:
  10.1 45.3 all-gather.2

commit v3 on v2

--- a/solution.py
+++ b/solution.py
@@ -16,7 +16,7 @@
 CTX = ("x", "zl", "core")
 F32 = jnp.float32
 BF16 = jnp.bfloat16
-VMEM_BYTES = 56 << 20
+VMEM_BYTES = 24 << 20
 
 
 def spread(total):
@@ -106,7 +106,7 @@
 
 
 def backward_kernel(
-    near, far, query, window, key, value, product, before, own, feat_taps, inner_taps, _,
+    col, near, far, query, window, key, value, product, before, own, feat_taps, inner_taps, _,
     grads, head, tail, tap_sums, feats, grad_window, grad_mixed,
 ):
     rows = own.shape[1]
@@ -119,7 +119,7 @@
         grad_mixed[j, HALO + rows :, :] = zeros[:LEAD]
     for start, count in spread(rows):
         at = HALO + start
-        total = near[start : start + count, :] + far[start : start + count, :].astype(F32)
+        total = near[start : start + count, :] + far[1 - col[0], start : start + count, :].astype(F32)
         grad_window[at : at + count, :] = total * query[LEAD + start : LEAD + start + count, :]
         grad_mixed[0, at : at + count, :] = total * window[start : start + count, :]
     for start, count in spread(rows + LEAD):
@@ -167,7 +167,7 @@
     put(3, sums)
 
 
-def backward(near, far, saved, before, own, feat_taps, inner_taps, after):
+def backward(col, near, far, saved, before, own, feat_taps, inner_taps, after):
     _, rows, channels = own.shape
     saved_spec = lane_spec(rows + LEAD)
     edge = jax.ShapeDtypeStruct((3, HALO, channels), F32)
@@ -178,8 +178,8 @@
         40 * rows * channels,
         grid=(channels // LANES,),
         in_specs=[
-            lane_spec(rows), lane_spec(rows), saved_spec, lane_spec(rows), saved_spec, saved_spec,
-            saved_spec, lane_spec(3, HALO), lane_spec(3, rows), lane_spec(3, TAPS),
+            SCALAR, lane_spec(rows), lane_spec(2, rows), saved_spec, lane_spec(rows), saved_spec,
+            saved_spec, saved_spec, lane_spec(3, HALO), lane_spec(3, rows), lane_spec(3, TAPS),
             lane_spec(TAPS), UNREAD,
         ],
         out_specs=[lane_spec(3, rows), lane_spec(3, HALO), lane_spec(3, HALO), lane_spec(4, 8)],
@@ -194,10 +194,10 @@
             pltpu.VMEM((rows + HALO + LEAD, LANES), F32),
             pltpu.VMEM((3, rows + HALO + LEAD, LANES), F32),
         ],
-    )(near, far, *saved, before, own, feat_taps, inner_taps, after)
-
-
-def gated_grad_kernel(col, grads, weight, far, near):
+    )(col, near, far, *saved, before, own, feat_taps, inner_taps, after)
+
+
+def gated_grad_kernel(col, grads, weight, _, far, near):
     wide = jnp.concatenate([grads[b] for b in range(grads.shape[0])], axis=1)
     total = lax.dot_general(
         wide, weight[...], (((1,), (1,)), ((), ())), preferred_element_type=F32
@@ -215,7 +215,7 @@
         far[...] = total[:, :half].astype(BF16)
 
 
-def gated_grad(col, grads, weight):
+def gated_grad(col, grads, weight, after):
     blocks, rows, width = grads.shape
     channels = weight.shape[0]
     half = channels // 2
@@ -230,20 +230,21 @@
             SCALAR,
             pl.BlockSpec((blocks, step, width), lambda i: (0, i, 0)),
             whole(weight.shape),
+            UNREAD,
         ],
         out_specs=[pl.BlockSpec((step, half), lambda i: (i, 0))] * 2,
         out_shape=[
             jax.ShapeDtypeStruct((rows, half), BF16),
             jax.ShapeDtypeStruct((rows, half), F32),
         ],
-    )(col, grads, weight)
-
-
-def sent_weight_kernel(gated, grad, _, out):
+    )(col, grads, weight, after)
+
+
+def sent_weight_kernel(gated, grad, out):
     out[0] = jnp.dot(gated[...], grad[0], preferred_element_type=F32).astype(BF16)
 
 
-def sent_weight(gated, grads, after):
+def sent_weight(gated, grads):
     channels, rows = gated.shape
     blocks, _, width = grads.shape
     return call(
@@ -255,107 +256,89 @@
         in_specs=[
             whole(gated.shape),
             pl.BlockSpec((1, rows, width), lambda i: (i, 0, 0)),
-            UNREAD,
         ],
         out_specs=pl.BlockSpec((1, channels, width), lambda i: (i, 0, 0)),
         out_shape=jax.ShapeDtypeStruct((blocks, channels, width), BF16),
-    )(gated, grads, after)
-
-
-def slices(place, held, parts, out_own, out_far):
-    size = held.shape[-2] // parts
-    out_own[...] = held[..., pl.ds(pl.multiple_of(place * size, size), size), :]
-    for step, out in enumerate(out_far, 1):
-        to = lax.rem(place + step, parts)
-        out[...] = held[..., pl.ds(pl.multiple_of(to * size, size), size), :].astype(BF16)
-
-
-def kept_weight_kernel(x, gated, grad, arrived, own, *rest):
-    *far, held = rest
-    held[0] = jnp.dot(gated[...], grad[0], preferred_element_type=F32) + arrived[0].astype(F32)
-    slices(x[0], held, len(far) + 1, own, far)
-
-
-def kept_weight(x, parts, gated, grads, arrived):
+    )(gated, grads)
+
+
+def kept_weight_kernel(gated, grad, arrived, _, out):
+    total = jnp.dot(gated[...], grad[0], preferred_element_type=F32) + arrived[0].astype(F32)
+    out[...] = total.astype(BF16).reshape(out.shape)
+
+
+def kept_weight(parts, gated, grads, arrived, after):
     channels, rows = gated.shape
     blocks, _, width = grads.shape
-    shape = (blocks, channels // parts, width)
-    spec = pl.BlockSpec((1, *shape[1:]), lambda i: (i, 0, 0))
+    size = channels // parts
     return call(
         kept_weight_kernel,
         "kept_weight",
         2 * rows * channels * blocks * width,
-        2 * blocks * width * (rows + 3 * channels) + 2 * rows * channels,
+        2 * blocks * width * (rows + 2 * channels) + 2 * rows * channels,
         grid=(blocks,),
         in_specs=[
-            SCALAR,
             whole(gated.shape),
             pl.BlockSpec((1, rows, width), lambda i: (i, 0, 0)),
             pl.BlockSpec((1, channels, width), lambda i: (i, 0, 0)),
-        ],
-        out_specs=[spec] * parts,
-        out_shape=[jax.ShapeDtypeStruct(shape, F32)]
-        + [jax.ShapeDtypeStruct(shape, BF16)] * (parts - 1),
-        scratch_shapes=[pltpu.VMEM((1, channels, width), F32)],
-    )(x, gated, grads, arrived)
-
-
-def middle_kernel(parts, z, own, *rest):
-    arrived, rest = rest[: parts - 1], rest[parts - 1 :]
-    taps, taps_arrived, tail, head, _, out_own, out_taps, *far, out_grads, held = rest
-    total = own[...]
-    for piece in arrived:
-        total = total + piece[...].astype(F32)
-    held[...] = total
-    blocks = held.shape[0]
-    slices(z[0], held, len(far) + 1, out_own, [out.at[0:blocks] for out in far])
+            UNREAD,
+        ],
+        out_specs=pl.BlockSpec((parts, 1, size, width), lambda i: (0, i, 0, 0)),
+        out_shape=jax.ShapeDtypeStruct((parts, blocks, size, width), BF16),
+    )(gated, grads, arrived, after)
+
+
+def middle_kernel(pair, taps, taps_arrived, tail, head, _, out, out_taps, out_grads):
+    parts, _, size, _ = out.shape
+    blocks = pair.shape[0]
     sums = taps[...] + taps_arrived[...]
     out_taps[...] = sums
     high = sums.astype(BF16).astype(F32)
     both = jnp.concatenate([high, sums - high], axis=1).astype(BF16)
-    for out in far:
-        out[blocks:, :, :] = both
+    for part in range(parts):
+        out[part, 0:blocks] = pair[:, part * size : (part + 1) * size, :]
+        out[part, blocks:] = both
     out_grads[...] = (tail[...] + head[...]).astype(BF16)
 
 
-def middle(z, parts, own, arrived, taps, taps_arrived, tail, head, grads):
-    blocks, channels, width = own.shape
-    shape = (blocks, channels // parts, width)
-    wire = (blocks + taps.shape[0], *shape[1:])
-    last = grads.shape[1] // HALO - 1
-    return call(
-        lambda *refs: middle_kernel(len(arrived) + 1, *refs),
+def middle(parts, pair, taps, taps_arrived, tail, head, grads):
+    blocks, channels, width = pair.shape
+    shape = (parts, blocks + taps.shape[0], channels // parts, width)
+    final = grads.shape[1] // HALO - 1
+    return call(
+        middle_kernel,
         "middle",
-        4 * own.size,
-        10 * own.size,
+        4 * pair.size,
+        4 * pair.size,
         grid=(1,),
-        in_specs=[SCALAR]
-        + [whole(v.shape) for v in (own, *arrived, taps, taps_arrived, tail, head)]
-        + [UNREAD],
-        out_specs=[whole(shape), whole(taps.shape)]
-        + [whole(wire)] * (parts - 1)
-        + [pl.BlockSpec(tail.shape, lambda i: (0, last, 0))],
-        out_shape=[jax.ShapeDtypeStruct(shape, F32), jax.ShapeDtypeStruct(taps.shape, F32)]
-        + [jax.ShapeDtypeStruct(wire, BF16)] * (parts - 1)
-        + [jax.ShapeDtypeStruct(grads.shape, grads.dtype)],
-        scratch_shapes=[pltpu.VMEM(own.shape, F32)],
-        input_output_aliases={len(arrived) + 6: parts + 1},
-    )(z, own, *arrived, taps, taps_arrived, tail, head, grads)
-
-
-def last_kernel(scale, own, taps, *rest):
-    *arrived, out, out_feat, out_inner = rest
-    blocks, _, width = own.shape
+        in_specs=[whole(v.shape) for v in (pair, taps, taps_arrived, tail, head)] + [UNREAD],
+        out_specs=[
+            whole(shape),
+            whole(taps.shape),
+            pl.BlockSpec(tail.shape, lambda i: (0, final, 0)),
+        ],
+        out_shape=[
+            jax.ShapeDtypeStruct(shape, BF16),
+            jax.ShapeDtypeStruct(taps.shape, F32),
+            jax.ShapeDtypeStruct(grads.shape, grads.dtype),
+        ],
+        input_output_aliases={5: 2},
+    )(pair, taps, taps_arrived, tail, head, grads)
+
+
+def last_kernel(scale, z, taps, arrived, out, out_feat, out_inner):
+    parts, _, _, width = arrived.shape
+    blocks = out.shape[1] // width
     for b in range(blocks):
-        total = own[b]
-        for piece in arrived:
-            total = total + piece[b].astype(F32)
+        total = arrived[0, b].astype(F32)
+        for part in range(1, parts):
+            total = total + arrived[part, b].astype(F32)
         out[:, b * width : (b + 1) * width] = (total * scale).astype(BF16)
     for j in range(4):
         total = taps[j]
-        for piece in arrived:
-            both = piece[blocks + j].astype(F32)
-            total = total + (both[:8] + both[8:])
+        for part in range(parts):
+            both = arrived[part, blocks + j].astype(F32)
+            total = total + jnp.where(z[0] == part, 0.0, both[:8] + both[8:])
         total = (total * scale)[:TAPS]
         if j < 3:
             out_feat[j] = total
@@ -363,8 +346,9 @@
             out_inner[...] = total
 
 
-def last(scale, own, taps, arrived):
-    blocks, channels, width = own.shape
+def last(scale, z, taps, arrived):
+    parts, count, channels, width = arrived.shape
+    blocks = count - taps.shape[0]
     shapes = [
         jax.ShapeDtypeStruct((channels, blocks * width), BF16),
         jax.ShapeDtypeStruct((3, TAPS, width), F32),
@@ -373,13 +357,13 @@
     return call(
         lambda *refs: last_kernel(scale, *refs),
         "last",
-        4 * own.size,
-        12 * own.size,
+        2 * arrived.size,
+        2 * arrived.size,
         grid=(1,),
-        in_specs=[whole(v.shape) for v in (own, taps, *arrived)],
+        in_specs=[SCALAR, whole(taps.shape), whole(arrived.shape)],
         out_specs=[whole(s.shape) for s in shapes],
         out_shape=shapes,
-    )(own, taps, *arrived)
+    )(z, taps, arrived)
 
 
 def ctx_permute(value, target):
@@ -400,29 +384,19 @@
     )
 
 
-def rotated(pieces, axis):
-    count = lax.axis_size(axis)
-    return [
-        lax.ppermute(piece, axis, [(i, (i + step) % count) for i in range(count)])
-        for step, piece in enumerate(pieces, 1)
-    ]
-
-
 def body(featured, feat_taps, inner_taps, out_weight, out_grad):
     rows = featured.shape[0]
     nx, nz, nc = (lax.axis_size(a) for a in CTX)
     inv_root = 1.0 / math.sqrt(rows * nx * nz * nc)
-    col, x, z, core = (lax.axis_index(a) for a in ("col", "x", "zl", "core"))
+    core = lax.axis_index("core")
+    col, z = (jnp.full((1,), lax.axis_index(a), jnp.int32) for a in ("col", "zl"))
 
     grads = lax.all_gather(out_grad, "row", axis=0)
 
     own = jnp.transpose(featured, (1, 0, 2))
     before = ctx_shift(own[:, rows - HALO :], 1)
     gated, *saved = forward(before, own, feat_taps, inner_taps)
-    other = lax.ppermute(gated, "col", [(0, 1), (1, 0)])
-    both = jnp.concatenate(
-        [jnp.where(col == 0, gated, other), jnp.where(col == 0, other, gated)], axis=1
-    )
+    both = lax.all_gather(gated, "col", axis=1, tiled=True)
     channels = both.shape[1]
     split = both.T.reshape(nx * nz, nc, channels // (nx * nz * nc), rows)
     kept, sent = (
@@ -430,27 +404,24 @@
         for c in (core, 1 - core)
     )
 
-    far, near = gated_grad(jnp.full((1,), col, jnp.int32), grads, out_weight)
-    arrived_far = lax.ppermute(far, "col", [(0, 1), (1, 0)])
-
-    arrived = ctx_permute(sent_weight(sent, grads, far), lambda x, z, c: (x, z, 1 - c))
-    own_x, *pieces = kept_weight(jnp.full((1,), x, jnp.int32), nx, kept, grads, arrived)
-    arrived = rotated(pieces, "x")
-
+    sent = sent_weight(sent, grads)
+    arrived = ctx_permute(sent, lambda x, z, c: (x, z, 1 - c))
+    far, near = gated_grad(col, grads, out_weight, sent)
+    pair = kept_weight(nx, kept, grads, arrived, far)
+    pair = lax.psum_scatter(pair, "x", scatter_dimension=0)
+
+    far = lax.all_gather(far, "col", axis=0)
     grad_own, head, tail, taps = backward(
-        near, arrived_far, saved, before, own, feat_taps, inner_taps, own_x
+        col, near, far, saved, before, own, feat_taps, inner_taps, far
     )
     head = ctx_shift(head, -1)
-    taps = taps + ctx_permute(taps, lambda x, z, c: (x, z, c ^ 1))
+    taps = lax.psum(taps, "core")
     taps = taps + ctx_permute(taps, lambda x, z, c: (x ^ 1, z, c))
     taps_arrived = ctx_permute(taps, lambda x, z, c: (nx - 1 - x, z, c))
-    own_z, taps, *rest = middle(
-        jnp.full((1,), z, jnp.int32), nz, own_x, arrived, taps, taps_arrived, tail, head, grad_own
-    )
-    *pieces, grad_own = rest
-    grad_weight, grad_feat_taps, grad_inner_taps = last(
-        inv_root, own_z, taps, rotated(pieces, "zl")
-    )
+
+    pieces, taps, grad_own = middle(nz, pair, taps, taps_arrived, tail, head, grad_own)
+    pieces = lax.all_to_all(pieces, "zl", split_axis=0, concat_axis=0)
+    grad_weight, grad_feat_taps, grad_inner_taps = last(inv_root, z, taps, pieces)
     return jnp.transpose(grad_own, (1, 0, 2)), grad_weight, grad_feat_taps, grad_inner_taps
 
 

time: 148 us -> 144 us (0.973)
  blocking collectives: 0 us -> 31.7 us
  starting transfers between devices: 56 us -> 28.9 us
  Pallas kernels: 30.6 us -> 17.9 us
  local copies, waits for them, and re-layouts: 5.61 us -> 17 us
  waiting for transfers between devices: 38.1 us -> 31.9 us
  other arithmetic: 1.8 us -> 0.01 us
    ppermute x8 -> x0, starting transfers between devices: 34.7 us -> none  [the longest x6 19.7 us: rotated(): lax.ppermute(piece, axis, [(i, (i + step) % count) for i in range(count)])]
    all_gather x0 -> x2, blocking collectives: none -> 27.8 us  [the longest x1 15.4 us: body(): far = lax.all_gather(far, 'col', axis=0)]
    unnamed x26 -> x48, local copies, waits for them, and re-layouts: 3.77 us -> 15.3 us
    ppermute x8 -> x0, waiting for transfers between devices: 10.5 us -> none  [the longest x1 6.53 us: body(): other = lax.ppermute(gated, 'col', [(0, 1), (1, 0)])]
    all_to_all x0 -> x1, waiting for transfers between devices: none -> 9.01 us  [body(): pieces = lax.all_to_all(pieces, 'zl', split_axis=0, concat_axis=0)]
    all_to_all x0 -> x1, starting transfers between devices: none -> 8.45 us  [body(): pieces = lax.all_to_all(pieces, 'zl', split_axis=0, concat_axis=0)]
    pallas_call x1, Pallas kernels: 6.32 us -> 1.89 us  [sent_weight(): call(sent_weight_kernel, 'sent_weight', 2 * rows * channels * blocks * wi...]
    psum x0 -> x1, blocking collectives: none -> 3.92 us  [body(): taps = lax.psum(taps, 'core')]
  transfers between devices with their start and end apart: 15 -> 8, of which waited for: 8 -> 4; matrix products, arithmetic and copies ran while one was open for 2% -> 1% of each run, Pallas kernels for 10% -> 6%
where the time goes in v3:
time: 144 us; the launch traced here: 142 us
  waiting for transfers between devices  31.9 us (22%)
  blocking collectives  31.7 us (22%)
  starting transfers between devices  28.9 us (20%)
  Pallas kernels  17.9 us (12%)
  local copies, waits for them, and re-layouts  17 us (12%)
  between operations  14.3 us (10%)
    all_gather x1, waiting for transfers between devices, body(): grads = lax.all_gather(out_grad, 'row', axis=0)  16.6 us
    all_gather x1, blocking collectives, body(): far = lax.all_gather(far, 'col', axis=0)  15.4 us
    unnamed x48, local copies, waits for them, and re-layouts  15.3 us
    ppermute x3, starting transfers between devices, ctx_permute(): return lax.ppermute(value, CTX, pairs)  12.7 us
    all_gather x1, blocking collectives, body(): both = lax.all_gather(gated, 'col', axis=1, tiled=True)  12.3 us
    all_to_all x1, waiting for transfers between devices, body(): pieces = lax.all_to_all(pieces, 'zl', split_axis=0, concat_axis=0)  9.01 us
    all_to_all x1, starting transfers between devices, body(): pieces = lax.all_to_all(pieces, 'zl', split_axis=0, concat_axis=0)  8.45 us
    ppermute x2, starting transfers between devices, ctx_shift(): lax.ppermute(value, CTX, [(i, i + steps) for i in range(count) if 0 <= i...  7.74 us
  transfers between devices with their start and end apart: 8, of which 4 were waited for; matrix products, arithmetic and copies ran while one was open for 1% of the time, Pallas kernels for 6%

profile of v3, /device:TPU:1, one launch (start us, length us, event | category | flops | bytes accessed | tf_op | source)
XLA Modules:
  0.0 141.7 jit_solution(16709123081470208955)
XLA Ops:
  8.7 5.4 %collective-permute-start = (bf16[3,16,256]{2,1,0:T(8,128)(2,1)S(1)}, bf16[3,16,256]{2,1,0:T(8,128)(2,1)S(1)}, u32[]{:S(2)}, u32[]{:S(2)}) collective-permute-start(bf16[3,16,256]{2,1,0:T(8,128)(2,1)S(1)} %slice.4), channel_id=1, source_target_pairs={{0,1},{1,2},{2,3},{3,4},{4,5},{5,6},{6,7},{7,8},{8,9},{9,10},{10,1... | collective-permute-start | bytes 73736 | tf_op jit(solution)/shard_map/ppermute | solution.py:382
  14.1 3.4 %collective-permute-done.before = bf16[3,16,256]{2,1,0:T(8,128)(2,1)S(1)} collective-permute-done((bf16[3,16,256]{2,1,0:T(8,128)(2,1)S(1)}, bf16[3,16,256]{2,1,0:T(8,128)(2,1)S(1)}, u32[]{:S(2)}, u32[]{:S(2)}) %collective-permute-start) | collective-permute-done | bytes 24608 | tf_op jit(solution)/shard_map/ppermute | solution.py:382
  17.5 1.1 copy-done.2
  20.1 1.5 %forward.1 = (bf16[512,256]{1,0:T(8,128)(2,1)S(1)}, f32[520,256]{1,0:T(8,128)S(1)}, f32[512,256]{1,0:T(8,128)S(1)}, f32[520,256]{1,0:T(8,128)S(1)}, f32[520,256]{1,0:T(8,128)S(1)}, /*index=5*/f32[520,256]{1,0:T(8,128)S(1)}) custom-call(bf16[3,16,256]{2,1,0:T(8,128)(2,1)S(1)} %collective-permute-done.before, bf16[3,512,256]{2,1,0:T(8,128)(2,1)S(1)} %bitcast.17, ...), custom_call_target="tpu_custom_call" | custom-call | flops 7864320 | bytes 3932160 | tf_op jit(solution)/shard_map/forward/pallas_call | solution.py:88
  21.6 0.8 copy-done.7
  22.4 0.8 copy-done.9
  23.2 0.8 copy-done.11
  24.0 0.8 copy-done.13
  24.8 0.8 copy-done.15
  25.7 12.3 %all_gather.15 = bf16[512,512]{1,0:T(8,128)(2,1)S(1)} all-gather(bf16[512,256]{1,0:T(8,128)(2,1)S(1)} %get-tuple-element.22), channel_id=1, replica_groups=mesh['row'=8,'col'=2,'x'=4,'zl'=4,'core'=2] {'col'}, dimensions={1}, use_global_device_ids=true | all-gather | bytes 786432 | tf_op jit(solution)/shard_map/all_gather | solution.py:399
  39.0 16.6 %all-gather.4.cloned.1.call-done = bf16[4096,256]{1,0:T(8,128)(2,1)} async-done(((bf16[512,256]{1,0:T(8,128)(2,1)}), bf16[4096,256]{1,0:T(8,128)(2,1)}) %all-gather.4.cloned.1.call-update) | async-done | bytes 2097168 | tf_op jit(solution)/shard_map/all_gather | solution.py:394
  55.5 1.6 %copy-done = bf16[4096,256]{1,0:T(8,128)(2,1)S(1)} copy-done((bf16[4096,256]{1,0:T(8,128)(2,1)S(1)}, bf16[4096,256]{1,0:T(8,128)(2,1)}, u32[]{:S(2)}) %copy-start) | copy-done | bytes 2097176
  57.1 0.9 copy-done.6
  58.0 1.9 %sent_weight.1._ = bf16[8,256,256]{2,1,0:T(8,128)(2,1)S(1)} custom-call(bf16[256,512]{1,0:T(8,128)(2,1)S(1)} %bitcast.20, bf16[8,512,256]{2,1,0:T(8,128)(2,1)S(1)} %bitcast.11), custom_call_target="tpu_custom_call" | custom-call | flops 536870912 | bytes 3407872 | tf_op jit(solution)/shard_map/sent_weight/pallas_call | solution.py:250
  59.9 6.5 %collective-permute-start.1 = (bf16[8,256,256]{2,1,0:T(8,128)(2,1)S(1)}, bf16[8,256,256]{2,1,0:T(8,128)(2,1)}, u32[]{:S(2)}, u32[]{:S(2)}) collective-permute-start(bf16[8,256,256]{2,1,0:T(8,128)(2,1)S(1)} %sent_weight.1._), channel_id=1, source_target_pairs={{0,1},{1,0},{2,3},{3,2},{4,5},{5,4},{6,7},{7,6},{8,9},{9,8},{10,11... | collective-permute-start | bytes 3145736 | tf_op jit(solution)/shard_map/ppermute | solution.py:377
  66.5 1.6 %copy-done.4 = bf16[512,2048]{1,0:T(8,128)(2,1)S(1)} copy-done((bf16[512,2048]{1,0:T(8,128)(2,1)S(1)}, bf16[512,2048]{1,0:T(8,128)(2,1)}, u32[]{:S(2)}) %copy-start.4) | copy-done | bytes 2097176
  68.0 3.5 %gated_grad.1 = (bf16[512,256]{1,0:T(8,128)(2,1)S(1)}, f32[512,256]{1,0:T(8,128)S(1)}) custom-call(s32[1]{0:T(128)} %bitcast.6.col, bf16[8,512,256]{2,1,0:T(8,128)(2,1)S(1)} %bitcast.12, bf16[512,2048]{1,0:T(8,128)(2,1)S(1)} %copy-done.4, bf16[8,256,256]{2,1,0:T(8,128)(2,1)S(1)} %sent_weight.1._), custom_call_target="tpu_custom_call" | custom-call | flops 1073741824 | bytes 4980736 | tf_op jit(solution)/shard_map/gated_grad/pallas_call | solution.py:223
  71.5 0.8 copy-done.17
  72.4 6.1 %kept_weight.1 = bf16[4,8,64,256]{3,2,1,0:T(8,128)(2,1)} custom-call(bf16[256,512]{1,0:T(8,128)(2,1)S(1)} %bitcast.19, bf16[8,512,256]{2,1,0:T(8,128)(2,1)S(1)} %bitcast.13, bf16[8,256,256]{2,1,0:T(8,128)(2,1)} %collective-permute-done.1.arrived, bf16[512,256]{1,0:T(8,128)(2,1)S(1)} %get-tuple-element.23._), custom_call_target="tpu_custom_call" | custom-call | flops 536870912 | bytes 4456448 | tf_op jit(solution)/shard_map/kept_weight/pallas_call | solution.py:274
  79.2 15.4 %all-gather.1 = bf16[1024,256]{1,0:T(8,128)(2,1)S(1)} all-gather(bf16[512,256]{1,0:T(8,128)(2,1)} %copy-done.5), channel_id=3, replica_groups=mesh['row'=8,'col'=2,'x'=4,'zl'=4,'core'=2] {'col'}, dimensions={0}, use_global_device_ids=true | all-gather | bytes 786432 | tf_op jit(solution)/shard_map/all_gather | solution.py:413
  94.7 1.0 copy-done.16
  95.7 1.0 copy-done.18
  96.8 3.4 %backward.1 = (bf16[3,512,256]{2,1,0:T(8,128)(2,1)}, f32[3,16,256]{2,1,0:T(8,128)S(1)}, f32[3,16,256]{2,1,0:T(8,128)S(1)}, f32[4,8,256]{2,1,0:T(8,128)S(1)}) custom-call(s32[1]{0:T(128)} %bitcast.6.col, f32[512,256]{1,0:T(8,128)S(1)} %copy-done.18, bf16[2,512,256]{2,1,0:T(8,128)(2,1)S(1)} %bitcast.14, f32[520,256]{1,0:T(8,128)S(1)} %copy-done.8, ...), custom_call_target="tpu_custom_call" | custom-call | flops 15728640 | bytes 5242880 | tf_op jit(solution)/shard_map/backward/pallas_call | solution.py:174
  100.2 3.9 %psum.7 = f32[4,8,256]{2,1,0:T(8,128)S(1)} all-reduce(f32[4,8,256]{2,1,0:T(8,128)S(1)} %get-tuple-element.30), channel_id=1, replica_groups=mesh['row'=8,'col'=2,'x'=4,'zl'=4,'core'=2] {'core'}, use_global_device_ids=true, to_apply=%region_1.2 | all-reduce | flops 8192 | bytes 65536 | tf_op jit(solution)/shard_map/psum | solution.py:418
  104.1 2.5 %collective-permute-start.2 = (f32[4,8,256]{2,1,0:T(8,128)S(1)}, f32[4,8,256]{2,1,0:T(8,128)S(1)}, u32[]{:S(2)}, u32[]{:S(2)}) collective-permute-start(f32[4,8,256]{2,1,0:T(8,128)S(1)} %psum.7), channel_id=1, source_target_pairs={{0,8},{1,9},{2,10},{3,11},{4,12},{5,13},{6,14},{7,15},{8,0},{9,1},... | collective-permute-start | bytes 98312 | tf_op jit(solution)/shard_map/ppermute | solution.py:377
  106.6 2.4 %collective-permute-start.4 = (f32[3,16,256]{2,1,0:T(8,128)S(1)}, f32[3,16,256]{2,1,0:T(8,128)S(1)}, u32[]{:S(2)}, u32[]{:S(2)}) collective-permute-start(f32[3,16,256]{2,1,0:T(8,128)S(1)} %get-tuple-element.32), channel_id=1, source_target_pairs={{1,0},{2,1},{3,2},{4,3},{5,4},{6,5},{7,6},{8,7},{9,8},{10,9},{11,1... | collective-permute-start | bytes 147464 | tf_op jit(solution)/shard_map/ppermute | solution.py:382
  109.0 3.7 %collective-permute-start.3 = (f32[4,8,256]{2,1,0:T(8,128)S(1)}, f32[4,8,256]{2,1,0:T(8,128)S(1)}, u32[]{:S(2)}, u32[]{:S(2)}) collective-permute-start(f32[4,8,256]{2,1,0:T(8,128)S(1)} %add.17.taps), channel_id=1, source_target_pairs={{0,24},{1,25},{2,26},{3,27},{4,28},{5,29},{6,30},{7,31},{8,16},{9,... | collective-permute-start | bytes 98312 | tf_op jit(solution)/shard_map/ppermute | solution.py:377
  112.7 2.2 %collective-permute-done.4.head = f32[3,16,256]{2,1,0:T(8,128)S(1)} collective-permute-done((f32[3,16,256]{2,1,0:T(8,128)S(1)}, f32[3,16,256]{2,1,0:T(8,128)S(1)}, u32[]{:S(2)}, u32[]{:S(2)}) %collective-permute-start.4) | collective-permute-done | bytes 49184 | tf_op jit(solution)/shard_map/ppermute | solution.py:382
  114.9 0.9 copy-done.19
  115.9 0.8 middle.1
  116.7 8.4 %all-to-all-start = ((bf16[4,12,16,256]{3,2,1,0:T(8,128)(2,1)}), bf16[4,12,16,256]{3,2,1,0:T(8,128)(2,1)S(1)}, u32[]{:S(2)}, u32[]{:S(2)}) async-start(bf16[4,12,16,256]{3,2,1,0:T(8,128)(2,1)} %get-tuple-element.36), calls=%async_computation.1 | async-start | bytes 786432 | tf_op jit(solution)/shard_map/all_to_all | solution.py:423
  125.1 9.0 %all-to-all-done.refs_2_ = bf16[4,12,16,256]{3,2,1,0:T(8,128)(2,1)S(1)} async-done(((bf16[4,12,16,256]{3,2,1,0:T(8,128)(2,1)}), bf16[4,12,16,256]{3,2,1,0:T(8,128)(2,1)S(1)}, u32[]{:S(2)}, u32[]{:S(2)}) %all-to-all-start) | async-done | bytes 393248 | tf_op jit(solution)/shard_map/all_to_all | solution.py:423
  (48 shorter events, 5.4 us)
Async XLA Ops:
  7.2 48.3 %all-gather.4.cloned.1.call-start = ((), (), s32[]{:S(2)}) async-start(), calls=%async_computation.3 | async-start | bytes 2359296 | tf_op jit(solution)/shard_map/all_gather | solution.py:394
  7.9 107.0 %reduce-scatter.2.cloned.1.call-start = ((), (), s32[]{:S(2)}) async-start(), calls=%async_computation.2 | async-start | bytes 1310720 | tf_op jit(solution)/shard_map/reduce_scatter | solution.py:411
  8.7 8.8 %collective-permute-start = (bf16[3,16,256]{2,1,0:T(8,128)(2,1)S(1)}, bf16[3,16,256]{2,1,0:T(8,128)(2,1)S(1)}, u32[]{:S(2)}, u32[]{:S(2)}) collective-permute-start(bf16[3,16,256]{2,1,0:T(8,128)(2,1)S(1)} %slice.4), channel_id=1, source_target_pairs={{0,1},{1,2},{2,3},{3,4},{4,5},{5,6},{6,7},{7,8},{8,9},{9,10},{10,1... | collective-permute-start | bytes 73736 | tf_op jit(solution)/shard_map/ppermute | solution.py:382
  17.5 1.1 copy-start.2
  18.7 0.7 copy-start.20
  19.4 0.7 copy-start.22
  21.6 0.8 copy-start.7
  22.4 0.8 copy-start.9
  23.2 0.8 copy-start.11
  24.0 0.8 copy-start.13
  24.8 0.8 copy-start.15
  55.5 1.6 %copy-start = (bf16[4096,256]{1,0:T(8,128)(2,1)S(1)}, bf16[4096,256]{1,0:T(8,128)(2,1)}, u32[]{:S(2)}) copy-start(bf16[4096,256]{1,0:T(8,128)(2,1)} %all-gather.4.cloned.1.call-done) | copy-start | bytes 6291460
  57.1 0.9 copy-start.6
  58.0 8.4 %copy-start.1 = (bf16[4096,256]{1,0:T(8,128)(2,1)S(1)}, bf16[4096,256]{1,0:T(8,128)(2,1)}, u32[]{:S(2)}) copy-start(bf16[4096,256]{1,0:T(8,128)(2,1)} %all-gather.4.cloned.1.call-done) | copy-start | bytes 6291460
  59.9 12.4 %collective-permute-start.1 = (bf16[8,256,256]{2,1,0:T(8,128)(2,1)S(1)}, bf16[8,256,256]{2,1,0:T(8,128)(2,1)}, u32[]{:S(2)}, u32[]{:S(2)}) collective-permute-start(bf16[8,256,256]{2,1,0:T(8,128)(2,1)S(1)} %sent_weight.1._), channel_id=1, source_target_pairs={{0,1},{1,0},{2,3},{3,2},{4,5},{5,4},{6,7},{7,6},{8,9},{9,8},{10,11... | collective-permute-start | bytes 3145736 | tf_op jit(solution)/shard_map/ppermute | solution.py:377
  66.4 1.6 %copy-start.4 = (bf16[512,2048]{1,0:T(8,128)(2,1)S(1)}, bf16[512,2048]{1,0:T(8,128)(2,1)}, u32[]{:S(2)}) copy-start(bf16[512,2048]{1,0:T(8,128)(2,1)} %weight.1) | copy-start | bytes 6291460
  71.5 0.8 copy-start.17
  72.3 22.3 %copy-start.12 = (f32[520,256]{1,0:T(8,128)S(1)}, f32[520,256]{1,0:T(8,128)}, u32[]{:S(2)}) copy-start(f32[520,256]{1,0:T(8,128)} %copy-done.11) | copy-start | bytes 1597444
  72.3 22.3 %copy-start.14 = (f32[520,256]{1,0:T(8,128)S(1)}, f32[520,256]{1,0:T(8,128)}, u32[]{:S(2)}) copy-start(f32[520,256]{1,0:T(8,128)} %copy-done.13) | copy-start | bytes 1597444
  72.3 22.3 %copy-start.21 = (f32[3,7,256]{2,1,0:T(8,128)S(1)}, f32[3,7,256]{2,1,0:T(8,128)}, u32[]{:S(2)}) copy-start(f32[3,7,256]{2,1,0:T(8,128)} %feat_taps.3) | copy-start | bytes 64516
  72.3 22.3 %copy-start.23 = (f32[7,256]{1,0:T(8,128)S(1)}, f32[7,256]{1,0:T(8,128)}, u32[]{:S(2)}) copy-start(f32[7,256]{1,0:T(8,128)} %inner_taps.3) | copy-start | bytes 21508
  78.4 0.7 copy-start.5
  79.1 15.5 %copy-start.3 = (bf16[512,3,256]{2,0,1:T(8,128)(2,1)S(1)}, bf16[512,3,256]{2,0,1:T(8,128)(2,1)}, u32[]{:S(2)}) copy-start(bf16[512,3,256]{2,0,1:T(8,128)(2,1)} %param.5) | copy-start | bytes 2359300
  79.1 15.5 %copy-start.8 = (f32[520,256]{1,0:T(8,128)S(1)}, f32[520,256]{1,0:T(8,128)}, u32[]{:S(2)}) copy-start(f32[520,256]{1,0:T(8,128)} %copy-done.7) | copy-start | bytes 1597444
  79.1 15.5 %copy-start.10 = (f32[520,256]{1,0:T(8,128)S(1)}, f32[520,256]{1,0:T(8,128)}, u32[]{:S(2)}) copy-start(f32[520,256]{1,0:T(8,128)} %copy-done.9) | copy-start | bytes 1597444
  94.7 1.0 copy-start.16
  95.7 1.0 copy-start.18
  104.1 4.9 %collective-permute-start.2 = (f32[4,8,256]{2,1,0:T(8,128)S(1)}, f32[4,8,256]{2,1,0:T(8,128)S(1)}, u32[]{:S(2)}, u32[]{:S(2)}) collective-permute-start(f32[4,8,256]{2,1,0:T(8,128)S(1)} %psum.7), channel_id=1, source_target_pairs={{0,8},{1,9},{2,10},{3,11},{4,12},{5,13},{6,14},{7,15},{8,0},{9,1},... | collective-permute-start | bytes 98312 | tf_op jit(solution)/shard_map/ppermute | solution.py:377
  106.6 8.3 %collective-permute-start.4 = (f32[3,16,256]{2,1,0:T(8,128)S(1)}, f32[3,16,256]{2,1,0:T(8,128)S(1)}, u32[]{:S(2)}, u32[]{:S(2)}) collective-permute-start(f32[3,16,256]{2,1,0:T(8,128)S(1)} %get-tuple-element.32), channel_id=1, source_target_pairs={{1,0},{2,1},{3,2},{4,3},{5,4},{6,5},{7,6},{8,7},{9,8},{10,9},{11,1... | collective-permute-start | bytes 147464 | tf_op jit(solution)/shard_map/ppermute | solution.py:382
  109.0 5.9 %collective-permute-start.3 = (f32[4,8,256]{2,1,0:T(8,128)S(1)}, f32[4,8,256]{2,1,0:T(8,128)S(1)}, u32[]{:S(2)}, u32[]{:S(2)}) collective-permute-start(f32[4,8,256]{2,1,0:T(8,128)S(1)} %add.17.taps), channel_id=1, source_target_pairs={{0,24},{1,25},{2,26},{3,27},{4,28},{5,29},{6,30},{7,31},{8,16},{9,... | collective-permute-start | bytes 98312 | tf_op jit(solution)/shard_map/ppermute | solution.py:377
  114.9 1.0 copy-start.19
  116.7 17.5 %all-to-all-start = ((bf16[4,12,16,256]{3,2,1,0:T(8,128)(2,1)}), bf16[4,12,16,256]{3,2,1,0:T(8,128)(2,1)S(1)}, u32[]{:S(2)}, u32[]{:S(2)}) async-start(bf16[4,12,16,256]{3,2,1,0:T(8,128)(2,1)} %get-tuple-element.36), calls=%async_computation.1 | async-start | bytes 786432 | tf_op jit(solution)/shard_map/all_to_all | solution.py:423
Sparse Core Ops, SparseCore 0:
  10.1 45.3 all-gather.3
  79.3 25.8 reduce-scatter.1

commit v4 on v3

v4 whole, which is shorter than its diff:
```python
import math

import jax
import jax.numpy as jnp
from jax import lax
from jax.experimental import pallas as pl
from jax.experimental.pallas import tpu as pltpu
from jax.sharding import Mesh
from jax.sharding import PartitionSpec as P

TAPS = 7
HALO = 16
LEAD = 8
CHUNK = 64
LANES = 128
CTX = ("x", "zl", "core")
F32 = jnp.float32
BF16 = jnp.bfloat16
VMEM_BYTES = 24 << 20
STREAM_BYTES = 56 << 20


def spread(total):
    return [(start, min(CHUNK, total - start)) for start in range(0, total, CHUNK)]


def lane_spec(*lead):
    return pl.BlockSpec((*lead, LANES), lambda i: (0,) * len(lead) + (i,))


def whole(shape):
    return pl.BlockSpec(shape, lambda *_: (0,) * len(shape))


SCALAR = pl.BlockSpec(memory_space=pltpu.SMEM)
UNREAD = pl.BlockSpec(memory_space=pl.ANY)
IN_HBM = pl.BlockSpec(memory_space=pltpu.HBM)


def call(kernel, name, flops, moved, vmem=VMEM_BYTES, **kwargs):
    return pl.pallas_call(
        kernel,
        name=name,
        compiler_params=pltpu.CompilerParams(vmem_limit_bytes=vmem),
        cost_estimate=pl.CostEstimate(flops=flops, bytes_accessed=moved, transcendentals=0),
        **kwargs,
    )


def load_features(before, own, feats):
    rows = own.shape[1]
    for j in range(3):
        feats[j, 0:HALO, :] = before[j].astype(F32)
        for start, count in spread(rows):
            feats[j, HALO + start : HALO + start + count, :] = own[
                j, start : start + count, :
            ].astype(F32)


def mixed_parts(feats, feat_taps, start, count):
    base = HALO - LEAD + start
    parts = []
    for j in range(3):
        total = feat_taps[j, 0:1, :] * feats[j, base : base + count, :]
        for s in range(1, TAPS):
            total = total + feat_taps[j, s : s + 1, :] * feats[j, base - s : base - s + count, :]
        parts.append(total)
    return parts


def window_rows(product, inner_taps, start, count):
    base = LEAD + start
    total = inner_taps[0:1, :] * product[base : base + count, :]
    for s in range(1, TAPS):
        total = total + inner_taps[s : s + 1, :] * product[base - s : base - s + count, :]
    return total


def forward_kernel(before, own, feat_taps, inner_taps, gated, feats, query, product):
    rows = own.shape[1]
    load_features(before, own, feats)
    for start, count in spread(rows + LEAD):
        parts = mixed_parts(feats, feat_taps, start, count)
        query[start : start + count, :] = parts[0]
        product[start : start + count, :] = parts[1] * parts[2]
    for start, count in spread(rows):
        base = LEAD + start
        gated[start : start + count, :] = (
            query[base : base + count, :] * window_rows(product, inner_taps, start, count)
        ).astype(BF16)


def forward(before, own, feat_taps, inner_taps):
    _, rows, channels = own.shape
    return call(
        forward_kernel,
        "forward",
        60 * rows * channels,
        8 * rows * channels,
        grid=(channels // LANES,),
        in_specs=[lane_spec(3, HALO), lane_spec(3, rows), lane_spec(3, TAPS), lane_spec(TAPS)],
        out_specs=lane_spec(rows),
        out_shape=jax.ShapeDtypeStruct((rows, channels), BF16),
        scratch_shapes=[
            pltpu.VMEM((3, rows + HALO, LANES), F32),
            pltpu.VMEM((rows + LEAD, LANES), F32),
            pltpu.VMEM((rows + LEAD, LANES), F32),
        ],
    )(before, own, feat_taps, inner_taps)


def backward_kernel(
    col, near, far, before, own, feat_taps, inner_taps, _,
    grads, head, tail, tap_sums, feats, query, key, value, product, grad_window, grad_mixed,
):
    rows = own.shape[1]
    load_features(before, own, feats)
    for start, count in spread(rows + LEAD):
        parts = mixed_parts(feats, feat_taps, start, count)
        query[start : start + count, :] = parts[0]
        key[start : start + count, :] = parts[1]
        value[start : start + count, :] = parts[2]
        product[start : start + count, :] = parts[1] * parts[2]
    zeros = jnp.zeros((HALO, LANES), F32)
    grad_window[0:HALO, :] = zeros
    grad_window[HALO + rows :, :] = zeros[:LEAD]
    for j in range(3):
        grad_mixed[j, 0:HALO, :] = zeros
        grad_mixed[j, HALO + rows :, :] = zeros[:LEAD]
    for start, count in spread(rows):
        at = HALO + start
        total = near[start : start + count, :] + far[
            1 - col[0], start : start + count, :
        ].astype(F32)
        grad_window[at : at + count, :] = total * query[LEAD + start : LEAD + start + count, :]
        grad_mixed[0, at : at + count, :] = total * window_rows(product, inner_taps, start, count)
    for start, count in spread(rows + LEAD):
        at = HALO - LEAD + start
        total = inner_taps[0:1, :] * grad_window[at : at + count, :]
        for s in range(1, TAPS):
            total = total + inner_taps[s : s + 1, :] * grad_window[at + s : at + s + count, :]
        grad_mixed[1, at : at + count, :] = total * value[start : start + count, :]
        grad_mixed[2, at : at + count, :] = total * key[start : start + count, :]

    def folded(terms):
        return jnp.sum(terms.reshape(terms.shape[0] // 8, 8, LANES), axis=0)

    def put(place, sums):
        for s in range(TAPS):
            tap_sums[place, s : s + 1, :] = jnp.sum(sums[s], axis=0, keepdims=True)
        tap_sums[place, TAPS : TAPS + 1, :] = jnp.zeros((1, LANES), F32)

    def transposed(j, at, count):
        total = feat_taps[j, 0:1, :] * grad_mixed[j, at : at + count, :]
        for s in range(1, TAPS):
            total = total + feat_taps[j, s : s + 1, :] * grad_mixed[j, at + s : at + s + count, :]
        return total

    for j in range(3):
        head[j] = transposed(j, 0, HALO)
        sums = [jnp.zeros((8, LANES), F32) for _ in range(TAPS)]
        spans = [(HALO + start, count) for start, count in spread(rows)]
        for at, count in ([(HALO - LEAD, LEAD)] if j > 0 else []) + spans:
            here = grad_mixed[j, at : at + count, :]
            for s in range(TAPS):
                sums[s] = sums[s] + folded(here * feats[j, at - s : at - s + count, :])
            if at >= HALO:
                total = transposed(j, at, count)
                grads[j, at - HALO : at - HALO + count, :] = total.astype(BF16)
                if at + count == HALO + rows:
                    tail[j] = total[count - HALO :]
        put(j, sums)
    sums = [jnp.zeros((8, LANES), F32) for _ in range(TAPS)]
    for start, count in spread(rows):
        here = grad_window[HALO + start : HALO + start + count, :]
        for s in range(TAPS):
            base = LEAD + start - s
            sums[s] = sums[s] + folded(here * product[base : base + count, :])
    put(3, sums)


def backward(col, near, far, before, own, feat_taps, inner_taps, after):
    _, rows, channels = own.shape
    edge = jax.ShapeDtypeStruct((3, HALO, channels), F32)
    return call(
        backward_kernel,
        "backward",
        160 * rows * channels,
        20 * rows * channels,
        grid=(channels // LANES,),
        in_specs=[
            SCALAR, lane_spec(rows), lane_spec(2, rows), lane_spec(3, HALO), lane_spec(3, rows),
            lane_spec(3, TAPS), lane_spec(TAPS), UNREAD,
        ],
        out_specs=[lane_spec(3, rows), lane_spec(3, HALO), lane_spec(3, HALO), lane_spec(4, 8)],
        out_shape=[
            jax.ShapeDtypeStruct((3, rows, channels), BF16),
            edge,
            edge,
            jax.ShapeDtypeStruct((4, 8, channels), F32),
        ],
        scratch_shapes=[pltpu.VMEM((3, rows + HALO, LANES), F32)]
        + [pltpu.VMEM((rows + LEAD, LANES), F32)] * 4
        + [
            pltpu.VMEM((rows + HALO + LEAD, LANES), F32),
            pltpu.VMEM((3, rows + HALO + LEAD, LANES), F32),
        ],
    )(col, near, far, before, own, feat_taps, inner_taps, after)


def fetch(source, target, sems):
    copies = [
        pltpu.make_async_copy(source.at[i], target.at[i], sems.at[i])
        for i in range(source.shape[0])
    ]
    for copy in copies:
        copy.start()
    return copies


def products_kernel(
    col, gated, grads, weight, sent, far, near, held_grads, held_weight, grad_sems, weight_sem
):
    copies = fetch(grads, held_grads, grad_sems)
    weights = pltpu.make_async_copy(weight, held_weight, weight_sem)
    weights.start()
    blocks, rows, _ = held_grads.shape
    half = near.shape[1]
    for b in range(blocks):
        copies[b].wait()
        sent[b] = jnp.dot(gated[...], held_grads[b], preferred_element_type=F32).astype(BF16)
    weights.wait()
    step = min(rows, 128)
    for start in range(0, rows, step):
        span = slice(start, start + step)
        wide = jnp.concatenate([held_grads[b, span, :] for b in range(blocks)], axis=1)
        total = lax.dot_general(
            wide, held_weight[...], (((1,), (1,)), ((), ())), preferred_element_type=F32
        )
        first = col[0] == 0
        near[span, :] = jnp.where(first, total[:, :half], total[:, half:])
        far[span, :] = jnp.where(first, total[:, half:], total[:, :half]).astype(BF16)


def products(col, gated, grads, weight):
    channels, rows = gated.shape
    blocks, _, width = grads.shape
    half = weight.shape[0] // 2
    return call(
        products_kernel,
        "products",
        2 * rows * (channels + 2 * half) * blocks * width,
        2 * blocks * width * (rows + channels + 2 * half) + 6 * rows * half,
        vmem=STREAM_BYTES,
        in_specs=[SCALAR, pl.BlockSpec(memory_space=pltpu.VMEM), IN_HBM, IN_HBM],
        out_specs=[pl.BlockSpec(memory_space=pltpu.VMEM)] * 3,
        out_shape=[
            jax.ShapeDtypeStruct((blocks, channels, width), BF16),
            jax.ShapeDtypeStruct((rows, half), BF16),
            jax.ShapeDtypeStruct((rows, half), F32),
        ],
        scratch_shapes=[
            pltpu.VMEM(grads.shape, BF16),
            pltpu.VMEM(weight.shape, BF16),
            pltpu.SemaphoreType.DMA((blocks,)),
            pltpu.SemaphoreType.DMA,
        ],
    )(col, gated, grads, weight)


def kept_weight_kernel(gated, grads, arrived, out, done, held_grads, held, grad_sems, sems):
    copies = fetch(grads, held_grads, grad_sems)
    others = fetch(arrived, held, sems)
    done[...] = jnp.zeros_like(done)
    parts, _, size, _ = out.shape
    for b in range(held.shape[0]):
        copies[b].wait()
        total = jnp.dot(gated[...], held_grads[b], preferred_element_type=F32)
        others[b].wait()
        total = (total + held[b].astype(F32)).astype(BF16)
        for part in range(parts):
            out[part, b] = total[part * size : (part + 1) * size]


def kept_weight(parts, gated, grads, arrived):
    channels, rows = gated.shape
    blocks, _, width = grads.shape
    size = channels // parts
    return call(
        kept_weight_kernel,
        "kept_weight",
        2 * rows * channels * blocks * width,
        2 * blocks * width * (rows + 2 * channels) + 2 * rows * channels,
        in_specs=[pl.BlockSpec(memory_space=pltpu.VMEM), IN_HBM, IN_HBM],
        out_specs=[pl.BlockSpec(memory_space=pltpu.VMEM)] * 2,
        out_shape=[
            jax.ShapeDtypeStruct((parts, blocks, size, width), BF16),
            jax.ShapeDtypeStruct((8, LANES), F32),
        ],
        scratch_shapes=[
            pltpu.VMEM(grads.shape, BF16),
            pltpu.VMEM(arrived.shape, BF16),
            pltpu.SemaphoreType.DMA((blocks,)),
            pltpu.SemaphoreType.DMA((blocks,)),
        ],
    )(gated, grads, arrived)


def middle_kernel(pair, taps, taps_arrived, head, out, out_taps, out_head):
    parts, _, size, _ = out.shape
    blocks = pair.shape[0]
    sums = taps[...] + taps_arrived[...]
    out_taps[...] = sums
    high = sums.astype(BF16).astype(F32)
    both = jnp.concatenate([high, sums - high], axis=1).astype(BF16)
    for part in range(parts):
        out[part, 0:blocks] = pair[:, part * size : (part + 1) * size, :]
        out[part, blocks:] = both
    out_head[...] = head[...]


def middle(parts, pair, taps, taps_arrived, head):
    blocks, channels, width = pair.shape
    shape = (parts, blocks + taps.shape[0], channels // parts, width)
    args = (pair, taps, taps_arrived, head)
    outs = [
        jax.ShapeDtypeStruct(shape, BF16),
        jax.ShapeDtypeStruct(taps.shape, F32),
        jax.ShapeDtypeStruct(head.shape, F32),
    ]
    return call(
        middle_kernel,
        "middle",
        4 * pair.size,
        4 * pair.size,
        grid=(1,),
        in_specs=[whole(v.shape) for v in args],
        out_specs=[whole(v.shape) for v in outs],
        out_shape=outs,
    )(*args)


def last_kernel(
    scale, z, taps, arrived, tail, head, _, out, out_feat, out_inner, out_grads
):
    parts, _, _, width = arrived.shape
    blocks = out.shape[1] // width
    out_grads[...] = (tail[...] + head[...]).astype(BF16)
    for b in range(blocks):
        total = arrived[0, b].astype(F32)
        for part in range(1, parts):
            total = total + arrived[part, b].astype(F32)
        out[:, b * width : (b + 1) * width] = (total * scale).astype(BF16)
    for j in range(4):
        total = taps[j]
        for part in range(parts):
            both = arrived[part, blocks + j].astype(F32)
            total = total + jnp.where(z[0] == part, 0.0, both[:8] + both[8:])
        total = (total * scale)[:TAPS]
        if j < 3:
            out_feat[j] = total
        else:
            out_inner[...] = total


def last(scale, z, taps, arrived, tail, head, grads):
    parts, count, channels, width = arrived.shape
    blocks = count - taps.shape[0]
    final = grads.shape[1] // HALO - 1
    args = (taps, arrived, tail, head)
    shapes = [
        jax.ShapeDtypeStruct((channels, blocks * width), BF16),
        jax.ShapeDtypeStruct((3, TAPS, width), F32),
        jax.ShapeDtypeStruct((TAPS, width), F32),
    ]
    return call(
        lambda *refs: last_kernel(scale, *refs),
        "last",
        2 * arrived.size,
        2 * arrived.size,
        grid=(1,),
        in_specs=[SCALAR] + [whole(v.shape) for v in args] + [UNREAD],
        out_specs=[whole(v.shape) for v in shapes]
        + [pl.BlockSpec(tail.shape, lambda i: (0, final, 0))],
        out_shape=shapes + [jax.ShapeDtypeStruct(grads.shape, grads.dtype)],
        input_output_aliases={5: 3},
    )(z, *args, grads)


def ctx_permute(value, target):
    nx, nz, nc = (lax.axis_size(a) for a in CTX)
    pairs = []
    for x in range(nx):
        for z in range(nz):
            for c in range(nc):
                to = target(x, z, c)
                pairs.append(((x * nz + z) * nc + c, (to[0] * nz + to[1]) * nc + to[2]))
    return lax.ppermute(value, CTX, pairs)


def ctx_shift(value, steps):
    count = math.prod(lax.axis_size(a) for a in CTX)
    return lax.ppermute(
        value, CTX, [(i, i + steps) for i in range(count) if 0 <= i + steps < count]
    )


def body(featured, feat_taps, inner_taps, out_weight, out_grad):
    rows = featured.shape[0]
    nx, nz, nc = (lax.axis_size(a) for a in CTX)
    inv_root = 1.0 / math.sqrt(rows * nx * nz * nc)
    core = lax.axis_index("core")
    col, z = (jnp.full((1,), lax.axis_index(a), jnp.int32) for a in ("col", "zl"))

    grads = lax.all_gather(out_grad, "row", axis=0)

    own = jnp.transpose(featured, (1, 0, 2))
    before = ctx_shift(own[:, rows - HALO :], 1)
    gated = forward(before, own, feat_taps, inner_taps)
    both = lax.all_gather(gated, "col", axis=1, tiled=True)
    channels = both.shape[1]
    split = both.T.reshape(nx * nz, nc, channels // (nx * nz * nc), rows)
    kept, sent = (
        lax.dynamic_index_in_dim(split, c, 1, keepdims=False).reshape(channels // nc, rows)
        for c in (core, 1 - core)
    )

    sent, far, near = products(col, sent, grads, out_weight)
    arrived = ctx_permute(sent, lambda x, z, c: (x, z, 1 - c))
    pair, done = kept_weight(nx, kept, grads, arrived)
    far = lax.all_gather(far, "col", axis=0)
    summed = lax.psum_scatter(pair, "x", scatter_dimension=0)

    grad_own, head, tail, taps = backward(
        col, near, far, before, own, feat_taps, inner_taps, done
    )
    taps = lax.psum(taps, "core")
    taps = taps + ctx_permute(taps, lambda x, z, c: (x ^ 1, z, c))
    taps_arrived = ctx_permute(taps, lambda x, z, c: (nx - 1 - x, z, c))

    pieces, taps, head = middle(nz, summed, taps, taps_arrived, head)
    pieces = lax.all_to_all(pieces, "zl", split_axis=0, concat_axis=0)
    head = ctx_shift(head, -1)
    grad_weight, grad_feat_taps, grad_inner_taps, grad_own = last(
        inv_root, z, taps, pieces, tail, head, grad_own
    )
    return jnp.transpose(grad_own, (1, 0, 2)), grad_weight, grad_feat_taps, grad_inner_taps


def fine_mesh(mesh):
    row, col, ctx = mesh.devices.shape
    return Mesh(mesh.devices.reshape(row, col, ctx // 8, 4, 2), ("row", "col", *CTX))


def solution(mesh):
    return jax.shard_map(
        body,
        mesh=fine_mesh(mesh),
        in_specs=(
            P(CTX, None, ("row", "col")),
            P(None, None, ("row", "col")),
            P(None, ("row", "col")),
            P("row", "col"),
            P(CTX, ("col", "row")),
        ),
        out_specs=(
            P(CTX, None, ("row", "col")),
            P(("row", *CTX), "col"),
            P(None, None, ("row", "col")),
            P(None, ("row", "col")),
        ),
        check_vma=False,
    )
```

time: 144 us -> 139 us (0.965)
  local copies, waits for them, and re-layouts: 17 us -> 5.24 us
  waiting for transfers between devices: 31.9 us -> 38.8 us
  starting transfers between devices: 28.9 us -> 25 us
  blocking collectives: 31.7 us -> 34.2 us
  Pallas kernels: 17.9 us -> 20.2 us
    unnamed x48 -> x20, local copies, waits for them, and re-layouts: 15.3 us -> 3.54 us
    ppermute x3, waiting for transfers between devices: 0.01 us -> 9.15 us  [ctx_permute(): return lax.ppermute(value, CTX, pairs)]
    all_to_all x1, waiting for transfers between devices: 9.01 us -> 0.01 us  [body(): pieces = lax.all_to_all(pieces, 'zl', split_axis=0, concat_axis=0)]
    all_gather x1, waiting for transfers between devices: 16.6 us -> 20.8 us  [body(): grads = lax.all_gather(out_grad, 'row', axis=0)]
    psum x1, blocking collectives: 3.92 us -> 7.73 us  [body(): taps = lax.psum(taps, 'core')]
    all_to_all x1, starting transfers between devices: 8.45 us -> 4.81 us  [body(): pieces = lax.all_to_all(pieces, 'zl', split_axis=0, concat_axis=0)]
    pallas_call x4 -> x3, Pallas kernels: 10.3 us -> 13.5 us  [the longest x1 8.13 us: products(): call(products_kernel, 'products', 2 * rows * (channels + 2 * half) * bloc...]
    ppermute x3, starting transfers between devices: 12.7 us -> 10 us  [ctx_permute(): return lax.ppermute(value, CTX, pairs)]
  transfers between devices with their start and end apart: 8 -> 8, of which waited for: 4 -> 6; matrix products, arithmetic and copies ran while one was open for 1% -> 1% of each run, Pallas kernels for 6% -> 4%
where the time goes in v4:
time: 139 us; the launch traced here: 138 us
  waiting for transfers between devices  38.8 us (28%)
  blocking collectives  34.2 us (25%)
  starting transfers between devices  25 us (18%)
  Pallas kernels  20.2 us (15%)
  between operations  14.2 us (10%)
  local copies, waits for them, and re-layouts  5.24 us (4%)
    all_gather x1, waiting for transfers between devices, body(): grads = lax.all_gather(out_grad, 'row', axis=0)  20.8 us
    all_gather x1, blocking collectives, body(): far = lax.all_gather(far, 'col', axis=0)  14.1 us
    all_gather x1, blocking collectives, body(): both = lax.all_gather(gated, 'col', axis=1, tiled=True)  12.3 us
    ppermute x3, starting transfers between devices, ctx_permute(): return lax.ppermute(value, CTX, pairs)  10 us
    ppermute x2, starting transfers between devices, ctx_shift(): lax.ppermute(value, CTX, [(i, i + steps) for i in range(count) if 0 <= i...  10 us
    ppermute x3, waiting for transfers between devices, ctx_permute(): return lax.ppermute(value, CTX, pairs)  9.15 us
    pallas_call x1, Pallas kernels, products(): call(products_kernel, 'products', 2 * rows * (channels + 2 * half) * bloc...  8.13 us
    ppermute x2, waiting for transfers between devices, ctx_shift(): lax.ppermute(value, CTX, [(i, i + steps) for i in range(count) if 0 <= i...  8.09 us
  transfers between devices with their start and end apart: 8, of which 6 were waited for; matrix products, arithmetic and copies ran while one was open for 1% of the time, Pallas kernels for 4%

profile of v4, /device:TPU:1, one launch (start us, length us, event | category | flops | bytes accessed | tf_op | source)
XLA Modules:
  0.0 137.5 jit_solution(10890350854828675971)
XLA Ops:
  7.2 0.0 all-gather.4.cloned.1.call-start
  7.2 0.7 all-gather.4.cloned.1.call-update
  7.9 0.0 reduce-scatter.2.cloned.1.call-start
  7.9 0.7 slice.4
  8.7 5.4 %collective-permute-start = (bf16[3,16,256]{2,1,0:T(8,128)(2,1)S(1)}, bf16[3,16,256]{2,1,0:T(8,128)(2,1)S(1)}, u32[]{:S(2)}, u32[]{:S(2)}) collective-permute-start(bf16[3,16,256]{2,1,0:T(8,128)(2,1)S(1)} %slice.4), channel_id=1, source_target_pairs={{0,1},{1,2},{2,3},{3,4},{4,5},{5,6},{6,7},{7,8},{8,9},{9,10},{10,1... | collective-permute-start | bytes 73736 | tf_op jit(solution)/shard_map/ppermute | solution.py:403
  14.1 3.4 %collective-permute-done.before = bf16[3,16,256]{2,1,0:T(8,128)(2,1)S(1)} collective-permute-done((bf16[3,16,256]{2,1,0:T(8,128)(2,1)S(1)}, bf16[3,16,256]{2,1,0:T(8,128)(2,1)S(1)}, u32[]{:S(2)}, u32[]{:S(2)}) %collective-permute-start) | collective-permute-done | bytes 24608 | tf_op jit(solution)/shard_map/ppermute | solution.py:403
  17.5 1.1 copy-done
  18.7 0.7 copy-done.5
  19.4 0.7 copy-done.7
  20.1 1.3 forward.1
  21.4 12.3 %all_gather.15 = bf16[512,512]{1,0:T(8,128)(2,1)S(1)} all-gather(bf16[512,256]{1,0:T(8,128)(2,1)S(1)} %forward.1), channel_id=1, replica_groups=mesh['row'=8,'col'=2,'x'=4,'zl'=4,'core'=2] {'col'}, dimensions={1}, use_global_device_ids=true | all-gather | bytes 786432 | tf_op jit(solution)/shard_map/all_gather | solution.py:420
  33.7 0.2 copy.12
  34.0 0.7 constant_dynamic-slice_fusion
  34.7 20.8 %all-gather.4.cloned.1.call-done = bf16[4096,256]{1,0:T(8,128)(2,1)} async-done(((bf16[512,256]{1,0:T(8,128)(2,1)}), bf16[4096,256]{1,0:T(8,128)(2,1)}) %all-gather.4.cloned.1.call-update) | async-done | bytes 2097168 | tf_op jit(solution)/shard_map/all_gather | solution.py:415
  55.5 8.1 %products.1 = (bf16[8,256,256]{2,1,0:T(8,128)(2,1)}, bf16[512,256]{1,0:T(8,128)(2,1)}, f32[512,256]{1,0:T(8,128)}) custom-call(s32[1]{0:T(128)} %bitcast.6.col, bf16[256,512]{1,0:T(8,128)(2,1)} %bitcast.22, bf16[8,512,256]{2,1,0:T(8,128)(2,1)} %bitcast.14, bf16[512,2048]{1,0:T(8,128)(2,1)} %weight.1), custom_call_target="tpu_custom_call" | custom-call | flops 1610612736 | bytes 6029312 | tf_op jit(solution)/shard_map/products/pallas_call | solution.py:249
  63.6 6.2 %collective-permute-start.1 = (bf16[8,256,256]{2,1,0:T(8,128)(2,1)}, bf16[8,256,256]{2,1,0:T(8,128)(2,1)S(1)}, u32[]{:S(2)}, u32[]{:S(2)}) collective-permute-start(bf16[8,256,256]{2,1,0:T(8,128)(2,1)} %get-tuple-element.20), channel_id=1, source_target_pairs={{0,1},{1,0},{2,3},{3,2},{4,5},{5,4},{6,7},{7,6},{8,9},{9,8},{10,11... | collective-permute-start | bytes 3145736 | tf_op jit(solution)/shard_map/ppermute | solution.py:398
  69.9 2.5 %collective-permute-done.1.arrived = bf16[8,256,256]{2,1,0:T(8,128)(2,1)S(1)} collective-permute-done((bf16[8,256,256]{2,1,0:T(8,128)(2,1)}, bf16[8,256,256]{2,1,0:T(8,128)(2,1)S(1)}, u32[]{:S(2)}, u32[]{:S(2)}) %collective-permute-start.1) | collective-permute-done | bytes 1048608 | tf_op jit(solution)/shard_map/ppermute | solution.py:398
  72.4 5.2 %kept_weight.1 = (bf16[4,8,64,256]{3,2,1,0:T(8,128)(2,1)}, f32[8,128]{1,0:T(8,128)S(1)}) custom-call(bf16[256,512]{1,0:T(8,128)(2,1)S(1)} %bitcast.17, bf16[8,512,256]{2,1,0:T(8,128)(2,1)S(1)} %bitcast.15, bf16[8,256,256]{2,1,0:T(8,128)(2,1)S(1)} %collective-permute-done.1.arrived), custom_call_target="tpu_custom_call" | custom-call | flops 536870912 | bytes 4456448 | tf_op jit(solution)/shard_map/kept_weight/pallas_call | solution.py:289
  77.6 0.0 reduce-scatter.2.cloned.1.call-update
  77.6 14.1 %all-gather.1 = bf16[1024,256]{1,0:T(8,128)(2,1)S(1)} all-gather(bf16[512,256]{1,0:T(8,128)(2,1)S(1)} %copy-done.9), channel_id=3, replica_groups=mesh['row'=8,'col'=2,'x'=4,'zl'=4,'core'=2] {'col'}, dimensions={0}, use_global_device_ids=true | all-gather | bytes 786432 | tf_op jit(solution)/shard_map/all_gather | solution.py:431
  91.8 4.1 %backward.1 = (bf16[3,512,256]{2,1,0:T(8,128)(2,1)}, f32[3,16,256]{2,1,0:T(8,128)S(1)}, f32[3,16,256]{2,1,0:T(8,128)S(1)}, f32[4,8,256]{2,1,0:T(8,128)S(1)}) custom-call(s32[1]{0:T(128)} %bitcast.6.col, f32[512,256]{1,0:T(8,128)S(1)} %copy-done.3, bf16[2,512,256]{2,1,0:T(8,128)(2,1)S(1)} %bitcast.16, bf16[3,16,256]{2,1,0:T(8,128)(2,1)S(1)} %collective-permute-done.before, ...), custom_call_target="tpu_custom_call" | custom-call | flops 20971520 | bytes 2621440 | tf_op jit(solution)/shard_map/backward/pallas_call | solution.py:185
  95.8 7.7 %psum.7 = f32[4,8,256]{2,1,0:T(8,128)S(1)} all-reduce(f32[4,8,256]{2,1,0:T(8,128)S(1)} %get-tuple-element.25), channel_id=1, replica_groups=mesh['row'=8,'col'=2,'x'=4,'zl'=4,'core'=2] {'core'}, use_global_device_ids=true, to_apply=%region_1.2 | all-reduce | flops 8192 | bytes 65536 | tf_op jit(solution)/shard_map/psum | solution.py:437
  103.6 1.9 %collective-permute-start.2 = (f32[4,8,256]{2,1,0:T(8,128)S(1)}, f32[4,8,256]{2,1,0:T(8,128)S(1)}, u32[]{:S(2)}, u32[]{:S(2)}) collective-permute-start(f32[4,8,256]{2,1,0:T(8,128)S(1)} %psum.7), channel_id=1, source_target_pairs={{0,8},{1,9},{2,10},{3,11},{4,12},{5,13},{6,14},{7,15},{8,0},{9,1},... | collective-permute-start | bytes 98312 | tf_op jit(solution)/shard_map/ppermute | solution.py:398
  105.5 2.7 %collective-permute-done.2 = f32[4,8,256]{2,1,0:T(8,128)S(1)} collective-permute-done((f32[4,8,256]{2,1,0:T(8,128)S(1)}, f32[4,8,256]{2,1,0:T(8,128)S(1)}, u32[]{:S(2)}, u32[]{:S(2)}) %collective-permute-start.2) | collective-permute-done | bytes 32800 | tf_op jit(solution)/shard_map/ppermute | solution.py:398
  108.3 1.9 %collective-permute-start.3 = (f32[4,8,256]{2,1,0:T(8,128)S(1)}, f32[4,8,256]{2,1,0:T(8,128)S(1)}, u32[]{:S(2)}, u32[]{:S(2)}) collective-permute-start(f32[4,8,256]{2,1,0:T(8,128)S(1)} %add.17.taps), channel_id=1, source_target_pairs={{0,24},{1,25},{2,26},{3,27},{4,28},{5,29},{6,30},{7,31},{8,16},{9,... | collective-permute-start | bytes 98312 | tf_op jit(solution)/shard_map/ppermute | solution.py:398
  110.2 3.9 %collective-permute-done.3.taps_arrived = f32[4,8,256]{2,1,0:T(8,128)S(1)} collective-permute-done((f32[4,8,256]{2,1,0:T(8,128)S(1)}, f32[4,8,256]{2,1,0:T(8,128)S(1)}, u32[]{:S(2)}, u32[]{:S(2)}) %collective-permute-start.3) | collective-permute-done | bytes 32800 | tf_op jit(solution)/shard_map/ppermute | solution.py:398
  114.1 0.9 copy-done.4
  115.1 0.8 middle.1
  115.8 4.8 %all-to-all-start = ((bf16[4,12,16,256]{3,2,1,0:T(8,128)(2,1)}), bf16[4,12,16,256]{3,2,1,0:T(8,128)(2,1)S(1)}, u32[]{:S(2)}, u32[]{:S(2)}) async-start(bf16[4,12,16,256]{3,2,1,0:T(8,128)(2,1)} %get-tuple-element.28), calls=%async_computation.1 | async-start | bytes 786432 | tf_op jit(solution)/shard_map/all_to_all | solution.py:442
  120.7 4.6 %collective-permute-start.4 = (f32[3,16,256]{2,1,0:T(8,128)S(1)}, f32[3,16,256]{2,1,0:T(8,128)S(1)}, u32[]{:S(2)}, u32[]{:S(2)}) collective-permute-start(f32[3,16,256]{2,1,0:T(8,128)S(1)} %get-tuple-element.30), channel_id=1, source_target_pairs={{1,0},{2,1},{3,2},{4,3},{5,4},{6,5},{7,6},{8,7},{9,8},{10,9},{11,1... | collective-permute-start | bytes 147464 | tf_op jit(solution)/shard_map/ppermute | solution.py:403
  125.3 4.7 %collective-permute-done.4.refs_4_ = f32[3,16,256]{2,1,0:T(8,128)S(1)} collective-permute-done((f32[3,16,256]{2,1,0:T(8,128)S(1)}, f32[3,16,256]{2,1,0:T(8,128)S(1)}, u32[]{:S(2)}, u32[]{:S(2)}) %collective-permute-start.4) | collective-permute-done | bytes 49184 | tf_op jit(solution)/shard_map/ppermute | solution.py:403
  130.0 0.7 last.1
  (19 shorter events, 0.0 us)
Async XLA Ops:
  7.2 48.3 %all-gather.4.cloned.1.call-start = ((), (), s32[]{:S(2)}) async-start(), calls=%async_computation.3 | async-start | bytes 2359296 | tf_op jit(solution)/shard_map/all_gather | solution.py:415
  7.9 106.2 %reduce-scatter.2.cloned.1.call-start = ((), (), s32[]{:S(2)}) async-start(), calls=%async_computation.2 | async-start | bytes 1310720 | tf_op jit(solution)/shard_map/reduce_scatter | solution.py:432
  8.7 8.8 %collective-permute-start = (bf16[3,16,256]{2,1,0:T(8,128)(2,1)S(1)}, bf16[3,16,256]{2,1,0:T(8,128)(2,1)S(1)}, u32[]{:S(2)}, u32[]{:S(2)}) collective-permute-start(bf16[3,16,256]{2,1,0:T(8,128)(2,1)S(1)} %slice.4), channel_id=1, source_target_pairs={{0,1},{1,2},{2,3},{3,4},{4,5},{5,6},{6,7},{7,8},{8,9},{9,10},{10,1... | collective-permute-start | bytes 73736 | tf_op jit(solution)/shard_map/ppermute | solution.py:403
  17.5 1.1 copy-start
  18.7 0.7 copy-start.5
  19.4 0.7 copy-start.7
  55.5 16.8 %copy-start.2 = (bf16[4096,256]{1,0:T(8,128)(2,1)S(1)}, bf16[4096,256]{1,0:T(8,128)(2,1)}, u32[]{:S(2)}) copy-start(bf16[4096,256]{1,0:T(8,128)(2,1)} %all-gather.4.cloned.1.call-done) | copy-start | bytes 6291460
  63.6 8.7 %collective-permute-start.1 = (bf16[8,256,256]{2,1,0:T(8,128)(2,1)}, bf16[8,256,256]{2,1,0:T(8,128)(2,1)S(1)}, u32[]{:S(2)}, u32[]{:S(2)}) collective-permute-start(bf16[8,256,256]{2,1,0:T(8,128)(2,1)} %get-tuple-element.20), channel_id=1, source_target_pairs={{0,1},{1,0},{2,3},{3,2},{4,5},{5,4},{6,7},{7,6},{8,9},{9,8},{10,11... | collective-permute-start | bytes 3145736 | tf_op jit(solution)/shard_map/ppermute | solution.py:398
  72.3 5.2 %copy-start.9 = (bf16[512,256]{1,0:T(8,128)(2,1)S(1)}, bf16[512,256]{1,0:T(8,128)(2,1)}, u32[]{:S(2)}) copy-start(bf16[512,256]{1,0:T(8,128)(2,1)} %get-tuple-element.23) | copy-start | bytes 786436
  72.3 19.4 %copy-start.1 = (bf16[512,3,256]{2,0,1:T(8,128)(2,1)S(1)}, bf16[512,3,256]{2,0,1:T(8,128)(2,1)}, u32[]{:S(2)}) copy-start(bf16[512,3,256]{2,0,1:T(8,128)(2,1)} %param.5) | copy-start | bytes 2359300
  72.3 19.4 %copy-start.3 = (f32[512,256]{1,0:T(8,128)S(1)}, f32[512,256]{1,0:T(8,128)}, u32[]{:S(2)}) copy-start(f32[512,256]{1,0:T(8,128)} %get-tuple-element.22.near) | copy-start | bytes 1572868
  72.4 19.4 %copy-start.6 = (f32[3,7,256]{2,1,0:T(8,128)S(1)}, f32[3,7,256]{2,1,0:T(8,128)}, u32[]{:S(2)}) copy-start(f32[3,7,256]{2,1,0:T(8,128)} %feat_taps.3) | copy-start | bytes 64516
  72.4 19.4 %copy-start.8 = (f32[7,256]{1,0:T(8,128)S(1)}, f32[7,256]{1,0:T(8,128)}, u32[]{:S(2)}) copy-start(f32[7,256]{1,0:T(8,128)} %inner_taps.3) | copy-start | bytes 21508
  103.6 4.7 %collective-permute-start.2 = (f32[4,8,256]{2,1,0:T(8,128)S(1)}, f32[4,8,256]{2,1,0:T(8,128)S(1)}, u32[]{:S(2)}, u32[]{:S(2)}) collective-permute-start(f32[4,8,256]{2,1,0:T(8,128)S(1)} %psum.7), channel_id=1, source_target_pairs={{0,8},{1,9},{2,10},{3,11},{4,12},{5,13},{6,14},{7,15},{8,0},{9,1},... | collective-permute-start | bytes 98312 | tf_op jit(solution)/shard_map/ppermute | solution.py:398
  108.3 5.9 %collective-permute-start.3 = (f32[4,8,256]{2,1,0:T(8,128)S(1)}, f32[4,8,256]{2,1,0:T(8,128)S(1)}, u32[]{:S(2)}, u32[]{:S(2)}) collective-permute-start(f32[4,8,256]{2,1,0:T(8,128)S(1)} %add.17.taps), channel_id=1, source_target_pairs={{0,24},{1,25},{2,26},{3,27},{4,28},{5,29},{6,30},{7,31},{8,16},{9,... | collective-permute-start | bytes 98312 | tf_op jit(solution)/shard_map/ppermute | solution.py:398
  114.1 1.0 copy-start.4
  115.8 14.1 %all-to-all-start = ((bf16[4,12,16,256]{3,2,1,0:T(8,128)(2,1)}), bf16[4,12,16,256]{3,2,1,0:T(8,128)(2,1)S(1)}, u32[]{:S(2)}, u32[]{:S(2)}) async-start(bf16[4,12,16,256]{3,2,1,0:T(8,128)(2,1)} %get-tuple-element.28), calls=%async_computation.1 | async-start | bytes 786432 | tf_op jit(solution)/shard_map/all_to_all | solution.py:442
  120.7 9.3 %collective-permute-start.4 = (f32[3,16,256]{2,1,0:T(8,128)S(1)}, f32[3,16,256]{2,1,0:T(8,128)S(1)}, u32[]{:S(2)}, u32[]{:S(2)}) collective-permute-start(f32[3,16,256]{2,1,0:T(8,128)S(1)} %get-tuple-element.30), channel_id=1, source_target_pairs={{1,0},{2,1},{3,2},{4,3},{5,4},{6,5},{7,6},{8,7},{9,8},{10,9},{11,1... | collective-permute-start | bytes 147464 | tf_op jit(solution)/shard_map/ppermute | solution.py:403
Sparse Core Ops, SparseCore 0:
  10.1 45.3 all-gather.3
  77.7 25.6 reduce-scatter.1

commit v5 on v4

--- a/solution.py
+++ b/solution.py
@@ -35,6 +35,7 @@
 SCALAR = pl.BlockSpec(memory_space=pltpu.SMEM)
 UNREAD = pl.BlockSpec(memory_space=pl.ANY)
 IN_HBM = pl.BlockSpec(memory_space=pltpu.HBM)
+IN_VMEM = pl.BlockSpec(memory_space=pltpu.VMEM)
 
 
 def call(kernel, name, flops, moved, vmem=VMEM_BYTES, **kwargs):
@@ -146,9 +147,10 @@
         return jnp.sum(terms.reshape(terms.shape[0] // 8, 8, LANES), axis=0)
 
     def put(place, sums):
-        for s in range(TAPS):
-            tap_sums[place, s : s + 1, :] = jnp.sum(sums[s], axis=0, keepdims=True)
-        tap_sums[place, TAPS : TAPS + 1, :] = jnp.zeros((1, LANES), F32)
+        rows = [jnp.sum(total, axis=0, keepdims=True) for total in sums]
+        tile = jnp.concatenate([*rows, jnp.zeros((1, LANES), F32)], axis=0)
+        for copy in range(tap_sums.shape[0]):
+            tap_sums[copy, place] = tile
 
     def transposed(j, at, count):
         total = feat_taps[j, 0:1, :] * grad_mixed[j, at : at + count, :]
@@ -179,7 +181,7 @@
     put(3, sums)
 
 
-def backward(col, near, far, before, own, feat_taps, inner_taps, after):
+def backward(copies, col, near, far, before, own, feat_taps, inner_taps, after):
     _, rows, channels = own.shape
     edge = jax.ShapeDtypeStruct((3, HALO, channels), F32)
     return call(
@@ -192,12 +194,14 @@
             SCALAR, lane_spec(rows), lane_spec(2, rows), lane_spec(3, HALO), lane_spec(3, rows),
             lane_spec(3, TAPS), lane_spec(TAPS), UNREAD,
         ],
-        out_specs=[lane_spec(3, rows), lane_spec(3, HALO), lane_spec(3, HALO), lane_spec(4, 8)],
+        out_specs=[
+            lane_spec(3, rows), lane_spec(3, HALO), lane_spec(3, HALO), lane_spec(copies, 4, 8)
+        ],
         out_shape=[
             jax.ShapeDtypeStruct((3, rows, channels), BF16),
             edge,
             edge,
-            jax.ShapeDtypeStruct((4, 8, channels), F32),
+            jax.ShapeDtypeStruct((copies, 4, 8, channels), F32),
         ],
         scratch_shapes=[pltpu.VMEM((3, rows + HALO, LANES), F32)]
         + [pltpu.VMEM((rows + LEAD, LANES), F32)] * 4
@@ -218,68 +222,116 @@
     return copies
 
 
-def products_kernel(
-    col, gated, grads, weight, sent, far, near, held_grads, held_weight, grad_sems, weight_sem
-):
-    copies = fetch(grads, held_grads, grad_sems)
-    weights = pltpu.make_async_copy(weight, held_weight, weight_sem)
-    weights.start()
-    blocks, rows, _ = held_grads.shape
-    half = near.shape[1]
-    for b in range(blocks):
+def sent_weight_kernel(gated, grads, sent, done, held, sems):
+    copies = fetch(grads, held, sems)
+    done[...] = jnp.zeros_like(done)
+    for b in range(held.shape[0]):
         copies[b].wait()
-        sent[b] = jnp.dot(gated[...], held_grads[b], preferred_element_type=F32).astype(BF16)
-    weights.wait()
-    step = min(rows, 128)
-    for start in range(0, rows, step):
-        span = slice(start, start + step)
-        wide = jnp.concatenate([held_grads[b, span, :] for b in range(blocks)], axis=1)
-        total = lax.dot_general(
-            wide, held_weight[...], (((1,), (1,)), ((), ())), preferred_element_type=F32
-        )
-        first = col[0] == 0
-        near[span, :] = jnp.where(first, total[:, :half], total[:, half:])
-        far[span, :] = jnp.where(first, total[:, half:], total[:, :half]).astype(BF16)
-
-
-def products(col, gated, grads, weight):
+        sent[b] = jnp.dot(gated[...], held[b], preferred_element_type=F32).astype(BF16)
+
+
+TOKEN = jax.ShapeDtypeStruct((8, LANES), F32)
+
+
+def sent_weight(gated, grads):
     channels, rows = gated.shape
     blocks, _, width = grads.shape
-    half = weight.shape[0] // 2
-    return call(
-        products_kernel,
-        "products",
-        2 * rows * (channels + 2 * half) * blocks * width,
-        2 * blocks * width * (rows + channels + 2 * half) + 6 * rows * half,
+    return call(
+        sent_weight_kernel,
+        "sent_weight",
+        2 * rows * channels * blocks * width,
+        2 * blocks * width * (rows + channels) + 2 * rows * channels,
         vmem=STREAM_BYTES,
-        in_specs=[SCALAR, pl.BlockSpec(memory_space=pltpu.VMEM), IN_HBM, IN_HBM],
-        out_specs=[pl.BlockSpec(memory_space=pltpu.VMEM)] * 3,
+        in_specs=[IN_VMEM, IN_HBM],
+        out_specs=[IN_VMEM] * 2,
+        out_shape=[jax.ShapeDtypeStruct((blocks, channels, width), BF16), TOKEN],
+        scratch_shapes=[pltpu.VMEM(grads.shape, BF16), pltpu.SemaphoreType.DMA((blocks,))],
+    )(gated, grads)
+
+
+def gated_grad_kernel(
+    col, grads, weight, _, far, near, held_grads, held_weight, grad_sems, weight_sems
+):
+    blocks, rows, width = held_grads.shape
+    halves = held_weight.shape[0]
+    per = blocks // halves
+    span = per * width
+    weights = [
+        pltpu.make_async_copy(
+            weight.at[:, part * span : (part + 1) * span], held_weight.at[part], weight_sems.at[part]
+        )
+        for part in range(halves)
+    ]
+    copies = [
+        pltpu.make_async_copy(grads.at[b], held_grads.at[b], grad_sems.at[b])
+        for b in range(blocks)
+    ]
+    for part in range(halves):
+        weights[part].start()
+        for b in range(part * per, (part + 1) * per):
+            copies[b].start()
+    half = near.shape[1]
+    own = col[0]
+    sums = [None, None]
+    for part in range(halves):
+        weights[part].wait()
+        for b in range(part * per, (part + 1) * per):
+            copies[b].wait()
+        wide = jnp.concatenate(
+            [held_grads[b] for b in range(part * per, (part + 1) * per)], axis=1
+        )
+        for at, which in enumerate((1 - own, own)):
+            rows_of = pl.ds(pl.multiple_of(which * half, half), half)
+            term = lax.dot_general(
+                wide,
+                held_weight[part, rows_of, :],
+                (((1,), (1,)), ((), ())),
+                preferred_element_type=F32,
+            )
+            sums[at] = term if part == 0 else sums[at] + term
+    far[...] = sums[0].astype(BF16)
+    near[...] = sums[1]
+
+
+def gated_grad(col, grads, weight, after):
+    blocks, rows, width = grads.shape
+    channels = weight.shape[0]
+    half = channels // 2
+    parts = min(2, blocks)
+    return call(
+        gated_grad_kernel,
+        "gated_grad",
+        2 * rows * channels * blocks * width,
+        2 * blocks * width * (rows + channels) + 6 * rows * half,
+        vmem=STREAM_BYTES,
+        in_specs=[SCALAR, IN_HBM, IN_HBM, UNREAD],
+        out_specs=[IN_VMEM] * 2,
         out_shape=[
-            jax.ShapeDtypeStruct((blocks, channels, width), BF16),
             jax.ShapeDtypeStruct((rows, half), BF16),
             jax.ShapeDtypeStruct((rows, half), F32),
         ],
         scratch_shapes=[
             pltpu.VMEM(grads.shape, BF16),
-            pltpu.VMEM(weight.shape, BF16),
+            pltpu.VMEM((parts, channels, blocks // parts * width), BF16),
             pltpu.SemaphoreType.DMA((blocks,)),
-            pltpu.SemaphoreType.DMA,
-        ],
-    )(col, gated, grads, weight)
-
-
-def kept_weight_kernel(gated, grads, arrived, out, done, held_grads, held, grad_sems, sems):
-    copies = fetch(grads, held_grads, grad_sems)
-    others = fetch(arrived, held, sems)
+            pltpu.SemaphoreType.DMA((parts,)),
+        ],
+    )(col, grads, weight, after)
+
+
+def kept_weight_kernel(gated, grads, arrived, out, done, held, sems):
     done[...] = jnp.zeros_like(done)
-    parts, _, size, _ = out.shape
-    for b in range(held.shape[0]):
-        copies[b].wait()
-        total = jnp.dot(gated[...], held_grads[b], preferred_element_type=F32)
-        others[b].wait()
-        total = (total + held[b].astype(F32)).astype(BF16)
+    blocks, parts, size, _ = held.shape
+    copies = []
+    for b in range(blocks):
+        total = jnp.dot(gated[...], grads[b], preferred_element_type=F32)
+        total = (total + arrived[b].astype(F32)).astype(BF16)
         for part in range(parts):
-            out[part, b] = total[part * size : (part + 1) * size]
+            held[b, part] = total[part * size : (part + 1) * size]
+        copies.append(pltpu.make_async_copy(held.at[b], out.at[:, b], sems.at[b]))
+        copies[-1].start()
+    for copy in copies:
+        copy.wait()
 
 
 def kept_weight(parts, gated, grads, arrived):
@@ -291,83 +343,111 @@
         "kept_weight",
         2 * rows * channels * blocks * width,
         2 * blocks * width * (rows + 2 * channels) + 2 * rows * channels,
-        in_specs=[pl.BlockSpec(memory_space=pltpu.VMEM), IN_HBM, IN_HBM],
-        out_specs=[pl.BlockSpec(memory_space=pltpu.VMEM)] * 2,
-        out_shape=[
-            jax.ShapeDtypeStruct((parts, blocks, size, width), BF16),
-            jax.ShapeDtypeStruct((8, LANES), F32),
-        ],
+        in_specs=[IN_VMEM] * 3,
+        out_specs=[IN_HBM, IN_VMEM],
+        out_shape=[jax.ShapeDtypeStruct((parts, blocks, size, width), BF16), TOKEN],
         scratch_shapes=[
-            pltpu.VMEM(grads.shape, BF16),
-            pltpu.VMEM(arrived.shape, BF16),
+            pltpu.VMEM((blocks, parts, size, width), BF16),
             pltpu.SemaphoreType.DMA((blocks,)),
-            pltpu.SemaphoreType.DMA((blocks,)),
         ],
     )(gated, grads, arrived)
 
 
-def middle_kernel(pair, taps, taps_arrived, head, out, out_taps, out_head):
-    parts, _, size, _ = out.shape
-    blocks = pair.shape[0]
-    sums = taps[...] + taps_arrived[...]
-    out_taps[...] = sums
+def two_roundings(sums):
     high = sums.astype(BF16).astype(F32)
-    both = jnp.concatenate([high, sums - high], axis=1).astype(BF16)
-    for part in range(parts):
-        out[part, 0:blocks] = pair[:, part * size : (part + 1) * size, :]
-        out[part, blocks:] = both
+    return jnp.concatenate([high, sums - high], axis=1).astype(BF16)
+
+
+def rejoined(both):
+    both = both.astype(F32)
+    return both[:, :8] + both[:, 8:]
+
+
+def first_half_kernel(z, pair, taps, head, out, kept, out_taps, out_head):
+    blocks, rows, _ = pair.shape
+    size = rows // 4
+    total = taps[0]
+    for copy in range(1, taps.shape[0]):
+        total = total + taps[copy]
+    out_taps[...] = total
     out_head[...] = head[...]
-
-
-def middle(parts, pair, taps, taps_arrived, head):
-    blocks, channels, width = pair.shape
-    shape = (parts, blocks + taps.shape[0], channels // parts, width)
-    args = (pair, taps, taps_arrived, head)
+    low = lax.rem(z[0], 2)
+    for high in range(2):
+        own, other = (
+            pl.ds(pl.multiple_of((2 * high + bit) * size, size), size) for bit in (low, 1 - low)
+        )
+        out[high * blocks : (high + 1) * blocks] = pair[:, other, :]
+        kept[high] = pair[:, own, :].astype(F32)
+    out[2 * blocks :] = two_roundings(total)
+
+
+def second_half_kernel(z, kept, taps, arrived, out, out_kept, out_taps):
+    _, blocks, _, _ = kept.shape
+    total = taps[...] + rejoined(arrived[2 * blocks :])
+    out_taps[...] = total
+    high = lax.div(z[0], 2)
+    own, other = (
+        kept[bit] + arrived[pl.ds(bit * blocks, blocks)].astype(F32) for bit in (high, 1 - high)
+    )
+    out_kept[...] = own
+    out[0:blocks] = other.astype(BF16)
+    out[blocks:] = two_roundings(total)
+
+
+def last_kernel(
+    scale, kept, taps, arrived, tail, head, _, out, out_feat, out_inner, out_grads
+):
+    blocks, _, width = kept.shape
+    out_grads[...] = (tail[...] + head[...]).astype(BF16)
+    for b in range(blocks):
+        total = kept[b] + arrived[b].astype(F32)
+        out[:, b * width : (b + 1) * width] = (total * scale).astype(BF16)
+    total = (taps[...] + rejoined(arrived[blocks:])) * scale
+    out_feat[...] = total[:3, :TAPS]
+    out_inner[...] = total[3, :TAPS]
+
+
+def small_call(kernel, name, args, outs, scalars=0, **kwargs):
+    moved = sum(v.size * v.dtype.itemsize for v in (*args, *outs))
+    return call(
+        kernel,
+        name,
+        moved,
+        moved,
+        grid=(1,),
+        in_specs=[SCALAR] * scalars + [whole(v.shape) for v in args[scalars:]],
+        out_specs=[whole(v.shape) for v in outs],
+        out_shape=outs,
+        **kwargs,
+    )(*args)
+
+
+def first_half(z, pair, taps, head):
+    blocks, rows, width = pair.shape
+    tile = (rows // 4, width)
     outs = [
-        jax.ShapeDtypeStruct(shape, BF16),
-        jax.ShapeDtypeStruct(taps.shape, F32),
+        jax.ShapeDtypeStruct((2 * blocks + taps.shape[1], *tile), BF16),
+        jax.ShapeDtypeStruct((2, blocks, *tile), F32),
+        jax.ShapeDtypeStruct(taps.shape[1:], F32),
         jax.ShapeDtypeStruct(head.shape, F32),
     ]
-    return call(
-        middle_kernel,
-        "middle",
-        4 * pair.size,
-        4 * pair.size,
-        grid=(1,),
-        in_specs=[whole(v.shape) for v in args],
-        out_specs=[whole(v.shape) for v in outs],
-        out_shape=outs,
-    )(*args)
-
-
-def last_kernel(
-    scale, z, taps, arrived, tail, head, _, out, out_feat, out_inner, out_grads
-):
-    parts, _, _, width = arrived.shape
-    blocks = out.shape[1] // width
-    out_grads[...] = (tail[...] + head[...]).astype(BF16)
-    for b in range(blocks):
-        total = arrived[0, b].astype(F32)
-        for part in range(1, parts):
-            total = total + arrived[part, b].astype(F32)
-        out[:, b * width : (b + 1) * width] = (total * scale).astype(BF16)
-    for j in range(4):
-        total = taps[j]
-        for part in range(parts):
-            both = arrived[part, blocks + j].astype(F32)
-            total = total + jnp.where(z[0] == part, 0.0, both[:8] + both[8:])
-        total = (total * scale)[:TAPS]
-        if j < 3:
-            out_feat[j] = total
-        else:
-            out_inner[...] = total
-
-
-def last(scale, z, taps, arrived, tail, head, grads):
-    parts, count, channels, width = arrived.shape
-    blocks = count - taps.shape[0]
+    return small_call(first_half_kernel, "first_half", (z, pair, taps, head), outs, scalars=1)
+
+
+def second_half(z, kept, taps, arrived):
+    _, blocks, *tile = kept.shape
+    outs = [
+        jax.ShapeDtypeStruct((blocks + taps.shape[0], *tile), BF16),
+        jax.ShapeDtypeStruct((blocks, *tile), F32),
+        jax.ShapeDtypeStruct(taps.shape, F32),
+    ]
+    return small_call(second_half_kernel, "second_half", (z, kept, taps, arrived), outs, scalars=1)
+
+
+def last(scale, kept, taps, arrived, tail, head, grads):
+    blocks, channels, width = kept.shape
     final = grads.shape[1] // HALO - 1
-    args = (taps, arrived, tail, head)
+    args = (kept, taps, arrived, tail, head)
     shapes = [
         jax.ShapeDtypeStruct((channels, blocks * width), BF16),
         jax.ShapeDtypeStruct((3, TAPS, width), F32),
@@ -379,12 +459,12 @@
         2 * arrived.size,
         2 * arrived.size,
         grid=(1,),
-        in_specs=[SCALAR] + [whole(v.shape) for v in args] + [UNREAD],
+        in_specs=[whole(v.shape) for v in args] + [UNREAD],
         out_specs=[whole(v.shape) for v in shapes]
         + [pl.BlockSpec(tail.shape, lambda i: (0, final, 0))],
         out_shape=shapes + [jax.ShapeDtypeStruct(grads.shape, grads.dtype)],
         input_output_aliases={5: 3},
-    )(z, *args, grads)
+    )(*args, grads)
 
 
 def ctx_permute(value, target):
@@ -425,24 +505,25 @@
         for c in (core, 1 - core)
     )
 
-    sent, far, near = products(col, sent, grads, out_weight)
+    sent, done = sent_weight(sent, grads)
     arrived = ctx_permute(sent, lambda x, z, c: (x, z, 1 - c))
+    far, near = gated_grad(col, grads, out_weight, done)
     pair, done = kept_weight(nx, kept, grads, arrived)
     far = lax.all_gather(far, "col", axis=0)
     summed = lax.psum_scatter(pair, "x", scatter_dimension=0)
 
     grad_own, head, tail, taps = backward(
-        col, near, far, before, own, feat_taps, inner_taps, done
-    )
-    taps = lax.psum(taps, "core")
-    taps = taps + ctx_permute(taps, lambda x, z, c: (x ^ 1, z, c))
-    taps_arrived = ctx_permute(taps, lambda x, z, c: (nx - 1 - x, z, c))
-
-    pieces, taps, head = middle(nz, summed, taps, taps_arrived, head)
-    pieces = lax.all_to_all(pieces, "zl", split_axis=0, concat_axis=0)
+        nx * nc, col, near, far, before, own, feat_taps, inner_taps, done
+    )
+    taps = lax.all_to_all(taps, ("x", "core"), split_axis=0, concat_axis=0)
+
+    piece, part, taps, head = first_half(z, summed, taps, head)
+    arrived = ctx_permute(piece, lambda x, z, c: (x, z ^ 1, c))
     head = ctx_shift(head, -1)
+    piece, part, taps = second_half(z, part, taps, arrived)
+    arrived = ctx_permute(piece, lambda x, z, c: (x, z ^ 2, c))
     grad_weight, grad_feat_taps, grad_inner_taps, grad_own = last(
-        inv_root, z, taps, pieces, tail, head, grad_own
+        inv_root, part, taps, arrived, tail, head, grad_own
     )
     return jnp.transpose(grad_own, (1, 0, 2)), grad_weight, grad_feat_taps, grad_inner_taps
 

time: 139 us -> 138 us (level)
  starting transfers between devices: 25 us -> 32.6 us
  blocking collectives: 34.2 us -> 26.7 us
  Pallas kernels: 20.2 us -> 17.5 us
    psum x1 -> x0, blocking collectives: 7.73 us -> none  [body(): taps = lax.psum(taps, 'core')]
    ppermute x3, starting transfers between devices: 10 us -> 17.3 us  [ctx_permute(): return lax.ppermute(value, CTX, pairs)]
    all_to_all x1, waiting for transfers between devices: 0.01 us -> 6.5 us  [body(): taps = lax.all_to_all(taps, ('x', 'core'), split_axis=0, concat_axis=0)]
    pallas_call x1, Pallas kernels: 5.18 us -> 1.51 us  [kept_weight(): call(kept_weight_kernel, 'kept_weight', 2 * rows * channels * blocks * wi...]
    ppermute x3, waiting for transfers between devices: 9.15 us -> 5.97 us  [ctx_permute(): return lax.ppermute(value, CTX, pairs)]
    ppermute x2, waiting for transfers between devices: 8.09 us -> 5.74 us  [ctx_shift(): lax.ppermute(value, CTX, [(i, i + steps) for i in range(count) if 0 <= i...]
    unnamed x20 -> x18, local copies, waits for them, and re-layouts: 3.54 us -> 4.58 us
    pallas_call x2 -> x4, Pallas kernels: 8.91 us -> 9.93 us  [the longest x1 5.4 us: sent_weight(): call(sent_weight_kernel, 'sent_weight', 2 * rows * channels * blocks * wi...]
  transfers between devices with their start and end apart: 8 -> 8, of which waited for: 6 -> 6; matrix products, arithmetic and copies ran while one was open for 1% -> 1% of each run, Pallas kernels for 4% -> 7%
where the time goes in v5:
time: 138 us; the launch traced here: 137 us
  waiting for transfers between devices  39.7 us (29%)
  starting transfers between devices  32.6 us (24%)
  blocking collectives  26.7 us (19%)
  Pallas kernels  17.5 us (13%)
  between operations  14.2 us (10%)
  local copies, waits for them, and re-layouts  6.29 us (5%)
    all_gather x1, waiting for transfers between devices, body(): grads = lax.all_gather(out_grad, 'row', axis=0)  20.8 us
    ppermute x3, starting transfers between devices, ctx_permute(): return lax.ppermute(value, CTX, pairs)  17.3 us
    all_gather x1, blocking collectives, body(): far = lax.all_gather(far, 'col', axis=0)  14.4 us
    all_gather x1, blocking collectives, body(): both = lax.all_gather(gated, 'col', axis=1, tiled=True)  12.3 us
    ppermute x2, starting transfers between devices, ctx_shift(): lax.ppermute(value, CTX, [(i, i + steps) for i in range(count) if 0 <= i...  9.53 us
    all_to_all x1, waiting for transfers between devices, body(): taps = lax.all_to_all(taps, ('x', 'core'), split_axis=0, concat_axis=0)  6.5 us
    ppermute x3, waiting for transfers between devices, ctx_permute(): return lax.ppermute(value, CTX, pairs)  5.97 us
    all_to_all x1, starting transfers between devices, body(): taps = lax.all_to_all(taps, ('x', 'core'), split_axis=0, concat_axis=0)  5.79 us
  transfers between devices with their start and end apart: 8, of which 6 were waited for; matrix products, arithmetic and copies ran while one was open for 1% of the time, Pallas kernels for 7%

profile of v5, /device:TPU:1, one launch (start us, length us, event | category | flops | bytes accessed | tf_op | source)
XLA Modules:
  0.0 137.1 jit_solution(10274693101632868748)
XLA Ops:
  7.2 0.0 all-gather.4.cloned.1.call-start
  7.2 0.7 all-gather.4.cloned.1.call-update
  7.9 0.0 reduce-scatter.2.cloned.1.call-start
  7.9 0.7 slice.4
  8.7 5.4 %collective-permute-start = (bf16[3,16,256]{2,1,0:T(8,128)(2,1)S(1)}, bf16[3,16,256]{2,1,0:T(8,128)(2,1)S(1)}, u32[]{:S(2)}, u32[]{:S(2)}) collective-permute-start(bf16[3,16,256]{2,1,0:T(8,128)(2,1)S(1)} %slice.4), channel_id=1, source_target_pairs={{0,1},{1,2},{2,3},{3,4},{4,5},{5,6},{6,7},{7,8},{8,9},{9,10},{10,1... | collective-permute-start | bytes 73736 | tf_op jit(solution)/shard_map/ppermute | solution.py:483
  14.1 3.4 %collective-permute-done.before = bf16[3,16,256]{2,1,0:T(8,128)(2,1)S(1)} collective-permute-done((bf16[3,16,256]{2,1,0:T(8,128)(2,1)S(1)}, bf16[3,16,256]{2,1,0:T(8,128)(2,1)S(1)}, u32[]{:S(2)}, u32[]{:S(2)}) %collective-permute-start) | collective-permute-done | bytes 24608 | tf_op jit(solution)/shard_map/ppermute | solution.py:483
  17.5 1.1 copy-done.1
  18.7 0.7 copy-done.5
  19.4 0.7 copy-done.7
  20.1 1.3 forward.1
  21.4 12.3 %all_gather.15 = bf16[512,512]{1,0:T(8,128)(2,1)S(1)} all-gather(bf16[512,256]{1,0:T(8,128)(2,1)S(1)} %forward.1), channel_id=1, replica_groups=mesh['row'=8,'col'=2,'x'=4,'zl'=4,'core'=2] {'col'}, dimensions={1}, use_global_device_ids=true | all-gather | bytes 786432 | tf_op jit(solution)/shard_map/all_gather | solution.py:500
  33.7 0.2 copy.12
  34.0 0.7 constant_dynamic-slice_fusion
  34.7 20.8 %all-gather.4.cloned.1.call-done = bf16[4096,256]{1,0:T(8,128)(2,1)} async-done(((bf16[512,256]{1,0:T(8,128)(2,1)}), bf16[4096,256]{1,0:T(8,128)(2,1)}) %all-gather.4.cloned.1.call-update) | async-done | bytes 2097168 | tf_op jit(solution)/shard_map/all_gather | solution.py:495
  55.5 5.4 %sent_weight.1 = (bf16[8,256,256]{2,1,0:T(8,128)(2,1)}, f32[8,128]{1,0:T(8,128)}) custom-call(bf16[256,512]{1,0:T(8,128)(2,1)} %bitcast.22, bf16[8,512,256]{2,1,0:T(8,128)(2,1)} %bitcast.11), custom_call_target="tpu_custom_call" | custom-call | flops 536870912 | bytes 3407872 | tf_op jit(solution)/shard_map/sent_weight/pallas_call | solution.py:239
  60.9 6.2 %collective-permute-start.1 = (bf16[8,256,256]{2,1,0:T(8,128)(2,1)}, bf16[8,256,256]{2,1,0:T(8,128)(2,1)S(1)}, u32[]{:S(2)}, u32[]{:S(2)}) collective-permute-start(bf16[8,256,256]{2,1,0:T(8,128)(2,1)} %get-tuple-element.25), channel_id=1, source_target_pairs={{0,1},{1,0},{2,3},{3,2},{4,5},{5,4},{6,7},{7,6},{8,9},{9,8},{10,11... | collective-permute-start | bytes 3145736 | tf_op jit(solution)/shard_map/ppermute | solution.py:478
  67.1 2.5 %collective-permute-done.1.arrived = bf16[8,256,256]{2,1,0:T(8,128)(2,1)S(1)} collective-permute-done((bf16[8,256,256]{2,1,0:T(8,128)(2,1)}, bf16[8,256,256]{2,1,0:T(8,128)(2,1)S(1)}, u32[]{:S(2)}, u32[]{:S(2)}) %collective-permute-start.1) | collective-permute-done | bytes 1048608 | tf_op jit(solution)/shard_map/ppermute | solution.py:478
  69.6 1.5 %kept_weight.1 = (bf16[4,8,64,256]{3,2,1,0:T(8,128)(2,1)}, f32[8,128]{1,0:T(8,128)S(1)}) custom-call(bf16[256,512]{1,0:T(8,128)(2,1)S(1)} %bitcast.18, bf16[8,512,256]{2,1,0:T(8,128)(2,1)S(1)} %bitcast.13, bf16[8,256,256]{2,1,0:T(8,128)(2,1)S(1)} %collective-permute-done.1.arrived), custom_call_target="tpu_custom_call" | custom-call | flops 536870912 | bytes 4456448 | tf_op jit(solution)/shard_map/kept_weight/pallas_call | solution.py:341
  71.1 0.0 reduce-scatter.2.cloned.1.call-update
  71.2 4.5 %gated_grad.1 = (bf16[512,256]{1,0:T(8,128)(2,1)}, f32[512,256]{1,0:T(8,128)}) custom-call(s32[1]{0:T(128)} %bitcast.8.col, bf16[8,512,256]{2,1,0:T(8,128)(2,1)} %bitcast.12, bf16[512,2048]{1,0:T(8,128)(2,1)} %weight.1, f32[8,128]{1,0:T(8,128)} %get-tuple-element.27._), custom_call_target="tpu_custom_call" | custom-call | flops 1073741824 | bytes 4980736 | tf_op jit(solution)/shard_map/gated_grad/pallas_call | solution.py:301
  75.7 14.4 %all-gather.1 = bf16[1024,256]{1,0:T(8,128)(2,1)S(1)} all-gather(bf16[512,256]{1,0:T(8,128)(2,1)} %get-tuple-element.29), channel_id=3, replica_groups=mesh['row'=8,'col'=2,'x'=4,'zl'=4,'core'=2] {'col'}, dimensions={0}, use_global_device_ids=true | all-gather | bytes 786432 | tf_op jit(solution)/shard_map/all_gather | solution.py:512
  90.1 1.0 copy-done.3
  91.1 4.1 %backward.1 = (bf16[3,512,256]{2,1,0:T(8,128)(2,1)}, f32[3,16,256]{2,1,0:T(8,128)S(1)}, f32[3,16,256]{2,1,0:T(8,128)S(1)}, f32[8,4,8,256]{3,2,1,0:T(8,128)}) custom-call(s32[1]{0:T(128)} %bitcast.8.col, f32[512,256]{1,0:T(8,128)S(1)} %copy-done.3, bf16[2,512,256]{2,1,0:T(8,128)(2,1)S(1)} %bitcast.17, bf16[3,16,256]{2,1,0:T(8,128)(2,1)S(1)} %collective-permute-done.before, ...), custom_call_target="tpu_custom_call" | custom-call | flops 20971520 | bytes 2621440 | tf_op jit(solution)/shard_map/backward/pallas_call | solution.py:187
  95.2 5.8 %all-to-all-start = ((f32[8,4,8,256]{3,2,1,0:T(8,128)}), f32[8,4,8,256]{3,2,1,0:T(8,128)S(1)}, u32[]{:S(2)}, u32[]{:S(2)}) async-start(f32[8,4,8,256]{3,2,1,0:T(8,128)} %get-tuple-element.31), calls=%async_computation.1 | async-start | bytes 524288 | tf_op jit(solution)/shard_map/all_to_all | solution.py:518
  101.0 6.5 %all-to-all-done.taps = f32[8,4,8,256]{3,2,1,0:T(8,128)S(1)} async-done(((f32[8,4,8,256]{3,2,1,0:T(8,128)}), f32[8,4,8,256]{3,2,1,0:T(8,128)S(1)}, u32[]{:S(2)}, u32[]{:S(2)}) %all-to-all-start) | async-done | bytes 262176 | tf_op jit(solution)/shard_map/all_to_all | solution.py:518
  107.5 0.9 copy-done.4
  108.5 6.5 %collective-permute-start.2 = (bf16[20,16,256]{2,1,0:T(8,128)(2,1)S(1)}, bf16[20,16,256]{2,1,0:T(8,128)(2,1)S(1)}, u32[]{:S(2)}, u32[]{:S(2)}) collective-permute-start(bf16[20,16,256]{2,1,0:T(8,128)(2,1)S(1)} %get-tuple-element.35), channel_id=1, source_target_pairs={{0,2},{1,3},{2,0},{3,1},{4,6},{5,7},{6,4},{7,5},{8,10},{9,11},{10,... | collective-permute-start | bytes 491528 | tf_op jit(solution)/shard_map/ppermute | solution.py:478
  115.1 3.5 %collective-permute-done.2.arrived = bf16[20,16,256]{2,1,0:T(8,128)(2,1)S(1)} collective-permute-done((bf16[20,16,256]{2,1,0:T(8,128)(2,1)S(1)}, bf16[20,16,256]{2,1,0:T(8,128)(2,1)S(1)}, u32[]{:S(2)}, u32[]{:S(2)}) %collective-permute-start.2) | collective-permute-done | bytes 163872 | tf_op jit(solution)/shard_map/ppermute | solution.py:478
  118.6 4.5 %collective-permute-start.3 = (bf16[12,16,256]{2,1,0:T(8,128)(2,1)S(1)}, bf16[12,16,256]{2,1,0:T(8,128)(2,1)S(1)}, u32[]{:S(2)}, u32[]{:S(2)}) collective-permute-start(bf16[12,16,256]{2,1,0:T(8,128)(2,1)S(1)} %get-tuple-element.38), channel_id=1, source_target_pairs={{0,4},{1,5},{2,6},{3,7},{4,0},{5,1},{6,2},{7,3},{8,12},{9,13},{10,... | collective-permute-start | bytes 294920 | tf_op jit(solution)/shard_map/ppermute | solution.py:478
  123.1 4.2 %collective-permute-start.4 = (f32[3,16,256]{2,1,0:T(8,128)S(1)}, f32[3,16,256]{2,1,0:T(8,128)S(1)}, u32[]{:S(2)}, u32[]{:S(2)}) collective-permute-start(f32[3,16,256]{2,1,0:T(8,128)S(1)} %get-tuple-element.40), channel_id=1, source_target_pairs={{1,0},{2,1},{3,2},{4,3},{5,4},{6,5},{7,6},{8,7},{9,8},{10,9},{11,1... | collective-permute-start | bytes 147464 | tf_op jit(solution)/shard_map/ppermute | solution.py:483
  127.3 2.3 %collective-permute-done.4.refs_4_ = f32[3,16,256]{2,1,0:T(8,128)S(1)} collective-permute-done((f32[3,16,256]{2,1,0:T(8,128)S(1)}, f32[3,16,256]{2,1,0:T(8,128)S(1)}, u32[]{:S(2)}, u32[]{:S(2)}) %collective-permute-start.4) | collective-permute-done | bytes 49184 | tf_op jit(solution)/shard_map/ppermute | solution.py:483
  129.6 0.7 last.1
  (17 shorter events, 0.1 us)
Async XLA Ops:
  7.2 48.3 %all-gather.4.cloned.1.call-start = ((), (), s32[]{:S(2)}) async-start(), calls=%async_computation.3 | async-start | bytes 2359296 | tf_op jit(solution)/shard_map/all_gather | solution.py:495
  7.9 99.6 %reduce-scatter.2.cloned.1.call-start = ((), (), s32[]{:S(2)}) async-start(), calls=%async_computation.2 | async-start | bytes 1310720 | tf_op jit(solution)/shard_map/reduce_scatter | solution.py:513
  8.7 8.8 %collective-permute-start = (bf16[3,16,256]{2,1,0:T(8,128)(2,1)S(1)}, bf16[3,16,256]{2,1,0:T(8,128)(2,1)S(1)}, u32[]{:S(2)}, u32[]{:S(2)}) collective-permute-start(bf16[3,16,256]{2,1,0:T(8,128)(2,1)S(1)} %slice.4), channel_id=1, source_target_pairs={{0,1},{1,2},{2,3},{3,4},{4,5},{5,6},{6,7},{7,8},{8,9},{9,10},{10,1... | collective-permute-start | bytes 73736 | tf_op jit(solution)/shard_map/ppermute | solution.py:483
  17.5 1.1 copy-start.1
  18.7 0.7 copy-start.5
  19.4 0.7 copy-start.7
  55.5 14.1 %copy-start = (bf16[4096,256]{1,0:T(8,128)(2,1)S(1)}, bf16[4096,256]{1,0:T(8,128)(2,1)}, u32[]{:S(2)}) copy-start(bf16[4096,256]{1,0:T(8,128)(2,1)} %all-gather.4.cloned.1.call-done) | copy-start | bytes 6291460
  60.9 8.7 %collective-permute-start.1 = (bf16[8,256,256]{2,1,0:T(8,128)(2,1)}, bf16[8,256,256]{2,1,0:T(8,128)(2,1)S(1)}, u32[]{:S(2)}, u32[]{:S(2)}) collective-permute-start(bf16[8,256,256]{2,1,0:T(8,128)(2,1)} %get-tuple-element.25), channel_id=1, source_target_pairs={{0,1},{1,0},{2,3},{3,2},{4,5},{5,4},{6,7},{7,6},{8,9},{9,8},{10,11... | collective-permute-start | bytes 3145736 | tf_op jit(solution)/shard_map/ppermute | solution.py:478
  71.2 18.9 %copy-start.2 = (bf16[512,3,256]{2,0,1:T(8,128)(2,1)S(1)}, bf16[512,3,256]{2,0,1:T(8,128)(2,1)}, u32[]{:S(2)}) copy-start(bf16[512,3,256]{2,0,1:T(8,128)(2,1)} %param.5) | copy-start | bytes 2359300
  71.2 18.9 %copy-start.6 = (f32[3,7,256]{2,1,0:T(8,128)S(1)}, f32[3,7,256]{2,1,0:T(8,128)}, u32[]{:S(2)}) copy-start(f32[3,7,256]{2,1,0:T(8,128)} %feat_taps.3) | copy-start | bytes 64516
  71.2 18.9 %copy-start.8 = (f32[7,256]{1,0:T(8,128)S(1)}, f32[7,256]{1,0:T(8,128)}, u32[]{:S(2)}) copy-start(f32[7,256]{1,0:T(8,128)} %inner_taps.3) | copy-start | bytes 21508
  90.1 1.0 copy-start.3
  95.2 12.3 %all-to-all-start = ((f32[8,4,8,256]{3,2,1,0:T(8,128)}), f32[8,4,8,256]{3,2,1,0:T(8,128)S(1)}, u32[]{:S(2)}, u32[]{:S(2)}) async-start(f32[8,4,8,256]{3,2,1,0:T(8,128)} %get-tuple-element.31), calls=%async_computation.1 | async-start | bytes 524288 | tf_op jit(solution)/shard_map/all_to_all | solution.py:518
  107.5 1.0 copy-start.4
  108.5 10.0 %collective-permute-start.2 = (bf16[20,16,256]{2,1,0:T(8,128)(2,1)S(1)}, bf16[20,16,256]{2,1,0:T(8,128)(2,1)S(1)}, u32[]{:S(2)}, u32[]{:S(2)}) collective-permute-start(bf16[20,16,256]{2,1,0:T(8,128)(2,1)S(1)} %get-tuple-element.35), channel_id=1, source_target_pairs={{0,2},{1,3},{2,0},{3,1},{4,6},{5,7},{6,4},{7,5},{8,10},{9,11},{10,... | collective-permute-start | bytes 491528 | tf_op jit(solution)/shard_map/ppermute | solution.py:478
  118.6 11.0 %collective-permute-start.3 = (bf16[12,16,256]{2,1,0:T(8,128)(2,1)S(1)}, bf16[12,16,256]{2,1,0:T(8,128)(2,1)S(1)}, u32[]{:S(2)}, u32[]{:S(2)}) collective-permute-start(bf16[12,16,256]{2,1,0:T(8,128)(2,1)S(1)} %get-tuple-element.38), channel_id=1, source_target_pairs={{0,4},{1,5},{2,6},{3,7},{4,0},{5,1},{6,2},{7,3},{8,12},{9,13},{10,... | collective-permute-start | bytes 294920 | tf_op jit(solution)/shard_map/ppermute | solution.py:478
  123.1 6.5 %collective-permute-start.4 = (f32[3,16,256]{2,1,0:T(8,128)S(1)}, f32[3,16,256]{2,1,0:T(8,128)S(1)}, u32[]{:S(2)}, u32[]{:S(2)}) collective-permute-start(f32[3,16,256]{2,1,0:T(8,128)S(1)} %get-tuple-element.40), channel_id=1, source_target_pairs={{1,0},{2,1},{3,2},{4,3},{5,4},{6,5},{7,6},{8,7},{9,8},{10,9},{11,1... | collective-permute-start | bytes 147464 | tf_op jit(solution)/shard_map/ppermute | solution.py:483
Sparse Core Ops, SparseCore 0:
  10.1 45.3 all-gather.3
  71.3 26.3 reduce-scatter.1

commit v6 on v5

--- a/solution.py
+++ b/solution.py
@@ -17,7 +17,7 @@
 F32 = jnp.float32
 BF16 = jnp.bfloat16
 VMEM_BYTES = 24 << 20
-STREAM_BYTES = 56 << 20
+BLOCKS = 8
 
 
 def spread(total):
@@ -212,145 +212,122 @@
     )(col, near, far, before, own, feat_taps, inner_taps, after)
 
 
-def fetch(source, target, sems):
-    copies = [
-        pltpu.make_async_copy(source.at[i], target.at[i], sems.at[i])
-        for i in range(source.shape[0])
+TOKEN = jax.ShapeDtypeStruct((8, LANES), F32)
+
+
+def blocks_of(refs):
+    own, right, left, rights, lefts, low, high = refs
+    return [
+        [own], [right], [rights.at[0]], [rights.at[1]], [low, high], [lefts.at[1]], [lefts.at[0]],
+        [left],
     ]
-    for copy in copies:
-        copy.start()
-    return copies
-
-
-def sent_weight_kernel(gated, grads, sent, done, held, sems):
-    copies = fetch(grads, held, sems)
+
+
+def times_block(gated, block):
+    total, at = None, 0
+    for ref in block:
+        rows = ref.shape[0]
+        term = jnp.dot(gated[:, at : at + rows], ref[...], preferred_element_type=F32)
+        total = term if total is None else total + term
+        at += rows
+    return total
+
+
+def sent_weight_kernel(gated, *refs):
+    *grads, sent, done = refs
     done[...] = jnp.zeros_like(done)
-    for b in range(held.shape[0]):
-        copies[b].wait()
-        sent[b] = jnp.dot(gated[...], held[b], preferred_element_type=F32).astype(BF16)
-
-
-TOKEN = jax.ShapeDtypeStruct((8, LANES), F32)
+    for b, block in enumerate(blocks_of(grads)):
+        sent[b] = times_block(gated, block).astype(BF16)
 
 
 def sent_weight(gated, grads):
     channels, rows = gated.shape
-    blocks, _, width = grads.shape
+    blocks, width = BLOCKS, grads[0].shape[1]
     return call(
         sent_weight_kernel,
         "sent_weight",
         2 * rows * channels * blocks * width,
         2 * blocks * width * (rows + channels) + 2 * rows * channels,
-        vmem=STREAM_BYTES,
-        in_specs=[IN_VMEM, IN_HBM],
+        in_specs=[IN_VMEM] * (1 + len(grads)),
         out_specs=[IN_VMEM] * 2,
         out_shape=[jax.ShapeDtypeStruct((blocks, channels, width), BF16), TOKEN],
-        scratch_shapes=[pltpu.VMEM(grads.shape, BF16), pltpu.SemaphoreType.DMA((blocks,))],
-    )(gated, grads)
-
-
-def gated_grad_kernel(
-    col, grads, weight, _, far, near, held_grads, held_weight, grad_sems, weight_sems
-):
-    blocks, rows, width = held_grads.shape
-    halves = held_weight.shape[0]
-    per = blocks // halves
-    span = per * width
-    weights = [
-        pltpu.make_async_copy(
-            weight.at[:, part * span : (part + 1) * span], held_weight.at[part], weight_sems.at[part]
+    )(gated, *grads)
+
+
+def gated_grad_kernel(place, weight, *refs):
+    *grads, _, far, near = refs
+    blocks = blocks_of(grads)
+    width = grads[0].shape[1]
+    wide = jnp.concatenate(
+        [
+            jnp.concatenate([ref[...] for ref in block], axis=0) if len(block) > 1 else block[0][...]
+            for block in blocks
+        ],
+        axis=1,
+    )
+    half = near.shape[1]
+    row, own = place[0], place[1]
+    for out, which in ((far, 1 - own), (near, own)):
+        rows_of = pl.ds(pl.multiple_of(which * half, half), half)
+        taken = []
+        for b in range(len(blocks)):
+            at = lax.rem(row + b, len(blocks)) * width
+            taken.append(weight[rows_of, pl.ds(pl.multiple_of(at, width), width)])
+        total = lax.dot_general(
+            wide,
+            jnp.concatenate(taken, axis=1),
+            (((1,), (1,)), ((), ())),
+            preferred_element_type=F32,
         )
-        for part in range(halves)
-    ]
-    copies = [
-        pltpu.make_async_copy(grads.at[b], held_grads.at[b], grad_sems.at[b])
-        for b in range(blocks)
-    ]
-    for part in range(halves):
-        weights[part].start()
-        for b in range(part * per, (part + 1) * per):
-            copies[b].start()
-    half = near.shape[1]
-    own = col[0]
-    sums = [None, None]
-    for part in range(halves):
-        weights[part].wait()
-        for b in range(part * per, (part + 1) * per):
-            copies[b].wait()
-        wide = jnp.concatenate(
-            [held_grads[b] for b in range(part * per, (part + 1) * per)], axis=1
-        )
-        for at, which in enumerate((1 - own, own)):
-            rows_of = pl.ds(pl.multiple_of(which * half, half), half)
-            term = lax.dot_general(
-                wide,
-                held_weight[part, rows_of, :],
-                (((1,), (1,)), ((), ())),
-                preferred_element_type=F32,
-            )
-            sums[at] = term if part == 0 else sums[at] + term
-    far[...] = sums[0].astype(BF16)
-    near[...] = sums[1]
-
-
-def gated_grad(col, grads, weight, after):
-    blocks, rows, width = grads.shape
+        out[...] = total.astype(out.dtype)
+
+
+def gated_grad(place, weight, grads, after):
+    rows, width = grads[0].shape
     channels = weight.shape[0]
     half = channels // 2
-    parts = min(2, blocks)
     return call(
         gated_grad_kernel,
         "gated_grad",
-        2 * rows * channels * blocks * width,
-        2 * blocks * width * (rows + channels) + 6 * rows * half,
-        vmem=STREAM_BYTES,
-        in_specs=[SCALAR, IN_HBM, IN_HBM, UNREAD],
+        2 * rows * channels * BLOCKS * width,
+        2 * BLOCKS * width * (rows + channels) + 6 * rows * half,
+        in_specs=[SCALAR] + [IN_VMEM] * (1 + len(grads)) + [UNREAD],
         out_specs=[IN_VMEM] * 2,
         out_shape=[
             jax.ShapeDtypeStruct((rows, half), BF16),
             jax.ShapeDtypeStruct((rows, half), F32),
         ],
-        scratch_shapes=[
-            pltpu.VMEM(grads.shape, BF16),
-            pltpu.VMEM((parts, channels, blocks // parts * width), BF16),
-            pltpu.SemaphoreType.DMA((blocks,)),
-            pltpu.SemaphoreType.DMA((parts,)),
-        ],
-    )(col, grads, weight, after)
-
-
-def kept_weight_kernel(gated, grads, arrived, out, done, held, sems):
+    )(place, weight, *grads, after)
+
+
+def kept_weight_kernel(x, gated, *refs):
+    *grads, arrived, own, right, middle, left, done, held = refs
     done[...] = jnp.zeros_like(done)
-    blocks, parts, size, _ = held.shape
-    copies = []
-    for b in range(blocks):
-        total = jnp.dot(gated[...], grads[b], preferred_element_type=F32)
-        total = (total + arrived[b].astype(F32)).astype(BF16)
-        for part in range(parts):
-            held[b, part] = total[part * size : (part + 1) * size]
-        copies.append(pltpu.make_async_copy(held.at[b], out.at[:, b], sems.at[b]))
-        copies[-1].start()
-    for copy in copies:
-        copy.wait()
-
-
-def kept_weight(parts, gated, grads, arrived):
+    size = own.shape[1]
+    parts = held.shape[0] // size
+    for b, block in enumerate(blocks_of(grads)):
+        held[...] = times_block(gated, block) + arrived[b].astype(F32)
+        for step, out in enumerate((own, right, middle, left)):
+            at = lax.rem(x[0] + step, parts) * size
+            out[b] = held[pl.ds(pl.multiple_of(at, size), size), :].astype(out.dtype)
+
+
+def kept_weight(x, parts, gated, grads, arrived):
     channels, rows = gated.shape
-    blocks, _, width = grads.shape
-    size = channels // parts
+    blocks, width = BLOCKS, grads[0].shape[1]
+    shape = (blocks, channels // parts, width)
     return call(
         kept_weight_kernel,
         "kept_weight",
         2 * rows * channels * blocks * width,
         2 * blocks * width * (rows + 2 * channels) + 2 * rows * channels,
-        in_specs=[IN_VMEM] * 3,
-        out_specs=[IN_HBM, IN_VMEM],
-        out_shape=[jax.ShapeDtypeStruct((parts, blocks, size, width), BF16), TOKEN],
-        scratch_shapes=[
-            pltpu.VMEM((blocks, parts, size, width), BF16),
-            pltpu.SemaphoreType.DMA((blocks,)),
-        ],
-    )(gated, grads, arrived)
+        in_specs=[SCALAR] + [IN_VMEM] * (2 + len(grads)),
+        out_specs=[IN_VMEM] * (parts + 1),
+        out_shape=[jax.ShapeDtypeStruct(shape, F32)]
+        + [jax.ShapeDtypeStruct(shape, BF16)] * (parts - 1)
+        + [TOKEN],
+        scratch_shapes=[pltpu.VMEM((channels, width), F32)],
+    )(x, gated, *grads, arrived)
 
 
 def two_roundings(sums):
@@ -363,88 +340,73 @@
     return both[:, :8] + both[:, 8:]
 
 
-def first_half_kernel(z, pair, taps, head, out, kept, out_taps, out_head):
-    blocks, rows, _ = pair.shape
-    size = rows // 4
-    total = taps[0]
+def middle_kernel(z, own, *refs):
+    *arrived, taps, head, out, kept, out_taps, out_head = refs
+    parts, _, size, _ = out.shape
+    blocks = own.shape[0]
+    total = own[...]
+    for piece in arrived:
+        total = total + piece[...].astype(F32)
+    sums = taps[0]
     for copy in range(1, taps.shape[0]):
-        total = total + taps[copy]
-    out_taps[...] = total
+        sums = sums + taps[copy]
+    out_taps[...] = sums
     out_head[...] = head[...]
-    low = lax.rem(z[0], 2)
-    for high in range(2):
-        own, other = (
-            pl.ds(pl.multiple_of((2 * high + bit) * size, size), size) for bit in (low, 1 - low)
-        )
-        out[high * blocks : (high + 1) * blocks] = pair[:, other, :]
-        kept[high] = pair[:, own, :].astype(F32)
-    out[2 * blocks :] = two_roundings(total)
-
-
-def second_half_kernel(z, kept, taps, arrived, out, out_kept, out_taps):
-    _, blocks, _, _ = kept.shape
-    total = taps[...] + rejoined(arrived[2 * blocks :])
-    out_taps[...] = total
-    high = lax.div(z[0], 2)
-    own, other = (
-        kept[bit] + arrived[pl.ds(bit * blocks, blocks)].astype(F32) for bit in (high, 1 - high)
-    )
-    out_kept[...] = own
-    out[0:blocks] = other.astype(BF16)
-    out[blocks:] = two_roundings(total)
+    both = two_roundings(sums)
+    for part in range(parts):
+        piece = total[:, part * size : (part + 1) * size, :]
+        out[part, 0:blocks] = piece.astype(BF16)
+        out[part, blocks:] = both
+
+        @pl.when(z[0] == part)
+        def _(piece=piece):
+            kept[...] = piece
 
 
 def last_kernel(
-    scale, kept, taps, arrived, tail, head, _, out, out_feat, out_inner, out_grads
+    scale, place, kept, taps, arrived, tail, head, _, out, out_feat, out_inner, out_grads
 ):
+    parts = arrived.shape[0]
     blocks, _, width = kept.shape
+    row, z = place[0], place[1]
     out_grads[...] = (tail[...] + head[...]).astype(BF16)
     for b in range(blocks):
-        total = kept[b] + arrived[b].astype(F32)
-        out[:, b * width : (b + 1) * width] = (total * scale).astype(BF16)
-    total = (taps[...] + rejoined(arrived[blocks:])) * scale
+        total = kept[b]
+        for part in range(parts):
+            total = total + jnp.where(z == part, 0.0, arrived[part, b].astype(F32))
+        at = pl.multiple_of(lax.rem(row + b, blocks) * width, width)
+        out[:, pl.ds(at, width)] = (total * scale).astype(BF16)
+    total = taps[...]
+    for part in range(parts):
+        total = total + jnp.where(z == part, 0.0, rejoined(arrived[part, blocks:]))
+    total = total * scale
     out_feat[...] = total[:3, :TAPS]
     out_inner[...] = total[3, :TAPS]
 
 
-def small_call(kernel, name, args, outs, scalars=0, **kwargs):
-    moved = sum(v.size * v.dtype.itemsize for v in (*args, *outs))
-    return call(
-        kernel,
-        name,
-        moved,
-        moved,
-        grid=(1,),
-        in_specs=[SCALAR] * scalars + [whole(v.shape) for v in args[scalars:]],
-        out_specs=[whole(v.shape) for v in outs],
-        out_shape=outs,
-        **kwargs,
-    )(*args)
-
-
-def first_half(z, pair, taps, head):
-    blocks, rows, width = pair.shape
-    tile = (rows // 4, width)
+def middle(z, parts, own, arrived, taps, head):
+    blocks, rows, width = own.shape
+    tile = (rows // parts, width)
+    args = (z, own, *arrived, taps, head)
     outs = [
-        jax.ShapeDtypeStruct((2 * blocks + taps.shape[1], *tile), BF16),
-        jax.ShapeDtypeStruct((2, blocks, *tile), F32),
+        jax.ShapeDtypeStruct((parts, blocks + taps.shape[1], *tile), BF16),
+        jax.ShapeDtypeStruct((blocks, *tile), F32),
         jax.ShapeDtypeStruct(taps.shape[1:], F32),
         jax.ShapeDtypeStruct(head.shape, F32),
     ]
-    return small_call(first_half_kernel, "first_half", (z, pair, taps, head), outs, scalars=1)
-
-
-def second_half(z, kept, taps, arrived):
-    _, blocks, *tile = kept.shape
-    outs = [
-        jax.ShapeDtypeStruct((blocks + taps.shape[0], *tile), BF16),
-        jax.ShapeDtypeStruct((blocks, *tile), F32),
-        jax.ShapeDtypeStruct(taps.shape, F32),
-    ]
-    return small_call(second_half_kernel, "second_half", (z, kept, taps, arrived), outs, scalars=1)
-
-
-def last(scale, kept, taps, arrived, tail, head, grads):
+    moved = 10 * own.size
+    return call(
+        middle_kernel,
+        "middle",
+        moved,
+        moved,
+        in_specs=[SCALAR] + [IN_VMEM] * (len(args) - 1),
+        out_specs=[IN_VMEM] * len(outs),
+        out_shape=outs,
+    )(*args)
+
+
+def last(scale, place, kept, taps, arrived, tail, head, grads):
     blocks, channels, width = kept.shape
     final = grads.shape[1] // HALO - 1
     args = (kept, taps, arrived, tail, head)
@@ -459,12 +421,12 @@
         2 * arrived.size,
         2 * arrived.size,
         grid=(1,),
-        in_specs=[whole(v.shape) for v in args] + [UNREAD],
+        in_specs=[SCALAR] + [whole(v.shape) for v in args] + [UNREAD],
         out_specs=[whole(v.shape) for v in shapes]
         + [pl.BlockSpec(tail.shape, lambda i: (0, final, 0))],
         out_shape=shapes + [jax.ShapeDtypeStruct(grads.shape, grads.dtype)],
-        input_output_aliases={5: 3},
-    )(*args, grads)
+        input_output_aliases={6: 3},
+    )(place, *args, grads)
 
 
 def ctx_permute(value, target):
@@ -485,19 +447,59 @@
     )
 
 
+def turned(value, axis, steps):
+    count = lax.axis_size(axis)
+    return lax.ppermute(value, axis, [(i, (i + steps) % count) for i in range(count)])
+
+
+def halves_kernel(rights, lefts, _, low, high):
+    rows = low.shape[0]
+    low[...] = rights[1, :rows, :]
+    high[...] = lefts[1, rows:, :]
+
+
+def halves(rights, lefts, after):
+    _, rows, width = rights.shape
+    half = jax.ShapeDtypeStruct((rows // 2, width), rights.dtype)
+    return call(
+        halves_kernel,
+        "halves",
+        rows * width,
+        4 * rows * width,
+        in_specs=[IN_VMEM] * 2 + [UNREAD],
+        out_specs=[IN_VMEM] * 2,
+        out_shape=[half] * 2,
+    )(rights, lefts, after)
+
+
+def two_steps(own):
+    right, left = turned(own, "row", -1), turned(own, "row", 1)
+    rights = turned(jnp.stack([own, right]), "row", -2)
+    lefts = turned(jnp.stack([own, left]), "row", 2)
+    return own, right, left, rights, lefts
+
+
+def third_step(blocks, after):
+    low, high = halves(*blocks[3:], after)
+    return *blocks, turned(low, "row", -1), turned(high, "row", 1)
+
+
 def body(featured, feat_taps, inner_taps, out_weight, out_grad):
     rows = featured.shape[0]
     nx, nz, nc = (lax.axis_size(a) for a in CTX)
     inv_root = 1.0 / math.sqrt(rows * nx * nz * nc)
     core = lax.axis_index("core")
-    col, z = (jnp.full((1,), lax.axis_index(a), jnp.int32) for a in ("col", "zl"))
-
-    grads = lax.all_gather(out_grad, "row", axis=0)
+    row, col, x, z = (
+        jnp.full((1,), lax.axis_index(a), jnp.int32) for a in ("row", "col", "x", "zl")
+    )
+
+    grads = two_steps(out_grad)
 
     own = jnp.transpose(featured, (1, 0, 2))
     before = ctx_shift(own[:, rows - HALO :], 1)
     gated = forward(before, own, feat_taps, inner_taps)
     both = lax.all_gather(gated, "col", axis=1, tiled=True)
+    grads = third_step(grads, both)
     channels = both.shape[1]
     split = both.T.reshape(nx * nz, nc, channels // (nx * nz * nc), rows)
     kept, sent = (
@@ -507,23 +509,21 @@
 
     sent, done = sent_weight(sent, grads)
     arrived = ctx_permute(sent, lambda x, z, c: (x, z, 1 - c))
-    far, near = gated_grad(col, grads, out_weight, done)
-    pair, done = kept_weight(nx, kept, grads, arrived)
+    own_x, *pieces, done = kept_weight(x, nx, kept, grads, arrived)
+    arrived = [turned(piece, "x", step) for step, piece in enumerate(pieces, 1)]
+    far, near = gated_grad(jnp.concatenate([row, col]), out_weight, grads, done)
     far = lax.all_gather(far, "col", axis=0)
-    summed = lax.psum_scatter(pair, "x", scatter_dimension=0)
 
     grad_own, head, tail, taps = backward(
         nx * nc, col, near, far, before, own, feat_taps, inner_taps, done
     )
     taps = lax.all_to_all(taps, ("x", "core"), split_axis=0, concat_axis=0)
 
-    piece, part, taps, head = first_half(z, summed, taps, head)
-    arrived = ctx_permute(piece, lambda x, z, c: (x, z ^ 1, c))
+    pieces, kept, taps, head = middle(z, nz, own_x, arrived, taps, head)
+    pieces = lax.all_to_all(pieces, "zl", split_axis=0, concat_axis=0)
     head = ctx_shift(head, -1)
-    piece, part, taps = second_half(z, part, taps, arrived)
-    arrived = ctx_permute(piece, lambda x, z, c: (x, z ^ 2, c))
     grad_weight, grad_feat_taps, grad_inner_taps, grad_own = last(
-        inv_root, part, taps, arrived, tail, head, grad_own
+        inv_root, jnp.concatenate([row, z]), kept, taps, pieces, tail, head, grad_own
     )
     return jnp.transpose(grad_own, (1, 0, 2)), grad_weight, grad_feat_taps, grad_inner_taps
 

time: 138 us -> 141 us (1.022)
  starting transfers between devices: 32.6 us -> 59.7 us
  waiting for transfers between devices: 39.7 us -> 26.2 us
  between operations: 14.2 us -> 0.86 us
  blocking collectives: 26.7 us -> 31.3 us
  local copies, waits for them, and re-layouts: 6.29 us -> 4.29 us
    ppermute x0 -> x9, starting transfers between devices: none -> 32.4 us  [turned(): lax.ppermute(value, axis, [(i, (i + steps) % count) for i in range(count)])]
    all_gather x1 -> x0, waiting for transfers between devices: 20.8 us -> none  [body(): grads = lax.all_gather(out_grad, 'row', axis=0)]
    ppermute x3 -> x1, starting transfers between devices: 17.3 us -> 1.91 us  [ctx_permute(): return lax.ppermute(value, CTX, pairs)]
    ppermute x0 -> x9, waiting for transfers between devices: none -> 9.35 us  [turned(): lax.ppermute(value, axis, [(i, (i + steps) % count) for i in range(count)])]
    all_to_all x0 -> x1, starting transfers between devices: none -> 8.61 us  [body(): pieces = lax.all_to_all(pieces, 'zl', split_axis=0, concat_axis=0)]
    all_gather x1, blocking collectives: 12.3 us -> 19.1 us  [body(): both = lax.all_gather(gated, 'col', axis=1, tiled=True)]
    pallas_call x1, Pallas kernels: 5.4 us -> 1.69 us  [sent_weight(): call(sent_weight_kernel, 'sent_weight', 2 * rows * channels * blocks * wi...]
    unnamed x18, local copies, waits for them, and re-layouts: 4.58 us -> 1.47 us
  transfers between devices with their start and end apart: 8 -> 14, of which waited for: 6 -> 8; matrix products, arithmetic and copies ran while one was open for 1% -> 2% of each run, Pallas kernels for 7% -> 5%
where the time goes in v6:
time: 141 us; the launch traced here: 140 us
  starting transfers between devices  59.7 us (42%)
  blocking collectives  31.3 us (22%)
  waiting for transfers between devices  26.2 us (19%)
  Pallas kernels  16.1 us (11%)
  local copies, waits for them, and re-layouts  4.29 us (3%)
    ppermute x9, starting transfers between devices, turned(): lax.ppermute(value, axis, [(i, (i + steps) % count) for i in range(count)])  32.4 us
    all_gather x1, blocking collectives, body(): both = lax.all_gather(gated, 'col', axis=1, tiled=True)  19.1 us
    all_gather x1, blocking collectives, body(): far = lax.all_gather(far, 'col', axis=0)  12.3 us
    ppermute x2, starting transfers between devices, ctx_shift(): lax.ppermute(value, CTX, [(i, i + steps) for i in range(count) if 0 <= i...  11.1 us
    ppermute x9, waiting for transfers between devices, turned(): lax.ppermute(value, axis, [(i, (i + steps) % count) for i in range(count)])  9.35 us
    all_to_all x1, starting transfers between devices, body(): pieces = lax.all_to_all(pieces, 'zl', split_axis=0, concat_axis=0)  8.61 us
    all_to_all x1, waiting for transfers between devices, body(): taps = lax.all_to_all(taps, ('x', 'core'), split_axis=0, concat_axis=0)  6.52 us
    ppermute x2, waiting for transfers between devices, ctx_shift(): lax.ppermute(value, CTX, [(i, i + steps) for i in range(count) if 0 <= i...  6.33 us
  transfers between devices with their start and end apart: 14, of which 8 were waited for; matrix products, arithmetic and copies ran while one was open for 2% of the time, Pallas kernels for 5%

profile of v6, /device:TPU:1, one launch (start us, length us, event | category | flops | bytes accessed | tf_op | source)
XLA Modules:
  0.0 139.7 jit_solution(4397004147769733324)
XLA Ops:
  0.6 6.1 %collective-permute-start.1 = (bf16[512,256]{1,0:T(8,128)(2,1)}, bf16[512,256]{1,0:T(8,128)(2,1)S(1)}, u32[]{:S(2)}, u32[]{:S(2)}) collective-permute-start(bf16[512,256]{1,0:T(8,128)(2,1)} %refs_0_.5), channel_id=1, source_target_pairs={{0,448},{64,0},{128,64},{192,128},{256,192},{320,256},{384,320},{4... | collective-permute-start | bytes 786440 | tf_op jit(solution)/shard_map/ppermute | solution.py:452
  6.7 1.9 %collective-permute-start.2 = (bf16[512,256]{1,0:T(8,128)(2,1)}, bf16[512,256]{1,0:T(8,128)(2,1)S(1)}, u32[]{:S(2)}, u32[]{:S(2)}) collective-permute-start(bf16[512,256]{1,0:T(8,128)(2,1)} %refs_0_.5), channel_id=1, source_target_pairs={{0,64},{64,128},{128,192},{192,256},{256,320},{320,384},{384,448},... | collective-permute-start | bytes 786440 | tf_op jit(solution)/shard_map/ppermute | solution.py:452
  8.6 1.7 %collective-permute-done.1.refs_1_ = bf16[512,256]{1,0:T(8,128)(2,1)S(1)} collective-permute-done((bf16[512,256]{1,0:T(8,128)(2,1)}, bf16[512,256]{1,0:T(8,128)(2,1)S(1)}, u32[]{:S(2)}, u32[]{:S(2)}) %collective-permute-start.1) | collective-permute-done | bytes 262176 | tf_op jit(solution)/shard_map/ppermute | solution.py:452
  10.3 4.9 %collective-permute-done.2.refs_2_ = bf16[512,256]{1,0:T(8,128)(2,1)S(1)} collective-permute-done((bf16[512,256]{1,0:T(8,128)(2,1)}, bf16[512,256]{1,0:T(8,128)(2,1)S(1)}, u32[]{:S(2)}, u32[]{:S(2)}) %collective-permute-start.2) | collective-permute-done | bytes 262176 | tf_op jit(solution)/shard_map/ppermute | solution.py:452
  15.2 1.0 pad_maximum_fusion
  16.3 4.2 %collective-permute-start.3 = (bf16[2,512,256]{2,1,0:T(8,128)(2,1)S(1)}, bf16[2,512,256]{2,1,0:T(8,128)(2,1)S(1)}, u32[]{:S(2)}, u32[]{:S(2)}) collective-permute-start(bf16[2,512,256]{2,1,0:T(8,128)(2,1)S(1)} %get-tuple-element.51), channel_id=1, source_target_pairs={{0,384},{64,448},{128,0},{192,64},{256,128},{320,192},{384,256},{4... | collective-permute-start | bytes 1572872 | tf_op jit(solution)/shard_map/ppermute | solution.py:452
  20.5 2.0 %collective-permute-start.4 = (bf16[2,512,256]{2,1,0:T(8,128)(2,1)S(1)}, bf16[2,512,256]{2,1,0:T(8,128)(2,1)S(1)}, u32[]{:S(2)}, u32[]{:S(2)}) collective-permute-start(bf16[2,512,256]{2,1,0:T(8,128)(2,1)S(1)} %get-tuple-element.50), channel_id=1, source_target_pairs={{0,128},{64,192},{128,256},{192,320},{256,384},{320,448},{384,0},{... | collective-permute-start | bytes 1572872 | tf_op jit(solution)/shard_map/ppermute | solution.py:452
  23.2 7.9 %collective-permute-start = (bf16[3,16,256]{2,1,0:T(8,128)(2,1)S(1)}, bf16[3,16,256]{2,1,0:T(8,128)(2,1)S(1)}, u32[]{:S(2)}, u32[]{:S(2)}) collective-permute-start(bf16[3,16,256]{2,1,0:T(8,128)(2,1)S(1)} %slice.4), channel_id=1, source_target_pairs={{0,1},{1,2},{2,3},{3,4},{4,5},{5,6},{6,7},{7,8},{8,9},{9,10},{10,1... | collective-permute-start | bytes 73736 | tf_op jit(solution)/shard_map/ppermute | solution.py:445
  33.5 1.3 forward.1
  34.8 19.1 %all_gather.9._ = bf16[512,512]{1,0:T(8,128)(2,1)S(1)} all-gather(bf16[512,256]{1,0:T(8,128)(2,1)S(1)} %forward.1), channel_id=1, replica_groups=mesh['row'=8,'col'=2,'x'=4,'zl'=4,'core'=2] {'col'}, dimensions={1}, use_global_device_ids=true | all-gather | bytes 786432 | tf_op jit(solution)/shard_map/all_gather | solution.py:501
  54.6 3.0 %collective-permute-start.5 = (bf16[256,256]{1,0:T(8,128)(2,1)}, bf16[256,256]{1,0:T(8,128)(2,1)S(1)}, u32[]{:S(2)}, u32[]{:S(2)}) collective-permute-start(bf16[256,256]{1,0:T(8,128)(2,1)} %get-tuple-element.26), channel_id=1, source_target_pairs={{0,448},{64,0},{128,64},{192,128},{256,192},{320,256},{384,320},{4... | collective-permute-start | bytes 393224 | tf_op jit(solution)/shard_map/ppermute | solution.py:452
  57.6 2.3 %collective-permute-start.6 = (bf16[256,256]{1,0:T(8,128)(2,1)}, bf16[256,256]{1,0:T(8,128)(2,1)S(1)}, u32[]{:S(2)}, u32[]{:S(2)}) collective-permute-start(bf16[256,256]{1,0:T(8,128)(2,1)} %get-tuple-element.27), channel_id=1, source_target_pairs={{0,64},{64,128},{128,192},{192,256},{256,320},{320,384},{384,448},... | collective-permute-start | bytes 393224 | tf_op jit(solution)/shard_map/ppermute | solution.py:452
  60.9 1.1 constant_dynamic-slice_fusion
  62.0 2.7 %collective-permute-done.6.refs_6_ = bf16[256,256]{1,0:T(8,128)(2,1)S(1)} collective-permute-done((bf16[256,256]{1,0:T(8,128)(2,1)}, bf16[256,256]{1,0:T(8,128)(2,1)S(1)}, u32[]{:S(2)}, u32[]{:S(2)}) %collective-permute-start.6) | collective-permute-done | bytes 131104 | tf_op jit(solution)/shard_map/ppermute | solution.py:452
  64.7 1.7 %sent_weight.1 = (bf16[8,256,256]{2,1,0:T(8,128)(2,1)}, f32[8,128]{1,0:T(8,128)}) custom-call(bf16[256,512]{1,0:T(8,128)(2,1)S(1)} %bitcast.23, bf16[512,256]{1,0:T(8,128)(2,1)S(1)} %copy-done, bf16[512,256]{1,0:T(8,128)(2,1)S(1)} %collective-permute-done.1.refs_1_, bf16[512,256]{1,0:T(8,128)(2,1)S(1)} %collective-permute-done.2.refs_2_, ...), custom_call_target="tpu_custom_call" | custom-call | flops 536870912 | bytes 3407872 | tf_op jit(solution)/shard_map/sent_weight/pallas_call | solution.py:246
  66.4 1.9 %collective-permute-start.7 = (bf16[8,256,256]{2,1,0:T(8,128)(2,1)}, bf16[8,256,256]{2,1,0:T(8,128)(2,1)}, u32[]{:S(2)}, u32[]{:S(2)}) collective-permute-start(bf16[8,256,256]{2,1,0:T(8,128)(2,1)} %get-tuple-element.28), channel_id=1, source_target_pairs={{0,1},{1,0},{2,3},{3,2},{4,5},{5,4},{6,7},{7,6},{8,9},{9,8},{10,11... | collective-permute-start | bytes 3145736 | tf_op jit(solution)/shard_map/ppermute | solution.py:440
  68.4 2.9 %collective-permute-done.7.refs_7_ = bf16[8,256,256]{2,1,0:T(8,128)(2,1)} collective-permute-done((bf16[8,256,256]{2,1,0:T(8,128)(2,1)}, bf16[8,256,256]{2,1,0:T(8,128)(2,1)}, u32[]{:S(2)}, u32[]{:S(2)}) %collective-permute-start.7) | collective-permute-done | bytes 1048608 | tf_op jit(solution)/shard_map/ppermute | solution.py:440
  71.3 3.2 %kept_weight.1 = (f32[8,64,256]{2,1,0:T(8,128)S(1)}, bf16[8,64,256]{2,1,0:T(8,128)(2,1)}, bf16[8,64,256]{2,1,0:T(8,128)(2,1)}, bf16[8,64,256]{2,1,0:T(8,128)(2,1)}, f32[8,128]{1,0:T(8,128)S(1)}) custom-call(s32[1]{0:T(128)} %bitcast.2.x, bf16[256,512]{1,0:T(8,128)(2,1)S(1)} %bitcast.22, bf16[512,256]{1,0:T(8,128)(2,1)S(1)} %copy-done, ...), custom_call_target="tpu_custom_call" | custom-call | flops 536870912 | bytes 4456448 | tf_op jit(solution)/shard_map/kept_weight/pallas_call | solution.py:319
  74.5 7.4 %collective-permute-start.10 = (bf16[8,64,256]{2,1,0:T(8,128)(2,1)}, bf16[8,64,256]{2,1,0:T(8,128)(2,1)S(1)}, u32[]{:S(2)}, u32[]{:S(2)}) collective-permute-start(bf16[8,64,256]{2,1,0:T(8,128)(2,1)} %get-tuple-element.32), channel_id=1, source_target_pairs={{0,24},{8,0},{16,8},{24,16},{1,25},{9,1},{17,9},{25,17},{2,26},{10... | collective-permute-start | bytes 786440 | tf_op jit(solution)/shard_map/ppermute | solution.py:452
  81.8 1.9 %collective-permute-start.8 = (bf16[8,64,256]{2,1,0:T(8,128)(2,1)}, bf16[8,64,256]{2,1,0:T(8,128)(2,1)}, u32[]{:S(2)}, u32[]{:S(2)}) collective-permute-start(bf16[8,64,256]{2,1,0:T(8,128)(2,1)} %get-tuple-element.30), channel_id=1, source_target_pairs={{0,8},{8,16},{16,24},{24,0},{1,9},{9,17},{17,25},{25,1},{2,10},{10... | collective-permute-start | bytes 786440 | tf_op jit(solution)/shard_map/ppermute | solution.py:452
  83.8 3.6 %collective-permute-start.9 = (bf16[8,64,256]{2,1,0:T(8,128)(2,1)}, bf16[8,64,256]{2,1,0:T(8,128)(2,1)}, u32[]{:S(2)}, u32[]{:S(2)}) collective-permute-start(bf16[8,64,256]{2,1,0:T(8,128)(2,1)} %get-tuple-element.31), channel_id=1, source_target_pairs={{0,16},{8,24},{16,0},{24,8},{1,17},{9,25},{17,1},{25,9},{2,18},{10... | collective-permute-start | bytes 786440 | tf_op jit(solution)/shard_map/ppermute | solution.py:452
  87.4 1.8 %gated_grad.1 = (bf16[512,256]{1,0:T(8,128)(2,1)S(1)}, f32[512,256]{1,0:T(8,128)S(1)}) custom-call(s32[2]{0:T(128)S(1)} %pad_add_fusion.1.place, bf16[512,2048]{1,0:T(8,128)(2,1)S(1)} %copy-done.2, bf16[512,256]{1,0:T(8,128)(2,1)S(1)} %copy-done, bf16[512,256]{1,0:T(8,128)(2,1)S(1)} %collective-permute-done.1.refs_1_, ...), custom_call_target="tpu_custom_call" | custom-call | flops 1073741824 | bytes 4980736 | tf_op jit(solution)/shard_map/gated_grad/pallas_call | solution.py:289
  89.3 12.3 %all-gather = bf16[1024,256]{1,0:T(8,128)(2,1)S(1)} all-gather(bf16[512,256]{1,0:T(8,128)(2,1)S(1)} %get-tuple-element.35), channel_id=2, replica_groups=mesh['row'=8,'col'=2,'x'=4,'zl'=4,'core'=2] {'col'}, dimensions={0}, use_global_device_ids=true | all-gather | bytes 786432 | tf_op jit(solution)/shard_map/all_gather | solution.py:515
  101.6 4.2 %backward.1 = (bf16[3,512,256]{2,1,0:T(8,128)(2,1)}, f32[3,16,256]{2,1,0:T(8,128)S(1)}, f32[3,16,256]{2,1,0:T(8,128)S(1)}, f32[8,4,8,256]{3,2,1,0:T(8,128)}) custom-call(s32[1]{0:T(128)} %bitcast.11.col, f32[512,256]{1,0:T(8,128)S(1)} %get-tuple-element.34.near, bf16[2,512,256]{2,1,0:T(8,128)(2,1)S(1)} %bitcast.21, ...), custom_call_target="tpu_custom_call" | custom-call | flops 20971520 | bytes 2621440 | tf_op jit(solution)/shard_map/backward/pallas_call | solution.py:187
  105.8 5.7 %all-to-all-start = ((f32[8,4,8,256]{3,2,1,0:T(8,128)}), f32[8,4,8,256]{3,2,1,0:T(8,128)S(1)}, u32[]{:S(2)}, u32[]{:S(2)}) async-start(f32[8,4,8,256]{3,2,1,0:T(8,128)} %get-tuple-element.36), calls=%async_computation | async-start | bytes 524288 | tf_op jit(solution)/shard_map/all_to_all | solution.py:520
  111.4 6.5 %all-to-all-done.refs_3_ = f32[8,4,8,256]{3,2,1,0:T(8,128)S(1)} async-done(((f32[8,4,8,256]{3,2,1,0:T(8,128)}), f32[8,4,8,256]{3,2,1,0:T(8,128)S(1)}, u32[]{:S(2)}, u32[]{:S(2)}) %all-to-all-start) | async-done | bytes 262176 | tf_op jit(solution)/shard_map/all_to_all | solution.py:520
  118.0 2.0 %middle.1 = (bf16[4,12,16,256]{3,2,1,0:T(8,128)(2,1)}, f32[8,16,256]{2,1,0:T(8,128)S(1)}, f32[4,8,256]{2,1,0:T(8,128)S(1)}, f32[3,16,256]{2,1,0:T(8,128)S(1)}) custom-call(s32[1]{0:T(128)} %bitcast.1.z, f32[8,64,256]{2,1,0:T(8,128)S(1)} %copy-done.4, bf16[8,64,256]{2,1,0:T(8,128)(2,1)} %collective-permute-done.8.refs_0_, ...), custom_call_target="tpu_custom_call" | custom-call | flops 1310720 | bytes 1310720 | tf_op jit(solution)/shard_map/middle/pallas_call | solution.py:398
  120.0 8.6 %all-to-all-start.1 = ((bf16[4,12,16,256]{3,2,1,0:T(8,128)(2,1)}), bf16[4,12,16,256]{3,2,1,0:T(8,128)(2,1)S(1)}, u32[]{:S(2)}, u32[]{:S(2)}) async-start(bf16[4,12,16,256]{3,2,1,0:T(8,128)(2,1)} %get-tuple-element.40), calls=%async_computation.1 | async-start | bytes 786432 | tf_op jit(solution)/shard_map/all_to_all | solution.py:523
  128.6 3.2 %collective-permute-start.11 = (f32[3,16,256]{2,1,0:T(8,128)S(1)}, f32[3,16,256]{2,1,0:T(8,128)S(1)}, u32[]{:S(2)}, u32[]{:S(2)}) collective-permute-start(f32[3,16,256]{2,1,0:T(8,128)S(1)} %get-tuple-element.42), channel_id=1, source_target_pairs={{1,0},{2,1},{3,2},{4,3},{5,4},{6,5},{7,6},{8,7},{9,8},{10,9},{11,1... | collective-permute-start | bytes 147464 | tf_op jit(solution)/shard_map/ppermute | solution.py:445
  131.9 5.4 %collective-permute-done.11.refs_5_ = f32[3,16,256]{2,1,0:T(8,128)S(1)} collective-permute-done((f32[3,16,256]{2,1,0:T(8,128)S(1)}, f32[3,16,256]{2,1,0:T(8,128)S(1)}, u32[]{:S(2)}, u32[]{:S(2)}) %collective-permute-start.11) | collective-permute-done | bytes 49184 | tf_op jit(solution)/shard_map/ppermute | solution.py:445
  137.3 1.1 all-to-all-done.1.refs_3_
  138.4 1.3 last.1
  (30 shorter events, 5.0 us)
Async XLA Ops:
  0.6 31.5 %copy-start.1 = (bf16[512,3,256]{2,0,1:T(8,128)(2,1)S(1)}, bf16[512,3,256]{2,0,1:T(8,128)(2,1)}, u32[]{:S(2)}) copy-start(bf16[512,3,256]{2,0,1:T(8,128)(2,1)} %param.5) | copy-start | bytes 2359300
  0.6 9.7 %collective-permute-start.1 = (bf16[512,256]{1,0:T(8,128)(2,1)}, bf16[512,256]{1,0:T(8,128)(2,1)S(1)}, u32[]{:S(2)}, u32[]{:S(2)}) collective-permute-start(bf16[512,256]{1,0:T(8,128)(2,1)} %refs_0_.5), channel_id=1, source_target_pairs={{0,448},{64,0},{128,64},{192,128},{256,192},{320,256},{384,320},{4... | collective-permute-start | bytes 786440 | tf_op jit(solution)/shard_map/ppermute | solution.py:452
  6.7 8.5 %collective-permute-start.2 = (bf16[512,256]{1,0:T(8,128)(2,1)}, bf16[512,256]{1,0:T(8,128)(2,1)S(1)}, u32[]{:S(2)}, u32[]{:S(2)}) collective-permute-start(bf16[512,256]{1,0:T(8,128)(2,1)} %refs_0_.5), channel_id=1, source_target_pairs={{0,64},{64,128},{128,192},{192,256},{256,320},{320,384},{384,448},... | collective-permute-start | bytes 786440 | tf_op jit(solution)/shard_map/ppermute | solution.py:452
  16.3 37.6 %collective-permute-start.3 = (bf16[2,512,256]{2,1,0:T(8,128)(2,1)S(1)}, bf16[2,512,256]{2,1,0:T(8,128)(2,1)S(1)}, u32[]{:S(2)}, u32[]{:S(2)}) collective-permute-start(bf16[2,512,256]{2,1,0:T(8,128)(2,1)S(1)} %get-tuple-element.51), channel_id=1, source_target_pairs={{0,384},{64,448},{128,0},{192,64},{256,128},{320,192},{384,256},{4... | collective-permute-start | bytes 1572872 | tf_op jit(solution)/shard_map/ppermute | solution.py:452
  20.5 33.4 %collective-permute-start.4 = (bf16[2,512,256]{2,1,0:T(8,128)(2,1)S(1)}, bf16[2,512,256]{2,1,0:T(8,128)(2,1)S(1)}, u32[]{:S(2)}, u32[]{:S(2)}) collective-permute-start(bf16[2,512,256]{2,1,0:T(8,128)(2,1)S(1)} %get-tuple-element.50), channel_id=1, source_target_pairs={{0,128},{64,192},{128,256},{192,320},{256,384},{320,448},{384,0},{... | collective-permute-start | bytes 1572872 | tf_op jit(solution)/shard_map/ppermute | solution.py:452
  23.2 8.9 %collective-permute-start = (bf16[3,16,256]{2,1,0:T(8,128)(2,1)S(1)}, bf16[3,16,256]{2,1,0:T(8,128)(2,1)S(1)}, u32[]{:S(2)}, u32[]{:S(2)}) collective-permute-start(bf16[3,16,256]{2,1,0:T(8,128)(2,1)S(1)} %slice.4), channel_id=1, source_target_pairs={{0,1},{1,2},{2,3},{3,4},{4,5},{5,6},{6,7},{7,8},{8,9},{9,10},{10,1... | collective-permute-start | bytes 73736 | tf_op jit(solution)/shard_map/ppermute | solution.py:445
  32.1 0.7 copy-start.5
  32.8 0.7 copy-start.7
  34.8 29.9 %copy-start = (bf16[512,256]{1,0:T(8,128)(2,1)S(1)}, bf16[512,256]{1,0:T(8,128)(2,1)}, u32[]{:S(2)}) copy-start(bf16[512,256]{1,0:T(8,128)(2,1)} %refs_0_.5) | copy-start | bytes 786436
  54.6 7.4 %collective-permute-start.5 = (bf16[256,256]{1,0:T(8,128)(2,1)}, bf16[256,256]{1,0:T(8,128)(2,1)S(1)}, u32[]{:S(2)}, u32[]{:S(2)}) collective-permute-start(bf16[256,256]{1,0:T(8,128)(2,1)} %get-tuple-element.26), channel_id=1, source_target_pairs={{0,448},{64,0},{128,64},{192,128},{256,192},{320,256},{384,320},{4... | collective-permute-start | bytes 393224 | tf_op jit(solution)/shard_map/ppermute | solution.py:452
  57.6 7.1 %collective-permute-start.6 = (bf16[256,256]{1,0:T(8,128)(2,1)}, bf16[256,256]{1,0:T(8,128)(2,1)S(1)}, u32[]{:S(2)}, u32[]{:S(2)}) collective-permute-start(bf16[256,256]{1,0:T(8,128)(2,1)} %get-tuple-element.27), channel_id=1, source_target_pairs={{0,64},{64,128},{128,192},{192,256},{256,320},{320,384},{384,448},... | collective-permute-start | bytes 393224 | tf_op jit(solution)/shard_map/ppermute | solution.py:452
  66.4 4.9 %collective-permute-start.7 = (bf16[8,256,256]{2,1,0:T(8,128)(2,1)}, bf16[8,256,256]{2,1,0:T(8,128)(2,1)}, u32[]{:S(2)}, u32[]{:S(2)}) collective-permute-start(bf16[8,256,256]{2,1,0:T(8,128)(2,1)} %get-tuple-element.28), channel_id=1, source_target_pairs={{0,1},{1,0},{2,3},{3,2},{4,5},{5,4},{6,7},{7,6},{8,9},{9,8},{10,11... | collective-permute-start | bytes 3145736 | tf_op jit(solution)/shard_map/ppermute | solution.py:440
  68.3 19.1 %copy-start.2 = (bf16[512,2048]{1,0:T(8,128)(2,1)S(1)}, bf16[512,2048]{1,0:T(8,128)(2,1)}, u32[]{:S(2)}) copy-start(bf16[512,2048]{1,0:T(8,128)(2,1)} %weight.1) | copy-start | bytes 6291460
  74.5 14.8 %copy-start.3 = (f32[8,64,256]{2,1,0:T(8,128)}, f32[8,64,256]{2,1,0:T(8,128)S(1)}, u32[]{:S(2)}) copy-start(f32[8,64,256]{2,1,0:T(8,128)S(1)} %get-tuple-element.29.own) | copy-start | bytes 1572868
  74.5 43.5 %collective-permute-start.10 = (bf16[8,64,256]{2,1,0:T(8,128)(2,1)}, bf16[8,64,256]{2,1,0:T(8,128)(2,1)S(1)}, u32[]{:S(2)}, u32[]{:S(2)}) collective-permute-start(bf16[8,64,256]{2,1,0:T(8,128)(2,1)} %get-tuple-element.32), channel_id=1, source_target_pairs={{0,24},{8,0},{16,8},{24,16},{1,25},{9,1},{17,9},{25,17},{2,26},{10... | collective-permute-start | bytes 786440 | tf_op jit(solution)/shard_map/ppermute | solution.py:452
  81.8 36.1 %collective-permute-start.8 = (bf16[8,64,256]{2,1,0:T(8,128)(2,1)}, bf16[8,64,256]{2,1,0:T(8,128)(2,1)}, u32[]{:S(2)}, u32[]{:S(2)}) collective-permute-start(bf16[8,64,256]{2,1,0:T(8,128)(2,1)} %get-tuple-element.30), channel_id=1, source_target_pairs={{0,8},{8,16},{16,24},{24,0},{1,9},{9,17},{17,25},{25,1},{2,10},{10... | collective-permute-start | bytes 786440 | tf_op jit(solution)/shard_map/ppermute | solution.py:452
  83.8 34.2 %collective-permute-start.9 = (bf16[8,64,256]{2,1,0:T(8,128)(2,1)}, bf16[8,64,256]{2,1,0:T(8,128)(2,1)}, u32[]{:S(2)}, u32[]{:S(2)}) collective-permute-start(bf16[8,64,256]{2,1,0:T(8,128)(2,1)} %get-tuple-element.31), channel_id=1, source_target_pairs={{0,16},{8,24},{16,0},{24,8},{1,17},{9,25},{17,1},{25,9},{2,18},{10... | collective-permute-start | bytes 786440 | tf_op jit(solution)/shard_map/ppermute | solution.py:452
  87.4 14.2 %copy-start.6 = (f32[3,7,256]{2,1,0:T(8,128)S(1)}, f32[3,7,256]{2,1,0:T(8,128)}, u32[]{:S(2)}) copy-start(f32[3,7,256]{2,1,0:T(8,128)} %feat_taps.3) | copy-start | bytes 64516
  87.4 14.2 %copy-start.8 = (f32[7,256]{1,0:T(8,128)S(1)}, f32[7,256]{1,0:T(8,128)}, u32[]{:S(2)}) copy-start(f32[7,256]{1,0:T(8,128)} %inner_taps.3) | copy-start | bytes 21508
  89.3 28.7 %copy-start.4 = (f32[8,64,256]{2,1,0:T(8,128)S(1)}, f32[8,64,256]{2,1,0:T(8,128)}, u32[]{:S(2)}) copy-start(f32[8,64,256]{2,1,0:T(8,128)} %copy-done.3) | copy-start | bytes 1572868
  105.8 12.2 %all-to-all-start = ((f32[8,4,8,256]{3,2,1,0:T(8,128)}), f32[8,4,8,256]{3,2,1,0:T(8,128)S(1)}, u32[]{:S(2)}, u32[]{:S(2)}) async-start(f32[8,4,8,256]{3,2,1,0:T(8,128)} %get-tuple-element.36), calls=%async_computation | async-start | bytes 524288 | tf_op jit(solution)/shard_map/all_to_all | solution.py:520
  120.0 18.4 %all-to-all-start.1 = ((bf16[4,12,16,256]{3,2,1,0:T(8,128)(2,1)}), bf16[4,12,16,256]{3,2,1,0:T(8,128)(2,1)S(1)}, u32[]{:S(2)}, u32[]{:S(2)}) async-start(bf16[4,12,16,256]{3,2,1,0:T(8,128)(2,1)} %get-tuple-element.40), calls=%async_computation.1 | async-start | bytes 786432 | tf_op jit(solution)/shard_map/all_to_all | solution.py:523
  128.6 8.7 %collective-permute-start.11 = (f32[3,16,256]{2,1,0:T(8,128)S(1)}, f32[3,16,256]{2,1,0:T(8,128)S(1)}, u32[]{:S(2)}, u32[]{:S(2)}) collective-permute-start(f32[3,16,256]{2,1,0:T(8,128)S(1)} %get-tuple-element.42), channel_id=1, source_target_pairs={{1,0},{2,1},{3,2},{4,3},{5,4},{6,5},{7,6},{8,7},{9,8},{10,9},{11,1... | collective-permute-start | bytes 147464 | tf_op jit(solution)/shard_map/ppermute | solution.py:445

commit v7 on v4

--- a/solution.py
+++ b/solution.py
@@ -17,7 +17,6 @@
 F32 = jnp.float32
 BF16 = jnp.bfloat16
 VMEM_BYTES = 24 << 20
-STREAM_BYTES = 56 << 20
 
 
 def spread(total):
@@ -35,13 +34,14 @@
 SCALAR = pl.BlockSpec(memory_space=pltpu.SMEM)
 UNREAD = pl.BlockSpec(memory_space=pl.ANY)
 IN_HBM = pl.BlockSpec(memory_space=pltpu.HBM)
-
-
-def call(kernel, name, flops, moved, vmem=VMEM_BYTES, **kwargs):
+IN_VMEM = pl.BlockSpec(memory_space=pltpu.VMEM)
+
+
+def call(kernel, name, flops, moved, **kwargs):
     return pl.pallas_call(
         kernel,
         name=name,
-        compiler_params=pltpu.CompilerParams(vmem_limit_bytes=vmem),
+        compiler_params=pltpu.CompilerParams(vmem_limit_bytes=VMEM_BYTES),
         cost_estimate=pl.CostEstimate(flops=flops, bytes_accessed=moved, transcendentals=0),
         **kwargs,
     )
@@ -146,9 +146,10 @@
         return jnp.sum(terms.reshape(terms.shape[0] // 8, 8, LANES), axis=0)
 
     def put(place, sums):
-        for s in range(TAPS):
-            tap_sums[place, s : s + 1, :] = jnp.sum(sums[s], axis=0, keepdims=True)
-        tap_sums[place, TAPS : TAPS + 1, :] = jnp.zeros((1, LANES), F32)
+        rows = [jnp.sum(total, axis=0, keepdims=True) for total in sums]
+        tile = jnp.concatenate([*rows, jnp.zeros((1, LANES), F32)], axis=0)
+        for copy in range(tap_sums.shape[0]):
+            tap_sums[copy, place] = tile
 
     def transposed(j, at, count):
         total = feat_taps[j, 0:1, :] * grad_mixed[j, at : at + count, :]
@@ -179,7 +180,7 @@
     put(3, sums)
 
 
-def backward(col, near, far, before, own, feat_taps, inner_taps, after):
+def backward(copies, col, near, far, before, own, feat_taps, inner_taps, after):
     _, rows, channels = own.shape
     edge = jax.ShapeDtypeStruct((3, HALO, channels), F32)
     return call(
@@ -192,12 +193,14 @@
             SCALAR, lane_spec(rows), lane_spec(2, rows), lane_spec(3, HALO), lane_spec(3, rows),
             lane_spec(3, TAPS), lane_spec(TAPS), UNREAD,
         ],
-        out_specs=[lane_spec(3, rows), lane_spec(3, HALO), lane_spec(3, HALO), lane_spec(4, 8)],
+        out_specs=[
+            lane_spec(3, rows), lane_spec(3, HALO), lane_spec(3, HALO), lane_spec(copies, 4, 8)
+        ],
         out_shape=[
             jax.ShapeDtypeStruct((3, rows, channels), BF16),
             edge,
             edge,
-            jax.ShapeDtypeStruct((4, 8, channels), F32),
+            jax.ShapeDtypeStruct((copies, 4, 8, channels), F32),
         ],
         scratch_shapes=[pltpu.VMEM((3, rows + HALO, LANES), F32)]
         + [pltpu.VMEM((rows + LEAD, LANES), F32)] * 4
@@ -208,78 +211,73 @@
     )(col, near, far, before, own, feat_taps, inner_taps, after)
 
 
-def fetch(source, target, sems):
-    copies = [
-        pltpu.make_async_copy(source.at[i], target.at[i], sems.at[i])
-        for i in range(source.shape[0])
-    ]
-    for copy in copies:
-        copy.start()
-    return copies
-
-
-def products_kernel(
-    col, gated, grads, weight, sent, far, near, held_grads, held_weight, grad_sems, weight_sem
-):
-    copies = fetch(grads, held_grads, grad_sems)
-    weights = pltpu.make_async_copy(weight, held_weight, weight_sem)
-    weights.start()
-    blocks, rows, _ = held_grads.shape
-    half = near.shape[1]
-    for b in range(blocks):
-        copies[b].wait()
-        sent[b] = jnp.dot(gated[...], held_grads[b], preferred_element_type=F32).astype(BF16)
-    weights.wait()
-    step = min(rows, 128)
-    for start in range(0, rows, step):
-        span = slice(start, start + step)
-        wide = jnp.concatenate([held_grads[b, span, :] for b in range(blocks)], axis=1)
-        total = lax.dot_general(
-            wide, held_weight[...], (((1,), (1,)), ((), ())), preferred_element_type=F32
-        )
-        first = col[0] == 0
-        near[span, :] = jnp.where(first, total[:, :half], total[:, half:])
-        far[span, :] = jnp.where(first, total[:, half:], total[:, :half]).astype(BF16)
-
-
-def products(col, gated, grads, weight):
+TOKEN = jax.ShapeDtypeStruct((8, LANES), F32)
+
+
+def sent_weight_kernel(gated, grads, sent, done):
+    done[...] = jnp.zeros_like(done)
+    for b in range(grads.shape[0]):
+        sent[b] = jnp.dot(gated[...], grads[b], preferred_element_type=F32).astype(BF16)
+
+
+def sent_weight(gated, grads):
     channels, rows = gated.shape
     blocks, _, width = grads.shape
-    half = weight.shape[0] // 2
-    return call(
-        products_kernel,
-        "products",
-        2 * rows * (channels + 2 * half) * blocks * width,
-        2 * blocks * width * (rows + channels + 2 * half) + 6 * rows * half,
-        vmem=STREAM_BYTES,
-        in_specs=[SCALAR, pl.BlockSpec(memory_space=pltpu.VMEM), IN_HBM, IN_HBM],
-        out_specs=[pl.BlockSpec(memory_space=pltpu.VMEM)] * 3,
+    return call(
+        sent_weight_kernel,
+        "sent_weight",
+        2 * rows * channels * blocks * width,
+        2 * blocks * width * (rows + channels) + 2 * rows * channels,
+        in_specs=[IN_VMEM] * 2,
+        out_specs=[IN_VMEM] * 2,
+        out_shape=[jax.ShapeDtypeStruct((blocks, channels, width), BF16), TOKEN],
+    )(gated, grads)
+
+
+def gated_grad_kernel(col, grads, weight, _, far, near):
+    half = near.shape[1]
+    wide = jnp.concatenate([grads[b] for b in range(grads.shape[0])], axis=1)
+    for out, which in ((far, 1 - col[0]), (near, col[0])):
+        total = lax.dot_general(
+            wide,
+            weight[pl.ds(pl.multiple_of(which * half, half), half), :],
+            (((1,), (1,)), ((), ())),
+            preferred_element_type=F32,
+        )
+        out[...] = total.astype(out.dtype)
+
+
+def gated_grad(col, grads, weight, after):
+    blocks, rows, width = grads.shape
+    channels = weight.shape[0]
+    half = channels // 2
+    return call(
+        gated_grad_kernel,
+        "gated_grad",
+        2 * rows * channels * blocks * width,
+        2 * blocks * width * (rows + channels) + 6 * rows * half,
+        in_specs=[SCALAR, IN_VMEM, IN_VMEM, UNREAD],
+        out_specs=[IN_VMEM] * 2,
         out_shape=[
-            jax.ShapeDtypeStruct((blocks, channels, width), BF16),
             jax.ShapeDtypeStruct((rows, half), BF16),
             jax.ShapeDtypeStruct((rows, half), F32),
         ],
-        scratch_shapes=[
-            pltpu.VMEM(grads.shape, BF16),
-            pltpu.VMEM(weight.shape, BF16),
-            pltpu.SemaphoreType.DMA((blocks,)),
-            pltpu.SemaphoreType.DMA,
-        ],
-    )(col, gated, grads, weight)
-
-
-def kept_weight_kernel(gated, grads, arrived, out, done, held_grads, held, grad_sems, sems):
-    copies = fetch(grads, held_grads, grad_sems)
-    others = fetch(arrived, held, sems)
+    )(col, grads, weight, after)
+
+
+def kept_weight_kernel(gated, grads, arrived, out, done, held, sems):
     done[...] = jnp.zeros_like(done)
-    parts, _, size, _ = out.shape
-    for b in range(held.shape[0]):
-        copies[b].wait()
-        total = jnp.dot(gated[...], held_grads[b], preferred_element_type=F32)
-        others[b].wait()
-        total = (total + held[b].astype(F32)).astype(BF16)
+    blocks, parts, size, _ = held.shape
+    copies = []
+    for b in range(blocks):
+        total = jnp.dot(gated[...], grads[b], preferred_element_type=F32)
+        total = (total + arrived[b].astype(F32)).astype(BF16)
         for part in range(parts):
-            out[part, b] = total[part * size : (part + 1) * size]
+            held[b, part] = total[part * size : (part + 1) * size]
+        copies.append(pltpu.make_async_copy(held.at[b], out.at[:, b], sems.at[b]))
+        copies[-1].start()
+    for copy in copies:
+        copy.wait()
 
 
 def kept_weight(parts, gated, grads, arrived):
@@ -291,41 +289,46 @@
         "kept_weight",
         2 * rows * channels * blocks * width,
         2 * blocks * width * (rows + 2 * channels) + 2 * rows * channels,
-        in_specs=[pl.BlockSpec(memory_space=pltpu.VMEM), IN_HBM, IN_HBM],
-        out_specs=[pl.BlockSpec(memory_space=pltpu.VMEM)] * 2,
-        out_shape=[
-            jax.ShapeDtypeStruct((parts, blocks, size, width), BF16),
-            jax.ShapeDtypeStruct((8, LANES), F32),
-        ],
+        in_specs=[IN_VMEM] * 3,
+        out_specs=[IN_HBM, IN_VMEM],
+        out_shape=[jax.ShapeDtypeStruct((parts, blocks, size, width), BF16), TOKEN],
         scratch_shapes=[
-            pltpu.VMEM(grads.shape, BF16),
-            pltpu.VMEM(arrived.shape, BF16),
+            pltpu.VMEM((blocks, parts, size, width), BF16),
             pltpu.SemaphoreType.DMA((blocks,)),
-            pltpu.SemaphoreType.DMA((blocks,)),
         ],
     )(gated, grads, arrived)
 
 
-def middle_kernel(pair, taps, taps_arrived, head, out, out_taps, out_head):
+def two_roundings(sums):
+    high = sums.astype(BF16).astype(F32)
+    return jnp.concatenate([high, sums - high], axis=1).astype(BF16)
+
+
+def rejoined(both):
+    both = both.astype(F32)
+    return both[:, :8] + both[:, 8:]
+
+
+def middle_kernel(pair, taps, head, out, out_taps, out_head):
     parts, _, size, _ = out.shape
     blocks = pair.shape[0]
-    sums = taps[...] + taps_arrived[...]
+    sums = taps[0]
+    for copy in range(1, taps.shape[0]):
+        sums = sums + taps[copy]
     out_taps[...] = sums
-    high = sums.astype(BF16).astype(F32)
-    both = jnp.concatenate([high, sums - high], axis=1).astype(BF16)
+    out_head[...] = head[...]
+    both = two_roundings(sums)
     for part in range(parts):
         out[part, 0:blocks] = pair[:, part * size : (part + 1) * size, :]
         out[part, blocks:] = both
-    out_head[...] = head[...]
-
-
-def middle(parts, pair, taps, taps_arrived, head):
+
+
+def middle(parts, pair, taps, head):
     blocks, channels, width = pair.shape
-    shape = (parts, blocks + taps.shape[0], channels // parts, width)
-    args = (pair, taps, taps_arrived, head)
+    shape = (parts, blocks + taps.shape[1], channels // parts, width)
     outs = [
         jax.ShapeDtypeStruct(shape, BF16),
-        jax.ShapeDtypeStruct(taps.shape, F32),
+        jax.ShapeDtypeStruct(taps.shape[1:], F32),
         jax.ShapeDtypeStruct(head.shape, F32),
     ]
     return call(
@@ -333,11 +336,10 @@
         "middle",
         4 * pair.size,
         4 * pair.size,
-        grid=(1,),
-        in_specs=[whole(v.shape) for v in args],
-        out_specs=[whole(v.shape) for v in outs],
+        in_specs=[IN_VMEM] * 3,
+        out_specs=[IN_VMEM] * 3,
         out_shape=outs,
-    )(*args)
+    )(pair, taps, head)
 
 
 def last_kernel(
@@ -351,16 +353,12 @@
         for part in range(1, parts):
             total = total + arrived[part, b].astype(F32)
         out[:, b * width : (b + 1) * width] = (total * scale).astype(BF16)
-    for j in range(4):
-        total = taps[j]
-        for part in range(parts):
-            both = arrived[part, blocks + j].astype(F32)
-            total = total + jnp.where(z[0] == part, 0.0, both[:8] + both[8:])
-        total = (total * scale)[:TAPS]
-        if j < 3:
-            out_feat[j] = total
-        else:
-            out_inner[...] = total
+    total = taps[...]
+    for part in range(parts):
+        total = total + jnp.where(z[0] == part, 0.0, rejoined(arrived[part, blocks:]))
+    total = total * scale
+    out_feat[...] = total[:3, :TAPS]
+    out_inner[...] = total[3, :TAPS]
 
 
 def last(scale, z, taps, arrived, tail, head, grads):
@@ -425,20 +423,19 @@
         for c in (core, 1 - core)
     )
 
-    sent, far, near = products(col, sent, grads, out_weight)
+    sent, done = sent_weight(sent, grads)
     arrived = ctx_permute(sent, lambda x, z, c: (x, z, 1 - c))
+    far, near = gated_grad(col, grads, out_weight, done)
     pair, done = kept_weight(nx, kept, grads, arrived)
     far = lax.all_gather(far, "col", axis=0)
     summed = lax.psum_scatter(pair, "x", scatter_dimension=0)
 
     grad_own, head, tail, taps = backward(
-        col, near, far, before, own, feat_taps, inner_taps, done
-    )
-    taps = lax.psum(taps, "core")
-    taps = taps + ctx_permute(taps, lambda x, z, c: (x ^ 1, z, c))
-    taps_arrived = ctx_permute(taps, lambda x, z, c: (nx - 1 - x, z, c))
-
-    pieces, taps, head = middle(nz, summed, taps, taps_arrived, head)
+        nx * nc, col, near, far, before, own, feat_taps, inner_taps, done
+    )
+    taps = lax.all_to_all(taps, ("x", "core"), split_axis=0, concat_axis=0)
+
+    pieces, taps, head = middle(nz, summed, taps, head)
     pieces = lax.all_to_all(pieces, "zl", split_axis=0, concat_axis=0)
     head = ctx_shift(head, -1)
     grad_weight, grad_feat_taps, grad_inner_taps, grad_own = last(

time: 139 us -> 129 us (0.928)
  Pallas kernels: 20.2 us -> 10.3 us
  blocking collectives: 34.2 us -> 39.9 us
  waiting for transfers between devices: 38.8 us -> 34.5 us
  starting transfers between devices: 25 us -> 21.4 us
  local copies, waits for them, and re-layouts: 5.24 us -> 7.71 us
    all_to_all x0 -> x1, blocking collectives: none -> 13.4 us  [body(): taps = lax.all_to_all(taps, ('x', 'core'), split_axis=0, concat_axis=0)]
    psum x1 -> x0, blocking collectives: 7.73 us -> none  [body(): taps = lax.psum(taps, 'core')]
    ppermute x3 -> x1, waiting for transfers between devices: 9.15 us -> 2.26 us  [ctx_permute(): return lax.ppermute(value, CTX, pairs)]
    pallas_call x2 -> x3, Pallas kernels: 8.91 us -> 2.78 us  [the longest x1 1.29 us: gated_grad(): call(gated_grad_kernel, 'gated_grad', 2 * rows * channels * blocks * widt...]
    ppermute x3 -> x1, starting transfers between devices: 10 us -> 6.21 us  [ctx_permute(): return lax.ppermute(value, CTX, pairs)]
    pallas_call x1, Pallas kernels: 5.18 us -> 1.48 us  [kept_weight(): call(kept_weight_kernel, 'kept_weight', 2 * rows * channels * blocks * wi...]
    unnamed x20, local copies, waits for them, and re-layouts: 3.54 us -> 6.71 us
    all_to_all x1, starting transfers between devices: 4.81 us -> 6.48 us  [body(): pieces = lax.all_to_all(pieces, 'zl', split_axis=0, concat_axis=0)]
  transfers between devices with their start and end apart: 8 -> 6, of which waited for: 6 -> 5; matrix products, arithmetic and copies ran while one was open for 1% -> 1% of each run, Pallas kernels for 4% -> 5%
where the time goes in v7:
time: 129 us; the launch traced here: 128 us
  blocking collectives  39.9 us (31%)
  waiting for transfers between devices  34.5 us (27%)
  starting transfers between devices  21.4 us (17%)
  between operations  14.1 us (11%)
  Pallas kernels  10.3 us (8%)
  local copies, waits for them, and re-layouts  7.71 us (6%)
    all_gather x1, waiting for transfers between devices, body(): grads = lax.all_gather(out_grad, 'row', axis=0)  21.5 us
    all_gather x1, blocking collectives, body(): far = lax.all_gather(far, 'col', axis=0)  14.2 us
    all_to_all x1, blocking collectives, body(): taps = lax.all_to_all(taps, ('x', 'core'), split_axis=0, concat_axis=0)  13.4 us
    all_gather x1, blocking collectives, body(): both = lax.all_gather(gated, 'col', axis=1, tiled=True)  12.3 us
    ppermute x2, waiting for transfers between devices, ctx_shift(): lax.ppermute(value, CTX, [(i, i + steps) for i in range(count) if 0 <= i...  8.92 us
    ppermute x2, starting transfers between devices, ctx_shift(): lax.ppermute(value, CTX, [(i, i + steps) for i in range(count) if 0 <= i...  8.6 us
    unnamed x20, local copies, waits for them, and re-layouts  6.71 us
    all_to_all x1, starting transfers between devices, body(): pieces = lax.all_to_all(pieces, 'zl', split_axis=0, concat_axis=0)  6.48 us
  transfers between devices with their start and end apart: 6, of which 5 were waited for; matrix products, arithmetic and copies ran while one was open for 1% of the time, Pallas kernels for 5%

profile of v7, /device:TPU:1, one launch (start us, length us, event | category | flops | bytes accessed | tf_op | source)
XLA Modules:
  0.0 128.0 jit_solution(14236226442858485536)
XLA Ops:
  7.2 0.0 all-gather.4.cloned.1.call-start
  7.2 0.7 all-gather.4.cloned.1.call-update
  7.9 0.0 reduce-scatter.2.cloned.1.call-start
  7.9 0.7 slice.4
  8.7 5.4 %collective-permute-start = (bf16[3,16,256]{2,1,0:T(8,128)(2,1)S(1)}, bf16[3,16,256]{2,1,0:T(8,128)(2,1)S(1)}, u32[]{:S(2)}, u32[]{:S(2)}) collective-permute-start(bf16[3,16,256]{2,1,0:T(8,128)(2,1)S(1)} %slice.4), channel_id=1, source_target_pairs={{0,1},{1,2},{2,3},{3,4},{4,5},{5,6},{6,7},{7,8},{8,9},{9,10},{10,1... | collective-permute-start | bytes 73736 | tf_op jit(solution)/shard_map/ppermute | solution.py:401
  14.1 3.4 %collective-permute-done.before = bf16[3,16,256]{2,1,0:T(8,128)(2,1)S(1)} collective-permute-done((bf16[3,16,256]{2,1,0:T(8,128)(2,1)S(1)}, bf16[3,16,256]{2,1,0:T(8,128)(2,1)S(1)}, u32[]{:S(2)}, u32[]{:S(2)}) %collective-permute-start) | collective-permute-done | bytes 24608 | tf_op jit(solution)/shard_map/ppermute | solution.py:401
  17.5 1.1 copy-done.2
  18.7 0.7 copy-done.6
  19.4 0.7 copy-done.8
  20.1 1.3 %forward.1 = bf16[512,256]{1,0:T(8,128)(2,1)S(1)} custom-call(bf16[3,16,256]{2,1,0:T(8,128)(2,1)S(1)} %collective-permute-done.before, bf16[3,512,256]{2,1,0:T(8,128)(2,1)S(1)} %bitcast.15, f32[3,7,256]{2,1,0:T(8,128)S(1)} %copy-done.6, f32[7,256]{1,0:T(8,128)S(1)} %copy-done.8), custom_call_target="tpu_custom_call" | custom-call | flops 7864320 | bytes 1048576 | tf_op jit(solution)/shard_map/forward/pallas_call | solution.py:95
  21.4 12.3 %all_gather.15 = bf16[512,512]{1,0:T(8,128)(2,1)S(1)} all-gather(bf16[512,256]{1,0:T(8,128)(2,1)S(1)} %forward.1), channel_id=1, replica_groups=mesh['row'=8,'col'=2,'x'=4,'zl'=4,'core'=2] {'col'}, dimensions={1}, use_global_device_ids=true | all-gather | bytes 786432 | tf_op jit(solution)/shard_map/all_gather | solution.py:418
  33.7 0.2 copy.12
  34.0 21.5 %all-gather.4.cloned.1.call-done = bf16[4096,256]{1,0:T(8,128)(2,1)} async-done(((bf16[512,256]{1,0:T(8,128)(2,1)}), bf16[4096,256]{1,0:T(8,128)(2,1)}) %all-gather.4.cloned.1.call-update) | async-done | bytes 2097168 | tf_op jit(solution)/shard_map/all_gather | solution.py:413
  55.5 1.6 %copy-done = bf16[4096,256]{1,0:T(8,128)(2,1)S(1)} copy-done((bf16[4096,256]{1,0:T(8,128)(2,1)S(1)}, bf16[4096,256]{1,0:T(8,128)(2,1)}, u32[]{:S(2)}) %copy-start) | copy-done | bytes 2097176
  57.1 0.7 sent_weight.1
  57.8 6.2 %collective-permute-start.1 = (bf16[8,256,256]{2,1,0:T(8,128)(2,1)S(1)}, bf16[8,256,256]{2,1,0:T(8,128)(2,1)S(1)}, u32[]{:S(2)}, u32[]{:S(2)}) collective-permute-start(bf16[8,256,256]{2,1,0:T(8,128)(2,1)S(1)} %get-tuple-element.21), channel_id=1, source_target_pairs={{0,1},{1,0},{2,3},{3,2},{4,5},{5,4},{6,7},{7,6},{8,9},{9,8},{10,11... | collective-permute-start | bytes 3145736 | tf_op jit(solution)/shard_map/ppermute | solution.py:396
  64.0 2.3 %collective-permute-done.1.arrived = bf16[8,256,256]{2,1,0:T(8,128)(2,1)S(1)} collective-permute-done((bf16[8,256,256]{2,1,0:T(8,128)(2,1)S(1)}, bf16[8,256,256]{2,1,0:T(8,128)(2,1)S(1)}, u32[]{:S(2)}, u32[]{:S(2)}) %collective-permute-start.1) | collective-permute-done | bytes 1048608 | tf_op jit(solution)/shard_map/ppermute | solution.py:396
  66.3 1.5 %kept_weight.1 = (bf16[4,8,64,256]{3,2,1,0:T(8,128)(2,1)}, f32[8,128]{1,0:T(8,128)S(1)}) custom-call(bf16[256,512]{1,0:T(8,128)(2,1)S(1)} %bitcast.19, bf16[8,512,256]{2,1,0:T(8,128)(2,1)S(1)} %bitcast.12, bf16[8,256,256]{2,1,0:T(8,128)(2,1)S(1)} %collective-permute-done.1.arrived), custom_call_target="tpu_custom_call" | custom-call | flops 536870912 | bytes 4456448 | tf_op jit(solution)/shard_map/kept_weight/pallas_call | solution.py:287
  67.8 0.0 reduce-scatter.2.cloned.1.call-update
  67.8 0.0 copy-start.4
  67.8 1.6 %copy-done.4 = bf16[512,2048]{1,0:T(8,128)(2,1)S(1)} copy-done((bf16[512,2048]{1,0:T(8,128)(2,1)S(1)}, bf16[512,2048]{1,0:T(8,128)(2,1)}, u32[]{:S(2)}) %copy-start.4) | copy-done | bytes 2097176
  69.4 1.3 %gated_grad.1 = (bf16[512,256]{1,0:T(8,128)(2,1)S(1)}, f32[512,256]{1,0:T(8,128)S(1)}) custom-call(s32[1]{0:T(128)} %bitcast.8.col, bf16[8,512,256]{2,1,0:T(8,128)(2,1)S(1)} %bitcast.13, bf16[512,2048]{1,0:T(8,128)(2,1)S(1)} %copy-done.4, f32[8,128]{1,0:T(8,128)S(1)} %get-tuple-element.23._), custom_call_target="tpu_custom_call" | custom-call | flops 1073741824 | bytes 4980736 | tf_op jit(solution)/shard_map/gated_grad/pallas_call | solution.py:254
  70.7 14.2 %all-gather.1 = bf16[1024,256]{1,0:T(8,128)(2,1)S(1)} all-gather(bf16[512,256]{1,0:T(8,128)(2,1)S(1)} %get-tuple-element.25), channel_id=3, replica_groups=mesh['row'=8,'col'=2,'x'=4,'zl'=4,'core'=2] {'col'}, dimensions={0}, use_global_device_ids=true | all-gather | bytes 786432 | tf_op jit(solution)/shard_map/all_gather | solution.py:430
  84.9 4.1 %backward.1 = (bf16[3,512,256]{2,1,0:T(8,128)(2,1)}, f32[3,16,256]{2,1,0:T(8,128)S(1)}, f32[3,16,256]{2,1,0:T(8,128)S(1)}, f32[8,4,8,256]{3,2,1,0:T(8,128)S(1)}) custom-call(s32[1]{0:T(128)} %bitcast.8.col, f32[512,256]{1,0:T(8,128)S(1)} %get-tuple-element.24.near, bf16[2,512,256]{2,1,0:T(8,128)(2,1)S(1)} %bitcast.17, ...), custom_call_target="tpu_custom_call" | custom-call | flops 20971520 | bytes 2621440 | tf_op jit(solution)/shard_map/backward/pallas_call | solution.py:186
  89.0 13.4 %all_to_all.10.taps = f32[8,4,8,256]{3,2,1,0:T(8,128)S(1)} all-to-all(f32[8,4,8,256]{3,2,1,0:T(8,128)S(1)} %get-tuple-element.27), channel_id=1, replica_groups=mesh['row'=8,'col'=2,'x'=4,'zl'=4,'core'=2] {'x','core'}, dimensions={0} | all-to-all | bytes 524288 | tf_op jit(solution)/shard_map/all_to_all | solution.py:436
  102.4 0.9 copy-done.5
  103.3 0.8 middle.1
  104.1 6.5 %all-to-all-start.1 = ((bf16[4,12,16,256]{3,2,1,0:T(8,128)(2,1)}), bf16[4,12,16,256]{3,2,1,0:T(8,128)(2,1)S(1)}, u32[]{:S(2)}, u32[]{:S(2)}) async-start(bf16[4,12,16,256]{3,2,1,0:T(8,128)(2,1)} %get-tuple-element.30), calls=%async_computation.2 | async-start | bytes 786432 | tf_op jit(solution)/shard_map/all_to_all | solution.py:439
  110.6 3.2 %collective-permute-start.2 = (f32[3,16,256]{2,1,0:T(8,128)S(1)}, f32[3,16,256]{2,1,0:T(8,128)S(1)}, u32[]{:S(2)}, u32[]{:S(2)}) collective-permute-start(f32[3,16,256]{2,1,0:T(8,128)S(1)} %get-tuple-element.32), channel_id=1, source_target_pairs={{1,0},{2,1},{3,2},{4,3},{5,4},{6,5},{7,6},{8,7},{9,8},{10,9},{11,1... | collective-permute-start | bytes 147464 | tf_op jit(solution)/shard_map/ppermute | solution.py:401
  113.8 5.5 %collective-permute-done.2.refs_4_ = f32[3,16,256]{2,1,0:T(8,128)S(1)} collective-permute-done((f32[3,16,256]{2,1,0:T(8,128)S(1)}, f32[3,16,256]{2,1,0:T(8,128)S(1)}, u32[]{:S(2)}, u32[]{:S(2)}) %collective-permute-start.2) | collective-permute-done | bytes 49184 | tf_op jit(solution)/shard_map/ppermute | solution.py:401
  119.3 1.1 all-to-all-done.1.refs_2_
  120.4 0.7 last.1
  (15 shorter events, 0.1 us)
Async XLA Ops:
  7.2 48.3 %all-gather.4.cloned.1.call-start = ((), (), s32[]{:S(2)}) async-start(), calls=%async_computation.4 | async-start | bytes 2359296 | tf_op jit(solution)/shard_map/all_gather | solution.py:413
  7.9 94.5 %reduce-scatter.2.cloned.1.call-start = ((), (), s32[]{:S(2)}) async-start(), calls=%async_computation.3 | async-start | bytes 1310720 | tf_op jit(solution)/shard_map/reduce_scatter | solution.py:431
  8.7 8.8 %collective-permute-start = (bf16[3,16,256]{2,1,0:T(8,128)(2,1)S(1)}, bf16[3,16,256]{2,1,0:T(8,128)(2,1)S(1)}, u32[]{:S(2)}, u32[]{:S(2)}) collective-permute-start(bf16[3,16,256]{2,1,0:T(8,128)(2,1)S(1)} %slice.4), channel_id=1, source_target_pairs={{0,1},{1,2},{2,3},{3,4},{4,5},{5,6},{6,7},{7,8},{8,9},{9,10},{10,1... | collective-permute-start | bytes 73736 | tf_op jit(solution)/shard_map/ppermute | solution.py:401
  17.5 1.1 copy-start.2
  18.7 0.7 copy-start.6
  19.4 0.7 copy-start.8
  55.5 1.6 %copy-start = (bf16[4096,256]{1,0:T(8,128)(2,1)S(1)}, bf16[4096,256]{1,0:T(8,128)(2,1)}, u32[]{:S(2)}) copy-start(bf16[4096,256]{1,0:T(8,128)(2,1)} %all-gather.4.cloned.1.call-done) | copy-start | bytes 6291460
  57.1 9.2 %copy-start.1 = (bf16[4096,256]{1,0:T(8,128)(2,1)S(1)}, bf16[4096,256]{1,0:T(8,128)(2,1)}, u32[]{:S(2)}) copy-start(bf16[4096,256]{1,0:T(8,128)(2,1)} %all-gather.4.cloned.1.call-done) | copy-start | bytes 6291460
  57.8 8.5 %collective-permute-start.1 = (bf16[8,256,256]{2,1,0:T(8,128)(2,1)S(1)}, bf16[8,256,256]{2,1,0:T(8,128)(2,1)S(1)}, u32[]{:S(2)}, u32[]{:S(2)}) collective-permute-start(bf16[8,256,256]{2,1,0:T(8,128)(2,1)S(1)} %get-tuple-element.21), channel_id=1, source_target_pairs={{0,1},{1,0},{2,3},{3,2},{4,5},{5,4},{6,7},{7,6},{8,9},{9,8},{10,11... | collective-permute-start | bytes 3145736 | tf_op jit(solution)/shard_map/ppermute | solution.py:396
  67.8 1.6 %copy-start.4 = (bf16[512,2048]{1,0:T(8,128)(2,1)S(1)}, bf16[512,2048]{1,0:T(8,128)(2,1)}, u32[]{:S(2)}) copy-start(bf16[512,2048]{1,0:T(8,128)(2,1)} %weight.1) | copy-start | bytes 6291460
  69.4 15.5 %copy-start.3 = (bf16[512,3,256]{2,0,1:T(8,128)(2,1)S(1)}, bf16[512,3,256]{2,0,1:T(8,128)(2,1)}, u32[]{:S(2)}) copy-start(bf16[512,3,256]{2,0,1:T(8,128)(2,1)} %param.5) | copy-start | bytes 2359300
  69.4 15.5 %copy-start.7 = (f32[3,7,256]{2,1,0:T(8,128)S(1)}, f32[3,7,256]{2,1,0:T(8,128)}, u32[]{:S(2)}) copy-start(f32[3,7,256]{2,1,0:T(8,128)} %feat_taps.3) | copy-start | bytes 64516
  69.4 15.5 %copy-start.9 = (f32[7,256]{1,0:T(8,128)S(1)}, f32[7,256]{1,0:T(8,128)}, u32[]{:S(2)}) copy-start(f32[7,256]{1,0:T(8,128)} %inner_taps.3) | copy-start | bytes 21508
  102.4 1.0 copy-start.5
  104.1 16.3 %all-to-all-start.1 = ((bf16[4,12,16,256]{3,2,1,0:T(8,128)(2,1)}), bf16[4,12,16,256]{3,2,1,0:T(8,128)(2,1)S(1)}, u32[]{:S(2)}, u32[]{:S(2)}) async-start(bf16[4,12,16,256]{3,2,1,0:T(8,128)(2,1)} %get-tuple-element.30), calls=%async_computation.2 | async-start | bytes 786432 | tf_op jit(solution)/shard_map/all_to_all | solution.py:439
  110.6 8.7 %collective-permute-start.2 = (f32[3,16,256]{2,1,0:T(8,128)S(1)}, f32[3,16,256]{2,1,0:T(8,128)S(1)}, u32[]{:S(2)}, u32[]{:S(2)}) collective-permute-start(f32[3,16,256]{2,1,0:T(8,128)S(1)} %get-tuple-element.32), channel_id=1, source_target_pairs={{1,0},{2,1},{3,2},{4,3},{5,4},{6,5},{7,6},{8,7},{9,8},{10,9},{11,1... | collective-permute-start | bytes 147464 | tf_op jit(solution)/shard_map/ppermute | solution.py:401
Sparse Core Ops, SparseCore 0:
  10.1 45.3 all-gather.3
  67.9 26.3 reduce-scatter.1

commit v8 on v7

--- a/solution.py
+++ b/solution.py
@@ -47,10 +47,12 @@
     )
 
 
-def load_features(before, own, feats):
+def load_features(before, own, feats, after=None):
     rows = own.shape[1]
     for j in range(3):
         feats[j, 0:HALO, :] = before[j].astype(F32)
+        if after is not None:
+            feats[j, HALO + rows :, :] = after[j].astype(F32)
         for start, count in spread(rows):
             feats[j, HALO + start : HALO + start + count, :] = own[
                 j, start : start + count, :
@@ -110,79 +112,71 @@
 
 
 def backward_kernel(
-    col, near, far, before, own, feat_taps, inner_taps, _,
-    grads, head, tail, tap_sums, feats, query, key, value, product, grad_window, grad_mixed,
+    col, near, far, before, own, after, feat_taps, inner_taps, _,
+    grads, tap_sums, feats, query, key, value, product, grad_window, grad_mixed,
 ):
     rows = own.shape[1]
-    load_features(before, own, feats)
-    for start, count in spread(rows + LEAD):
+    load_features(before, own, feats, after)
+    for start, count in spread(rows + HALO + LEAD):
         parts = mixed_parts(feats, feat_taps, start, count)
         query[start : start + count, :] = parts[0]
         key[start : start + count, :] = parts[1]
         value[start : start + count, :] = parts[2]
         product[start : start + count, :] = parts[1] * parts[2]
-    zeros = jnp.zeros((HALO, LANES), F32)
-    grad_window[0:HALO, :] = zeros
-    grad_window[HALO + rows :, :] = zeros[:LEAD]
-    for j in range(3):
-        grad_mixed[j, 0:HALO, :] = zeros
-        grad_mixed[j, HALO + rows :, :] = zeros[:LEAD]
-    for start, count in spread(rows):
-        at = HALO + start
+    for start, count in spread(rows + HALO):
         total = near[start : start + count, :] + far[
             1 - col[0], start : start + count, :
         ].astype(F32)
-        grad_window[at : at + count, :] = total * query[LEAD + start : LEAD + start + count, :]
-        grad_mixed[0, at : at + count, :] = total * window_rows(product, inner_taps, start, count)
+        grad_window[start : start + count, :] = (
+            total * query[LEAD + start : LEAD + start + count, :]
+        )
+        grad_mixed[0, start : start + count, :] = total * window_rows(
+            product, inner_taps, start, count
+        )
     for start, count in spread(rows + LEAD):
-        at = HALO - LEAD + start
-        total = inner_taps[0:1, :] * grad_window[at : at + count, :]
+        total = inner_taps[0:1, :] * grad_window[start : start + count, :]
         for s in range(1, TAPS):
-            total = total + inner_taps[s : s + 1, :] * grad_window[at + s : at + s + count, :]
-        grad_mixed[1, at : at + count, :] = total * value[start : start + count, :]
-        grad_mixed[2, at : at + count, :] = total * key[start : start + count, :]
+            total = total + inner_taps[s : s + 1, :] * grad_window[start + s : start + s + count, :]
+        grad_mixed[1, start : start + count, :] = (
+            total * value[LEAD + start : LEAD + start + count, :]
+        )
+        grad_mixed[2, start : start + count, :] = total * key[LEAD + start : LEAD + start + count, :]
 
     def folded(terms):
         return jnp.sum(terms.reshape(terms.shape[0] // 8, 8, LANES), axis=0)
 
     def put(place, sums):
-        rows = [jnp.sum(total, axis=0, keepdims=True) for total in sums]
-        tile = jnp.concatenate([*rows, jnp.zeros((1, LANES), F32)], axis=0)
+        tile = [jnp.sum(total, axis=0, keepdims=True) for total in sums]
+        tile = jnp.concatenate([*tile, jnp.zeros((1, LANES), F32)], axis=0)
         for copy in range(tap_sums.shape[0]):
             tap_sums[copy, place] = tile
 
-    def transposed(j, at, count):
-        total = feat_taps[j, 0:1, :] * grad_mixed[j, at : at + count, :]
-        for s in range(1, TAPS):
-            total = total + feat_taps[j, s : s + 1, :] * grad_mixed[j, at + s : at + s + count, :]
-        return total
-
     for j in range(3):
-        head[j] = transposed(j, 0, HALO)
         sums = [jnp.zeros((8, LANES), F32) for _ in range(TAPS)]
-        spans = [(HALO + start, count) for start, count in spread(rows)]
-        for at, count in ([(HALO - LEAD, LEAD)] if j > 0 else []) + spans:
-            here = grad_mixed[j, at : at + count, :]
+        for start, count in spread(rows):
+            here = grad_mixed[j, start : start + count, :]
+            total = feat_taps[j, 0:1, :] * here
+            for s in range(1, TAPS):
+                total = (
+                    total
+                    + feat_taps[j, s : s + 1, :] * grad_mixed[j, start + s : start + s + count, :]
+                )
+            grads[j, start : start + count, :] = total.astype(BF16)
             for s in range(TAPS):
-                sums[s] = sums[s] + folded(here * feats[j, at - s : at - s + count, :])
-            if at >= HALO:
-                total = transposed(j, at, count)
-                grads[j, at - HALO : at - HALO + count, :] = total.astype(BF16)
-                if at + count == HALO + rows:
-                    tail[j] = total[count - HALO :]
+                base = HALO + start - s
+                sums[s] = sums[s] + folded(here * feats[j, base : base + count, :])
         put(j, sums)
     sums = [jnp.zeros((8, LANES), F32) for _ in range(TAPS)]
     for start, count in spread(rows):
-        here = grad_window[HALO + start : HALO + start + count, :]
+        here = grad_window[start : start + count, :]
         for s in range(TAPS):
             base = LEAD + start - s
             sums[s] = sums[s] + folded(here * product[base : base + count, :])
     put(3, sums)
 
 
-def backward(copies, col, near, far, before, own, feat_taps, inner_taps, after):
+def backward(copies, col, near, far, before, own, after, feat_taps, inner_taps, later):
     _, rows, channels = own.shape
-    edge = jax.ShapeDtypeStruct((3, HALO, channels), F32)
     return call(
         backward_kernel,
         "backward",
@@ -190,37 +184,33 @@
         20 * rows * channels,
         grid=(channels // LANES,),
         in_specs=[
-            SCALAR, lane_spec(rows), lane_spec(2, rows), lane_spec(3, HALO), lane_spec(3, rows),
-            lane_spec(3, TAPS), lane_spec(TAPS), UNREAD,
-        ],
-        out_specs=[
-            lane_spec(3, rows), lane_spec(3, HALO), lane_spec(3, HALO), lane_spec(copies, 4, 8)
-        ],
+            SCALAR, lane_spec(rows + HALO), lane_spec(2, rows + HALO), lane_spec(3, HALO),
+            lane_spec(3, rows), lane_spec(3, HALO), lane_spec(3, TAPS), lane_spec(TAPS), UNREAD,
+        ],
+        out_specs=[lane_spec(3, rows), lane_spec(copies, 4, 8)],
         out_shape=[
             jax.ShapeDtypeStruct((3, rows, channels), BF16),
-            edge,
-            edge,
             jax.ShapeDtypeStruct((copies, 4, 8, channels), F32),
         ],
-        scratch_shapes=[pltpu.VMEM((3, rows + HALO, LANES), F32)]
-        + [pltpu.VMEM((rows + LEAD, LANES), F32)] * 4
+        scratch_shapes=[pltpu.VMEM((3, rows + 2 * HALO, LANES), F32)]
+        + [pltpu.VMEM((rows + HALO + LEAD, LANES), F32)] * 4
         + [
-            pltpu.VMEM((rows + HALO + LEAD, LANES), F32),
-            pltpu.VMEM((3, rows + HALO + LEAD, LANES), F32),
-        ],
-    )(col, near, far, before, own, feat_taps, inner_taps, after)
+            pltpu.VMEM((rows + HALO, LANES), F32),
+            pltpu.VMEM((3, rows + HALO, LANES), F32),
+        ],
+    )(col, near, far, before, own, after, feat_taps, inner_taps, later)
 
 
 TOKEN = jax.ShapeDtypeStruct((8, LANES), F32)
 
 
-def sent_weight_kernel(gated, grads, sent, done):
+def sent_weight_kernel(gated, grads, _, sent, done):
     done[...] = jnp.zeros_like(done)
     for b in range(grads.shape[0]):
         sent[b] = jnp.dot(gated[...], grads[b], preferred_element_type=F32).astype(BF16)
 
 
-def sent_weight(gated, grads):
+def sent_weight(gated, grads, later):
     channels, rows = gated.shape
     blocks, _, width = grads.shape
     return call(
@@ -228,15 +218,22 @@
         "sent_weight",
         2 * rows * channels * blocks * width,
         2 * blocks * width * (rows + channels) + 2 * rows * channels,
-        in_specs=[IN_VMEM] * 2,
+        in_specs=[IN_VMEM] * 2 + [UNREAD],
         out_specs=[IN_VMEM] * 2,
         out_shape=[jax.ShapeDtypeStruct((blocks, channels, width), BF16), TOKEN],
-    )(gated, grads)
-
-
-def gated_grad_kernel(col, grads, weight, _, far, near):
+    )(gated, grads, later)
+
+
+def gated_grad_kernel(col, grads, halo, weight, _, far, near):
     half = near.shape[1]
-    wide = jnp.concatenate([grads[b] for b in range(grads.shape[0])], axis=1)
+    blocks = range(grads.shape[0])
+    wide = jnp.concatenate(
+        [
+            jnp.concatenate([grads[b] for b in blocks], axis=1),
+            jnp.concatenate([halo[b] for b in blocks], axis=1),
+        ],
+        axis=0,
+    )
     for out, which in ((far, 1 - col[0]), (near, col[0])):
         total = lax.dot_general(
             wide,
@@ -247,8 +244,9 @@
         out[...] = total.astype(out.dtype)
 
 
-def gated_grad(col, grads, weight, after):
+def gated_grad(col, grads, halo, weight, later):
     blocks, rows, width = grads.shape
+    rows = rows + halo.shape[1]
     channels = weight.shape[0]
     half = channels // 2
     return call(
@@ -256,13 +254,13 @@
         "gated_grad",
         2 * rows * channels * blocks * width,
         2 * blocks * width * (rows + channels) + 6 * rows * half,
-        in_specs=[SCALAR, IN_VMEM, IN_VMEM, UNREAD],
+        in_specs=[SCALAR, IN_VMEM, IN_VMEM, IN_VMEM, UNREAD],
         out_specs=[IN_VMEM] * 2,
         out_shape=[
             jax.ShapeDtypeStruct((rows, half), BF16),
             jax.ShapeDtypeStruct((rows, half), F32),
         ],
-    )(col, grads, weight, after)
+    )(col, grads, halo, weight, later)
 
 
 def kept_weight_kernel(gated, grads, arrived, out, done, held, sems):
@@ -309,45 +307,39 @@
     return both[:, :8] + both[:, 8:]
 
 
-def middle_kernel(pair, taps, head, out, out_taps, out_head):
+def middle_kernel(pair, taps, out, out_taps):
     parts, _, size, _ = out.shape
     blocks = pair.shape[0]
     sums = taps[0]
     for copy in range(1, taps.shape[0]):
         sums = sums + taps[copy]
     out_taps[...] = sums
-    out_head[...] = head[...]
     both = two_roundings(sums)
     for part in range(parts):
         out[part, 0:blocks] = pair[:, part * size : (part + 1) * size, :]
         out[part, blocks:] = both
 
 
-def middle(parts, pair, taps, head):
+def middle(parts, pair, taps):
     blocks, channels, width = pair.shape
     shape = (parts, blocks + taps.shape[1], channels // parts, width)
-    outs = [
-        jax.ShapeDtypeStruct(shape, BF16),
-        jax.ShapeDtypeStruct(taps.shape[1:], F32),
-        jax.ShapeDtypeStruct(head.shape, F32),
-    ]
     return call(
         middle_kernel,
         "middle",
         4 * pair.size,
         4 * pair.size,
-        in_specs=[IN_VMEM] * 3,
-        out_specs=[IN_VMEM] * 3,
-        out_shape=outs,
-    )(pair, taps, head)
-
-
-def last_kernel(
-    scale, z, taps, arrived, tail, head, _, out, out_feat, out_inner, out_grads
-):
+        in_specs=[IN_VMEM] * 2,
+        out_specs=[IN_VMEM] * 2,
+        out_shape=[
+            jax.ShapeDtypeStruct(shape, BF16),
+            jax.ShapeDtypeStruct(taps.shape[1:], F32),
+        ],
+    )(pair, taps)
+
+
+def last_kernel(scale, z, taps, arrived, out, out_feat, out_inner):
     parts, _, _, width = arrived.shape
     blocks = out.shape[1] // width
-    out_grads[...] = (tail[...] + head[...]).astype(BF16)
     for b in range(blocks):
         total = arrived[0, b].astype(F32)
         for part in range(1, parts):
@@ -361,28 +353,22 @@
     out_inner[...] = total[3, :TAPS]
 
 
-def last(scale, z, taps, arrived, tail, head, grads):
+def last(scale, z, taps, arrived):
     parts, count, channels, width = arrived.shape
     blocks = count - taps.shape[0]
-    final = grads.shape[1] // HALO - 1
-    args = (taps, arrived, tail, head)
-    shapes = [
-        jax.ShapeDtypeStruct((channels, blocks * width), BF16),
-        jax.ShapeDtypeStruct((3, TAPS, width), F32),
-        jax.ShapeDtypeStruct((TAPS, width), F32),
-    ]
     return call(
         lambda *refs: last_kernel(scale, *refs),
         "last",
         2 * arrived.size,
         2 * arrived.size,
-        grid=(1,),
-        in_specs=[SCALAR] + [whole(v.shape) for v in args] + [UNREAD],
-        out_specs=[whole(v.shape) for v in shapes]
-        + [pl.BlockSpec(tail.shape, lambda i: (0, final, 0))],
-        out_shape=shapes + [jax.ShapeDtypeStruct(grads.shape, grads.dtype)],
-        input_output_aliases={5: 3},
-    )(z, *args, grads)
+        in_specs=[SCALAR] + [IN_VMEM] * 2,
+        out_specs=[IN_VMEM] * 3,
+        out_shape=[
+            jax.ShapeDtypeStruct((channels, blocks * width), BF16),
+            jax.ShapeDtypeStruct((3, TAPS, width), F32),
+            jax.ShapeDtypeStruct((TAPS, width), F32),
+        ],
+    )(z, taps, arrived)
 
 
 def ctx_permute(value, target):
@@ -422,25 +408,25 @@
         lax.dynamic_index_in_dim(split, c, 1, keepdims=False).reshape(channels // nc, rows)
         for c in (core, 1 - core)
     )
-
-    sent, done = sent_weight(sent, grads)
+    after = ctx_shift(jnp.concatenate([own[:, :HALO], out_grad[None, :HALO]]), -1)
+    halo = jnp.broadcast_to(after[3], (lax.axis_size("row"), *after.shape[1:]))
+    halo = lax.all_to_all(halo, "row", split_axis=0, concat_axis=0)
+
+    sent, done = sent_weight(sent, grads, halo)
     arrived = ctx_permute(sent, lambda x, z, c: (x, z, 1 - c))
-    far, near = gated_grad(col, grads, out_weight, done)
+    far, near = gated_grad(col, grads, halo, out_weight, done)
     pair, done = kept_weight(nx, kept, grads, arrived)
     far = lax.all_gather(far, "col", axis=0)
     summed = lax.psum_scatter(pair, "x", scatter_dimension=0)
 
-    grad_own, head, tail, taps = backward(
-        nx * nc, col, near, far, before, own, feat_taps, inner_taps, done
+    grad_own, taps = backward(
+        nx * nc, col, near, far, before, own, after, feat_taps, inner_taps, done
     )
     taps = lax.all_to_all(taps, ("x", "core"), split_axis=0, concat_axis=0)
 
-    pieces, taps, head = middle(nz, summed, taps, head)
+    pieces, taps = middle(nz, summed, taps)
     pieces = lax.all_to_all(pieces, "zl", split_axis=0, concat_axis=0)
-    head = ctx_shift(head, -1)
-    grad_weight, grad_feat_taps, grad_inner_taps, grad_own = last(
-        inv_root, z, taps, pieces, tail, head, grad_own
-    )
+    grad_weight, grad_feat_taps, grad_inner_taps = last(inv_root, z, taps, pieces)
     return jnp.transpose(grad_own, (1, 0, 2)), grad_weight, grad_feat_taps, grad_inner_taps
 
 

time: 129 us -> 131 us (1.016)
  starting transfers between devices: 21.4 us -> 34.2 us
  waiting for transfers between devices: 34.5 us -> 22 us
  local copies, waits for them, and re-layouts: 7.71 us -> 9.07 us
    all_gather x1, waiting for transfers between devices: 21.5 us -> 1.75 us  [body(): grads = lax.all_gather(out_grad, 'row', axis=0)]
    all_to_all x0 -> x1, starting transfers between devices: none -> 10.1 us  [body(): halo = lax.all_to_all(halo, 'row', split_axis=0, concat_axis=0)]
    ppermute x2, waiting for transfers between devices: 8.92 us -> 0.01 us  [ctx_shift(): lax.ppermute(value, CTX, [(i, i + steps) for i in range(count) if 0 <= i...]
    all_to_all x1, waiting for transfers between devices: 1.13 us -> 9.84 us  [body(): pieces = lax.all_to_all(pieces, 'zl', split_axis=0, concat_axis=0)]
    all_to_all x0 -> x1, waiting for transfers between devices: none -> 7.46 us  [body(): halo = lax.all_to_all(halo, 'row', split_axis=0, concat_axis=0)]
    all_to_all x1, blocking collectives: 13.4 us -> 11.5 us  [body(): taps = lax.all_to_all(taps, ('x', 'core'), split_axis=0, concat_axis=0)]
    all_to_all x1, starting transfers between devices: 6.48 us -> 8.08 us  [body(): pieces = lax.all_to_all(pieces, 'zl', split_axis=0, concat_axis=0)]
    ppermute x2, starting transfers between devices: 8.6 us -> 10.1 us  [ctx_shift(): lax.ppermute(value, CTX, [(i, i + steps) for i in range(count) if 0 <= i...]
  transfers between devices with their start and end apart: 6 -> 7, of which waited for: 5 -> 4; matrix products, arithmetic and copies ran while one was open for 1% -> 2% of each run, Pallas kernels for 5% -> 5%
where the time goes in v8:
time: 131 us; the launch traced here: 129 us
  blocking collectives  39 us (30%)
  starting transfers between devices  34.2 us (26%)
  waiting for transfers between devices  22 us (17%)
  between operations  14.2 us (11%)
  Pallas kernels  10.4 us (8%)
  local copies, waits for them, and re-layouts  9.07 us (7%)
    all_gather x1, blocking collectives, body(): far = lax.all_gather(far, 'col', axis=0)  14.7 us
    all_gather x1, blocking collectives, body(): both = lax.all_gather(gated, 'col', axis=1, tiled=True)  12.8 us
    all_to_all x1, blocking collectives, body(): taps = lax.all_to_all(taps, ('x', 'core'), split_axis=0, concat_axis=0)  11.5 us
    all_to_all x1, starting transfers between devices, body(): halo = lax.all_to_all(halo, 'row', split_axis=0, concat_axis=0)  10.1 us
    ppermute x2, starting transfers between devices, ctx_shift(): lax.ppermute(value, CTX, [(i, i + steps) for i in range(count) if 0 <= i...  10.1 us
    all_to_all x1, waiting for transfers between devices, body(): pieces = lax.all_to_all(pieces, 'zl', split_axis=0, concat_axis=0)  9.84 us
    all_to_all x1, starting transfers between devices, body(): pieces = lax.all_to_all(pieces, 'zl', split_axis=0, concat_axis=0)  8.08 us
    all_to_all x1, waiting for transfers between devices, body(): halo = lax.all_to_all(halo, 'row', split_axis=0, concat_axis=0)  7.46 us
  transfers between devices with their start and end apart: 7, of which 4 were waited for; matrix products, arithmetic and copies ran while one was open for 2% of the time, Pallas kernels for 5%

profile of v8, /device:TPU:1, one launch (start us, length us, event | category | flops | bytes accessed | tf_op | source)
XLA Modules:
  0.0 128.9 jit_solution(13273972611500464781)
XLA Ops:
  7.2 0.0 all-gather.4.cloned.1.call-start
  7.2 0.7 all-gather.4.cloned.1.call-update
  7.9 0.8 fusion
  8.7 5.4 %collective-permute-start.1 = (bf16[3,16,256]{2,1,0:T(8,128)(2,1)S(1)}, bf16[3,16,256]{2,1,0:T(8,128)(2,1)S(1)}, u32[]{:S(2)}, u32[]{:S(2)}) collective-permute-start(bf16[3,16,256]{2,1,0:T(8,128)(2,1)S(1)} %get-tuple-element.30), channel_id=1, source_target_pairs={{0,1},{1,2},{2,3},{3,4},{4,5},{5,6},{6,7},{7,8},{8,9},{9,10},{10,1... | collective-permute-start | bytes 73736 | tf_op jit(solution)/shard_map/ppermute | solution.py:387
  14.1 0.7 slice_bitcast_fusion.1
  14.8 4.7 %collective-permute-start = (bf16[4,16,256]{2,1,0:T(8,128)(2,1)S(1)}, bf16[4,16,256]{2,1,0:T(8,128)(2,1)S(1)}, u32[]{:S(2)}, u32[]{:S(2)}) collective-permute-start(bf16[4,16,256]{2,1,0:T(8,128)(2,1)S(1)} %pad_maximum_fusion), channel_id=1, source_target_pairs={{1,0},{2,1},{3,2},{4,3},{5,4},{6,5},{7,6},{8,7},{9,8},{10,9},{11,1... | collective-permute-start | bytes 98312 | tf_op jit(solution)/shard_map/ppermute | solution.py:387
  19.5 1.1 copy-done.2
  20.6 0.7 copy-done.6
  21.3 0.7 copy-done.8
  22.0 1.3 %forward.1 = bf16[512,256]{1,0:T(8,128)(2,1)S(1)} custom-call(bf16[3,16,256]{2,1,0:T(8,128)(2,1)S(1)} %collective-permute-done.1.before, bf16[3,512,256]{2,1,0:T(8,128)(2,1)S(1)} %bitcast.19, f32[3,7,256]{2,1,0:T(8,128)S(1)} %copy-done.6, f32[7,256]{1,0:T(8,128)S(1)} %copy-done.8), custom_call_target="tpu_custom_call" | custom-call | flops 7864320 | bytes 1048576 | tf_op jit(solution)/shard_map/forward/pallas_call | solution.py:97
  23.3 12.8 %all_gather.17 = bf16[512,512]{1,0:T(8,128)(2,1)S(1)} all-gather(bf16[512,256]{1,0:T(8,128)(2,1)S(1)} %forward.1), channel_id=1, replica_groups=mesh['row'=8,'col'=2,'x'=4,'zl'=4,'core'=2] {'col'}, dimensions={1}, use_global_device_ids=true | all-gather | bytes 786432 | tf_op jit(solution)/shard_map/all_gather | solution.py:404
  36.1 0.2 copy.11
  36.3 0.6 broadcast_in_dim.14
  37.0 10.1 %all-to-all-start = ((bf16[8,16,256]{2,1,0:T(8,128)(2,1)}), bf16[8,16,256]{2,1,0:T(8,128)(2,1)S(1)}, u32[]{:S(2)}, u32[]{:S(2)}) async-start(bf16[8,16,256]{2,1,0:T(8,128)(2,1)} %broadcast_in_dim.14), calls=%async_computation | async-start | bytes 131072 | tf_op jit(solution)/shard_map/all_to_all | solution.py:413
  47.1 0.0 reduce-scatter.2.cloned.1.call-start
  47.2 7.5 %all-to-all-done._.halo = bf16[8,16,256]{2,1,0:T(8,128)(2,1)S(1)} async-done(((bf16[8,16,256]{2,1,0:T(8,128)(2,1)}), bf16[8,16,256]{2,1,0:T(8,128)(2,1)S(1)}, u32[]{:S(2)}, u32[]{:S(2)}) %all-to-all-start) | async-done | bytes 65568 | tf_op jit(solution)/shard_map/all_to_all | solution.py:413
  54.7 1.8 %all-gather.4.cloned.1.call-done = bf16[4096,256]{1,0:T(8,128)(2,1)} async-done(((bf16[512,256]{1,0:T(8,128)(2,1)}), bf16[4096,256]{1,0:T(8,128)(2,1)}) %all-gather.4.cloned.1.call-update) | async-done | bytes 2097168 | tf_op jit(solution)/shard_map/all_gather | solution.py:399
  56.4 1.6 %copy-done = bf16[4096,256]{1,0:T(8,128)(2,1)S(1)} copy-done((bf16[4096,256]{1,0:T(8,128)(2,1)S(1)}, bf16[4096,256]{1,0:T(8,128)(2,1)}, u32[]{:S(2)}) %copy-start) | copy-done | bytes 2097176
  58.0 0.7 sent_weight.1
  58.7 5.9 %collective-permute-start.2 = (bf16[8,256,256]{2,1,0:T(8,128)(2,1)S(1)}, bf16[8,256,256]{2,1,0:T(8,128)(2,1)S(1)}, u32[]{:S(2)}, u32[]{:S(2)}) collective-permute-start(bf16[8,256,256]{2,1,0:T(8,128)(2,1)S(1)} %get-tuple-element.20), channel_id=1, source_target_pairs={{0,1},{1,0},{2,3},{3,2},{4,5},{5,4},{6,7},{7,6},{8,9},{9,8},{10,11... | collective-permute-start | bytes 3145736 | tf_op jit(solution)/shard_map/ppermute | solution.py:382
  64.6 2.3 %collective-permute-done.2.arrived = bf16[8,256,256]{2,1,0:T(8,128)(2,1)S(1)} collective-permute-done((bf16[8,256,256]{2,1,0:T(8,128)(2,1)S(1)}, bf16[8,256,256]{2,1,0:T(8,128)(2,1)S(1)}, u32[]{:S(2)}, u32[]{:S(2)}) %collective-permute-start.2) | collective-permute-done | bytes 1048608 | tf_op jit(solution)/shard_map/ppermute | solution.py:382
  66.9 1.5 %kept_weight.1 = (bf16[4,8,64,256]{3,2,1,0:T(8,128)(2,1)}, f32[8,128]{1,0:T(8,128)S(1)}) custom-call(bf16[256,512]{1,0:T(8,128)(2,1)S(1)} %bitcast.23, bf16[8,512,256]{2,1,0:T(8,128)(2,1)S(1)} %bitcast.16, bf16[8,256,256]{2,1,0:T(8,128)(2,1)S(1)} %collective-permute-done.2.arrived), custom_call_target="tpu_custom_call" | custom-call | flops 536870912 | bytes 4456448 | tf_op jit(solution)/shard_map/kept_weight/pallas_call | solution.py:285
  68.5 1.6 %copy-done.4 = bf16[512,2048]{1,0:T(8,128)(2,1)S(1)} copy-done((bf16[512,2048]{1,0:T(8,128)(2,1)S(1)}, bf16[512,2048]{1,0:T(8,128)(2,1)}, u32[]{:S(2)}) %copy-start.4) | copy-done | bytes 2097176
  70.0 1.3 %gated_grad.1 = (bf16[528,256]{1,0:T(8,128)(2,1)S(1)}, f32[528,256]{1,0:T(8,128)S(1)}) custom-call(s32[1]{0:T(128)} %bitcast.col, bf16[8,512,256]{2,1,0:T(8,128)(2,1)S(1)} %bitcast.17, bf16[8,16,256]{2,1,0:T(8,128)(2,1)S(1)} %all-to-all-done._.halo, bf16[512,2048]{1,0:T(8,128)(2,1)S(1)} %copy-done.4, f32[8,128]{1,0:T(8,128)S(1)} %get-tuple-element.17._), custom_call_target="tpu_custom_call" | custom-call | flops 1107296256 | bytes 5070848 | tf_op jit(solution)/shard_map/gated_grad/pallas_call | solution.py:252
  71.4 14.7 %all-gather.1 = bf16[1056,256]{1,0:T(8,128)(2,1)S(1)} all-gather(bf16[528,256]{1,0:T(8,128)(2,1)S(1)} %get-tuple-element.19), channel_id=3, replica_groups=mesh['row'=8,'col'=2,'x'=4,'zl'=4,'core'=2] {'col'}, dimensions={0}, use_global_device_ids=true | all-gather | bytes 811008 | tf_op jit(solution)/shard_map/all_gather | solution.py:419
  86.1 4.1 %backward.1 = (bf16[3,512,256]{2,1,0:T(8,128)(2,1)}, f32[8,4,8,256]{3,2,1,0:T(8,128)S(1)}) custom-call(s32[1]{0:T(128)} %bitcast.col, f32[528,256]{1,0:T(8,128)S(1)} %get-tuple-element.18.near, bf16[2,528,256]{2,1,0:T(8,128)(2,1)S(1)} %bitcast.21, bf16[3,16,256]{2,1,0:T(8,128)(2,1)S(1)} %collective-permute-done.1.before, bf16[3,512,256]{2,1,0:T(8,128)(2,1)S(1)} %bitcast.20, ...), custom_call_target="tpu_custom_call" | custom-call | flops 20971520 | bytes 2621440 | tf_op jit(solution)/shard_map/backward/pallas_call | solution.py:180
  90.2 11.5 %all_to_all.15.taps = f32[8,4,8,256]{3,2,1,0:T(8,128)S(1)} all-to-all(f32[8,4,8,256]{3,2,1,0:T(8,128)S(1)} %get-tuple-element.24), channel_id=1, replica_groups=mesh['row'=8,'col'=2,'x'=4,'zl'=4,'core'=2] {'x','core'}, dimensions={0} | all-to-all | bytes 524288 | tf_op jit(solution)/shard_map/all_to_all | solution.py:425
  101.7 0.9 copy-done.5
  102.7 0.8 middle.1
  103.5 8.1 %all-to-all-start.2 = ((bf16[4,12,16,256]{3,2,1,0:T(8,128)(2,1)}), bf16[4,12,16,256]{3,2,1,0:T(8,128)(2,1)S(1)}, u32[]{:S(2)}, u32[]{:S(2)}) async-start(bf16[4,12,16,256]{3,2,1,0:T(8,128)(2,1)} %get-tuple-element.26), calls=%async_computation.3 | async-start | bytes 786432 | tf_op jit(solution)/shard_map/all_to_all | solution.py:428
  111.5 9.8 %all-to-all-done.2.refs_2_ = bf16[4,12,16,256]{3,2,1,0:T(8,128)(2,1)S(1)} async-done(((bf16[4,12,16,256]{3,2,1,0:T(8,128)(2,1)}), bf16[4,12,16,256]{3,2,1,0:T(8,128)(2,1)S(1)}, u32[]{:S(2)}, u32[]{:S(2)}) %all-to-all-start.2) | async-done | bytes 393248 | tf_op jit(solution)/shard_map/all_to_all | solution.py:428
  121.4 0.7 last.1
  (21 shorter events, 0.1 us)
Async XLA Ops:
  7.2 49.2 %all-gather.4.cloned.1.call-start = ((), (), s32[]{:S(2)}) async-start(), calls=%async_computation.5 | async-start | bytes 2359296 | tf_op jit(solution)/shard_map/all_gather | solution.py:399
  8.7 10.8 %collective-permute-start.1 = (bf16[3,16,256]{2,1,0:T(8,128)(2,1)S(1)}, bf16[3,16,256]{2,1,0:T(8,128)(2,1)S(1)}, u32[]{:S(2)}, u32[]{:S(2)}) collective-permute-start(bf16[3,16,256]{2,1,0:T(8,128)(2,1)S(1)} %get-tuple-element.30), channel_id=1, source_target_pairs={{0,1},{1,2},{2,3},{3,4},{4,5},{5,6},{6,7},{7,8},{8,9},{9,10},{10,1... | collective-permute-start | bytes 73736 | tf_op jit(solution)/shard_map/ppermute | solution.py:387
  14.8 21.5 %collective-permute-start = (bf16[4,16,256]{2,1,0:T(8,128)(2,1)S(1)}, bf16[4,16,256]{2,1,0:T(8,128)(2,1)S(1)}, u32[]{:S(2)}, u32[]{:S(2)}) collective-permute-start(bf16[4,16,256]{2,1,0:T(8,128)(2,1)S(1)} %pad_maximum_fusion), channel_id=1, source_target_pairs={{1,0},{2,1},{3,2},{4,3},{5,4},{6,5},{7,6},{8,7},{9,8},{10,9},{11,1... | collective-permute-start | bytes 98312 | tf_op jit(solution)/shard_map/ppermute | solution.py:387
  19.5 1.1 copy-start.2
  20.6 0.7 copy-start.6
  21.3 0.7 copy-start.8
  37.0 17.7 %all-to-all-start = ((bf16[8,16,256]{2,1,0:T(8,128)(2,1)}), bf16[8,16,256]{2,1,0:T(8,128)(2,1)S(1)}, u32[]{:S(2)}, u32[]{:S(2)}) async-start(bf16[8,16,256]{2,1,0:T(8,128)(2,1)} %broadcast_in_dim.14), calls=%async_computation | async-start | bytes 131072 | tf_op jit(solution)/shard_map/all_to_all | solution.py:413
  47.1 54.6 %reduce-scatter.2.cloned.1.call-start = ((), (), s32[]{:S(2)}) async-start(), calls=%async_computation.4 | async-start | bytes 1310720 | tf_op jit(solution)/shard_map/reduce_scatter | solution.py:420
  56.4 1.6 %copy-start = (bf16[4096,256]{1,0:T(8,128)(2,1)S(1)}, bf16[4096,256]{1,0:T(8,128)(2,1)}, u32[]{:S(2)}) copy-start(bf16[4096,256]{1,0:T(8,128)(2,1)} %all-gather.4.cloned.1.call-done) | copy-start | bytes 6291460
  58.0 8.9 %copy-start.1 = (bf16[4096,256]{1,0:T(8,128)(2,1)S(1)}, bf16[4096,256]{1,0:T(8,128)(2,1)}, u32[]{:S(2)}) copy-start(bf16[4096,256]{1,0:T(8,128)(2,1)} %all-gather.4.cloned.1.call-done) | copy-start | bytes 6291460
  58.7 8.2 %collective-permute-start.2 = (bf16[8,256,256]{2,1,0:T(8,128)(2,1)S(1)}, bf16[8,256,256]{2,1,0:T(8,128)(2,1)S(1)}, u32[]{:S(2)}, u32[]{:S(2)}) collective-permute-start(bf16[8,256,256]{2,1,0:T(8,128)(2,1)S(1)} %get-tuple-element.20), channel_id=1, source_target_pairs={{0,1},{1,0},{2,3},{3,2},{4,5},{5,4},{6,7},{7,6},{8,9},{9,8},{10,11... | collective-permute-start | bytes 3145736 | tf_op jit(solution)/shard_map/ppermute | solution.py:382
  68.4 1.6 %copy-start.4 = (bf16[512,2048]{1,0:T(8,128)(2,1)S(1)}, bf16[512,2048]{1,0:T(8,128)(2,1)}, u32[]{:S(2)}) copy-start(bf16[512,2048]{1,0:T(8,128)(2,1)} %weight.1) | copy-start | bytes 6291460
  70.0 16.1 %copy-start.3 = (bf16[512,3,256]{2,0,1:T(8,128)(2,1)S(1)}, bf16[512,3,256]{2,0,1:T(8,128)(2,1)}, u32[]{:S(2)}) copy-start(bf16[512,3,256]{2,0,1:T(8,128)(2,1)} %param.5) | copy-start | bytes 2359300
  70.0 16.1 %copy-start.7 = (f32[3,7,256]{2,1,0:T(8,128)S(1)}, f32[3,7,256]{2,1,0:T(8,128)}, u32[]{:S(2)}) copy-start(f32[3,7,256]{2,1,0:T(8,128)} %feat_taps.3) | copy-start | bytes 64516
  70.0 16.1 %copy-start.9 = (f32[7,256]{1,0:T(8,128)S(1)}, f32[7,256]{1,0:T(8,128)}, u32[]{:S(2)}) copy-start(f32[7,256]{1,0:T(8,128)} %inner_taps.3) | copy-start | bytes 21508
  101.7 1.0 copy-start.5
  103.5 17.9 %all-to-all-start.2 = ((bf16[4,12,16,256]{3,2,1,0:T(8,128)(2,1)}), bf16[4,12,16,256]{3,2,1,0:T(8,128)(2,1)S(1)}, u32[]{:S(2)}, u32[]{:S(2)}) async-start(bf16[4,12,16,256]{3,2,1,0:T(8,128)(2,1)} %get-tuple-element.26), calls=%async_computation.3 | async-start | bytes 786432 | tf_op jit(solution)/shard_map/all_to_all | solution.py:428
Sparse Core Ops, SparseCore 0:
  10.1 46.2 all-gather.3
  68.6 26.6 reduce-scatter.1

commit v9 on v8

--- a/solution.py
+++ b/solution.py
@@ -78,7 +78,7 @@
     return total
 
 
-def forward_kernel(before, own, feat_taps, inner_taps, gated, feats, query, product):
+def forward_kernel(_, before, own, feat_taps, inner_taps, gated, feats, query, product):
     rows = own.shape[1]
     load_features(before, own, feats)
     for start, count in spread(rows + LEAD):
@@ -92,7 +92,7 @@
         ).astype(BF16)
 
 
-def forward(before, own, feat_taps, inner_taps):
+def forward(place, before, own, feat_taps, inner_taps):
     _, rows, channels = own.shape
     return call(
         forward_kernel,
@@ -100,7 +100,9 @@
         60 * rows * channels,
         8 * rows * channels,
         grid=(channels // LANES,),
-        in_specs=[lane_spec(3, HALO), lane_spec(3, rows), lane_spec(3, TAPS), lane_spec(TAPS)],
+        in_specs=[
+            SCALAR, lane_spec(3, HALO), lane_spec(3, rows), lane_spec(3, TAPS), lane_spec(TAPS)
+        ],
         out_specs=lane_spec(rows),
         out_shape=jax.ShapeDtypeStruct((rows, channels), BF16),
         scratch_shapes=[
@@ -108,11 +110,11 @@
             pltpu.VMEM((rows + LEAD, LANES), F32),
             pltpu.VMEM((rows + LEAD, LANES), F32),
         ],
-    )(before, own, feat_taps, inner_taps)
+    )(place, before, own, feat_taps, inner_taps)
 
 
 def backward_kernel(
-    col, near, far, before, own, after, feat_taps, inner_taps, _,
+    place, near, far, before, own, after, feat_taps, inner_taps, _,
     grads, tap_sums, feats, query, key, value, product, grad_window, grad_mixed,
 ):
     rows = own.shape[1]
@@ -125,7 +127,7 @@
         product[start : start + count, :] = parts[1] * parts[2]
     for start, count in spread(rows + HALO):
         total = near[start : start + count, :] + far[
-            1 - col[0], start : start + count, :
+            1 - place[0], start : start + count, :
         ].astype(F32)
         grad_window[start : start + count, :] = (
             total * query[LEAD + start : LEAD + start + count, :]
@@ -175,7 +177,7 @@
     put(3, sums)
 
 
-def backward(copies, col, near, far, before, own, after, feat_taps, inner_taps, later):
+def backward(copies, place, near, far, before, own, after, feat_taps, inner_taps, later):
     _, rows, channels = own.shape
     return call(
         backward_kernel,
@@ -198,7 +200,7 @@
             pltpu.VMEM((rows + HALO, LANES), F32),
             pltpu.VMEM((3, rows + HALO, LANES), F32),
         ],
-    )(col, near, far, before, own, after, feat_taps, inner_taps, later)
+    )(place, near, far, before, own, after, feat_taps, inner_taps, later)
 
 
 TOKEN = jax.ShapeDtypeStruct((8, LANES), F32)
@@ -224,7 +226,7 @@
     )(gated, grads, later)
 
 
-def gated_grad_kernel(col, grads, halo, weight, _, far, near):
+def gated_grad_kernel(place, grads, halo, weight, _, far, near):
     half = near.shape[1]
     blocks = range(grads.shape[0])
     wide = jnp.concatenate(
@@ -234,7 +236,7 @@
         ],
         axis=0,
     )
-    for out, which in ((far, 1 - col[0]), (near, col[0])):
+    for out, which in ((far, 1 - place[0]), (near, place[0])):
         total = lax.dot_general(
             wide,
             weight[pl.ds(pl.multiple_of(which * half, half), half), :],
@@ -244,7 +246,7 @@
         out[...] = total.astype(out.dtype)
 
 
-def gated_grad(col, grads, halo, weight, later):
+def gated_grad(place, grads, halo, weight, later):
     blocks, rows, width = grads.shape
     rows = rows + halo.shape[1]
     channels = weight.shape[0]
@@ -260,7 +262,7 @@
             jax.ShapeDtypeStruct((rows, half), BF16),
             jax.ShapeDtypeStruct((rows, half), F32),
         ],
-    )(col, grads, halo, weight, later)
+    )(place, grads, halo, weight, later)
 
 
 def kept_weight_kernel(gated, grads, arrived, out, done, held, sems):
@@ -337,7 +339,7 @@
     )(pair, taps)
 
 
-def last_kernel(scale, z, taps, arrived, out, out_feat, out_inner):
+def last_kernel(scale, place, taps, arrived, out, out_feat, out_inner):
     parts, _, _, width = arrived.shape
     blocks = out.shape[1] // width
     for b in range(blocks):
@@ -347,13 +349,13 @@
         out[:, b * width : (b + 1) * width] = (total * scale).astype(BF16)
     total = taps[...]
     for part in range(parts):
-        total = total + jnp.where(z[0] == part, 0.0, rejoined(arrived[part, blocks:]))
+        total = total + jnp.where(place[1] == part, 0.0, rejoined(arrived[part, blocks:]))
     total = total * scale
     out_feat[...] = total[:3, :TAPS]
     out_inner[...] = total[3, :TAPS]
 
 
-def last(scale, z, taps, arrived):
+def last(scale, place, taps, arrived):
     parts, count, channels, width = arrived.shape
     blocks = count - taps.shape[0]
     return call(
@@ -368,7 +370,7 @@
             jax.ShapeDtypeStruct((3, TAPS, width), F32),
             jax.ShapeDtypeStruct((TAPS, width), F32),
         ],
-    )(z, taps, arrived)
+    )(place, taps, arrived)
 
 
 def ctx_permute(value, target):
@@ -394,13 +396,13 @@
     nx, nz, nc = (lax.axis_size(a) for a in CTX)
     inv_root = 1.0 / math.sqrt(rows * nx * nz * nc)
     core = lax.axis_index("core")
-    col, z = (jnp.full((1,), lax.axis_index(a), jnp.int32) for a in ("col", "zl"))
+    place = jnp.stack([lax.axis_index("col"), lax.axis_index("zl")])
 
     grads = lax.all_gather(out_grad, "row", axis=0)
 
     own = jnp.transpose(featured, (1, 0, 2))
     before = ctx_shift(own[:, rows - HALO :], 1)
-    gated = forward(before, own, feat_taps, inner_taps)
+    gated = forward(place, before, own, feat_taps, inner_taps)
     both = lax.all_gather(gated, "col", axis=1, tiled=True)
     channels = both.shape[1]
     split = both.T.reshape(nx * nz, nc, channels // (nx * nz * nc), rows)
@@ -414,19 +416,19 @@
 
     sent, done = sent_weight(sent, grads, halo)
     arrived = ctx_permute(sent, lambda x, z, c: (x, z, 1 - c))
-    far, near = gated_grad(col, grads, halo, out_weight, done)
+    far, near = gated_grad(place, grads, halo, out_weight, done)
     pair, done = kept_weight(nx, kept, grads, arrived)
     far = lax.all_gather(far, "col", axis=0)
     summed = lax.psum_scatter(pair, "x", scatter_dimension=0)
 
     grad_own, taps = backward(
-        nx * nc, col, near, far, before, own, after, feat_taps, inner_taps, done
+        nx * nc, place, near, far, before, own, after, feat_taps, inner_taps, done
     )
     taps = lax.all_to_all(taps, ("x", "core"), split_axis=0, concat_axis=0)
 
     pieces, taps = middle(nz, summed, taps)
     pieces = lax.all_to_all(pieces, "zl", split_axis=0, concat_axis=0)
-    grad_weight, grad_feat_taps, grad_inner_taps = last(inv_root, z, taps, pieces)
+    grad_weight, grad_feat_taps, grad_inner_taps = last(inv_root, place, taps, pieces)
     return jnp.transpose(grad_own, (1, 0, 2)), grad_weight, grad_feat_taps, grad_inner_taps
 
 

time: 131 us -> 132 us (level)
  blocking collectives: 39 us -> 56.9 us
  waiting for transfers between devices: 22 us -> 12.3 us
  starting transfers between devices: 34.2 us -> 25.8 us
    all_to_all x0 -> x1, blocking collectives: none -> 18.1 us  [body(): pieces = lax.all_to_all(pieces, 'zl', split_axis=0, concat_axis=0)]
    all_to_all x1 -> x0, waiting for transfers between devices: 9.84 us -> none  [body(): pieces = lax.all_to_all(pieces, 'zl', split_axis=0, concat_axis=0)]
    all_to_all x1 -> x0, starting transfers between devices: 8.08 us -> none  [body(): pieces = lax.all_to_all(pieces, 'zl', split_axis=0, concat_axis=0)]
  transfers between devices with their start and end apart: 7 -> 6, of which waited for: 4 -> 3; matrix products, arithmetic and copies ran while one was open for 2% -> 2% of each run, Pallas kernels for 5% -> 6%
where the time goes in v9:
time: 132 us; the launch traced here: 130 us
  blocking collectives  56.9 us (43%)
  starting transfers between devices  25.8 us (20%)
  between operations  14.2 us (11%)
  waiting for transfers between devices  12.3 us (9%)
  Pallas kernels  11.6 us (9%)
  local copies, waits for them, and re-layouts  9.07 us (7%)
    all_to_all x1, blocking collectives, body(): pieces = lax.all_to_all(pieces, 'zl', split_axis=0, concat_axis=0)  18.1 us
    all_gather x1, blocking collectives, body(): far = lax.all_gather(far, 'col', axis=0)  13.8 us
    all_gather x1, blocking collectives, body(): both = lax.all_gather(gated, 'col', axis=1, tiled=True)  12.8 us
    all_to_all x1, blocking collectives, body(): taps = lax.all_to_all(taps, ('x', 'core'), split_axis=0, concat_axis=0)  12.2 us
    all_to_all x1, starting transfers between devices, body(): halo = lax.all_to_all(halo, 'row', split_axis=0, concat_axis=0)  10.1 us
    ppermute x2, starting transfers between devices, ctx_shift(): lax.ppermute(value, CTX, [(i, i + steps) for i in range(count) if 0 <= i...  10.1 us
    all_to_all x1, waiting for transfers between devices, body(): halo = lax.all_to_all(halo, 'row', split_axis=0, concat_axis=0)  7.45 us
    unnamed x20, local copies, waits for them, and re-layouts  6.71 us
  transfers between devices with their start and end apart: 6, of which 3 were waited for; matrix products, arithmetic and copies ran while one was open for 2% of the time, Pallas kernels for 6%

profile of v9, /device:TPU:1, one launch (start us, length us, event | category | flops | bytes accessed | tf_op | source)
XLA Modules:
  0.0 129.9 jit_solution(15663261898444707989)
XLA Ops:
  7.2 0.0 all-gather.4.cloned.1.call-start
  7.2 0.7 all-gather.4.cloned.1.call-update
  7.9 0.8 fusion
  8.7 5.4 %collective-permute-start.1 = (bf16[3,16,256]{2,1,0:T(8,128)(2,1)S(1)}, bf16[3,16,256]{2,1,0:T(8,128)(2,1)S(1)}, u32[]{:S(2)}, u32[]{:S(2)}) collective-permute-start(bf16[3,16,256]{2,1,0:T(8,128)(2,1)S(1)} %get-tuple-element.30), channel_id=1, source_target_pairs={{0,1},{1,2},{2,3},{3,4},{4,5},{5,6},{6,7},{7,8},{8,9},{9,10},{10,1... | collective-permute-start | bytes 73736 | tf_op jit(solution)/shard_map/ppermute | solution.py:389
  14.1 0.7 slice_bitcast_fusion.1
  14.8 4.7 %collective-permute-start = (bf16[4,16,256]{2,1,0:T(8,128)(2,1)S(1)}, bf16[4,16,256]{2,1,0:T(8,128)(2,1)S(1)}, u32[]{:S(2)}, u32[]{:S(2)}) collective-permute-start(bf16[4,16,256]{2,1,0:T(8,128)(2,1)S(1)} %pad_maximum_fusion), channel_id=1, source_target_pairs={{1,0},{2,1},{3,2},{4,3},{5,4},{6,5},{7,6},{8,7},{9,8},{10,9},{11,1... | collective-permute-start | bytes 98312 | tf_op jit(solution)/shard_map/ppermute | solution.py:389
  19.5 0.1 pad_add_fusion._.place.refs_0_
  19.5 1.1 copy-done.2
  20.7 0.7 copy-done.6
  21.4 0.7 copy-done.8
  22.1 1.8 %forward.1 = bf16[512,256]{1,0:T(8,128)(2,1)S(1)} custom-call(s32[2]{0:T(128)S(1)} %pad_add_fusion._.place.refs_0_, bf16[3,16,256]{2,1,0:T(8,128)(2,1)S(1)} %collective-permute-done.1.before, bf16[3,512,256]{2,1,0:T(8,128)(2,1)S(1)} %bitcast.19, f32[3,7,256]{2,1,0:T(8,128)S(1)} %copy-done.6, f32[7,256]{1,0:T(8,128)S(1)} %copy-done.8), custom_call_target="tpu_custom_call" | custom-call | flops 7864320 | bytes 1048576 | tf_op jit(solution)/shard_map/forward/pallas_call | solution.py:97
  23.9 12.8 %all_gather.17 = bf16[512,512]{1,0:T(8,128)(2,1)S(1)} all-gather(bf16[512,256]{1,0:T(8,128)(2,1)S(1)} %forward.1), channel_id=1, replica_groups=mesh['row'=8,'col'=2,'x'=4,'zl'=4,'core'=2] {'col'}, dimensions={1}, use_global_device_ids=true | all-gather | bytes 786432 | tf_op jit(solution)/shard_map/all_gather | solution.py:406
  36.6 0.2 copy.11
  36.9 0.6 broadcast_in_dim.7
  37.5 10.1 %all-to-all-start = ((bf16[8,16,256]{2,1,0:T(8,128)(2,1)}), bf16[8,16,256]{2,1,0:T(8,128)(2,1)S(1)}, u32[]{:S(2)}, u32[]{:S(2)}) async-start(bf16[8,16,256]{2,1,0:T(8,128)(2,1)} %broadcast_in_dim.7), calls=%async_computation | async-start | bytes 131072 | tf_op jit(solution)/shard_map/all_to_all | solution.py:415
  47.6 0.0 reduce-scatter.2.cloned.1.call-start
  47.7 7.4 %all-to-all-done._.halo = bf16[8,16,256]{2,1,0:T(8,128)(2,1)S(1)} async-done(((bf16[8,16,256]{2,1,0:T(8,128)(2,1)}), bf16[8,16,256]{2,1,0:T(8,128)(2,1)S(1)}, u32[]{:S(2)}, u32[]{:S(2)}) %all-to-all-start) | async-done | bytes 65568 | tf_op jit(solution)/shard_map/all_to_all | solution.py:415
  55.2 1.9 %all-gather.4.cloned.1.call-done = bf16[4096,256]{1,0:T(8,128)(2,1)} async-done(((bf16[512,256]{1,0:T(8,128)(2,1)}), bf16[4096,256]{1,0:T(8,128)(2,1)}) %all-gather.4.cloned.1.call-update) | async-done | bytes 2097168 | tf_op jit(solution)/shard_map/all_gather | solution.py:401
  57.0 1.6 %copy-done = bf16[4096,256]{1,0:T(8,128)(2,1)S(1)} copy-done((bf16[4096,256]{1,0:T(8,128)(2,1)S(1)}, bf16[4096,256]{1,0:T(8,128)(2,1)}, u32[]{:S(2)}) %copy-start) | copy-done | bytes 2097176
  58.6 0.7 sent_weight.1
  59.4 5.5 %collective-permute-start.2 = (bf16[8,256,256]{2,1,0:T(8,128)(2,1)S(1)}, bf16[8,256,256]{2,1,0:T(8,128)(2,1)S(1)}, u32[]{:S(2)}, u32[]{:S(2)}) collective-permute-start(bf16[8,256,256]{2,1,0:T(8,128)(2,1)S(1)} %get-tuple-element.20), channel_id=1, source_target_pairs={{0,1},{1,0},{2,3},{3,2},{4,5},{5,4},{6,7},{7,6},{8,9},{9,8},{10,11... | collective-permute-start | bytes 3145736 | tf_op jit(solution)/shard_map/ppermute | solution.py:384
  64.9 2.3 %collective-permute-done.2.arrived = bf16[8,256,256]{2,1,0:T(8,128)(2,1)S(1)} collective-permute-done((bf16[8,256,256]{2,1,0:T(8,128)(2,1)S(1)}, bf16[8,256,256]{2,1,0:T(8,128)(2,1)S(1)}, u32[]{:S(2)}, u32[]{:S(2)}) %collective-permute-start.2) | collective-permute-done | bytes 1048608 | tf_op jit(solution)/shard_map/ppermute | solution.py:384
  67.1 1.5 %kept_weight.1 = (bf16[4,8,64,256]{3,2,1,0:T(8,128)(2,1)}, f32[8,128]{1,0:T(8,128)S(1)}) custom-call(bf16[256,512]{1,0:T(8,128)(2,1)S(1)} %bitcast.23, bf16[8,512,256]{2,1,0:T(8,128)(2,1)S(1)} %bitcast.16, bf16[8,256,256]{2,1,0:T(8,128)(2,1)S(1)} %collective-permute-done.2.arrived), custom_call_target="tpu_custom_call" | custom-call | flops 536870912 | bytes 4456448 | tf_op jit(solution)/shard_map/kept_weight/pallas_call | solution.py:287
  68.7 0.0 reduce-scatter.2.cloned.1.call-update
  68.7 1.6 %copy-done.4 = bf16[512,2048]{1,0:T(8,128)(2,1)S(1)} copy-done((bf16[512,2048]{1,0:T(8,128)(2,1)S(1)}, bf16[512,2048]{1,0:T(8,128)(2,1)}, u32[]{:S(2)}) %copy-start.4) | copy-done | bytes 2097176
  70.3 1.9 %gated_grad.1 = (bf16[528,256]{1,0:T(8,128)(2,1)S(1)}, f32[528,256]{1,0:T(8,128)S(1)}) custom-call(s32[2]{0:T(128)S(1)} %pad_add_fusion._.place.refs_0_, bf16[8,512,256]{2,1,0:T(8,128)(2,1)S(1)} %bitcast.17, bf16[8,16,256]{2,1,0:T(8,128)(2,1)S(1)} %all-to-all-done._.halo, bf16[512,2048]{1,0:T(8,128)(2,1)S(1)} %copy-done.4, f32[8,128]{1,0:T(8,128)S(1)} %get-tuple-element.17._), custom_call_target="tpu_custom_call" | custom-call | flops 1107296256 | bytes 5070848 | tf_op jit(solution)/shard_map/gated_grad/pallas_call | solution.py:254
  72.2 13.8 %all-gather.1 = bf16[1056,256]{1,0:T(8,128)(2,1)S(1)} all-gather(bf16[528,256]{1,0:T(8,128)(2,1)S(1)} %get-tuple-element.19), channel_id=3, replica_groups=mesh['row'=8,'col'=2,'x'=4,'zl'=4,'core'=2] {'col'}, dimensions={0}, use_global_device_ids=true | all-gather | bytes 811008 | tf_op jit(solution)/shard_map/all_gather | solution.py:421
  86.0 4.5 %backward.1 = (bf16[3,512,256]{2,1,0:T(8,128)(2,1)}, f32[8,4,8,256]{3,2,1,0:T(8,128)S(1)}) custom-call(s32[2]{0:T(128)S(1)} %pad_add_fusion._.place.refs_0_, f32[528,256]{1,0:T(8,128)S(1)} %get-tuple-element.18.near, bf16[2,528,256]{2,1,0:T(8,128)(2,1)S(1)} %bitcast.21, bf16[3,16,256]{2,1,0:T(8,128)(2,1)S(1)} %collective-permute-done.1.before, ...), custom_call_target="tpu_custom_call" | custom-call | flops 20971520 | bytes 2621440 | tf_op jit(solution)/shard_map/backward/pallas_call | solution.py:182
  90.5 12.2 %all_to_all.15.taps = f32[8,4,8,256]{3,2,1,0:T(8,128)S(1)} all-to-all(f32[8,4,8,256]{3,2,1,0:T(8,128)S(1)} %get-tuple-element.24), channel_id=1, replica_groups=mesh['row'=8,'col'=2,'x'=4,'zl'=4,'core'=2] {'x','core'}, dimensions={0} | all-to-all | bytes 524288 | tf_op jit(solution)/shard_map/all_to_all | solution.py:427
  102.7 0.9 copy-done.5
  103.7 18.1 %all_to_all.16.refs_2_ = bf16[4,12,16,256]{3,2,1,0:T(8,128)(2,1)S(1)} all-to-all(bf16[4,12,16,256]{3,2,1,0:T(8,128)(2,1)S(1)} %get-tuple-element.26), channel_id=1, replica_groups=mesh['row'=8,'col'=2,'x'=4,'zl'=4,'core'=2] {'zl'}, dimensions={0} | all-to-all | bytes 786432 | tf_op jit(solution)/shard_map/all_to_all | solution.py:430
  121.8 1.2 last.1
  (21 shorter events, 0.1 us)
Async XLA Ops:
  7.2 49.9 %all-gather.4.cloned.1.call-start = ((), (), s32[]{:S(2)}) async-start(), calls=%async_computation.5 | async-start | bytes 2359296 | tf_op jit(solution)/shard_map/all_gather | solution.py:401
  8.7 10.9 %collective-permute-start.1 = (bf16[3,16,256]{2,1,0:T(8,128)(2,1)S(1)}, bf16[3,16,256]{2,1,0:T(8,128)(2,1)S(1)}, u32[]{:S(2)}, u32[]{:S(2)}) collective-permute-start(bf16[3,16,256]{2,1,0:T(8,128)(2,1)S(1)} %get-tuple-element.30), channel_id=1, source_target_pairs={{0,1},{1,2},{2,3},{3,4},{4,5},{5,6},{6,7},{7,8},{8,9},{9,10},{10,1... | collective-permute-start | bytes 73736 | tf_op jit(solution)/shard_map/ppermute | solution.py:389
  14.8 22.1 %collective-permute-start = (bf16[4,16,256]{2,1,0:T(8,128)(2,1)S(1)}, bf16[4,16,256]{2,1,0:T(8,128)(2,1)S(1)}, u32[]{:S(2)}, u32[]{:S(2)}) collective-permute-start(bf16[4,16,256]{2,1,0:T(8,128)(2,1)S(1)} %pad_maximum_fusion), channel_id=1, source_target_pairs={{1,0},{2,1},{3,2},{4,3},{5,4},{6,5},{7,6},{8,7},{9,8},{10,9},{11,1... | collective-permute-start | bytes 98312 | tf_op jit(solution)/shard_map/ppermute | solution.py:389
  19.5 1.1 copy-start.2
  20.7 0.7 copy-start.6
  21.4 0.7 copy-start.8
  37.5 17.7 %all-to-all-start = ((bf16[8,16,256]{2,1,0:T(8,128)(2,1)}), bf16[8,16,256]{2,1,0:T(8,128)(2,1)S(1)}, u32[]{:S(2)}, u32[]{:S(2)}) async-start(bf16[8,16,256]{2,1,0:T(8,128)(2,1)} %broadcast_in_dim.7), calls=%async_computation | async-start | bytes 131072 | tf_op jit(solution)/shard_map/all_to_all | solution.py:415
  47.6 55.1 %reduce-scatter.2.cloned.1.call-start = ((), (), s32[]{:S(2)}) async-start(), calls=%async_computation.4 | async-start | bytes 1310720 | tf_op jit(solution)/shard_map/reduce_scatter | solution.py:422
  57.0 1.6 %copy-start = (bf16[4096,256]{1,0:T(8,128)(2,1)S(1)}, bf16[4096,256]{1,0:T(8,128)(2,1)}, u32[]{:S(2)}) copy-start(bf16[4096,256]{1,0:T(8,128)(2,1)} %all-gather.4.cloned.1.call-done) | copy-start | bytes 6291460
  58.6 8.5 %copy-start.1 = (bf16[4096,256]{1,0:T(8,128)(2,1)S(1)}, bf16[4096,256]{1,0:T(8,128)(2,1)}, u32[]{:S(2)}) copy-start(bf16[4096,256]{1,0:T(8,128)(2,1)} %all-gather.4.cloned.1.call-done) | copy-start | bytes 6291460
  59.4 7.8 %collective-permute-start.2 = (bf16[8,256,256]{2,1,0:T(8,128)(2,1)S(1)}, bf16[8,256,256]{2,1,0:T(8,128)(2,1)S(1)}, u32[]{:S(2)}, u32[]{:S(2)}) collective-permute-start(bf16[8,256,256]{2,1,0:T(8,128)(2,1)S(1)} %get-tuple-element.20), channel_id=1, source_target_pairs={{0,1},{1,0},{2,3},{3,2},{4,5},{5,4},{6,7},{7,6},{8,9},{9,8},{10,11... | collective-permute-start | bytes 3145736 | tf_op jit(solution)/shard_map/ppermute | solution.py:384
  68.7 1.6 %copy-start.4 = (bf16[512,2048]{1,0:T(8,128)(2,1)S(1)}, bf16[512,2048]{1,0:T(8,128)(2,1)}, u32[]{:S(2)}) copy-start(bf16[512,2048]{1,0:T(8,128)(2,1)} %weight.1) | copy-start | bytes 6291460
  70.3 15.7 %copy-start.3 = (bf16[512,3,256]{2,0,1:T(8,128)(2,1)S(1)}, bf16[512,3,256]{2,0,1:T(8,128)(2,1)}, u32[]{:S(2)}) copy-start(bf16[512,3,256]{2,0,1:T(8,128)(2,1)} %param.5) | copy-start | bytes 2359300
  70.3 15.7 %copy-start.7 = (f32[3,7,256]{2,1,0:T(8,128)S(1)}, f32[3,7,256]{2,1,0:T(8,128)}, u32[]{:S(2)}) copy-start(f32[3,7,256]{2,1,0:T(8,128)} %feat_taps.3) | copy-start | bytes 64516
  70.3 15.7 %copy-start.9 = (f32[7,256]{1,0:T(8,128)S(1)}, f32[7,256]{1,0:T(8,128)}, u32[]{:S(2)}) copy-start(f32[7,256]{1,0:T(8,128)} %inner_taps.3) | copy-start | bytes 21508
  102.7 1.0 copy-start.5
Sparse Core Ops, SparseCore 0:
  10.1 46.9 all-gather.3
  68.8 26.0 reduce-scatter.1

commit v10 on v7

--- a/solution.py
+++ b/solution.py
@@ -35,6 +35,10 @@
 UNREAD = pl.BlockSpec(memory_space=pl.ANY)
 IN_HBM = pl.BlockSpec(memory_space=pltpu.HBM)
 IN_VMEM = pl.BlockSpec(memory_space=pltpu.VMEM)
+
+
+def in_hbm(value):
+    return pltpu.with_memory_space_constraint(value, pltpu.HBM)
 
 
 def call(kernel, name, flops, moved, **kwargs):
@@ -98,7 +102,9 @@
         60 * rows * channels,
         8 * rows * channels,
         grid=(channels // LANES,),
-        in_specs=[lane_spec(3, HALO), lane_spec(3, rows), lane_spec(3, TAPS), lane_spec(TAPS)],
+        in_specs=[
+            lane_spec(3, HALO), lane_spec(3, rows), lane_spec(3, TAPS), lane_spec(TAPS)
+        ],
         out_specs=lane_spec(rows),
         out_shape=jax.ShapeDtypeStruct((rows, channels), BF16),
         scratch_shapes=[
@@ -214,89 +220,70 @@
 TOKEN = jax.ShapeDtypeStruct((8, LANES), F32)
 
 
-def sent_weight_kernel(gated, grads, sent, done):
+def products_kernel(
+    col, core, own, other, grads, weight, far, near, out, done, held, held_weight, sems, weight_sems
+):
+    half = near.shape[1]
+    fetches = [
+        pltpu.make_async_copy(
+            weight.at[pl.ds(pl.multiple_of(which * half, half), half), :],
+            held_weight.at[at],
+            weight_sems.at[at],
+        )
+        for at, which in enumerate((1 - col[0], col[0]))
+    ]
+    for copy in fetches:
+        copy.start()
     done[...] = jnp.zeros_like(done)
-    for b in range(grads.shape[0]):
-        sent[b] = jnp.dot(gated[...], grads[b], preferred_element_type=F32).astype(BF16)
-
-
-def sent_weight(gated, grads):
-    channels, rows = gated.shape
+    blocks, parts, size, _ = held.shape
+    mine = [2 * b + core[0] for b in range(blocks)]
+    copies = []
+    for b in range(blocks):
+        total = jnp.dot(own[...], grads[mine[b]], preferred_element_type=F32)
+        total = total + jnp.dot(
+            other[...], grads[4 * b + 1 - mine[b]], preferred_element_type=F32
+        )
+        for part in range(parts):
+            held[b, part] = total[part * size : (part + 1) * size].astype(BF16)
+        copies.append(pltpu.make_async_copy(held.at[b], out.at[:, b], sems.at[b]))
+        copies[-1].start()
+    wide = jnp.concatenate([grads[at] for at in mine], axis=1)
+    for at, result in enumerate((far, near)):
+        fetches[at].wait()
+        total = lax.dot_general(
+            wide, held_weight[at], (((1,), (1,)), ((), ())), preferred_element_type=F32
+        )
+        result[...] = total.astype(result.dtype)
+    for copy in copies:
+        copy.wait()
+
+
+def products(parts, col, core, own, other, grads, weight):
+    channels, rows = own.shape
     blocks, _, width = grads.shape
+    blocks = blocks // 2
+    half = weight.shape[0] // 2
+    size = channels // parts
     return call(
-        sent_weight_kernel,
-        "sent_weight",
-        2 * rows * channels * blocks * width,
-        2 * blocks * width * (rows + channels) + 2 * rows * channels,
-        in_specs=[IN_VMEM] * 2,
-        out_specs=[IN_VMEM] * 2,
-        out_shape=[jax.ShapeDtypeStruct((blocks, channels, width), BF16), TOKEN],
-    )(gated, grads)
-
-
-def gated_grad_kernel(col, grads, weight, _, far, near):
-    half = near.shape[1]
-    wide = jnp.concatenate([grads[b] for b in range(grads.shape[0])], axis=1)
-    for out, which in ((far, 1 - col[0]), (near, col[0])):
-        total = lax.dot_general(
-            wide,
-            weight[pl.ds(pl.multiple_of(which * half, half), half), :],
-            (((1,), (1,)), ((), ())),
-            preferred_element_type=F32,
-        )
-        out[...] = total.astype(out.dtype)
-
-
-def gated_grad(col, grads, weight, after):
-    blocks, rows, width = grads.shape
-    channels = weight.shape[0]
-    half = channels // 2
-    return call(
-        gated_grad_kernel,
-        "gated_grad",
-        2 * rows * channels * blocks * width,
-        2 * blocks * width * (rows + channels) + 6 * rows * half,
-        in_specs=[SCALAR, IN_VMEM, IN_VMEM, UNREAD],
-        out_specs=[IN_VMEM] * 2,
+        products_kernel,
+        "products",
+        4 * rows * (channels + half) * blocks * width,
+        4 * blocks * width * (rows + channels) + 4 * rows * channels,
+        in_specs=[SCALAR] * 2 + [IN_VMEM] * 3 + [IN_HBM],
+        out_specs=[IN_VMEM, IN_VMEM, IN_HBM, IN_VMEM],
         out_shape=[
             jax.ShapeDtypeStruct((rows, half), BF16),
             jax.ShapeDtypeStruct((rows, half), F32),
-        ],
-    )(col, grads, weight, after)
-
-
-def kept_weight_kernel(gated, grads, arrived, out, done, held, sems):
-    done[...] = jnp.zeros_like(done)
-    blocks, parts, size, _ = held.shape
-    copies = []
-    for b in range(blocks):
-        total = jnp.dot(gated[...], grads[b], preferred_element_type=F32)
-        total = (total + arrived[b].astype(F32)).astype(BF16)
-        for part in range(parts):
-            held[b, part] = total[part * size : (part + 1) * size]
-        copies.append(pltpu.make_async_copy(held.at[b], out.at[:, b], sems.at[b]))
-        copies[-1].start()
-    for copy in copies:
-        copy.wait()
-
-
-def kept_weight(parts, gated, grads, arrived):
-    channels, rows = gated.shape
-    blocks, _, width = grads.shape
-    size = channels // parts
-    return call(
-        kept_weight_kernel,
-        "kept_weight",
-        2 * rows * channels * blocks * width,
-        2 * blocks * width * (rows + 2 * channels) + 2 * rows * channels,
-        in_specs=[IN_VMEM] * 3,
-        out_specs=[IN_HBM, IN_VMEM],
-        out_shape=[jax.ShapeDtypeStruct((parts, blocks, size, width), BF16), TOKEN],
+            pltpu.HBM((parts, blocks, size, width), BF16),
+            TOKEN,
+        ],
         scratch_shapes=[
             pltpu.VMEM((blocks, parts, size, width), BF16),
+            pltpu.VMEM((2, half, blocks * width), BF16),
             pltpu.SemaphoreType.DMA((blocks,)),
-        ],
-    )(gated, grads, arrived)
+            pltpu.SemaphoreType.DMA((2,)),
+        ],
+    )(col, core, own, other, grads, in_hbm(weight))
 
 
 def two_roundings(sums):
@@ -407,10 +394,11 @@
     rows = featured.shape[0]
     nx, nz, nc = (lax.axis_size(a) for a in CTX)
     inv_root = 1.0 / math.sqrt(rows * nx * nz * nc)
-    core = lax.axis_index("core")
-    col, z = (jnp.full((1,), lax.axis_index(a), jnp.int32) for a in ("col", "zl"))
-
-    grads = lax.all_gather(out_grad, "row", axis=0)
+    col, core, z = (
+        jnp.full((1,), lax.axis_index(a), jnp.int32) for a in ("col", "core", "zl")
+    )
+
+    grads = lax.all_gather(out_grad, ("row", "core"), axis=0)
 
     own = jnp.transpose(featured, (1, 0, 2))
     before = ctx_shift(own[:, rows - HALO :], 1)
@@ -420,15 +408,13 @@
     split = both.T.reshape(nx * nz, nc, channels // (nx * nz * nc), rows)
     kept, sent = (
         lax.dynamic_index_in_dim(split, c, 1, keepdims=False).reshape(channels // nc, rows)
-        for c in (core, 1 - core)
-    )
-
-    sent, done = sent_weight(sent, grads)
+        for c in (core[0], 1 - core[0])
+    )
     arrived = ctx_permute(sent, lambda x, z, c: (x, z, 1 - c))
-    far, near = gated_grad(col, grads, out_weight, done)
-    pair, done = kept_weight(nx, kept, grads, arrived)
+
+    far, near, pair, done = products(nx, col, core, kept, arrived, grads, out_weight)
+    summed = lax.psum_scatter(pair, "x", scatter_dimension=0)
     far = lax.all_gather(far, "col", axis=0)
-    summed = lax.psum_scatter(pair, "x", scatter_dimension=0)
 
     grad_own, head, tail, taps = backward(
         nx * nc, col, near, far, before, own, feat_taps, inner_taps, done

time: 129 us -> 126 us (0.977)
  starting transfers between devices: 21.4 us -> 18.1 us
  Pallas kernels: 10.3 us -> 11.9 us
    ppermute x1, starting transfers between devices: 6.21 us -> 2.98 us  [ctx_permute(): return lax.ppermute(value, CTX, pairs)]
    pallas_call x3 -> x1, Pallas kernels: 3.48 us -> 5.05 us  [products(): call(products_kernel, 'products', 4 * rows * (channels + half) * blocks *...]
    unnamed x20 -> x16, local copies, waits for them, and re-layouts: 6.71 us -> 5.72 us
  transfers between devices with their start and end apart: 6 -> 6, of which waited for: 5 -> 5; matrix products, arithmetic and copies ran while one was open for 1% -> 1% of each run, Pallas kernels for 5% -> 4%
where the time goes in v10:
time: 126 us; the launch traced here: 125 us
  blocking collectives  39.9 us (32%)
  waiting for transfers between devices  34.4 us (27%)
  starting transfers between devices  18.1 us (14%)
  between operations  14.1 us (11%)
  Pallas kernels  11.9 us (9%)
  local copies, waits for them, and re-layouts  6.72 us (5%)
    all_gather x1, waiting for transfers between devices, body(): grads = lax.all_gather(out_grad, ('row', 'core'), axis=0)  22.5 us
    all_gather x1, blocking collectives, body(): far = lax.all_gather(far, 'col', axis=0)  14.3 us
    all_to_all x1, blocking collectives, body(): taps = lax.all_to_all(taps, ('x', 'core'), split_axis=0, concat_axis=0)  13.3 us
    all_gather x1, blocking collectives, body(): both = lax.all_gather(gated, 'col', axis=1, tiled=True)  12.3 us
    ppermute x2, waiting for transfers between devices, ctx_shift(): lax.ppermute(value, CTX, [(i, i + steps) for i in range(count) if 0 <= i...  8.92 us
    ppermute x2, starting transfers between devices, ctx_shift(): lax.ppermute(value, CTX, [(i, i + steps) for i in range(count) if 0 <= i...  8.6 us
    all_to_all x1, starting transfers between devices, body(): pieces = lax.all_to_all(pieces, 'zl', split_axis=0, concat_axis=0)  6.47 us
    unnamed x16, local copies, waits for them, and re-layouts  5.72 us
  transfers between devices with their start and end apart: 6, of which 5 were waited for; matrix products, arithmetic and copies ran while one was open for 1% of the time, Pallas kernels for 4%

profile of v10, /device:TPU:1, one launch (start us, length us, event | category | flops | bytes accessed | tf_op | source)
XLA Modules:
  0.0 125.1 jit_solution(17864618886847562895)
XLA Ops:
  7.2 0.0 all-gather.4.cloned.1.call-start
  7.2 0.7 all-gather.4.cloned.1.call-update
  7.9 0.0 reduce-scatter.2.cloned.1.call-start
  7.9 0.7 slice.4
  8.7 5.4 %collective-permute-start = (bf16[3,16,256]{2,1,0:T(8,128)(2,1)S(1)}, bf16[3,16,256]{2,1,0:T(8,128)(2,1)S(1)}, u32[]{:S(2)}, u32[]{:S(2)}) collective-permute-start(bf16[3,16,256]{2,1,0:T(8,128)(2,1)S(1)} %slice.4), channel_id=1, source_target_pairs={{0,1},{1,2},{2,3},{3,4},{4,5},{5,6},{6,7},{7,8},{8,9},{9,10},{10,1... | collective-permute-start | bytes 73736 | tf_op jit(solution)/shard_map/ppermute | solution.py:388
  14.1 3.4 %collective-permute-done.before = bf16[3,16,256]{2,1,0:T(8,128)(2,1)S(1)} collective-permute-done((bf16[3,16,256]{2,1,0:T(8,128)(2,1)S(1)}, bf16[3,16,256]{2,1,0:T(8,128)(2,1)S(1)}, u32[]{:S(2)}, u32[]{:S(2)}) %collective-permute-start) | collective-permute-done | bytes 24608 | tf_op jit(solution)/shard_map/ppermute | solution.py:388
  17.5 0.0 copy-start
  17.5 1.1 copy-done
  18.7 0.7 copy-done.3
  19.4 0.7 copy-done.5
  20.1 1.3 %forward.1 = bf16[512,256]{1,0:T(8,128)(2,1)S(1)} custom-call(bf16[3,16,256]{2,1,0:T(8,128)(2,1)S(1)} %collective-permute-done.before, bf16[3,512,256]{2,1,0:T(8,128)(2,1)S(1)} %bitcast.13, f32[3,7,256]{2,1,0:T(8,128)S(1)} %copy-done.3, f32[7,256]{1,0:T(8,128)S(1)} %copy-done.5), custom_call_target="tpu_custom_call" | custom-call | flops 7864320 | bytes 1048576 | tf_op jit(solution)/shard_map/forward/pallas_call | solution.py:99
  21.4 12.3 %all_gather.15 = bf16[512,512]{1,0:T(8,128)(2,1)S(1)} all-gather(bf16[512,256]{1,0:T(8,128)(2,1)S(1)} %forward.1), channel_id=1, replica_groups=mesh['row'=8,'col'=2,'x'=4,'zl'=4,'core'=2] {'col'}, dimensions={1}, use_global_device_ids=true | all-gather | bytes 786432 | tf_op jit(solution)/shard_map/all_gather | solution.py:406
  33.7 0.2 copy.12
  34.0 3.0 %collective-permute-start.1 = (bf16[256,512]{1,0:T(8,128)(2,1)S(1)}, bf16[256,512]{1,0:T(8,128)(2,1)S(1)}, u32[]{:S(2)}, u32[]{:S(2)}) collective-permute-start(bf16[256,512]{1,0:T(8,128)(2,1)S(1)} %bitcast.22), channel_id=1, source_target_pairs={{0,1},{1,0},{2,3},{3,2},{4,5},{5,4},{6,7},{7,6},{8,9},{9,8},{10,11... | collective-permute-start | bytes 786440 | tf_op jit(solution)/shard_map/ppermute | solution.py:383
  37.0 1.1 collective-permute-done.1.other
  38.1 22.5 %all-gather.4.cloned.1.call-done = bf16[8192,256]{1,0:T(8,128)(2,1)} async-done(((bf16[512,256]{1,0:T(8,128)(2,1)}), bf16[8192,256]{1,0:T(8,128)(2,1)}) %all-gather.4.cloned.1.call-update) | async-done | bytes 4194320 | tf_op jit(solution)/shard_map/all_gather | solution.py:401
  60.6 2.2 %copy-done.7 = bf16[8192,256]{1,0:T(8,128)(2,1)S(1)} copy-done((bf16[8192,256]{1,0:T(8,128)(2,1)S(1)}, bf16[8192,256]{1,0:T(8,128)(2,1)}, u32[]{:S(2)}) %copy-start.7) | copy-done | bytes 4194328
  62.8 5.0 %products.1 = (bf16[512,256]{1,0:T(8,128)(2,1)S(1)}, f32[512,256]{1,0:T(8,128)S(1)}, bf16[4,8,64,256]{3,2,1,0:T(8,128)(2,1)}, f32[8,128]{1,0:T(8,128)S(1)}) custom-call(s32[1]{0:T(128)} %bitcast.1.col, s32[1]{0:T(128)} %bitcast.2.core, bf16[256,512]{1,0:T(8,128)(2,1)S(1)} %bitcast.16, bf16[256,512]{1,0:T(8,128)(2,1)S(1)} %collective-permute-done.1.other, ...), custom_call_target="tpu_custom_call" | custom-call | flops 2147483648 | bytes 6815744 | tf_op jit(solution)/shard_map/products/pallas_call | solution.py:267
  67.9 0.0 reduce-scatter.2.cloned.1.call-update
  67.9 14.3 %all-gather.1 = bf16[1024,256]{1,0:T(8,128)(2,1)S(1)} all-gather(bf16[512,256]{1,0:T(8,128)(2,1)S(1)} %get-tuple-element.21), channel_id=3, replica_groups=mesh['row'=8,'col'=2,'x'=4,'zl'=4,'core'=2] {'col'}, dimensions={0}, use_global_device_ids=true | all-gather | bytes 786432 | tf_op jit(solution)/shard_map/all_gather | solution.py:417
  82.2 0.0 copy-done.1
  82.2 0.0 copy-done.4
  82.2 0.0 copy-done.6
  82.2 4.1 %backward.1 = (bf16[3,512,256]{2,1,0:T(8,128)(2,1)}, f32[3,16,256]{2,1,0:T(8,128)S(1)}, f32[3,16,256]{2,1,0:T(8,128)S(1)}, f32[8,4,8,256]{3,2,1,0:T(8,128)S(1)}) custom-call(s32[1]{0:T(128)} %bitcast.1.col, f32[512,256]{1,0:T(8,128)S(1)} %get-tuple-element.20.near, bf16[2,512,256]{2,1,0:T(8,128)(2,1)S(1)} %bitcast.15, ...), custom_call_target="tpu_custom_call" | custom-call | flops 20971520 | bytes 2621440 | tf_op jit(solution)/shard_map/backward/pallas_call | solution.py:192
  86.3 13.3 %all_to_all.10.taps = f32[8,4,8,256]{3,2,1,0:T(8,128)S(1)} all-to-all(f32[8,4,8,256]{3,2,1,0:T(8,128)S(1)} %get-tuple-element.23), channel_id=1, replica_groups=mesh['row'=8,'col'=2,'x'=4,'zl'=4,'core'=2] {'x','core'}, dimensions={0} | all-to-all | bytes 524288 | tf_op jit(solution)/shard_map/all_to_all | solution.py:422
  99.5 0.9 copy-done.2
  100.5 0.8 middle.1
  101.3 6.5 %all-to-all-start.1 = ((bf16[4,12,16,256]{3,2,1,0:T(8,128)(2,1)}), bf16[4,12,16,256]{3,2,1,0:T(8,128)(2,1)S(1)}, u32[]{:S(2)}, u32[]{:S(2)}) async-start(bf16[4,12,16,256]{3,2,1,0:T(8,128)(2,1)} %get-tuple-element.26), calls=%async_computation.2 | async-start | bytes 786432 | tf_op jit(solution)/shard_map/all_to_all | solution.py:425
  107.7 3.2 %collective-permute-start.2 = (f32[3,16,256]{2,1,0:T(8,128)S(1)}, f32[3,16,256]{2,1,0:T(8,128)S(1)}, u32[]{:S(2)}, u32[]{:S(2)}) collective-permute-start(f32[3,16,256]{2,1,0:T(8,128)S(1)} %get-tuple-element.28), channel_id=1, source_target_pairs={{1,0},{2,1},{3,2},{4,3},{5,4},{6,5},{7,6},{8,7},{9,8},{10,9},{11,1... | collective-permute-start | bytes 147464 | tf_op jit(solution)/shard_map/ppermute | solution.py:388
  111.0 5.5 %collective-permute-done.2.refs_4_ = f32[3,16,256]{2,1,0:T(8,128)S(1)} collective-permute-done((f32[3,16,256]{2,1,0:T(8,128)S(1)}, f32[3,16,256]{2,1,0:T(8,128)S(1)}, u32[]{:S(2)}, u32[]{:S(2)}) %collective-permute-start.2) | collective-permute-done | bytes 49184 | tf_op jit(solution)/shard_map/ppermute | solution.py:388
  116.5 1.1 all-to-all-done.1.refs_2_
  117.6 0.7 last.1
  (9 shorter events, 0.1 us)
Async XLA Ops:
  7.2 53.5 %all-gather.4.cloned.1.call-start = ((), (), s32[]{:S(2)}) async-start(), calls=%async_computation.4 | async-start | bytes 4456448 | tf_op jit(solution)/shard_map/all_gather | solution.py:401
  7.9 91.6 %reduce-scatter.2.cloned.1.call-start = ((), (), s32[]{:S(2)}) async-start(), calls=%async_computation.3 | async-start | bytes 1310720 | tf_op jit(solution)/shard_map/reduce_scatter | solution.py:416
  8.7 8.8 %collective-permute-start = (bf16[3,16,256]{2,1,0:T(8,128)(2,1)S(1)}, bf16[3,16,256]{2,1,0:T(8,128)(2,1)S(1)}, u32[]{:S(2)}, u32[]{:S(2)}) collective-permute-start(bf16[3,16,256]{2,1,0:T(8,128)(2,1)S(1)} %slice.4), channel_id=1, source_target_pairs={{0,1},{1,2},{2,3},{3,4},{4,5},{5,6},{6,7},{7,8},{8,9},{9,10},{10,1... | collective-permute-start | bytes 73736 | tf_op jit(solution)/shard_map/ppermute | solution.py:388
  17.5 1.1 copy-start
  18.7 0.7 copy-start.3
  19.4 0.7 copy-start.5
  34.0 4.1 %collective-permute-start.1 = (bf16[256,512]{1,0:T(8,128)(2,1)S(1)}, bf16[256,512]{1,0:T(8,128)(2,1)S(1)}, u32[]{:S(2)}, u32[]{:S(2)}) collective-permute-start(bf16[256,512]{1,0:T(8,128)(2,1)S(1)} %bitcast.22), channel_id=1, source_target_pairs={{0,1},{1,0},{2,3},{3,2},{4,5},{5,4},{6,7},{7,6},{8,9},{9,8},{10,11... | collective-permute-start | bytes 786440 | tf_op jit(solution)/shard_map/ppermute | solution.py:383
  60.6 2.2 %copy-start.7 = (bf16[8192,256]{1,0:T(8,128)(2,1)S(1)}, bf16[8192,256]{1,0:T(8,128)(2,1)}, u32[]{:S(2)}) copy-start(bf16[8192,256]{1,0:T(8,128)(2,1)} %all-gather.4.cloned.1.call-done) | copy-start | bytes 12582916
  62.8 19.4 %copy-start.1 = (bf16[512,3,256]{2,0,1:T(8,128)(2,1)S(1)}, bf16[512,3,256]{2,0,1:T(8,128)(2,1)}, u32[]{:S(2)}) copy-start(bf16[512,3,256]{2,0,1:T(8,128)(2,1)} %param.5) | copy-start | bytes 2359300
  62.8 19.4 %copy-start.4 = (f32[3,7,256]{2,1,0:T(8,128)S(1)}, f32[3,7,256]{2,1,0:T(8,128)}, u32[]{:S(2)}) copy-start(f32[3,7,256]{2,1,0:T(8,128)} %feat_taps.3) | copy-start | bytes 64516
  62.8 19.4 %copy-start.6 = (f32[7,256]{1,0:T(8,128)S(1)}, f32[7,256]{1,0:T(8,128)}, u32[]{:S(2)}) copy-start(f32[7,256]{1,0:T(8,128)} %inner_taps.3) | copy-start | bytes 21508
  99.5 1.0 copy-start.2
  101.3 16.3 %all-to-all-start.1 = ((bf16[4,12,16,256]{3,2,1,0:T(8,128)(2,1)}), bf16[4,12,16,256]{3,2,1,0:T(8,128)(2,1)S(1)}, u32[]{:S(2)}, u32[]{:S(2)}) async-start(bf16[4,12,16,256]{3,2,1,0:T(8,128)(2,1)} %get-tuple-element.26), calls=%async_computation.2 | async-start | bytes 786432 | tf_op jit(solution)/shard_map/all_to_all | solution.py:425
  107.7 8.7 %collective-permute-start.2 = (f32[3,16,256]{2,1,0:T(8,128)S(1)}, f32[3,16,256]{2,1,0:T(8,128)S(1)}, u32[]{:S(2)}, u32[]{:S(2)}) collective-permute-start(f32[3,16,256]{2,1,0:T(8,128)S(1)} %get-tuple-element.28), channel_id=1, source_target_pairs={{1,0},{2,1},{3,2},{4,3},{5,4},{6,5},{7,6},{8,7},{9,8},{10,9},{11,1... | collective-permute-start | bytes 147464 | tf_op jit(solution)/shard_map/ppermute | solution.py:388
Sparse Core Ops, SparseCore 0:
  10.1 50.4 all-gather.3
  68.0 25.8 reduce-scatter.1

commit v11 on v10

--- a/solution.py
+++ b/solution.py
@@ -117,6 +117,27 @@
 
 def backward_kernel(
     col, near, far, before, own, feat_taps, inner_taps, _,
+    grads, head, tail, tap_sums, held, sems, *scratch,
+):
+    copies = []
+    for at in range(near.shape[1] // LANES):
+        lanes = slice(at * LANES, (at + 1) * LANES)
+        backward_lanes(
+            col, near.at[:, lanes], far.at[:, :, lanes], before.at[:, :, lanes],
+            own.at[:, :, lanes], feat_taps.at[:, :, lanes], inner_taps.at[:, lanes],
+            held.at[at], head.at[:, :, lanes], tail.at[:, :, lanes], tap_sums.at[:, :, :, lanes],
+            *scratch,
+        )
+        copies.append(
+            pltpu.make_async_copy(held.at[at], grads.at[:, :, lanes], sems.at[at])
+        )
+        copies[-1].start()
+    for copy in copies:
+        copy.wait()
+
+
+def backward_lanes(
+    col, near, far, before, own, feat_taps, inner_taps,
     grads, head, tail, tap_sums, feats, query, key, value, product, grad_window, grad_mixed,
 ):
     rows = own.shape[1]
@@ -194,21 +215,19 @@
         "backward",
         160 * rows * channels,
         20 * rows * channels,
-        grid=(channels // LANES,),
-        in_specs=[
-            SCALAR, lane_spec(rows), lane_spec(2, rows), lane_spec(3, HALO), lane_spec(3, rows),
-            lane_spec(3, TAPS), lane_spec(TAPS), UNREAD,
-        ],
-        out_specs=[
-            lane_spec(3, rows), lane_spec(3, HALO), lane_spec(3, HALO), lane_spec(copies, 4, 8)
-        ],
+        in_specs=[SCALAR] + [IN_VMEM] * 6 + [UNREAD],
+        out_specs=[IN_HBM] + [IN_VMEM] * 3,
         out_shape=[
-            jax.ShapeDtypeStruct((3, rows, channels), BF16),
+            pltpu.HBM((3, rows, channels), BF16),
             edge,
             edge,
             jax.ShapeDtypeStruct((copies, 4, 8, channels), F32),
         ],
-        scratch_shapes=[pltpu.VMEM((3, rows + HALO, LANES), F32)]
+        scratch_shapes=[
+            pltpu.VMEM((channels // LANES, 3, rows, LANES), BF16),
+            pltpu.SemaphoreType.DMA((channels // LANES,)),
+            pltpu.VMEM((3, rows + HALO, LANES), F32),
+        ]
         + [pltpu.VMEM((rows + LEAD, LANES), F32)] * 4
         + [
             pltpu.VMEM((rows + HALO + LEAD, LANES), F32),
@@ -224,32 +243,37 @@
     col, core, own, other, grads, weight, far, near, out, done, held, held_weight, sems, weight_sems
 ):
     half = near.shape[1]
+    pieces = weight_sems.shape[1]
+    size = half // pieces
     fetches = [
-        pltpu.make_async_copy(
-            weight.at[pl.ds(pl.multiple_of(which * half, half), half), :],
-            held_weight.at[at],
-            weight_sems.at[at],
-        )
+        [
+            pltpu.make_async_copy(
+                weight.at[pl.ds(pl.multiple_of(which * half + piece * size, size), size), :],
+                held_weight.at[at, piece * size : (piece + 1) * size],
+                weight_sems.at[at, piece],
+            )
+            for piece in range(pieces)
+        ]
         for at, which in enumerate((1 - col[0], col[0]))
     ]
-    for copy in fetches:
+    for copy in fetches[0] + fetches[1]:
         copy.start()
     done[...] = jnp.zeros_like(done)
     blocks, parts, size, _ = held.shape
     mine = [2 * b + core[0] for b in range(blocks)]
     copies = []
+    gated = jnp.concatenate([own[...], other[...]], axis=1)
     for b in range(blocks):
-        total = jnp.dot(own[...], grads[mine[b]], preferred_element_type=F32)
-        total = total + jnp.dot(
-            other[...], grads[4 * b + 1 - mine[b]], preferred_element_type=F32
-        )
+        pair = jnp.concatenate([grads[mine[b]], grads[4 * b + 1 - mine[b]]], axis=0)
+        total = jnp.dot(gated, pair, preferred_element_type=F32)
         for part in range(parts):
             held[b, part] = total[part * size : (part + 1) * size].astype(BF16)
         copies.append(pltpu.make_async_copy(held.at[b], out.at[:, b], sems.at[b]))
         copies[-1].start()
     wide = jnp.concatenate([grads[at] for at in mine], axis=1)
     for at, result in enumerate((far, near)):
-        fetches[at].wait()
+        for copy in fetches[at]:
+            copy.wait()
         total = lax.dot_general(
             wide, held_weight[at], (((1,), (1,)), ((), ())), preferred_element_type=F32
         )
@@ -281,7 +305,7 @@
             pltpu.VMEM((blocks, parts, size, width), BF16),
             pltpu.VMEM((2, half, blocks * width), BF16),
             pltpu.SemaphoreType.DMA((blocks,)),
-            pltpu.SemaphoreType.DMA((2,)),
+            pltpu.SemaphoreType.DMA((2, 4)),
         ],
     )(col, core, own, other, grads, in_hbm(weight))
 

time: 126 us -> 126 us (level)
  no operation moved by 1% of the time
where the time goes in v11:
time: 126 us; the launch traced here: 125 us
  blocking collectives  39.9 us (32%)
  waiting for transfers between devices  34.4 us (27%)
  starting transfers between devices  18.1 us (14%)
  between operations  14.1 us (11%)
  Pallas kernels  11.6 us (9%)
  local copies, waits for them, and re-layouts  6.72 us (5%)
    all_gather x1, waiting for transfers between devices, body(): grads = lax.all_gather(out_grad, ('row', 'core'), axis=0)  22.5 us
    all_gather x1, blocking collectives, body(): far = lax.all_gather(far, 'col', axis=0)  14.3 us
    all_to_all x1, blocking collectives, body(): taps = lax.all_to_all(taps, ('x', 'core'), split_axis=0, concat_axis=0)  13.3 us
    all_gather x1, blocking collectives, body(): both = lax.all_gather(gated, 'col', axis=1, tiled=True)  12.3 us
    ppermute x2, waiting for transfers between devices, ctx_shift(): lax.ppermute(value, CTX, [(i, i + steps) for i in range(count) if 0 <= i...  8.92 us
    ppermute x2, starting transfers between devices, ctx_shift(): lax.ppermute(value, CTX, [(i, i + steps) for i in range(count) if 0 <= i...  8.6 us
    all_to_all x1, starting transfers between devices, body(): pieces = lax.all_to_all(pieces, 'zl', split_axis=0, concat_axis=0)  6.45 us
    unnamed x16, local copies, waits for them, and re-layouts  5.72 us
  transfers between devices with their start and end apart: 6, of which 5 were waited for; matrix products, arithmetic and copies ran while one was open for 1% of the time, Pallas kernels for 4%

profile of v11, /device:TPU:1, one launch (start us, length us, event | category | flops | bytes accessed | tf_op | source)
XLA Modules:
  0.0 124.8 jit_solution(1044945748082492652)
XLA Ops:
  7.2 0.0 all-gather.4.cloned.1.call-start
  7.2 0.7 all-gather.4.cloned.1.call-update
  7.9 0.0 reduce-scatter.2.cloned.1.call-start
  7.9 0.7 slice.4
  8.7 5.4 %collective-permute-start = (bf16[3,16,256]{2,1,0:T(8,128)(2,1)S(1)}, bf16[3,16,256]{2,1,0:T(8,128)(2,1)S(1)}, u32[]{:S(2)}, u32[]{:S(2)}) collective-permute-start(bf16[3,16,256]{2,1,0:T(8,128)(2,1)S(1)} %slice.4), channel_id=1, source_target_pairs={{0,1},{1,2},{2,3},{3,4},{4,5},{5,6},{6,7},{7,8},{8,9},{9,10},{10,1... | collective-permute-start | bytes 73736 | tf_op jit(solution)/shard_map/ppermute | solution.py:412
  14.1 3.4 %collective-permute-done.before = bf16[3,16,256]{2,1,0:T(8,128)(2,1)S(1)} collective-permute-done((bf16[3,16,256]{2,1,0:T(8,128)(2,1)S(1)}, bf16[3,16,256]{2,1,0:T(8,128)(2,1)S(1)}, u32[]{:S(2)}, u32[]{:S(2)}) %collective-permute-start) | collective-permute-done | bytes 24608 | tf_op jit(solution)/shard_map/ppermute | solution.py:412
  17.5 0.0 copy-start
  17.5 1.1 copy-done
  18.7 0.7 copy-done.3
  19.4 0.7 copy-done.5
  20.1 1.3 %forward.1 = bf16[512,256]{1,0:T(8,128)(2,1)S(1)} custom-call(bf16[3,16,256]{2,1,0:T(8,128)(2,1)S(1)} %collective-permute-done.before, bf16[3,512,256]{2,1,0:T(8,128)(2,1)S(1)} %bitcast.13, f32[3,7,256]{2,1,0:T(8,128)S(1)} %copy-done.3, f32[7,256]{1,0:T(8,128)S(1)} %copy-done.5), custom_call_target="tpu_custom_call" | custom-call | flops 7864320 | bytes 1048576 | tf_op jit(solution)/shard_map/forward/pallas_call | solution.py:99
  21.4 12.3 %all_gather.15 = bf16[512,512]{1,0:T(8,128)(2,1)S(1)} all-gather(bf16[512,256]{1,0:T(8,128)(2,1)S(1)} %forward.1), channel_id=1, replica_groups=mesh['row'=8,'col'=2,'x'=4,'zl'=4,'core'=2] {'col'}, dimensions={1}, use_global_device_ids=true | all-gather | bytes 786432 | tf_op jit(solution)/shard_map/all_gather | solution.py:430
  33.7 0.2 copy.12
  34.0 3.0 %collective-permute-start.1 = (bf16[256,512]{1,0:T(8,128)(2,1)S(1)}, bf16[256,512]{1,0:T(8,128)(2,1)S(1)}, u32[]{:S(2)}, u32[]{:S(2)}) collective-permute-start(bf16[256,512]{1,0:T(8,128)(2,1)S(1)} %bitcast.22), channel_id=1, source_target_pairs={{0,1},{1,0},{2,3},{3,2},{4,5},{5,4},{6,7},{7,6},{8,9},{9,8},{10,11... | collective-permute-start | bytes 786440 | tf_op jit(solution)/shard_map/ppermute | solution.py:407
  37.0 1.1 collective-permute-done.1.other
  38.1 22.5 %all-gather.4.cloned.1.call-done = bf16[8192,256]{1,0:T(8,128)(2,1)} async-done(((bf16[512,256]{1,0:T(8,128)(2,1)}), bf16[8192,256]{1,0:T(8,128)(2,1)}) %all-gather.4.cloned.1.call-update) | async-done | bytes 4194320 | tf_op jit(solution)/shard_map/all_gather | solution.py:425
  60.6 2.2 %copy-done.7 = bf16[8192,256]{1,0:T(8,128)(2,1)S(1)} copy-done((bf16[8192,256]{1,0:T(8,128)(2,1)S(1)}, bf16[8192,256]{1,0:T(8,128)(2,1)}, u32[]{:S(2)}) %copy-start.7) | copy-done | bytes 4194328
  62.8 5.1 %products.1 = (bf16[512,256]{1,0:T(8,128)(2,1)S(1)}, f32[512,256]{1,0:T(8,128)S(1)}, bf16[4,8,64,256]{3,2,1,0:T(8,128)(2,1)}, f32[8,128]{1,0:T(8,128)S(1)}) custom-call(s32[1]{0:T(128)} %bitcast.1.col, s32[1]{0:T(128)} %bitcast.2.core, bf16[256,512]{1,0:T(8,128)(2,1)S(1)} %bitcast.16, bf16[256,512]{1,0:T(8,128)(2,1)S(1)} %collective-permute-done.1.other, ...), custom_call_target="tpu_custom_call" | custom-call | flops 2147483648 | bytes 6815744 | tf_op jit(solution)/shard_map/products/pallas_call | solution.py:291
  67.9 0.0 reduce-scatter.2.cloned.1.call-update
  67.9 14.3 %all-gather.1 = bf16[1024,256]{1,0:T(8,128)(2,1)S(1)} all-gather(bf16[512,256]{1,0:T(8,128)(2,1)S(1)} %get-tuple-element.21), channel_id=3, replica_groups=mesh['row'=8,'col'=2,'x'=4,'zl'=4,'core'=2] {'col'}, dimensions={0}, use_global_device_ids=true | all-gather | bytes 786432 | tf_op jit(solution)/shard_map/all_gather | solution.py:441
  82.2 0.0 copy-done.1
  82.2 0.0 copy-done.4
  82.2 0.0 copy-done.6
  82.2 3.7 %backward.1 = (bf16[3,512,256]{2,1,0:T(8,128)(2,1)}, f32[3,16,256]{2,1,0:T(8,128)S(1)}, f32[3,16,256]{2,1,0:T(8,128)S(1)}, f32[8,4,8,256]{3,2,1,0:T(8,128)S(1)}) custom-call(s32[1]{0:T(128)} %bitcast.1.col, f32[512,256]{1,0:T(8,128)S(1)} %get-tuple-element.20.near, bf16[2,512,256]{2,1,0:T(8,128)(2,1)S(1)} %bitcast.15, ...), custom_call_target="tpu_custom_call" | custom-call | flops 20971520 | bytes 2621440 | tf_op jit(solution)/shard_map/backward/pallas_call | solution.py:213
  85.9 13.3 %all_to_all.10.taps = f32[8,4,8,256]{3,2,1,0:T(8,128)S(1)} all-to-all(f32[8,4,8,256]{3,2,1,0:T(8,128)S(1)} %get-tuple-element.23), channel_id=1, replica_groups=mesh['row'=8,'col'=2,'x'=4,'zl'=4,'core'=2] {'x','core'}, dimensions={0} | all-to-all | bytes 524288 | tf_op jit(solution)/shard_map/all_to_all | solution.py:446
  99.2 0.9 copy-done.2
  100.2 0.8 middle.1
  101.0 6.5 %all-to-all-start.1 = ((bf16[4,12,16,256]{3,2,1,0:T(8,128)(2,1)}), bf16[4,12,16,256]{3,2,1,0:T(8,128)(2,1)S(1)}, u32[]{:S(2)}, u32[]{:S(2)}) async-start(bf16[4,12,16,256]{3,2,1,0:T(8,128)(2,1)} %get-tuple-element.26), calls=%async_computation.2 | async-start | bytes 786432 | tf_op jit(solution)/shard_map/all_to_all | solution.py:449
  107.4 3.2 %collective-permute-start.2 = (f32[3,16,256]{2,1,0:T(8,128)S(1)}, f32[3,16,256]{2,1,0:T(8,128)S(1)}, u32[]{:S(2)}, u32[]{:S(2)}) collective-permute-start(f32[3,16,256]{2,1,0:T(8,128)S(1)} %get-tuple-element.28), channel_id=1, source_target_pairs={{1,0},{2,1},{3,2},{4,3},{5,4},{6,5},{7,6},{8,7},{9,8},{10,9},{11,1... | collective-permute-start | bytes 147464 | tf_op jit(solution)/shard_map/ppermute | solution.py:412
  110.7 5.5 %collective-permute-done.2.refs_4_ = f32[3,16,256]{2,1,0:T(8,128)S(1)} collective-permute-done((f32[3,16,256]{2,1,0:T(8,128)S(1)}, f32[3,16,256]{2,1,0:T(8,128)S(1)}, u32[]{:S(2)}, u32[]{:S(2)}) %collective-permute-start.2) | collective-permute-done | bytes 49184 | tf_op jit(solution)/shard_map/ppermute | solution.py:412
  116.1 1.1 all-to-all-done.1.refs_2_
  117.3 0.7 last.1
  (9 shorter events, 0.1 us)
Async XLA Ops:
  7.2 53.5 %all-gather.4.cloned.1.call-start = ((), (), s32[]{:S(2)}) async-start(), calls=%async_computation.4 | async-start | bytes 4456448 | tf_op jit(solution)/shard_map/all_gather | solution.py:425
  7.9 91.3 %reduce-scatter.2.cloned.1.call-start = ((), (), s32[]{:S(2)}) async-start(), calls=%async_computation.3 | async-start | bytes 1310720 | tf_op jit(solution)/shard_map/reduce_scatter | solution.py:440
  8.7 8.8 %collective-permute-start = (bf16[3,16,256]{2,1,0:T(8,128)(2,1)S(1)}, bf16[3,16,256]{2,1,0:T(8,128)(2,1)S(1)}, u32[]{:S(2)}, u32[]{:S(2)}) collective-permute-start(bf16[3,16,256]{2,1,0:T(8,128)(2,1)S(1)} %slice.4), channel_id=1, source_target_pairs={{0,1},{1,2},{2,3},{3,4},{4,5},{5,6},{6,7},{7,8},{8,9},{9,10},{10,1... | collective-permute-start | bytes 73736 | tf_op jit(solution)/shard_map/ppermute | solution.py:412
  17.5 1.1 copy-start
  18.7 0.7 copy-start.3
  19.4 0.7 copy-start.5
  34.0 4.1 %collective-permute-start.1 = (bf16[256,512]{1,0:T(8,128)(2,1)S(1)}, bf16[256,512]{1,0:T(8,128)(2,1)S(1)}, u32[]{:S(2)}, u32[]{:S(2)}) collective-permute-start(bf16[256,512]{1,0:T(8,128)(2,1)S(1)} %bitcast.22), channel_id=1, source_target_pairs={{0,1},{1,0},{2,3},{3,2},{4,5},{5,4},{6,7},{7,6},{8,9},{9,8},{10,11... | collective-permute-start | bytes 786440 | tf_op jit(solution)/shard_map/ppermute | solution.py:407
  60.6 2.2 %copy-start.7 = (bf16[8192,256]{1,0:T(8,128)(2,1)S(1)}, bf16[8192,256]{1,0:T(8,128)(2,1)}, u32[]{:S(2)}) copy-start(bf16[8192,256]{1,0:T(8,128)(2,1)} %all-gather.4.cloned.1.call-done) | copy-start | bytes 12582916
  62.8 19.4 %copy-start.1 = (bf16[512,3,256]{2,0,1:T(8,128)(2,1)S(1)}, bf16[512,3,256]{2,0,1:T(8,128)(2,1)}, u32[]{:S(2)}) copy-start(bf16[512,3,256]{2,0,1:T(8,128)(2,1)} %param.5) | copy-start | bytes 2359300
  62.8 19.4 %copy-start.4 = (f32[3,7,256]{2,1,0:T(8,128)S(1)}, f32[3,7,256]{2,1,0:T(8,128)}, u32[]{:S(2)}) copy-start(f32[3,7,256]{2,1,0:T(8,128)} %feat_taps.3) | copy-start | bytes 64516
  62.8 19.4 %copy-start.6 = (f32[7,256]{1,0:T(8,128)S(1)}, f32[7,256]{1,0:T(8,128)}, u32[]{:S(2)}) copy-start(f32[7,256]{1,0:T(8,128)} %inner_taps.3) | copy-start | bytes 21508
  99.2 1.0 copy-start.2
  101.0 16.3 %all-to-all-start.1 = ((bf16[4,12,16,256]{3,2,1,0:T(8,128)(2,1)}), bf16[4,12,16,256]{3,2,1,0:T(8,128)(2,1)S(1)}, u32[]{:S(2)}, u32[]{:S(2)}) async-start(bf16[4,12,16,256]{3,2,1,0:T(8,128)(2,1)} %get-tuple-element.26), calls=%async_computation.2 | async-start | bytes 786432 | tf_op jit(solution)/shard_map/all_to_all | solution.py:449
  107.4 8.7 %collective-permute-start.2 = (f32[3,16,256]{2,1,0:T(8,128)S(1)}, f32[3,16,256]{2,1,0:T(8,128)S(1)}, u32[]{:S(2)}, u32[]{:S(2)}) collective-permute-start(f32[3,16,256]{2,1,0:T(8,128)S(1)} %get-tuple-element.28), channel_id=1, source_target_pairs={{1,0},{2,1},{3,2},{4,3},{5,4},{6,5},{7,6},{8,7},{9,8},{10,9},{11,1... | collective-permute-start | bytes 147464 | tf_op jit(solution)/shard_map/ppermute | solution.py:412
Sparse Core Ops, SparseCore 0:
  10.1 50.4 all-gather.3
  68.0 25.8 reduce-scatter.1

commit v12 on v11

--- a/solution.py
+++ b/solution.py
@@ -310,14 +310,13 @@
     )(col, core, own, other, grads, in_hbm(weight))
 
 
-def two_roundings(sums):
-    high = sums.astype(BF16).astype(F32)
-    return jnp.concatenate([high, sums - high], axis=1).astype(BF16)
-
-
-def rejoined(both):
-    both = both.astype(F32)
-    return both[:, :8] + both[:, 8:]
+def paired(sums):
+    return jnp.concatenate([sums[:2], sums[2:]], axis=1).astype(BF16)
+
+
+def parted(tiles):
+    tiles = tiles.astype(F32)
+    return jnp.concatenate([tiles[:, :8], tiles[:, 8:]], axis=0)
 
 
 def middle_kernel(pair, taps, head, out, out_taps, out_head):
@@ -327,8 +326,8 @@
     for copy in range(1, taps.shape[0]):
         sums = sums + taps[copy]
     out_taps[...] = sums
-    out_head[...] = head[...]
-    both = two_roundings(sums)
+    out_head[...] = head[...].astype(BF16)
+    both = paired(sums)
     for part in range(parts):
         out[part, 0:blocks] = pair[:, part * size : (part + 1) * size, :]
         out[part, blocks:] = both
@@ -336,11 +335,11 @@
 
 def middle(parts, pair, taps, head):
     blocks, channels, width = pair.shape
-    shape = (parts, blocks + taps.shape[1], channels // parts, width)
+    shape = (parts, blocks + taps.shape[1] // 2, channels // parts, width)
     outs = [
         jax.ShapeDtypeStruct(shape, BF16),
         jax.ShapeDtypeStruct(taps.shape[1:], F32),
-        jax.ShapeDtypeStruct(head.shape, F32),
+        jax.ShapeDtypeStruct(head.shape, BF16),
     ]
     return call(
         middle_kernel,
@@ -358,7 +357,7 @@
 ):
     parts, _, _, width = arrived.shape
     blocks = out.shape[1] // width
-    out_grads[...] = (tail[...] + head[...]).astype(BF16)
+    out_grads[...] = (tail[...] + head[...].astype(F32)).astype(BF16)
     for b in range(blocks):
         total = arrived[0, b].astype(F32)
         for part in range(1, parts):
@@ -366,7 +365,7 @@
         out[:, b * width : (b + 1) * width] = (total * scale).astype(BF16)
     total = taps[...]
     for part in range(parts):
-        total = total + jnp.where(z[0] == part, 0.0, rejoined(arrived[part, blocks:]))
+        total = total + jnp.where(z[0] == part, 0.0, parted(arrived[part, blocks:]))
     total = total * scale
     out_feat[...] = total[:3, :TAPS]
     out_inner[...] = total[3, :TAPS]
@@ -374,7 +373,7 @@
 
 def last(scale, z, taps, arrived, tail, head, grads):
     parts, count, channels, width = arrived.shape
-    blocks = count - taps.shape[0]
+    blocks = count - taps.shape[0] // 2
     final = grads.shape[1] // HALO - 1
     args = (taps, arrived, tail, head)
     shapes = [

time: 126 us -> 125 us (level)
  waiting for transfers between devices: 34.4 us -> 33.1 us
where the time goes in v12:
time: 125 us; the launch traced here: 124 us
  blocking collectives  39.9 us (32%)
  waiting for transfers between devices  33.1 us (26%)
  starting transfers between devices  18.1 us (14%)
  between operations  14.1 us (11%)
  Pallas kernels  11.5 us (9%)
  local copies, waits for them, and re-layouts  6.72 us (5%)
    all_gather x1, waiting for transfers between devices, body(): grads = lax.all_gather(out_grad, ('row', 'core'), axis=0)  22.5 us
    all_gather x1, blocking collectives, body(): far = lax.all_gather(far, 'col', axis=0)  14.3 us
    all_to_all x1, blocking collectives, body(): taps = lax.all_to_all(taps, ('x', 'core'), split_axis=0, concat_axis=0)  13.3 us
    all_gather x1, blocking collectives, body(): both = lax.all_gather(gated, 'col', axis=1, tiled=True)  12.3 us
    ppermute x2, starting transfers between devices, ctx_shift(): lax.ppermute(value, CTX, [(i, i + steps) for i in range(count) if 0 <= i...  8.6 us
    ppermute x2, waiting for transfers between devices, ctx_shift(): lax.ppermute(value, CTX, [(i, i + steps) for i in range(count) if 0 <= i...  8.16 us
    all_to_all x1, starting transfers between devices, body(): pieces = lax.all_to_all(pieces, 'zl', split_axis=0, concat_axis=0)  6.45 us
    unnamed x16, local copies, waits for them, and re-layouts  5.72 us
  transfers between devices with their start and end apart: 6, of which 5 were waited for; matrix products, arithmetic and copies ran while one was open for 1% of the time, Pallas kernels for 4%

profile of v12, /device:TPU:1, one launch (start us, length us, event | category | flops | bytes accessed | tf_op | source)
XLA Modules:
  0.0 123.5 jit_solution(5914380546330079543)
XLA Ops:
  7.2 0.0 all-gather.4.cloned.1.call-start
  7.2 0.7 all-gather.4.cloned.1.call-update
  7.9 0.0 reduce-scatter.2.cloned.1.call-start
  7.9 0.7 slice.4
  8.7 5.4 %collective-permute-start = (bf16[3,16,256]{2,1,0:T(8,128)(2,1)S(1)}, bf16[3,16,256]{2,1,0:T(8,128)(2,1)S(1)}, u32[]{:S(2)}, u32[]{:S(2)}) collective-permute-start(bf16[3,16,256]{2,1,0:T(8,128)(2,1)S(1)} %slice.4), channel_id=1, source_target_pairs={{0,1},{1,2},{2,3},{3,4},{4,5},{5,6},{6,7},{7,8},{8,9},{9,10},{10,1... | collective-permute-start | bytes 73736 | tf_op jit(solution)/shard_map/ppermute | solution.py:411
  14.1 3.4 %collective-permute-done.before = bf16[3,16,256]{2,1,0:T(8,128)(2,1)S(1)} collective-permute-done((bf16[3,16,256]{2,1,0:T(8,128)(2,1)S(1)}, bf16[3,16,256]{2,1,0:T(8,128)(2,1)S(1)}, u32[]{:S(2)}, u32[]{:S(2)}) %collective-permute-start) | collective-permute-done | bytes 24608 | tf_op jit(solution)/shard_map/ppermute | solution.py:411
  17.5 0.0 copy-start
  17.5 1.1 copy-done
  18.7 0.7 copy-done.3
  19.4 0.7 copy-done.5
  20.1 1.3 %forward.1 = bf16[512,256]{1,0:T(8,128)(2,1)S(1)} custom-call(bf16[3,16,256]{2,1,0:T(8,128)(2,1)S(1)} %collective-permute-done.before, bf16[3,512,256]{2,1,0:T(8,128)(2,1)S(1)} %bitcast.13, f32[3,7,256]{2,1,0:T(8,128)S(1)} %copy-done.3, f32[7,256]{1,0:T(8,128)S(1)} %copy-done.5), custom_call_target="tpu_custom_call" | custom-call | flops 7864320 | bytes 1048576 | tf_op jit(solution)/shard_map/forward/pallas_call | solution.py:99
  21.4 12.3 %all_gather.15 = bf16[512,512]{1,0:T(8,128)(2,1)S(1)} all-gather(bf16[512,256]{1,0:T(8,128)(2,1)S(1)} %forward.1), channel_id=1, replica_groups=mesh['row'=8,'col'=2,'x'=4,'zl'=4,'core'=2] {'col'}, dimensions={1}, use_global_device_ids=true | all-gather | bytes 786432 | tf_op jit(solution)/shard_map/all_gather | solution.py:429
  33.7 0.2 copy.12
  34.0 3.0 %collective-permute-start.1 = (bf16[256,512]{1,0:T(8,128)(2,1)S(1)}, bf16[256,512]{1,0:T(8,128)(2,1)S(1)}, u32[]{:S(2)}, u32[]{:S(2)}) collective-permute-start(bf16[256,512]{1,0:T(8,128)(2,1)S(1)} %bitcast.22), channel_id=1, source_target_pairs={{0,1},{1,0},{2,3},{3,2},{4,5},{5,4},{6,7},{7,6},{8,9},{9,8},{10,11... | collective-permute-start | bytes 786440 | tf_op jit(solution)/shard_map/ppermute | solution.py:406
  37.0 1.1 collective-permute-done.1.other
  38.1 22.5 %all-gather.4.cloned.1.call-done = bf16[8192,256]{1,0:T(8,128)(2,1)} async-done(((bf16[512,256]{1,0:T(8,128)(2,1)}), bf16[8192,256]{1,0:T(8,128)(2,1)}) %all-gather.4.cloned.1.call-update) | async-done | bytes 4194320 | tf_op jit(solution)/shard_map/all_gather | solution.py:424
  60.6 2.2 %copy-done.7 = bf16[8192,256]{1,0:T(8,128)(2,1)S(1)} copy-done((bf16[8192,256]{1,0:T(8,128)(2,1)S(1)}, bf16[8192,256]{1,0:T(8,128)(2,1)}, u32[]{:S(2)}) %copy-start.7) | copy-done | bytes 4194328
  62.8 5.1 %products.1 = (bf16[512,256]{1,0:T(8,128)(2,1)S(1)}, f32[512,256]{1,0:T(8,128)S(1)}, bf16[4,8,64,256]{3,2,1,0:T(8,128)(2,1)}, f32[8,128]{1,0:T(8,128)S(1)}) custom-call(s32[1]{0:T(128)} %bitcast.1.col, s32[1]{0:T(128)} %bitcast.2.core, bf16[256,512]{1,0:T(8,128)(2,1)S(1)} %bitcast.16, bf16[256,512]{1,0:T(8,128)(2,1)S(1)} %collective-permute-done.1.other, ...), custom_call_target="tpu_custom_call" | custom-call | flops 2147483648 | bytes 6815744 | tf_op jit(solution)/shard_map/products/pallas_call | solution.py:291
  67.9 0.0 reduce-scatter.2.cloned.1.call-update
  67.9 14.3 %all-gather.1 = bf16[1024,256]{1,0:T(8,128)(2,1)S(1)} all-gather(bf16[512,256]{1,0:T(8,128)(2,1)S(1)} %get-tuple-element.21), channel_id=3, replica_groups=mesh['row'=8,'col'=2,'x'=4,'zl'=4,'core'=2] {'col'}, dimensions={0}, use_global_device_ids=true | all-gather | bytes 786432 | tf_op jit(solution)/shard_map/all_gather | solution.py:440
  82.2 0.0 copy-done.1
  82.2 0.0 copy-done.4
  82.2 0.0 copy-done.6
  82.2 3.7 %backward.1 = (bf16[3,512,256]{2,1,0:T(8,128)(2,1)}, f32[3,16,256]{2,1,0:T(8,128)S(1)}, f32[3,16,256]{2,1,0:T(8,128)S(1)}, f32[8,4,8,256]{3,2,1,0:T(8,128)S(1)}) custom-call(s32[1]{0:T(128)} %bitcast.1.col, f32[512,256]{1,0:T(8,128)S(1)} %get-tuple-element.20.near, bf16[2,512,256]{2,1,0:T(8,128)(2,1)S(1)} %bitcast.15, ...), custom_call_target="tpu_custom_call" | custom-call | flops 20971520 | bytes 2621440 | tf_op jit(solution)/shard_map/backward/pallas_call | solution.py:213
  85.9 13.3 %all_to_all.10.taps = f32[8,4,8,256]{3,2,1,0:T(8,128)S(1)} all-to-all(f32[8,4,8,256]{3,2,1,0:T(8,128)S(1)} %get-tuple-element.23), channel_id=1, replica_groups=mesh['row'=8,'col'=2,'x'=4,'zl'=4,'core'=2] {'x','core'}, dimensions={0} | all-to-all | bytes 524288 | tf_op jit(solution)/shard_map/all_to_all | solution.py:445
  99.2 0.9 copy-done.2
  100.2 0.8 middle.1
  100.9 6.5 %all-to-all-start.1 = ((bf16[4,10,16,256]{3,2,1,0:T(8,128)(2,1)}), bf16[4,10,16,256]{3,2,1,0:T(8,128)(2,1)S(1)}, u32[]{:S(2)}, u32[]{:S(2)}) async-start(bf16[4,10,16,256]{3,2,1,0:T(8,128)(2,1)} %get-tuple-element.26), calls=%async_computation.2 | async-start | bytes 655360 | tf_op jit(solution)/shard_map/all_to_all | solution.py:448
  107.4 3.2 %collective-permute-start.2 = (bf16[3,16,256]{2,1,0:T(8,128)(2,1)S(1)}, bf16[3,16,256]{2,1,0:T(8,128)(2,1)S(1)}, u32[]{:S(2)}, u32[]{:S(2)}) collective-permute-start(bf16[3,16,256]{2,1,0:T(8,128)(2,1)S(1)} %get-tuple-element.28), channel_id=1, source_target_pairs={{1,0},{2,1},{3,2},{4,3},{5,4},{6,5},{7,6},{8,7},{9,8},{10,9},{11,1... | collective-permute-start | bytes 73736 | tf_op jit(solution)/shard_map/ppermute | solution.py:411
  110.6 4.7 %collective-permute-done.2.refs_4_ = bf16[3,16,256]{2,1,0:T(8,128)(2,1)S(1)} collective-permute-done((bf16[3,16,256]{2,1,0:T(8,128)(2,1)S(1)}, bf16[3,16,256]{2,1,0:T(8,128)(2,1)S(1)}, u32[]{:S(2)}, u32[]{:S(2)}) %collective-permute-start.2) | collective-permute-done | bytes 24608 | tf_op jit(solution)/shard_map/ppermute | solution.py:411
  115.3 0.7 all-to-all-done.1.refs_2_
  116.0 0.7 last.1
  (9 shorter events, 0.1 us)
Async XLA Ops:
  7.2 53.5 %all-gather.4.cloned.1.call-start = ((), (), s32[]{:S(2)}) async-start(), calls=%async_computation.4 | async-start | bytes 4456448 | tf_op jit(solution)/shard_map/all_gather | solution.py:424
  7.9 91.3 %reduce-scatter.2.cloned.1.call-start = ((), (), s32[]{:S(2)}) async-start(), calls=%async_computation.3 | async-start | bytes 1310720 | tf_op jit(solution)/shard_map/reduce_scatter | solution.py:439
  8.7 8.8 %collective-permute-start = (bf16[3,16,256]{2,1,0:T(8,128)(2,1)S(1)}, bf16[3,16,256]{2,1,0:T(8,128)(2,1)S(1)}, u32[]{:S(2)}, u32[]{:S(2)}) collective-permute-start(bf16[3,16,256]{2,1,0:T(8,128)(2,1)S(1)} %slice.4), channel_id=1, source_target_pairs={{0,1},{1,2},{2,3},{3,4},{4,5},{5,6},{6,7},{7,8},{8,9},{9,10},{10,1... | collective-permute-start | bytes 73736 | tf_op jit(solution)/shard_map/ppermute | solution.py:411
  17.5 1.1 copy-start
  18.7 0.7 copy-start.3
  19.4 0.7 copy-start.5
  34.0 4.1 %collective-permute-start.1 = (bf16[256,512]{1,0:T(8,128)(2,1)S(1)}, bf16[256,512]{1,0:T(8,128)(2,1)S(1)}, u32[]{:S(2)}, u32[]{:S(2)}) collective-permute-start(bf16[256,512]{1,0:T(8,128)(2,1)S(1)} %bitcast.22), channel_id=1, source_target_pairs={{0,1},{1,0},{2,3},{3,2},{4,5},{5,4},{6,7},{7,6},{8,9},{9,8},{10,11... | collective-permute-start | bytes 786440 | tf_op jit(solution)/shard_map/ppermute | solution.py:406
  60.6 2.2 %copy-start.7 = (bf16[8192,256]{1,0:T(8,128)(2,1)S(1)}, bf16[8192,256]{1,0:T(8,128)(2,1)}, u32[]{:S(2)}) copy-start(bf16[8192,256]{1,0:T(8,128)(2,1)} %all-gather.4.cloned.1.call-done) | copy-start | bytes 12582916
  62.8 19.4 %copy-start.1 = (bf16[512,3,256]{2,0,1:T(8,128)(2,1)S(1)}, bf16[512,3,256]{2,0,1:T(8,128)(2,1)}, u32[]{:S(2)}) copy-start(bf16[512,3,256]{2,0,1:T(8,128)(2,1)} %param.5) | copy-start | bytes 2359300
  62.8 19.4 %copy-start.4 = (f32[3,7,256]{2,1,0:T(8,128)S(1)}, f32[3,7,256]{2,1,0:T(8,128)}, u32[]{:S(2)}) copy-start(f32[3,7,256]{2,1,0:T(8,128)} %feat_taps.3) | copy-start | bytes 64516
  62.8 19.4 %copy-start.6 = (f32[7,256]{1,0:T(8,128)S(1)}, f32[7,256]{1,0:T(8,128)}, u32[]{:S(2)}) copy-start(f32[7,256]{1,0:T(8,128)} %inner_taps.3) | copy-start | bytes 21508
  99.2 1.0 copy-start.2
  100.9 15.1 %all-to-all-start.1 = ((bf16[4,10,16,256]{3,2,1,0:T(8,128)(2,1)}), bf16[4,10,16,256]{3,2,1,0:T(8,128)(2,1)S(1)}, u32[]{:S(2)}, u32[]{:S(2)}) async-start(bf16[4,10,16,256]{3,2,1,0:T(8,128)(2,1)} %get-tuple-element.26), calls=%async_computation.2 | async-start | bytes 655360 | tf_op jit(solution)/shard_map/all_to_all | solution.py:448
  107.4 7.9 %collective-permute-start.2 = (bf16[3,16,256]{2,1,0:T(8,128)(2,1)S(1)}, bf16[3,16,256]{2,1,0:T(8,128)(2,1)S(1)}, u32[]{:S(2)}, u32[]{:S(2)}) collective-permute-start(bf16[3,16,256]{2,1,0:T(8,128)(2,1)S(1)} %get-tuple-element.28), channel_id=1, source_target_pairs={{1,0},{2,1},{3,2},{4,3},{5,4},{6,5},{7,6},{8,7},{9,8},{10,9},{11,1... | collective-permute-start | bytes 73736 | tf_op jit(solution)/shard_map/ppermute | solution.py:411
Sparse Core Ops, SparseCore 0:
  10.1 50.4 all-gather.3
  68.0 25.8 reduce-scatter.1

commit v13 on v12

--- a/solution.py
+++ b/solution.py
@@ -172,11 +172,11 @@
     def folded(terms):
         return jnp.sum(terms.reshape(terms.shape[0] // 8, 8, LANES), axis=0)
 
+    tiles = [None] * 4
+
     def put(place, sums):
         rows = [jnp.sum(total, axis=0, keepdims=True) for total in sums]
-        tile = jnp.concatenate([*rows, jnp.zeros((1, LANES), F32)], axis=0)
-        for copy in range(tap_sums.shape[0]):
-            tap_sums[copy, place] = tile
+        tiles[place] = jnp.concatenate([*rows, jnp.zeros((1, LANES), F32)], axis=0)
 
     def transposed(j, at, count):
         total = feat_taps[j, 0:1, :] * grad_mixed[j, at : at + count, :]
@@ -205,6 +205,10 @@
             base = LEAD + start - s
             sums[s] = sums[s] + folded(here * product[base : base + count, :])
     put(3, sums)
+    for at in range(2):
+        pair = jnp.concatenate([tiles[at], tiles[2 + at]], axis=0).astype(BF16)
+        for copy in range(tap_sums.shape[0]):
+            tap_sums[copy, at] = pair
 
 
 def backward(copies, col, near, far, before, own, feat_taps, inner_taps, after):
@@ -221,7 +225,7 @@
             pltpu.HBM((3, rows, channels), BF16),
             edge,
             edge,
-            jax.ShapeDtypeStruct((copies, 4, 8, channels), F32),
+            jax.ShapeDtypeStruct((copies, 2, 16, channels), BF16),
         ],
         scratch_shapes=[
             pltpu.VMEM((channels // LANES, 3, rows, LANES), BF16),
@@ -322,9 +326,9 @@
 def middle_kernel(pair, taps, head, out, out_taps, out_head):
     parts, _, size, _ = out.shape
     blocks = pair.shape[0]
-    sums = taps[0]
+    sums = parted(taps[0])
     for copy in range(1, taps.shape[0]):
-        sums = sums + taps[copy]
+        sums = sums + parted(taps[copy])
     out_taps[...] = sums
     out_head[...] = head[...].astype(BF16)
     both = paired(sums)
@@ -335,10 +339,10 @@
 
 def middle(parts, pair, taps, head):
     blocks, channels, width = pair.shape
-    shape = (parts, blocks + taps.shape[1] // 2, channels // parts, width)
+    shape = (parts, blocks + taps.shape[1], channels // parts, width)
     outs = [
         jax.ShapeDtypeStruct(shape, BF16),
-        jax.ShapeDtypeStruct(taps.shape[1:], F32),
+        jax.ShapeDtypeStruct((2 * taps.shape[1], 8, width), F32),
         jax.ShapeDtypeStruct(head.shape, BF16),
     ]
     return call(

time: 125 us -> 124 us (level)
    all_to_all x1, blocking collectives: 13.3 us -> 12 us  [body(): taps = lax.all_to_all(taps, ('x', 'core'), split_axis=0, concat_axis=0)]
where the time goes in v13:
time: 124 us; the launch traced here: 122 us
  blocking collectives  38.7 us (31%)
  waiting for transfers between devices  33.4 us (27%)
  starting transfers between devices  18 us (15%)
  between operations  14.1 us (11%)
  Pallas kernels  11.5 us (9%)
  local copies, waits for them, and re-layouts  6.72 us (5%)
    all_gather x1, waiting for transfers between devices, body(): grads = lax.all_gather(out_grad, ('row', 'core'), axis=0)  22.5 us
    all_gather x1, blocking collectives, body(): far = lax.all_gather(far, 'col', axis=0)  14.3 us
    all_gather x1, blocking collectives, body(): both = lax.all_gather(gated, 'col', axis=1, tiled=True)  12.3 us
    all_to_all x1, blocking collectives, body(): taps = lax.all_to_all(taps, ('x', 'core'), split_axis=0, concat_axis=0)  12 us
    ppermute x2, starting transfers between devices, ctx_shift(): lax.ppermute(value, CTX, [(i, i + steps) for i in range(count) if 0 <= i...  8.42 us
    ppermute x2, waiting for transfers between devices, ctx_shift(): lax.ppermute(value, CTX, [(i, i + steps) for i in range(count) if 0 <= i...  8.12 us
    all_to_all x1, starting transfers between devices, body(): pieces = lax.all_to_all(pieces, 'zl', split_axis=0, concat_axis=0)  6.48 us
    unnamed x16, local copies, waits for them, and re-layouts  5.72 us
  transfers between devices with their start and end apart: 6, of which 5 were waited for; matrix products, arithmetic and copies ran while one was open for 1% of the time, Pallas kernels for 4%

profile of v13, /device:TPU:1, one launch (start us, length us, event | category | flops | bytes accessed | tf_op | source)
XLA Modules:
  0.0 122.3 jit_solution(9375040808776171203)
XLA Ops:
  7.2 0.0 all-gather.4.cloned.1.call-start
  7.2 0.7 all-gather.4.cloned.1.call-update
  7.9 0.0 reduce-scatter.2.cloned.1.call-start
  7.9 0.7 slice.4
  8.7 5.4 %collective-permute-start = (bf16[3,16,256]{2,1,0:T(8,128)(2,1)S(1)}, bf16[3,16,256]{2,1,0:T(8,128)(2,1)S(1)}, u32[]{:S(2)}, u32[]{:S(2)}) collective-permute-start(bf16[3,16,256]{2,1,0:T(8,128)(2,1)S(1)} %slice.4), channel_id=1, source_target_pairs={{0,1},{1,2},{2,3},{3,4},{4,5},{5,6},{6,7},{7,8},{8,9},{9,10},{10,1... | collective-permute-start | bytes 73736 | tf_op jit(solution)/shard_map/ppermute | solution.py:415
  14.1 3.4 %collective-permute-done.before = bf16[3,16,256]{2,1,0:T(8,128)(2,1)S(1)} collective-permute-done((bf16[3,16,256]{2,1,0:T(8,128)(2,1)S(1)}, bf16[3,16,256]{2,1,0:T(8,128)(2,1)S(1)}, u32[]{:S(2)}, u32[]{:S(2)}) %collective-permute-start) | collective-permute-done | bytes 24608 | tf_op jit(solution)/shard_map/ppermute | solution.py:415
  17.5 0.0 copy-start
  17.5 1.1 copy-done
  18.7 0.7 copy-done.3
  19.4 0.7 copy-done.5
  20.1 1.3 %forward.1 = bf16[512,256]{1,0:T(8,128)(2,1)S(1)} custom-call(bf16[3,16,256]{2,1,0:T(8,128)(2,1)S(1)} %collective-permute-done.before, bf16[3,512,256]{2,1,0:T(8,128)(2,1)S(1)} %bitcast.13, f32[3,7,256]{2,1,0:T(8,128)S(1)} %copy-done.3, f32[7,256]{1,0:T(8,128)S(1)} %copy-done.5), custom_call_target="tpu_custom_call" | custom-call | flops 7864320 | bytes 1048576 | tf_op jit(solution)/shard_map/forward/pallas_call | solution.py:99
  21.4 12.3 %all_gather.15 = bf16[512,512]{1,0:T(8,128)(2,1)S(1)} all-gather(bf16[512,256]{1,0:T(8,128)(2,1)S(1)} %forward.1), channel_id=1, replica_groups=mesh['row'=8,'col'=2,'x'=4,'zl'=4,'core'=2] {'col'}, dimensions={1}, use_global_device_ids=true | all-gather | bytes 786432 | tf_op jit(solution)/shard_map/all_gather | solution.py:433
  33.7 0.2 copy.12
  34.0 3.0 %collective-permute-start.1 = (bf16[256,512]{1,0:T(8,128)(2,1)S(1)}, bf16[256,512]{1,0:T(8,128)(2,1)S(1)}, u32[]{:S(2)}, u32[]{:S(2)}) collective-permute-start(bf16[256,512]{1,0:T(8,128)(2,1)S(1)} %bitcast.22), channel_id=1, source_target_pairs={{0,1},{1,0},{2,3},{3,2},{4,5},{5,4},{6,7},{7,6},{8,9},{9,8},{10,11... | collective-permute-start | bytes 786440 | tf_op jit(solution)/shard_map/ppermute | solution.py:410
  37.0 1.1 collective-permute-done.1.other
  38.1 22.5 %all-gather.4.cloned.1.call-done = bf16[8192,256]{1,0:T(8,128)(2,1)} async-done(((bf16[512,256]{1,0:T(8,128)(2,1)}), bf16[8192,256]{1,0:T(8,128)(2,1)}) %all-gather.4.cloned.1.call-update) | async-done | bytes 4194320 | tf_op jit(solution)/shard_map/all_gather | solution.py:428
  60.6 2.2 %copy-done.7 = bf16[8192,256]{1,0:T(8,128)(2,1)S(1)} copy-done((bf16[8192,256]{1,0:T(8,128)(2,1)S(1)}, bf16[8192,256]{1,0:T(8,128)(2,1)}, u32[]{:S(2)}) %copy-start.7) | copy-done | bytes 4194328
  62.8 5.1 %products.1 = (bf16[512,256]{1,0:T(8,128)(2,1)S(1)}, f32[512,256]{1,0:T(8,128)S(1)}, bf16[4,8,64,256]{3,2,1,0:T(8,128)(2,1)}, f32[8,128]{1,0:T(8,128)S(1)}) custom-call(s32[1]{0:T(128)} %bitcast.1.col, s32[1]{0:T(128)} %bitcast.2.core, bf16[256,512]{1,0:T(8,128)(2,1)S(1)} %bitcast.16, bf16[256,512]{1,0:T(8,128)(2,1)S(1)} %collective-permute-done.1.other, ...), custom_call_target="tpu_custom_call" | custom-call | flops 2147483648 | bytes 6815744 | tf_op jit(solution)/shard_map/products/pallas_call | solution.py:295
  67.9 0.0 reduce-scatter.2.cloned.1.call-update
  67.9 14.3 %all-gather.1 = bf16[1024,256]{1,0:T(8,128)(2,1)S(1)} all-gather(bf16[512,256]{1,0:T(8,128)(2,1)S(1)} %get-tuple-element.21), channel_id=3, replica_groups=mesh['row'=8,'col'=2,'x'=4,'zl'=4,'core'=2] {'col'}, dimensions={0}, use_global_device_ids=true | all-gather | bytes 786432 | tf_op jit(solution)/shard_map/all_gather | solution.py:444
  82.2 0.0 copy-done.1
  82.2 0.0 copy-done.4
  82.2 0.0 copy-done.6
  82.2 3.7 %backward.1 = (bf16[3,512,256]{2,1,0:T(8,128)(2,1)}, f32[3,16,256]{2,1,0:T(8,128)S(1)}, f32[3,16,256]{2,1,0:T(8,128)S(1)}, bf16[8,2,16,256]{3,2,1,0:T(8,128)(2,1)S(1)}) custom-call(s32[1]{0:T(128)} %bitcast.1.col, f32[512,256]{1,0:T(8,128)S(1)} %get-tuple-element.20.near, bf16[2,512,256]{2,1,0:T(8,128)(2,1)S(1)} %bitcast.15, ...), custom_call_target="tpu_custom_call" | custom-call | flops 20971520 | bytes 2621440 | tf_op jit(solution)/shard_map/backward/pallas_call | solution.py:217
  85.9 12.0 %all_to_all.10.taps = bf16[8,2,16,256]{3,2,1,0:T(8,128)(2,1)S(1)} all-to-all(bf16[8,2,16,256]{3,2,1,0:T(8,128)(2,1)S(1)} %get-tuple-element.23), channel_id=1, replica_groups=mesh['row'=8,'col'=2,'x'=4,'zl'=4,'core'=2] {'x','core'}, dimensions={0} | all-to-all | bytes 262144 | tf_op jit(solution)/shard_map/all_to_all | solution.py:449
  98.0 0.9 copy-done.2
  98.9 0.8 middle.1
  99.7 6.5 %all-to-all-start.1 = ((bf16[4,10,16,256]{3,2,1,0:T(8,128)(2,1)}), bf16[4,10,16,256]{3,2,1,0:T(8,128)(2,1)S(1)}, u32[]{:S(2)}, u32[]{:S(2)}) async-start(bf16[4,10,16,256]{3,2,1,0:T(8,128)(2,1)} %get-tuple-element.26), calls=%async_computation.2 | async-start | bytes 655360 | tf_op jit(solution)/shard_map/all_to_all | solution.py:452
  106.2 3.0 %collective-permute-start.2 = (bf16[3,16,256]{2,1,0:T(8,128)(2,1)S(1)}, bf16[3,16,256]{2,1,0:T(8,128)(2,1)S(1)}, u32[]{:S(2)}, u32[]{:S(2)}) collective-permute-start(bf16[3,16,256]{2,1,0:T(8,128)(2,1)S(1)} %get-tuple-element.28), channel_id=1, source_target_pairs={{1,0},{2,1},{3,2},{4,3},{5,4},{6,5},{7,6},{8,7},{9,8},{10,9},{11,1... | collective-permute-start | bytes 73736 | tf_op jit(solution)/shard_map/ppermute | solution.py:415
  109.2 4.7 %collective-permute-done.2.refs_4_ = bf16[3,16,256]{2,1,0:T(8,128)(2,1)S(1)} collective-permute-done((bf16[3,16,256]{2,1,0:T(8,128)(2,1)S(1)}, bf16[3,16,256]{2,1,0:T(8,128)(2,1)S(1)}, u32[]{:S(2)}, u32[]{:S(2)}) %collective-permute-start.2) | collective-permute-done | bytes 24608 | tf_op jit(solution)/shard_map/ppermute | solution.py:415
  113.9 0.9 all-to-all-done.1.refs_2_
  114.8 0.7 last.1
  (9 shorter events, 0.1 us)
Async XLA Ops:
  7.2 53.5 %all-gather.4.cloned.1.call-start = ((), (), s32[]{:S(2)}) async-start(), calls=%async_computation.4 | async-start | bytes 4456448 | tf_op jit(solution)/shard_map/all_gather | solution.py:428
  7.9 90.1 %reduce-scatter.2.cloned.1.call-start = ((), (), s32[]{:S(2)}) async-start(), calls=%async_computation.3 | async-start | bytes 1310720 | tf_op jit(solution)/shard_map/reduce_scatter | solution.py:443
  8.7 8.8 %collective-permute-start = (bf16[3,16,256]{2,1,0:T(8,128)(2,1)S(1)}, bf16[3,16,256]{2,1,0:T(8,128)(2,1)S(1)}, u32[]{:S(2)}, u32[]{:S(2)}) collective-permute-start(bf16[3,16,256]{2,1,0:T(8,128)(2,1)S(1)} %slice.4), channel_id=1, source_target_pairs={{0,1},{1,2},{2,3},{3,4},{4,5},{5,6},{6,7},{7,8},{8,9},{9,10},{10,1... | collective-permute-start | bytes 73736 | tf_op jit(solution)/shard_map/ppermute | solution.py:415
  17.5 1.1 copy-start
  18.7 0.7 copy-start.3
  19.4 0.7 copy-start.5
  34.0 4.1 %collective-permute-start.1 = (bf16[256,512]{1,0:T(8,128)(2,1)S(1)}, bf16[256,512]{1,0:T(8,128)(2,1)S(1)}, u32[]{:S(2)}, u32[]{:S(2)}) collective-permute-start(bf16[256,512]{1,0:T(8,128)(2,1)S(1)} %bitcast.22), channel_id=1, source_target_pairs={{0,1},{1,0},{2,3},{3,2},{4,5},{5,4},{6,7},{7,6},{8,9},{9,8},{10,11... | collective-permute-start | bytes 786440 | tf_op jit(solution)/shard_map/ppermute | solution.py:410
  60.6 2.2 %copy-start.7 = (bf16[8192,256]{1,0:T(8,128)(2,1)S(1)}, bf16[8192,256]{1,0:T(8,128)(2,1)}, u32[]{:S(2)}) copy-start(bf16[8192,256]{1,0:T(8,128)(2,1)} %all-gather.4.cloned.1.call-done) | copy-start | bytes 12582916
  62.8 19.4 %copy-start.1 = (bf16[512,3,256]{2,0,1:T(8,128)(2,1)S(1)}, bf16[512,3,256]{2,0,1:T(8,128)(2,1)}, u32[]{:S(2)}) copy-start(bf16[512,3,256]{2,0,1:T(8,128)(2,1)} %param.5) | copy-start | bytes 2359300
  62.8 19.4 %copy-start.4 = (f32[3,7,256]{2,1,0:T(8,128)S(1)}, f32[3,7,256]{2,1,0:T(8,128)}, u32[]{:S(2)}) copy-start(f32[3,7,256]{2,1,0:T(8,128)} %feat_taps.3) | copy-start | bytes 64516
  62.8 19.4 %copy-start.6 = (f32[7,256]{1,0:T(8,128)S(1)}, f32[7,256]{1,0:T(8,128)}, u32[]{:S(2)}) copy-start(f32[7,256]{1,0:T(8,128)} %inner_taps.3) | copy-start | bytes 21508
  98.0 1.0 copy-start.2
  99.7 15.1 %all-to-all-start.1 = ((bf16[4,10,16,256]{3,2,1,0:T(8,128)(2,1)}), bf16[4,10,16,256]{3,2,1,0:T(8,128)(2,1)S(1)}, u32[]{:S(2)}, u32[]{:S(2)}) async-start(bf16[4,10,16,256]{3,2,1,0:T(8,128)(2,1)} %get-tuple-element.26), calls=%async_computation.2 | async-start | bytes 655360 | tf_op jit(solution)/shard_map/all_to_all | solution.py:452
  106.2 7.7 %collective-permute-start.2 = (bf16[3,16,256]{2,1,0:T(8,128)(2,1)S(1)}, bf16[3,16,256]{2,1,0:T(8,128)(2,1)S(1)}, u32[]{:S(2)}, u32[]{:S(2)}) collective-permute-start(bf16[3,16,256]{2,1,0:T(8,128)(2,1)S(1)} %get-tuple-element.28), channel_id=1, source_target_pairs={{1,0},{2,1},{3,2},{4,3},{5,4},{6,5},{7,6},{8,7},{9,8},{10,9},{11,1... | collective-permute-start | bytes 73736 | tf_op jit(solution)/shard_map/ppermute | solution.py:415
Sparse Core Ops, SparseCore 0:
  10.1 50.4 all-gather.3
  68.0 25.8 reduce-scatter.1

commit v14 on v13

--- a/solution.py
+++ b/solution.py
@@ -323,9 +323,11 @@
     return jnp.concatenate([tiles[:, :8], tiles[:, 8:]], axis=0)
 
 
-def middle_kernel(pair, taps, head, out, out_taps, out_head):
+def middle_kernel(pair, taps, head, out, out_taps, out_head, held, sem):
     parts, _, size, _ = out.shape
     blocks = pair.shape[0]
+    copy_in = pltpu.make_async_copy(pair, held, sem)
+    copy_in.start()
     sums = parted(taps[0])
     for copy in range(1, taps.shape[0]):
         sums = sums + parted(taps[copy])
@@ -333,8 +335,10 @@
     out_head[...] = head[...].astype(BF16)
     both = paired(sums)
     for part in range(parts):
-        out[part, 0:blocks] = pair[:, part * size : (part + 1) * size, :]
         out[part, blocks:] = both
+    copy_in.wait()
+    for part in range(parts):
+        out[part, 0:blocks] = held[:, part * size : (part + 1) * size, :]
 
 
 def middle(parts, pair, taps, head):
@@ -350,10 +354,11 @@
         "middle",
         4 * pair.size,
         4 * pair.size,
-        in_specs=[IN_VMEM] * 3,
+        in_specs=[IN_HBM, IN_VMEM, IN_VMEM],
         out_specs=[IN_VMEM] * 3,
         out_shape=outs,
-    )(pair, taps, head)
+        scratch_shapes=[pltpu.VMEM(pair.shape, pair.dtype), pltpu.SemaphoreType.DMA],
+    )(in_hbm(pair), taps, head)
 
 
 def last_kernel(

time: 124 us -> 124 us (level)
    unnamed x16 -> x14, local copies, waits for them, and re-layouts: 5.72 us -> 4.76 us
where the time goes in v14:
time: 124 us; the launch traced here: 122 us
  blocking collectives  38.7 us (31%)
  waiting for transfers between devices  33.4 us (27%)
  starting transfers between devices  18 us (15%)
  between operations  14.1 us (11%)
  Pallas kernels  12.5 us (10%)
  local copies, waits for them, and re-layouts  5.77 us (5%)
    all_gather x1, waiting for transfers between devices, body(): grads = lax.all_gather(out_grad, ('row', 'core'), axis=0)  22.5 us
    all_gather x1, blocking collectives, body(): far = lax.all_gather(far, 'col', axis=0)  14.3 us
    all_gather x1, blocking collectives, body(): both = lax.all_gather(gated, 'col', axis=1, tiled=True)  12.3 us
    all_to_all x1, blocking collectives, body(): taps = lax.all_to_all(taps, ('x', 'core'), split_axis=0, concat_axis=0)  12 us
    ppermute x2, starting transfers between devices, ctx_shift(): lax.ppermute(value, CTX, [(i, i + steps) for i in range(count) if 0 <= i...  8.42 us
    ppermute x2, waiting for transfers between devices, ctx_shift(): lax.ppermute(value, CTX, [(i, i + steps) for i in range(count) if 0 <= i...  8.12 us
    all_to_all x1, starting transfers between devices, body(): pieces = lax.all_to_all(pieces, 'zl', split_axis=0, concat_axis=0)  6.49 us
    pallas_call x1, Pallas kernels, products(): call(products_kernel, 'products', 4 * rows * (channels + half) * blocks *...  5.06 us
  transfers between devices with their start and end apart: 6, of which 5 were waited for; matrix products, arithmetic and copies ran while one was open for 1% of the time, Pallas kernels for 4%

profile of v14, /device:TPU:1, one launch (start us, length us, event | category | flops | bytes accessed | tf_op | source)
XLA Modules:
  0.0 122.4 jit_solution(1029923183869172831)
XLA Ops:
  7.2 0.0 all-gather.4.cloned.1.call-start
  7.2 0.7 all-gather.4.cloned.1.call-update
  7.9 0.0 reduce-scatter.2.cloned.1.call-start
  7.9 0.7 slice.4
  8.7 5.4 %collective-permute-start = (bf16[3,16,256]{2,1,0:T(8,128)(2,1)S(1)}, bf16[3,16,256]{2,1,0:T(8,128)(2,1)S(1)}, u32[]{:S(2)}, u32[]{:S(2)}) collective-permute-start(bf16[3,16,256]{2,1,0:T(8,128)(2,1)S(1)} %slice.4), channel_id=1, source_target_pairs={{0,1},{1,2},{2,3},{3,4},{4,5},{5,6},{6,7},{7,8},{8,9},{9,10},{10,1... | collective-permute-start | bytes 73736 | tf_op jit(solution)/shard_map/ppermute | solution.py:420
  14.1 3.4 %collective-permute-done.before = bf16[3,16,256]{2,1,0:T(8,128)(2,1)S(1)} collective-permute-done((bf16[3,16,256]{2,1,0:T(8,128)(2,1)S(1)}, bf16[3,16,256]{2,1,0:T(8,128)(2,1)S(1)}, u32[]{:S(2)}, u32[]{:S(2)}) %collective-permute-start) | collective-permute-done | bytes 24608 | tf_op jit(solution)/shard_map/ppermute | solution.py:420
  17.5 0.0 copy-start
  17.5 1.1 copy-done
  18.7 0.0 copy-start.2
  18.7 0.7 copy-done.2
  19.4 0.7 copy-done.4
  20.1 1.3 %forward.1 = bf16[512,256]{1,0:T(8,128)(2,1)S(1)} custom-call(bf16[3,16,256]{2,1,0:T(8,128)(2,1)S(1)} %collective-permute-done.before, bf16[3,512,256]{2,1,0:T(8,128)(2,1)S(1)} %bitcast.13, f32[3,7,256]{2,1,0:T(8,128)S(1)} %copy-done.2, f32[7,256]{1,0:T(8,128)S(1)} %copy-done.4), custom_call_target="tpu_custom_call" | custom-call | flops 7864320 | bytes 1048576 | tf_op jit(solution)/shard_map/forward/pallas_call | solution.py:99
  21.4 12.3 %all_gather.15 = bf16[512,512]{1,0:T(8,128)(2,1)S(1)} all-gather(bf16[512,256]{1,0:T(8,128)(2,1)S(1)} %forward.1), channel_id=1, replica_groups=mesh['row'=8,'col'=2,'x'=4,'zl'=4,'core'=2] {'col'}, dimensions={1}, use_global_device_ids=true | all-gather | bytes 786432 | tf_op jit(solution)/shard_map/all_gather | solution.py:438
  33.7 0.2 copy.12
  34.0 3.0 %collective-permute-start.1 = (bf16[256,512]{1,0:T(8,128)(2,1)S(1)}, bf16[256,512]{1,0:T(8,128)(2,1)S(1)}, u32[]{:S(2)}, u32[]{:S(2)}) collective-permute-start(bf16[256,512]{1,0:T(8,128)(2,1)S(1)} %bitcast.21), channel_id=1, source_target_pairs={{0,1},{1,0},{2,3},{3,2},{4,5},{5,4},{6,7},{7,6},{8,9},{9,8},{10,11... | collective-permute-start | bytes 786440 | tf_op jit(solution)/shard_map/ppermute | solution.py:415
  37.0 1.1 collective-permute-done.1.other
  38.1 22.5 %all-gather.4.cloned.1.call-done = bf16[8192,256]{1,0:T(8,128)(2,1)} async-done(((bf16[512,256]{1,0:T(8,128)(2,1)}), bf16[8192,256]{1,0:T(8,128)(2,1)}) %all-gather.4.cloned.1.call-update) | async-done | bytes 4194320 | tf_op jit(solution)/shard_map/all_gather | solution.py:433
  60.6 2.2 %copy-done.6 = bf16[8192,256]{1,0:T(8,128)(2,1)S(1)} copy-done((bf16[8192,256]{1,0:T(8,128)(2,1)S(1)}, bf16[8192,256]{1,0:T(8,128)(2,1)}, u32[]{:S(2)}) %copy-start.6) | copy-done | bytes 4194328
  62.8 5.1 %products.1 = (bf16[512,256]{1,0:T(8,128)(2,1)S(1)}, f32[512,256]{1,0:T(8,128)S(1)}, bf16[4,8,64,256]{3,2,1,0:T(8,128)(2,1)}, f32[8,128]{1,0:T(8,128)S(1)}) custom-call(s32[1]{0:T(128)} %bitcast.1.col, s32[1]{0:T(128)} %bitcast.2.core, bf16[256,512]{1,0:T(8,128)(2,1)S(1)} %bitcast.16, bf16[256,512]{1,0:T(8,128)(2,1)S(1)} %collective-permute-done.1.other, ...), custom_call_target="tpu_custom_call" | custom-call | flops 2147483648 | bytes 6815744 | tf_op jit(solution)/shard_map/products/pallas_call | solution.py:295
  67.9 0.0 reduce-scatter.2.cloned.1.call-update
  67.9 14.3 %all-gather.1 = bf16[1024,256]{1,0:T(8,128)(2,1)S(1)} all-gather(bf16[512,256]{1,0:T(8,128)(2,1)S(1)} %get-tuple-element.21), channel_id=3, replica_groups=mesh['row'=8,'col'=2,'x'=4,'zl'=4,'core'=2] {'col'}, dimensions={0}, use_global_device_ids=true | all-gather | bytes 786432 | tf_op jit(solution)/shard_map/all_gather | solution.py:449
  82.2 0.0 copy-done.1
  82.2 0.0 copy-done.3
  82.2 0.0 copy-done.5
  82.2 3.7 %backward.1 = (bf16[3,512,256]{2,1,0:T(8,128)(2,1)}, f32[3,16,256]{2,1,0:T(8,128)S(1)}, f32[3,16,256]{2,1,0:T(8,128)S(1)}, bf16[8,2,16,256]{3,2,1,0:T(8,128)(2,1)S(1)}) custom-call(s32[1]{0:T(128)} %bitcast.1.col, f32[512,256]{1,0:T(8,128)S(1)} %get-tuple-element.20.near, bf16[2,512,256]{2,1,0:T(8,128)(2,1)S(1)} %bitcast.15, ...), custom_call_target="tpu_custom_call" | custom-call | flops 20971520 | bytes 2621440 | tf_op jit(solution)/shard_map/backward/pallas_call | solution.py:217
  85.9 12.0 %all_to_all.10.taps = bf16[8,2,16,256]{3,2,1,0:T(8,128)(2,1)S(1)} all-to-all(bf16[8,2,16,256]{3,2,1,0:T(8,128)(2,1)S(1)} %get-tuple-element.23), channel_id=1, replica_groups=mesh['row'=8,'col'=2,'x'=4,'zl'=4,'core'=2] {'x','core'}, dimensions={0} | all-to-all | bytes 262144 | tf_op jit(solution)/shard_map/all_to_all | solution.py:454
  98.0 1.7 %middle.1 = (bf16[4,10,16,256]{3,2,1,0:T(8,128)(2,1)}, f32[4,8,256]{2,1,0:T(8,128)S(1)}, bf16[3,16,256]{2,1,0:T(8,128)(2,1)S(1)}) custom-call(bf16[8,64,256]{2,1,0:T(8,128)(2,1)} %bitcast.22, bf16[8,2,16,256]{3,2,1,0:T(8,128)(2,1)S(1)} %all_to_all.10.taps, f32[3,16,256]{2,1,0:T(8,128)S(1)} %get-tuple-element.24.head), custom_call_target="tpu_custom_call" | custom-call | flops 524288 | bytes 524288 | tf_op jit(solution)/shard_map/middle/pallas_call | solution.py:352
  99.7 6.5 %all-to-all-start.1 = ((bf16[4,10,16,256]{3,2,1,0:T(8,128)(2,1)}), bf16[4,10,16,256]{3,2,1,0:T(8,128)(2,1)S(1)}, u32[]{:S(2)}, u32[]{:S(2)}) async-start(bf16[4,10,16,256]{3,2,1,0:T(8,128)(2,1)} %get-tuple-element.26), calls=%async_computation.2 | async-start | bytes 655360 | tf_op jit(solution)/shard_map/all_to_all | solution.py:457
  106.2 3.0 %collective-permute-start.2 = (bf16[3,16,256]{2,1,0:T(8,128)(2,1)S(1)}, bf16[3,16,256]{2,1,0:T(8,128)(2,1)S(1)}, u32[]{:S(2)}, u32[]{:S(2)}) collective-permute-start(bf16[3,16,256]{2,1,0:T(8,128)(2,1)S(1)} %get-tuple-element.28), channel_id=1, source_target_pairs={{1,0},{2,1},{3,2},{4,3},{5,4},{6,5},{7,6},{8,7},{9,8},{10,9},{11,1... | collective-permute-start | bytes 73736 | tf_op jit(solution)/shard_map/ppermute | solution.py:420
  109.2 4.7 %collective-permute-done.2.refs_4_ = bf16[3,16,256]{2,1,0:T(8,128)(2,1)S(1)} collective-permute-done((bf16[3,16,256]{2,1,0:T(8,128)(2,1)S(1)}, bf16[3,16,256]{2,1,0:T(8,128)(2,1)S(1)}, u32[]{:S(2)}, u32[]{:S(2)}) %collective-permute-start.2) | collective-permute-done | bytes 24608 | tf_op jit(solution)/shard_map/ppermute | solution.py:420
  113.9 0.9 all-to-all-done.1.refs_2_
  114.8 0.7 last.1
  (7 shorter events, 0.1 us)
Async XLA Ops:
  7.2 53.5 %all-gather.4.cloned.1.call-start = ((), (), s32[]{:S(2)}) async-start(), calls=%async_computation.4 | async-start | bytes 4456448 | tf_op jit(solution)/shard_map/all_gather | solution.py:433
  7.9 90.1 %reduce-scatter.2.cloned.1.call-start = ((), (), s32[]{:S(2)}) async-start(), calls=%async_computation.3 | async-start | bytes 1310720 | tf_op jit(solution)/shard_map/reduce_scatter | solution.py:448
  8.7 8.8 %collective-permute-start = (bf16[3,16,256]{2,1,0:T(8,128)(2,1)S(1)}, bf16[3,16,256]{2,1,0:T(8,128)(2,1)S(1)}, u32[]{:S(2)}, u32[]{:S(2)}) collective-permute-start(bf16[3,16,256]{2,1,0:T(8,128)(2,1)S(1)} %slice.4), channel_id=1, source_target_pairs={{0,1},{1,2},{2,3},{3,4},{4,5},{5,6},{6,7},{7,8},{8,9},{9,10},{10,1... | collective-permute-start | bytes 73736 | tf_op jit(solution)/shard_map/ppermute | solution.py:420
  17.5 1.1 copy-start
  18.7 0.7 copy-start.2
  19.4 0.7 copy-start.4
  34.0 4.1 %collective-permute-start.1 = (bf16[256,512]{1,0:T(8,128)(2,1)S(1)}, bf16[256,512]{1,0:T(8,128)(2,1)S(1)}, u32[]{:S(2)}, u32[]{:S(2)}) collective-permute-start(bf16[256,512]{1,0:T(8,128)(2,1)S(1)} %bitcast.21), channel_id=1, source_target_pairs={{0,1},{1,0},{2,3},{3,2},{4,5},{5,4},{6,7},{7,6},{8,9},{9,8},{10,11... | collective-permute-start | bytes 786440 | tf_op jit(solution)/shard_map/ppermute | solution.py:415
  60.6 2.2 %copy-start.6 = (bf16[8192,256]{1,0:T(8,128)(2,1)S(1)}, bf16[8192,256]{1,0:T(8,128)(2,1)}, u32[]{:S(2)}) copy-start(bf16[8192,256]{1,0:T(8,128)(2,1)} %all-gather.4.cloned.1.call-done) | copy-start | bytes 12582916
  62.8 19.4 %copy-start.1 = (bf16[512,3,256]{2,0,1:T(8,128)(2,1)S(1)}, bf16[512,3,256]{2,0,1:T(8,128)(2,1)}, u32[]{:S(2)}) copy-start(bf16[512,3,256]{2,0,1:T(8,128)(2,1)} %param.5) | copy-start | bytes 2359300
  62.8 19.4 %copy-start.3 = (f32[3,7,256]{2,1,0:T(8,128)S(1)}, f32[3,7,256]{2,1,0:T(8,128)}, u32[]{:S(2)}) copy-start(f32[3,7,256]{2,1,0:T(8,128)} %feat_taps.3) | copy-start | bytes 64516
  62.8 19.4 %copy-start.5 = (f32[7,256]{1,0:T(8,128)S(1)}, f32[7,256]{1,0:T(8,128)}, u32[]{:S(2)}) copy-start(f32[7,256]{1,0:T(8,128)} %inner_taps.3) | copy-start | bytes 21508
  99.7 15.1 %all-to-all-start.1 = ((bf16[4,10,16,256]{3,2,1,0:T(8,128)(2,1)}), bf16[4,10,16,256]{3,2,1,0:T(8,128)(2,1)S(1)}, u32[]{:S(2)}, u32[]{:S(2)}) async-start(bf16[4,10,16,256]{3,2,1,0:T(8,128)(2,1)} %get-tuple-element.26), calls=%async_computation.2 | async-start | bytes 655360 | tf_op jit(solution)/shard_map/all_to_all | solution.py:457
  106.2 7.7 %collective-permute-start.2 = (bf16[3,16,256]{2,1,0:T(8,128)(2,1)S(1)}, bf16[3,16,256]{2,1,0:T(8,128)(2,1)S(1)}, u32[]{:S(2)}, u32[]{:S(2)}) collective-permute-start(bf16[3,16,256]{2,1,0:T(8,128)(2,1)S(1)} %get-tuple-element.28), channel_id=1, source_target_pairs={{1,0},{2,1},{3,2},{4,3},{5,4},{6,5},{7,6},{8,7},{9,8},{10,9},{11,1... | collective-permute-start | bytes 73736 | tf_op jit(solution)/shard_map/ppermute | solution.py:420
Sparse Core Ops, SparseCore 0:
  10.1 50.4 all-gather.3
  68.0 25.8 reduce-scatter.1
